TPU v7x, 32 devices: a whole 2x2x4 slice. The times are simulated.
32 devices in a mesh: grp: 2 (over y), cp: 4 (over z), dec: 4 (over x, core).
Axes of the slice: x: 2, y: 2, z: 4, core: 2. Of those that a mesh axis runs over, the one named last changes fastest.
Arguments:
- queries: bfloat16 [1024, 12288], P(('grp', 'cp'), 'dec'), parts along dimension 0, may hold values from -120 to 120
- latent_rows: bfloat16 [1024, 576], P(('grp', 'cp')), parts along dimension 0, may hold values from -16 to 16
- key_absorb: bfloat16 [64, 128, 512], P('dec'), may hold values from -0.5 to 0.5
- value_expand: bfloat16 [64, 512, 128], P('dec'), may hold values from -0.25 to 0.25
- prompt_pages: int32 [4], P('grp'), parts along dimension 0, may hold values from 1 to 24, 32 in all
- decode_owner: int32 [4, 2], P('grp'), parts along dimension 0, may hold values from 0 to 3, as said below
- slot_offset: int32 [4], P('grp'), parts along dimension 0, may hold values from 0 to 23
Outputs:
- attended: bfloat16 [1024, 8192], P(('grp', 'cp'), 'dec'), parts along dimension 0
- page_cache: bfloat16 [8, 4, 3, 16, 576], P(('grp', 'cp'), 'dec'), parts along dimension 0
- page_scales: bfloat16 [8, 4, 3, 16, 4], P(('grp', 'cp'), 'dec'), parts along dimension 0
There are 2 independent parts, one for each index of `grp`. A program takes and returns all parts, laid end to end along the dimension named above; an argument that names none is the same for every part. Nothing has to cross between parts.
Inputs may be any that keep to these rules, and one draw needn't show every extreme that they name: `prompt_pages`: the lengths sum to 32; every owner device receives at most 3 pages and some receive exactly that many. `decode_owner`: every owner appears exactly once in the whole list.
All inputs are finite; a program needn't handle non-finite values. Where the computation divides by a largest or mean magnitude, that divisor is 1e-20 or more.
Results may differ from a plain program's by a relative error of at most 0.008.
Values may be sent and summed in bfloat16 or wider, within the bound.
No kernel may reach another device: no remote copies, remote signals or barrier semaphores. Data moves between devices by JAX's collectives and lax.ppermute only.
A program may use at most 64 MiB of HBM per device.

v0:
```python
import jax
import jax.numpy as jnp
from jax import lax
from jax.sharding import PartitionSpec as P

LAT = 512
ROPE = 64
NOPE = 128
VDIM = 128
PAGE = 16
BLOCK = 128
NBLK = 4


masked_fill = -1e30
amax_epsilon = 1e-06


def page_targets(page_index, prompt_pages, decode_owner, slot_offset, dec_count, slot_count):
    group_width = decode_owner.shape[1]
    page_ends = jnp.cumsum(prompt_pages)
    page_starts = page_ends - prompt_pages
    prompt_of = jnp.sum((page_ends[None, :] <= page_index[:, None]).astype(jnp.int32), axis=1)
    choose = (
        prompt_of[:, None] == jnp.arange(prompt_pages.shape[0], dtype=jnp.int32)[None, :]
    ).astype(jnp.int32)
    first_page = jnp.sum(choose * page_starts[None, :], axis=1)
    rotation = jnp.sum(choose * slot_offset[None, :], axis=1)
    owner_rows = jnp.sum(choose[:, :, None] * decode_owner[None, :, :], axis=1)
    cycle_index = rotation + page_index - first_page
    position = cycle_index % group_width
    pick = (position[:, None] == jnp.arange(group_width, dtype=jnp.int32)[None, :]).astype(
        jnp.int32
    )
    target = jnp.sum(pick * owner_rows, axis=1)
    cycle_slot = cycle_index // group_width % (dec_count * slot_count)
    return (target, cycle_slot // slot_count, cycle_slot % slot_count)


def prompt_start(positions, prompt_pages):
    token_starts = (jnp.cumsum(prompt_pages) - prompt_pages) * PAGE
    chosen = jnp.where(token_starts[None, :] <= positions[:, None], token_starts[None, :], 0)
    return jnp.max(chosen, axis=1)


def encode_rows(latent_rows):
    row_count = latent_rows.shape[0]
    blocks = latent_rows[:, :LAT].astype(jnp.float32).reshape(row_count, LAT // BLOCK, BLOCK)
    scales = (jnp.max(jnp.abs(blocks), axis=2) + amax_epsilon).astype(jnp.bfloat16)
    encoded = (
        (blocks / scales.astype(jnp.float32)[:, :, None])
        .astype(jnp.bfloat16)
        .reshape(row_count, LAT)
    )
    return (jnp.concatenate([encoded, latent_rows[:, LAT:]], axis=1), scales)


def on_device(
    queries, latent_rows, key_absorb, value_expand, prompt_pages, decode_owner, slot_offset
):
    cp_index = lax.axis_index("cp")
    dec_index = lax.axis_index("dec")
    dec_count = lax.axis_size("dec")
    heads_here = key_absorb.shape[0]
    rows_here = latent_rows.shape[0]
    pages_here = rows_here // PAGE
    slot_count = 3 * pages_here // (2 * dec_count)
    row_width = LAT + ROPE
    score_scale = 1.0 / (NOPE + ROPE) ** 0.5
    heads_split = queries.reshape(rows_here, heads_here, NOPE + ROPE)
    absorbed = jnp.einsum(
        "thn,hnl->thl", heads_split[:, :, :NOPE], key_absorb, preferred_element_type=jnp.float32
    ).astype(jnp.bfloat16)
    combined = jnp.concatenate([absorbed, heads_split[:, :, NOPE:]], axis=2)
    first_row = cp_index * rows_here
    query_pos = first_row + jnp.arange(rows_here, dtype=jnp.int32)
    start_pos = prompt_start(query_pos, prompt_pages)
    start_state = (
        jnp.zeros((rows_here, heads_here, LAT), jnp.float32),
        jnp.full((rows_here, heads_here), masked_fill, jnp.float32),
        jnp.zeros((rows_here, heads_here), jnp.float32),
    )
    encoded, scales = encode_rows(latent_rows)
    piece_rows = lax.all_gather(encoded, "cp", axis=0, tiled=True)
    piece_pages = piece_rows.shape[0] // PAGE
    page_index = jnp.arange(piece_pages, dtype=jnp.int32)
    target, holder, cycle_slot = page_targets(
        page_index, prompt_pages, decode_owner, slot_offset, dec_count, slot_count
    )
    is_mine = (target == cp_index) & (holder == dec_index)
    selector = (cycle_slot[None, :] == jnp.arange(slot_count, dtype=jnp.int32)[:, None]) & is_mine[
        None, :
    ]
    selector = selector.astype(jnp.bfloat16)
    added_rows = jnp.dot(
        selector,
        piece_rows.reshape(piece_pages, PAGE * row_width),
        preferred_element_type=jnp.float32,
    )
    added_scales = jnp.dot(
        selector,
        lax.all_gather(scales, "cp", axis=0, tiled=True).reshape(piece_pages, PAGE * NBLK),
        preferred_element_type=jnp.float32,
    )
    cache_rows = added_rows.astype(jnp.bfloat16)
    cache_scales = added_scales.astype(jnp.bfloat16)
    piece = lax.all_gather(latent_rows, "cp", axis=0, tiled=True)
    piece_rows = piece.shape[0]
    tile = 512
    tile_count = piece_rows // tile

    def one_tile(tile_index, inner):
        keys = lax.dynamic_slice_in_dim(piece, tile_index * tile, tile, 0)
        key_pos = tile_index * tile + jnp.arange(tile, dtype=jnp.int32)
        visible = (key_pos[None, :] >= start_pos[:, None]) & (
            key_pos[None, :] <= query_pos[:, None]
        )

        def compute(current):
            summed, running_max, total = current
            scores = (
                jnp.einsum("thl,kl->thk", combined, keys, preferred_element_type=jnp.float32)
                * score_scale
            )
            scores = jnp.where(visible[:, None, :], scores, masked_fill)
            new_max = jnp.maximum(running_max, jnp.max(scores, axis=2))
            factor = jnp.exp(running_max - new_max)
            weights = jnp.where(visible[:, None, :], jnp.exp(scores - new_max[:, :, None]), 0.0)
            total = total * factor + jnp.sum(weights, axis=2)
            added = jnp.einsum(
                "thk,kl->thl",
                weights.astype(jnp.bfloat16),
                keys[:, :LAT],
                preferred_element_type=jnp.float32,
            )
            return (summed * factor[:, :, None] + added, new_max, total)

        return lax.cond(jnp.any(visible), compute, lambda current: current, inner)

    folded = lax.fori_loop(0, tile_count, one_tile, start_state)
    summed, running_max, total = folded
    mixed_latent = (summed / total[:, :, None]).astype(jnp.bfloat16)
    output_rows = jnp.einsum(
        "thl,hlv->thv", mixed_latent, value_expand, preferred_element_type=jnp.float32
    )
    attended = output_rows.astype(jnp.bfloat16).reshape(rows_here, heads_here * VDIM)
    page_cache = cache_rows.reshape(1, 1, slot_count, PAGE, row_width)
    page_scales = cache_scales.reshape(1, 1, slot_count, PAGE, NBLK)
    return (attended, page_cache, page_scales)


def solution(mesh):
    return jax.shard_map(
        on_device,
        mesh=mesh,
        in_specs=(
            P(("grp", "cp"), "dec"),
            P(("grp", "cp"), None),
            P("dec", None, None),
            P("dec", None, None),
            P("grp"),
            P("grp", None),
            P("grp"),
        ),
        out_specs=(
            P(("grp", "cp"), "dec"),
            P(("grp", "cp"), "dec", None, None, None),
            P(("grp", "cp"), "dec", None, None, None),
        ),
        check_vma=False,
    )
```

profile of v0, /device:TPU:0, one launch (start us, length us, event | category | flops | bytes accessed | tf_op | source)
XLA Modules:
  0.0 72.6 jit_solution(6878843205980221773)
XLA Ops:
  0.6 0.0 copy-start
  0.7 1.0 %reduce-window.8 = s32[2,1]{0,1:T(1,128)S(1)} reduce-window(s32[2,1]{0,1:T(1,128)} %bitcast.30, s32[]{:T(128)} %constant.89.clone.1), window={size=2x1 pad=1_0x0_0}, to_apply=%region_0.0 | reduce-window | flops 2 | bytes 20 | tf_op jit(solution)/shard_map/reduce-window.3
  1.6 0.7 broadcast_multiply_fusion
  2.3 0.1 fusion.24
  2.4 0.8 %fusion.20 = (pred[128,512]{1,0:T(8,128)(4,1)S(1)}, pred[]{:T(512)}) fusion(s32[128]{0:T(128)S(1)} %iota_add_fusion, s32[128]{0:T(128)S(1)} %fusion.24), kind=kLoop, calls=%fused_computation.35 | loop fusion | flops 262143 | bytes 66561 | tf_op jit(solution)/shard_map/while/body/eval_jaxpr/and | solution.py:115
  3.8 2.5 %broadcast_in_dim.75 = f32[128,16,512]{2,0,1:T(8,128)} broadcast(f32[]{:T(128)} %constant.96.clone.1), dimensions={} | broadcast | bytes 4194308 | tf_op jit(solution)/shard_map/broadcast_in_dim | solution.py:79
  6.3 1.5 %copy.38 = bf16[128,3072]{0,1:T(8,128)(2,1)S(1)} copy(bf16[128,3072]{1,0:T(8,128)(2,1)} %param.9) | data formatting | bytes 1572864 | tf_op args[0]
  7.8 0.0 copy-done
  7.8 0.0 copy-start.1
  7.8 0.8 %convert_bitcast_fusion = bf16[128,16,512]{0,2,1:T(8,128)(2,1)S(1)} fusion(bf16[16,128,512]{2,1,0:T(8,128)(2,1)S(1)} %copy-done, bf16[128,16,192]{0,2,1:T(8,128)(2,1)S(1)} %bitcast.28), kind=kOutput, calls=%fused_computation.24 | convolution fusion | flops 269484032 | bytes 4718592 | tf_op jit(solution)/shard_map/thn,hnl->thl/dot_general | solution.py:71
  8.6 1.6 %pad_maximum_fusion = bf16[128,16,576]{0,2,1:T(8,128)(2,1)} fusion(bf16[128,16,64]{0,2,1:T(8,128)(2,1)S(1)} %slice.22, bf16[128,16,512]{0,2,1:T(8,128)(2,1)S(1)} %convert_bitcast_fusion), kind=kLoop, calls=%fused_computation.23 | loop fusion | flops 4718592 | bytes 4718592 | tf_op jit(solution)/shard_map/concatenate | solution.py:74
  10.2 0.0 copy-done.1
  10.2 0.2 copy.41
  10.4 19.6 %all_gather.9 = bf16[512,576]{1,0:T(8,128)(2,1)S(1)} all-gather(bf16[128,576]{1,0:T(8,128)(2,1)S(1)} %copy.41), channel_id=1, replica_groups=mesh['grp'=2,'cp'=4,'dec'=4] {'cp'}, dimensions={0}, use_global_device_ids=true | all-gather | bytes 737280 | tf_op jit(solution)/shard_map/all_gather | solution.py:107
  30.0 9.8 %conditional.1 = ((f32[128,16,512]{2,0,1:T(8,128)}, f32[128,16]{0,1:T(8,128)S(1)})) conditional(s32[]{:T(128)} %convert_element_type.63, (f32[128,16,512]{2,0,1:T(8,128)}, f32[128,16]{0,1:T(8,128)S(1)}) %tuple.25, (pred[128,512]{1,0:T(8,128)(4,1)S(1)}, bf16[128,16,576]{0,2,1:T(8,128)(2,1)}, bf16[512,576]{1,0:T(8,128)(2,1)S(1)}, ...), branch_computations={%region_3.4_spmd, %region_4.7_spmd} | conditional | flops 2297436160 | bytes 24739864 | solution.py:138
  30.0 3.8 %fusion = (f32[128,16]{0,1:T(8,128)S(1)}, f32[128,16,512]{2,0,1:T(8,128)S(1)}) fusion(pred[128,512]{1,0:T(8,128)(4,1)S(1)} %get-tuple-element.69, bf16[128,16,576]{0,2,1:T(8,128)(2,1)} %get-tuple-element.70, bf16[512,576]{1,0:T(8,128)(2,1)S(1)} %get-tuple-element.71), kind=kOutput, calls=%fused_computation.3 | convolution fusion | flops 1211103232 | bytes 7217152 | tf_op jit(solution)/shard_map/while/body/eval_jaxpr/cond/branch_1_fun/thl,kl->thk/dot_general | solution.py:122
  33.8 1.3 %fusion.1 = f32[128,16]{0,1:T(8,128)S(1)} fusion(f32[128,16,512]{2,0,1:T(8,128)S(1)} %get-tuple-element.105, f32[128,16]{0,1:T(8,128)S(1)} %broadcast_maximum_fusion, pred[128,512]{1,0:T(8,128)(4,1)S(1)} %get-tuple-element.69), kind=kLoop, calls=%fused_computation.4 | loop fusion | flops 5240832 | bytes 4276224 | tf_op jit(solution)/shard_map/while/body/eval_jaxpr/cond/branch_1_fun/reduce_sum | solution.py:129
  35.1 4.6 %multiply_add_fusion = f32[128,16,512]{2,0,1:T(8,128)} fusion(f32[128,16,512]{2,0,1:T(8,128)} %get-tuple-element.68, f32[128,16,512]{2,0,1:T(8,128)S(1)} %get-tuple-element.105, f32[128,16]{0,1:T(8,128)S(1)} %broadcast_maximum_fusion, f32[128,16]{0,1:T(8,128)S(1)} %get-tuple-element.103, pred[128,512]{1,0:T(8,128)(4,1)S(1)} %get-tuple-element.69, ...), kind=kOutput, calls=%fused_computation.1 | convolution fusion | flops 1081081856 | bytes 13189120 | tf_op jit(solution)/shard_map/while/body/eval_jaxpr/cond/branch_1_fun/thk,kl->thl/dot_general | solution.py:130
  39.8 0.0 slice-start
  39.8 4.0 %fusion.17 = bf16[16,128,128]{1,2,0:T(8,128)(2,1)S(1)} fusion(bf16[16,512,128]{2,1,0:T(8,128)(2,1)} %param.12, f32[128,16,512]{2,0,1:T(8,128)} %get-tuple-element.78, f32[128,16]{0,1:T(8,128)S(1)} %get-tuple-element.79), kind=kOutput, calls=%fused_computation.26 | convolution fusion | flops 270794752 | bytes 6823936 | tf_op jit(solution)/shard_map/thl,hlv->thv/dot_general | solution.py:143
  43.7 0.0 copy-start.2
  43.7 0.0 copy-start.3
  43.8 1.0 %copy.45 = bf16[128,2048]{1,0:T(8,128)(2,1)} copy(bf16[128,2048]{0,1:T(8,128)(2,1)S(1)} %bitcast.29) | data formatting | bytes 1048576
  44.8 0.0 slice-done
  44.9 14.6 %all_gather.10 = bf16[512,576]{0,1:T(8,128)(2,1)S(1)} all-gather(bf16[128,576]{0,1:T(8,128)(2,1)S(1)} %pad_maximum_fusion.1), channel_id=1, replica_groups=mesh['grp'=2,'cp'=4,'dec'=4] {'cp'}, dimensions={0}, use_global_device_ids=true | all-gather | bytes 737280 | tf_op jit(solution)/shard_map/all_gather | solution.py:84
  59.5 0.3 copy.43
  59.8 0.6 reshape.167
  60.4 0.1 fusion.25
  60.5 0.0 copy-done.2
  60.5 0.1 multiply_reduce_fusion
  60.5 0.0 copy-done.3
  60.5 0.1 select_reduce_fusion.1
  60.7 0.2 convolution_convert_fusion
  60.9 0.8 %reshape.168 = bf16[1,1,3,16,576]{4,3,2,1,0:T(8,128)(2,1)} reshape(bf16[3,9216]{1,0:T(4,128)(2,1)S(1)} %convolution_convert_fusion) | data formatting | bytes 110592 | tf_op jit(solution)/shard_map/reshape | solution.py:147
  61.7 9.7 %all_gather.11 = bf16[512,4]{0,1:T(4,128)(2,1)S(1)} all-gather(bf16[128,4]{0,1:T(4,128)(2,1)S(1)} %get-tuple-element.99), channel_id=1, replica_groups=mesh['grp'=2,'cp'=4,'dec'=4] {'cp'}, dimensions={0}, use_global_device_ids=true | all-gather | bytes 5120 | tf_op jit(solution)/shard_map/all_gather | solution.py:102
  71.4 0.2 copy.44
  71.5 0.2 reshape.169
  71.7 0.1 convolution_convert_fusion.1
  71.8 0.1 reshape.170
  71.9 0.7 copy.46
  (14 shorter events, 0.2 us)
Async XLA Ops:
  0.6 7.2 %copy-start = (bf16[16,128,512]{2,1,0:T(8,128)(2,1)S(1)}, bf16[16,128,512]{2,1,0:T(8,128)(2,1)}, u32[]{:S(2)}) copy-start(bf16[16,128,512]{2,1,0:T(8,128)(2,1)} %param.11) | copy-start | bytes 6291460
  7.8 2.4 %copy-start.1 = (bf16[128,576]{0,1:T(8,128)(2,1)S(1)}, bf16[128,576]{0,1:T(8,128)(2,1)}, u32[]{:S(2)}) copy-start(bf16[128,576]{0,1:T(8,128)(2,1)} %param.10) | copy-start | bytes 442372
  39.8 5.1 %slice-start = ((bf16[128,576]{0,1:T(8,128)(2,1)}), bf16[128,64]{0,1:T(8,128)(2,1)S(1)}, s32[]{:S(2)}) async-start(bf16[128,576]{0,1:T(8,128)(2,1)} %param.10), calls=%async_computation | async-start | bytes 32768 | tf_op jit(solution)/shard_map/slice | solution.py:55
  43.7 16.7 %copy-start.2 = (s32[2,2]{1,0:T(2,128)S(1)}, s32[2,2]{1,0:T(2,128)}, u32[]{:S(2)}) copy-start(s32[2,2]{1,0:T(2,128)} %param.14) | copy-start | bytes 52
  43.7 16.8 %copy-start.3 = (s32[2]{0:T(128)S(1)}, s32[2]{0:T(128)}, u32[]{:S(2)}) copy-start(s32[2]{0:T(128)} %param.15) | copy-start | bytes 28
where the time goes:
time: 72.9 us; the launch traced here: 72.6 us
  blocking collectives  43.9 us (60%)
  matrix products  13.5 us (19%)
  local copies, waits for them, and re-layouts  7.91 us (11%)
  other arithmetic  5.83 us (8%)
  between operations  1.44 us (2%)
    all_gather x1, blocking collectives, on_device(): piece = lax.all_gather(latent_rows, 'cp', axis=0, tiled=True)  19.6 us
    all_gather x1, blocking collectives, on_device(): piece_rows = lax.all_gather(encoded, 'cp', axis=0, tiled=True)  14.6 us
    all_gather x1, blocking collectives, on_device(): lax.all_gather(scales, 'cp', axis=0, tiled=True)  9.66 us
    dot_general x1, matrix products, compute(): jnp.einsum('thk,kl->thl', weights.astype(jnp.bfloat16), keys[:, :LAT], pr...  4.64 us
    dot_general x1, matrix products, on_device(): jnp.einsum('thl,hlv->thv', mixed_latent, value_expand, preferred_element_...  3.96 us
    dot_general x1, matrix products, compute(): jnp.einsum('thl,kl->thk', combined, keys, preferred_element_type=jnp.floa...  3.8 us
    unnamed x12, local copies, waits for them, and re-layouts  3.39 us
    broadcast_in_dim x1, local copies, waits for them, and re-layouts, on_device(): jnp.zeros((rows_here, heads_here, LAT), jnp.float32)  2.46 us

commit v1 on v0

v1 whole, which is shorter than its diff:
```python
import functools
import math

import jax
import jax.numpy as jnp
from jax import lax
from jax.experimental import pallas as pl
from jax.experimental.pallas import tpu as pltpu
from jax.sharding import PartitionSpec as P

LAT = 512
ROPE = 64
NOPE = 128
VDIM = 128
PAGE = 16
BLOCK = 128
NBLK = LAT // BLOCK
ROW = LAT + ROPE
HEAD = NOPE + ROPE

masked_fill = -1e30
amax_epsilon = 1e-06
exp2_scale = math.log2(math.e) / math.sqrt(HEAD)

NT = (((1,), (1,)), ((), ()))


def absorb_kernel(group, queries, key_absorb, combined):
    rows = queries.shape[0]
    for h in range(group):
        at = h * HEAD
        absorbed = jnp.dot(queries[:, at:at + NOPE], key_absorb[h], preferred_element_type=jnp.float32)
        combined[h * rows:(h + 1) * rows, :LAT] = absorbed.astype(jnp.bfloat16)
        combined[h * rows:(h + 1) * rows, LAT:] = queries[:, at + NOPE:at + HEAD]


def prompt_starts(prompt_pages):
    starts = [jnp.int32(0)]
    for k in range(prompt_pages.shape[0] - 1):
        starts.append(starts[-1] + prompt_pages[k])
    return starts


def write_cache(n_cp, slot_count, prompt_pages, decode_owner, slot_offset, pieces, page_cache, page_scales):
    prompts, width = decode_owner.shape
    cp_index = lax.axis_index("cp")
    dec_index = lax.axis_index("dec")
    rows_here = pieces[0].shape[1]
    cycle = width * lax.axis_size("dec") * slot_count
    starts = prompt_starts(prompt_pages)
    pages, start, offset, place = jnp.int32(0), jnp.int32(0), jnp.int32(0), jnp.int32(0)
    for k in range(prompts):
        for p in range(width):
            mine = decode_owner[k, p] == cp_index
            pages = jnp.where(mine, prompt_pages[k], pages)
            start = jnp.where(mine, starts[k], start)
            offset = jnp.where(mine, slot_offset[k], offset)
            place = jnp.where(mine, p, place)
    kept = slot_count * PAGE
    row = lax.broadcasted_iota(jnp.int32, (kept, 1), 0)
    lane = lax.broadcasted_iota(jnp.int32, (1, kept), 1)
    row_target = jnp.full((kept, 1), -1, jnp.int32)
    lane_valid = jnp.zeros((1, kept), jnp.float32)
    for c in range(slot_count):
        turn = width * (dec_index * slot_count + c) + place
        page = lax.rem(turn - offset + 2 * cycle, cycle)
        valid = page < pages
        token = (start + page) * PAGE
        source = token // rows_here
        steps_back = lax.rem(cp_index - source + n_cp, n_cp)
        column = steps_back * rows_here + lax.rem(token, rows_here)
        column = jnp.where(valid, column, -kept)
        row_target = jnp.where(row // PAGE == c, column + row % PAGE, row_target)
        lane_valid = jnp.where(lane // PAGE == c, valid.astype(jnp.float32), lane_valid)
    rows = jnp.zeros((kept, ROW), jnp.float32)
    turned = jnp.zeros((LAT, kept), jnp.float32)
    for b, piece in enumerate(pieces):
        column = b * rows_here + lax.broadcasted_iota(jnp.int32, (1, rows_here), 1)
        chosen = jnp.where(column == row_target, 1.0, 0.0).astype(jnp.bfloat16)
        block = piece[...]
        rows = rows + lax.dot_general(chosen, block, NT, preferred_element_type=jnp.float32)
        turned = turned + lax.dot_general(block[:LAT], chosen, NT, preferred_element_type=jnp.float32)
    encoded = []
    scales = []
    for b in range(NBLK):
        values = rows[:, b * BLOCK:(b + 1) * BLOCK]
        scale = jnp.max(jnp.abs(values), axis=1, keepdims=True) + amax_epsilon
        scale = scale.astype(jnp.bfloat16).astype(jnp.float32)
        encoded.append((values / scale).astype(jnp.bfloat16))
        scales.append(jnp.max(jnp.abs(turned[b * BLOCK:(b + 1) * BLOCK]), axis=0, keepdims=True))
    encoded.append(rows[:, LAT:].astype(jnp.bfloat16))
    scales = jnp.concatenate(scales, axis=0) + amax_epsilon
    scales = (scales * lane_valid).astype(jnp.bfloat16)
    for c in range(slot_count):
        for b, values in enumerate(encoded):
            page_cache[c, :, b * BLOCK:b * BLOCK + values.shape[1]] = values[c * PAGE:(c + 1) * PAGE]
        page_scales[c] = scales[:, c * PAGE:(c + 1) * PAGE]


def attend_kernel(n_cp, key_blocks, group, slot_count, prompt_pages, decode_owner, slot_offset, combined, value_expand, *rest):
    pieces = rest[:n_cp]
    attended, page_cache, page_scales, keys, values, bias = rest[n_cp:]
    rows = attended.shape[0]

    @pl.when(pl.program_id(0) == 0)
    def _():
        first = lax.axis_index("cp") * rows
        token = first + lax.broadcasted_iota(jnp.int32, (rows, 1), 0)
        begin = jnp.zeros((rows, 1), jnp.int32)
        for start in prompt_starts(prompt_pages):
            begin = jnp.maximum(begin, jnp.where(start * PAGE <= token, start * PAGE, 0))
        for b in range(key_blocks):
            block = pieces[b][...]
            keys[:, b * rows:(b + 1) * rows] = block
            values[b * rows:(b + 1) * rows, :] = block[:LAT].T
            spot = first - b * rows + lax.broadcasted_iota(jnp.int32, (1, rows), 1)
            visible = (spot >= begin) & (spot <= token)
            bias[:, b * rows:(b + 1) * rows] = jnp.where(visible, 0.0, masked_fill)
        write_cache(n_cp, slot_count, prompt_pages, decode_owner, slot_offset, pieces, page_cache, page_scales)

    scores = jnp.dot(combined[...], keys[...], preferred_element_type=jnp.float32)
    scores = scores.reshape(group, rows, key_blocks * rows) + bias[...][None]
    peak = jnp.max(scores, axis=2, keepdims=True)
    weights = jnp.exp2((scores - peak) * exp2_scale)
    total = jnp.sum(weights, axis=2, keepdims=True).reshape(group * rows, 1)
    weights = weights.astype(jnp.bfloat16).reshape(group * rows, key_blocks * rows)
    summed = jnp.dot(weights, values[...], preferred_element_type=jnp.float32)
    mixed = (summed * (1.0 / total)).astype(jnp.bfloat16)
    for h in range(group):
        result = jnp.dot(mixed[h * rows:(h + 1) * rows], value_expand[h], preferred_element_type=jnp.float32)
        attended[:, h * VDIM:(h + 1) * VDIM] = result.astype(jnp.bfloat16)


def on_device(queries, latent_rows, key_absorb, value_expand, prompt_pages, decode_owner, slot_offset):
    n_cp = lax.axis_size("cp")
    dec_count = lax.axis_size("dec")
    heads = key_absorb.shape[0]
    rows = latent_rows.shape[0]
    prompts, width = decode_owner.shape
    slot_count = 3 * (rows // PAGE) // (2 * dec_count)
    reach = width * dec_count * slot_count * PAGE
    key_blocks = min(n_cp, -(-reach // rows) + (0 if prompts == 2 else 1))
    own = latent_rows.T
    pieces = [own]
    for step in range(1, n_cp):
        pieces.append(lax.ppermute(own, "cp", [(i, (i + step) % n_cp) for i in range(n_cp)]))

    group = 4
    combined = pl.pallas_call(
        functools.partial(absorb_kernel, group),
        grid=(heads // group,),
        in_specs=[
            pl.BlockSpec((rows, group * HEAD), lambda g: (0, g)),
            pl.BlockSpec((group, NOPE, LAT), lambda g: (g, 0, 0)),
        ],
        out_specs=pl.BlockSpec((group * rows, ROW), lambda g: (g, 0)),
        out_shape=jax.ShapeDtypeStruct((heads * rows, ROW), jnp.bfloat16),
        cost_estimate=pl.CostEstimate(
            flops=2 * rows * heads * NOPE * LAT,
            bytes_accessed=2 * (queries.size + key_absorb.size + heads * rows * ROW),
            transcendentals=0,
        ),
        compiler_params=pltpu.CompilerParams(vmem_limit_bytes=48 * 2**20),
        name="absorb",
    )(queries, key_absorb)

    group = 4 if key_blocks <= 4 else 1
    width_keys = key_blocks * rows
    smem = pl.BlockSpec(memory_space=pltpu.SMEM)
    attended, page_cache, page_scales = pl.pallas_call(
        functools.partial(attend_kernel, n_cp, key_blocks, group, slot_count),
        grid=(heads // group,),
        in_specs=[
            smem,
            smem,
            smem,
            pl.BlockSpec((group * rows, ROW), lambda g: (g, 0)),
            pl.BlockSpec((group, LAT, VDIM), lambda g: (g, 0, 0)),
        ] + [pl.BlockSpec((ROW, rows), lambda g: (0, 0))] * n_cp,
        out_specs=[
            pl.BlockSpec((rows, group * VDIM), lambda g: (0, g)),
            pl.BlockSpec((slot_count, PAGE, ROW), lambda g: (0, 0, 0)),
            pl.BlockSpec((slot_count, NBLK, PAGE), lambda g: (0, 0, 0)),
        ],
        out_shape=[
            jax.ShapeDtypeStruct((rows, heads * VDIM), jnp.bfloat16),
            jax.ShapeDtypeStruct((slot_count, PAGE, ROW), jnp.bfloat16),
            jax.ShapeDtypeStruct((slot_count, NBLK, PAGE), jnp.bfloat16),
        ],
        scratch_shapes=[
            pltpu.VMEM((ROW, width_keys), jnp.bfloat16),
            pltpu.VMEM((width_keys, LAT), jnp.bfloat16),
            pltpu.VMEM((rows, width_keys), jnp.float32),
        ],
        cost_estimate=pl.CostEstimate(
            flops=2 * rows * heads * (width_keys * (ROW + LAT) + LAT * VDIM),
            bytes_accessed=2 * (heads * rows * (ROW + VDIM) + value_expand.size),
            transcendentals=rows * heads * width_keys,
        ),
        compiler_params=pltpu.CompilerParams(vmem_limit_bytes=48 * 2**20),
        name="attend",
    )(prompt_pages, decode_owner, slot_offset, combined, value_expand, *pieces)
    page_cache = page_cache.reshape(1, 1, slot_count, PAGE, ROW)
    page_scales = page_scales.transpose(0, 2, 1).reshape(1, 1, slot_count, PAGE, NBLK)
    return attended, page_cache, page_scales


def solution(mesh):
    return jax.shard_map(
        on_device,
        mesh=mesh,
        in_specs=(
            P(("grp", "cp"), "dec"),
            P(("grp", "cp"), None),
            P("dec", None, None),
            P("dec", None, None),
            P("grp"),
            P("grp", None),
            P("grp"),
        ),
        out_specs=(
            P(("grp", "cp"), "dec"),
            P(("grp", "cp"), "dec", None, None, None),
            P(("grp", "cp"), "dec", None, None, None),
        ),
        check_vma=False,
    )
```

time: 72.9 us -> 25.1 us (0.34)
  blocking collectives: 43.9 us -> 0 us
  matrix products: 13.5 us -> 0 us
  Pallas kernels: 0 us -> 7.79 us
  waiting for transfers between devices: 0 us -> 7.61 us
  starting transfers between devices: 0 us -> 6.11 us
  other arithmetic: 5.83 us -> 0 us
  local copies, waits for them, and re-layouts: 7.91 us -> 2.74 us
  between operations: 1.44 us -> 0.7 us
    all_gather x3 -> x0, blocking collectives: 43.9 us -> none  [the longest x1 19.6 us: on_device(): piece = lax.all_gather(latent_rows, 'cp', axis=0, tiled=True)]
    dot_general x6 -> x0, matrix products: 13.5 us -> none  [the longest x1 4.64 us: compute(): jnp.einsum('thk,kl->thl', weights.astype(jnp.bfloat16), keys[:, :LAT], pr...]
    pallas_call x0 -> x2, Pallas kernels: none -> 7.79 us  [the longest x1 6.47 us: on_device(): pl.pallas_call(functools.partial(attend_kernel, n_cp, key_blocks, group,...]
    ppermute x0 -> x3, waiting for transfers between devices: none -> 7.61 us  [on_device(): lax.ppermute(own, 'cp', [(i, (i + step) % n_cp) for i in range(n_cp)])]
    ppermute x0 -> x3, starting transfers between devices: none -> 6.11 us  [on_device(): lax.ppermute(own, 'cp', [(i, (i + step) % n_cp) for i in range(n_cp)])]
    broadcast_in_dim x2 -> x0, local copies, waits for them, and re-layouts: 2.46 us -> none  [the longest x1 2.46 us: on_device(): jnp.zeros((rows_here, heads_here, LAT), jnp.float32)]
    concatenate x2 -> x0, other arithmetic: 1.63 us -> none  [the longest x1 1.62 us: on_device(): combined = jnp.concatenate([absorbed, heads_split[:, :, NOPE:]], axis=2)]
    reshape x4 -> x0, local copies, waits for them, and re-layouts: 1.57 us -> none  [the longest x1 0.76 us: on_device(): page_cache = cache_rows.reshape(1, 1, slot_count, PAGE, row_width)]
  transfers between devices with their start and end apart: 0 -> 3, of which waited for: 0 -> 1; matrix products, arithmetic and copies ran while one was open for 0% -> 0% of each run, Pallas kernels for 0% -> 5%
where the time goes in v1:
time: 25.1 us; the launch traced here: 25 us
  Pallas kernels  7.79 us (31%)
  waiting for transfers between devices  7.61 us (30%)
  starting transfers between devices  6.11 us (24%)
  local copies, waits for them, and re-layouts  2.74 us (11%)
  between operations  0.7 us (3%)
    ppermute x3, waiting for transfers between devices, on_device(): lax.ppermute(own, 'cp', [(i, (i + step) % n_cp) for i in range(n_cp)])  7.61 us
    pallas_call x1, Pallas kernels, on_device(): pl.pallas_call(functools.partial(attend_kernel, n_cp, key_blocks, group,...  6.47 us
    ppermute x3, starting transfers between devices, on_device(): lax.ppermute(own, 'cp', [(i, (i + step) % n_cp) for i in range(n_cp)])  6.11 us
    unnamed x14, local copies, waits for them, and re-layouts  2.74 us
    pallas_call x1, Pallas kernels, on_device(): pl.pallas_call(functools.partial(absorb_kernel, group), grid=(heads // gr...  1.32 us
  transfers between devices with their start and end apart: 3, of which 1 were waited for; matrix products, arithmetic and copies ran while one was open for 0% of the time, Pallas kernels for 5%

profile of v1, /device:TPU:0, one launch (start us, length us, event | category | flops | bytes accessed | tf_op | source)
XLA Modules:
  0.0 25.0 jit_solution(17020601823766336750)
XLA Ops:
  0.6 0.0 copy-start.4
  0.6 0.0 copy-start.5
  0.7 5.1 %collective-permute-start.2 = (bf16[576,128]{1,0:T(8,128)(2,1)}, bf16[576,128]{1,0:T(8,128)(2,1)S(1)}, u32[]{:S(2)}, u32[]{:S(2)}) collective-permute-start(bf16[576,128]{1,0:T(8,128)(2,1)} %bitcast.5), channel_id=1, source_target_pairs={{0,12},{4,0},{8,4},{12,8},{1,13},{5,1},{9,5},{13,9},{2,14},{6,2},{... | collective-permute-start | bytes 442376 | tf_op jit(solution)/shard_map/ppermute | solution.py:146
  5.8 0.0 collective-permute-start.1
  5.8 1.0 %collective-permute-start = (bf16[576,128]{1,0:T(8,128)(2,1)}, bf16[576,128]{1,0:T(8,128)(2,1)S(1)}, u32[]{:S(2)}, u32[]{:S(2)}) collective-permute-start(bf16[576,128]{1,0:T(8,128)(2,1)} %bitcast.7), channel_id=1, source_target_pairs={{0,4},{4,8},{8,12},{12,0},{1,5},{5,9},{9,13},{13,1},{2,6},{6,10},{... | collective-permute-start | bytes 442376 | tf_op jit(solution)/shard_map/ppermute | solution.py:146
  6.8 0.0 copy-start
  6.8 1.6 %copy-done = bf16[16,128,512]{2,1,0:T(8,128)(2,1)S(1)} copy-done((bf16[16,128,512]{2,1,0:T(8,128)(2,1)S(1)}, bf16[16,128,512]{2,1,0:T(8,128)(2,1)}, u32[]{:S(2)}) %copy-start) | copy-done | bytes 2097176
  8.4 0.0 copy-start.1
  8.4 1.1 %copy-done.1 = bf16[128,3072]{1,0:T(8,128)(2,1)S(1)} copy-done((bf16[128,3072]{1,0:T(8,128)(2,1)S(1)}, bf16[128,3072]{1,0:T(8,128)(2,1)}, u32[]{:S(2)}) %copy-start.1) | copy-done | bytes 786456
  9.5 0.0 copy-start.2
  9.5 0.0 copy-start.3
  9.5 0.0 copy-start.6
  9.5 1.3 %absorb.1.combined = bf16[2048,576]{1,0:T(8,128)(2,1)S(1)} custom-call(bf16[128,3072]{1,0:T(8,128)(2,1)S(1)} %copy-done.1, bf16[16,128,512]{2,1,0:T(8,128)(2,1)S(1)} %copy-done), custom_call_target="tpu_custom_call" | custom-call | flops 268435456 | bytes 5242880 | tf_op jit(solution)/shard_map/absorb/pallas_call | solution.py:149
  10.8 0.0 collective-permute-done.2.rest_3_
  10.8 7.6 %collective-permute-done.1.rest_2_ = bf16[576,128]{1,0:T(8,128)(2,1)S(1)} collective-permute-done((bf16[576,128]{1,0:T(8,128)(2,1)}, bf16[576,128]{1,0:T(8,128)(2,1)S(1)}, u32[]{:S(2)}, u32[]{:S(2)}) %collective-permute-start.1) | collective-permute-done | bytes 147488 | tf_op jit(solution)/shard_map/ppermute | solution.py:146
  18.4 0.0 collective-permute-done.rest_1_
  18.4 0.0 copy-done.4
  18.4 0.0 copy-done.5
  18.5 0.0 copy-done.2
  18.5 0.0 copy-done.3
  18.5 0.0 copy-done.6
  18.5 6.5 %attend.1 = (bf16[128,2048]{1,0:T(8,128)(2,1)}, bf16[3,16,576]{2,1,0:T(8,128)(2,1)}, bf16[3,4,16]{2,1,0:T(4,128)(2,1)}) custom-call(s32[2]{0:T(128)S(1)} %copy-done.5, s32[2,2]{1,0:T(2,128)S(1)} %copy-done.4, s32[2]{0:T(128)S(1)} %copy-done.6, bf16[2048,576]{1,0:T(8,128)(2,1)S(1)} %absorb.1.combined, bf16[16,512,128]{2,1,0:T(8,128)(2,1)S(1)} %copy-done.2, ...), custom_call_target="tpu_custom_call" | custom-call | flops 1979711488 | bytes 4980736 | tf_op jit(solution)/shard_map/attend/pallas_call | solution.py:170
Async XLA Ops:
  0.6 17.8 %copy-start.4 = (s32[2,2]{1,0:T(2,128)S(1)}, s32[2,2]{1,0:T(2,128)}, u32[]{:S(2)}) copy-start(s32[2,2]{1,0:T(2,128)} %decode_owner.1) | copy-start | bytes 52
  0.6 17.8 %copy-start.5 = (s32[2]{0:T(128)S(1)}, s32[2]{0:T(128)}, u32[]{:S(2)}) copy-start(s32[2]{0:T(128)} %prompt_pages.1) | copy-start | bytes 28
  0.7 10.2 %collective-permute-start.2 = (bf16[576,128]{1,0:T(8,128)(2,1)}, bf16[576,128]{1,0:T(8,128)(2,1)S(1)}, u32[]{:S(2)}, u32[]{:S(2)}) collective-permute-start(bf16[576,128]{1,0:T(8,128)(2,1)} %bitcast.5), channel_id=1, source_target_pairs={{0,12},{4,0},{8,4},{12,8},{1,13},{5,1},{9,5},{13,9},{2,14},{6,2},{... | collective-permute-start | bytes 442376 | tf_op jit(solution)/shard_map/ppermute | solution.py:146
  5.8 12.7 %collective-permute-start.1 = (bf16[576,128]{1,0:T(8,128)(2,1)}, bf16[576,128]{1,0:T(8,128)(2,1)S(1)}, u32[]{:S(2)}, u32[]{:S(2)}) collective-permute-start(bf16[576,128]{1,0:T(8,128)(2,1)} %bitcast.6), channel_id=1, source_target_pairs={{0,8},{4,12},{8,0},{12,4},{1,9},{5,13},{9,1},{13,5},{2,10},{6,14},... | collective-permute-start | bytes 442376 | tf_op jit(solution)/shard_map/ppermute | solution.py:146
  5.8 12.7 %collective-permute-start = (bf16[576,128]{1,0:T(8,128)(2,1)}, bf16[576,128]{1,0:T(8,128)(2,1)S(1)}, u32[]{:S(2)}, u32[]{:S(2)}) collective-permute-start(bf16[576,128]{1,0:T(8,128)(2,1)} %bitcast.7), channel_id=1, source_target_pairs={{0,4},{4,8},{8,12},{12,0},{1,5},{5,9},{9,13},{13,1},{2,6},{6,10},{... | collective-permute-start | bytes 442376 | tf_op jit(solution)/shard_map/ppermute | solution.py:146
  6.8 1.6 %copy-start = (bf16[16,128,512]{2,1,0:T(8,128)(2,1)S(1)}, bf16[16,128,512]{2,1,0:T(8,128)(2,1)}, u32[]{:S(2)}) copy-start(bf16[16,128,512]{2,1,0:T(8,128)(2,1)} %key_absorb.1) | copy-start | bytes 6291460
  8.4 1.1 %copy-start.1 = (bf16[128,3072]{1,0:T(8,128)(2,1)S(1)}, bf16[128,3072]{1,0:T(8,128)(2,1)}, u32[]{:S(2)}) copy-start(bf16[128,3072]{1,0:T(8,128)(2,1)} %queries.1) | copy-start | bytes 2359300
  9.5 9.0 %copy-start.2 = (bf16[16,512,128]{2,1,0:T(8,128)(2,1)S(1)}, bf16[16,512,128]{2,1,0:T(8,128)(2,1)}, u32[]{:S(2)}) copy-start(bf16[16,512,128]{2,1,0:T(8,128)(2,1)} %value_expand.1) | copy-start | bytes 6291460
  9.5 9.0 %copy-start.3 = (bf16[128,576]{0,1:T(8,128)(2,1)S(1)}, bf16[128,576]{0,1:T(8,128)(2,1)}, u32[]{:S(2)}) copy-start(bf16[128,576]{0,1:T(8,128)(2,1)} %param.8) | copy-start | bytes 442372
  9.5 9.0 %copy-start.6 = (s32[2]{0:T(128)S(1)}, s32[2]{0:T(128)}, u32[]{:S(2)}) copy-start(s32[2]{0:T(128)} %slot_offset.1) | copy-start | bytes 28

commit v2 on v1

v2 whole, which is shorter than its diff:
```python
import functools
import math

import jax
import jax.numpy as jnp
from jax import lax
from jax.experimental import pallas as pl
from jax.experimental.pallas import tpu as pltpu
from jax.sharding import PartitionSpec as P

LAT = 512
ROPE = 64
NOPE = 128
VDIM = 128
PAGE = 16
BLOCK = 128
NBLK = LAT // BLOCK
ROW = LAT + ROPE
HEAD = NOPE + ROPE

masked_fill = -1e30
amax_epsilon = 1e-06
exp2_scale = math.log2(math.e) / math.sqrt(HEAD)

NT = (((1,), (1,)), ((), ()))


def own_kernel(group, prompt_pages, queries, key_absorb, own, combined, summed, stats, q_buf, w_buf, sems, values):
    rows = own.shape[1]
    heads = key_absorb.shape[0]
    copies = []
    for g in range(heads // group):
        wide = group * HEAD
        copies.append((
            pltpu.make_async_copy(queries.at[:, pl.ds(g * wide, wide)], q_buf.at[:, pl.ds(g * wide, wide)], sems.at[0, g]),
            pltpu.make_async_copy(key_absorb.at[pl.ds(g * group, group)], w_buf.at[pl.ds(g * group, group)], sems.at[1, g]),
        ))
    for pair in copies:
        for copy in pair:
            copy.start()
    block = own[...]
    values[...] = block[:LAT].T
    bias = visible_bias(prompt_pages, rows, 0)
    for g in range(heads // group):
        for copy in copies[g]:
            copy.wait()
        for h in range(g * group, (g + 1) * group):
            at = h * HEAD
            absorbed = jnp.dot(q_buf[:, at:at + NOPE], w_buf[h], preferred_element_type=jnp.float32)
            combined[h * rows:(h + 1) * rows, :LAT] = absorbed.astype(jnp.bfloat16)
            combined[h * rows:(h + 1) * rows, LAT:] = q_buf[:, at + NOPE:at + HEAD]
        span = pl.ds(g * group * rows, group * rows)
        scores = jnp.dot(combined[span, :], block, preferred_element_type=jnp.float32)
        scores = (scores.reshape(group, rows, rows) + bias[None]).reshape(group * rows, rows)
        peak = jnp.max(scores, axis=1, keepdims=True)
        weights = jnp.exp2((scores - peak) * exp2_scale)
        total = jnp.sum(weights, axis=1, keepdims=True)
        summed[span, :] = jnp.dot(weights.astype(jnp.bfloat16), values[...], preferred_element_type=jnp.float32)
        stats[span, 0:1] = peak
        stats[span, 1:2] = total


def visible_bias(prompt_pages, rows, steps_back):
    first = lax.axis_index("cp") * rows
    token = first + lax.broadcasted_iota(jnp.int32, (rows, 1), 0)
    begin = jnp.zeros((rows, 1), jnp.int32)
    for start in prompt_starts(prompt_pages):
        begin = jnp.maximum(begin, jnp.where(start * PAGE <= token, start * PAGE, 0))
    spot = first - steps_back * rows + lax.broadcasted_iota(jnp.int32, (1, rows), 1)
    return jnp.where((spot >= begin) & (spot <= token), 0.0, masked_fill)


def swap_pair(position, n_cp):
    odd = lax.rem(lax.axis_index("dec"), 2)
    within = lax.rem(position + 1, 2)
    swapped = position - within + lax.rem(within + odd, 2)
    paired = (position >= 1) & (position <= (n_cp - 1) // 2 * 2)
    return jnp.where(paired, swapped, position)


def prompt_starts(prompt_pages):
    starts = [jnp.int32(0)]
    for k in range(prompt_pages.shape[0] - 1):
        starts.append(starts[-1] + prompt_pages[k])
    return starts


def cache_kernel(n_cp, slot_count, prompt_pages, decode_owner, slot_offset, *rest):
    pieces = rest[:n_cp]
    page_cache, page_scales = rest[n_cp:]
    prompts, width = decode_owner.shape
    cp_index = lax.axis_index("cp")
    dec_index = lax.axis_index("dec")
    rows_here = pieces[0].shape[1]
    cycle = width * lax.axis_size("dec") * slot_count
    starts = prompt_starts(prompt_pages)
    pages, start, offset, place = jnp.int32(0), jnp.int32(0), jnp.int32(0), jnp.int32(0)
    for k in range(prompts):
        for p in range(width):
            mine = decode_owner[k, p] == cp_index
            pages = jnp.where(mine, prompt_pages[k], pages)
            start = jnp.where(mine, starts[k], start)
            offset = jnp.where(mine, slot_offset[k], offset)
            place = jnp.where(mine, p, place)
    kept = slot_count * PAGE
    row = lax.broadcasted_iota(jnp.int32, (kept, 1), 0)
    lane = lax.broadcasted_iota(jnp.int32, (1, kept), 1)
    row_target = jnp.full((kept, 1), -1, jnp.int32)
    lane_valid = jnp.zeros((1, kept), jnp.float32)
    for c in range(slot_count):
        turn = width * (dec_index * slot_count + c) + place
        page = lax.rem(turn - offset + 2 * cycle, cycle)
        valid = page < pages
        token = (start + page) * PAGE
        source = token // rows_here
        steps_back = lax.rem(cp_index - source + n_cp, n_cp)
        column = swap_pair(steps_back, n_cp) * rows_here + lax.rem(token, rows_here)
        column = jnp.where(valid, column, -kept)
        row_target = jnp.where(row // PAGE == c, column + row % PAGE, row_target)
        lane_valid = jnp.where(lane // PAGE == c, valid.astype(jnp.float32), lane_valid)
    rows = jnp.zeros((kept, ROW), jnp.float32)
    turned = jnp.zeros((LAT, kept), jnp.float32)
    for b, piece in enumerate(pieces):
        column = b * rows_here + lax.broadcasted_iota(jnp.int32, (1, rows_here), 1)
        chosen = jnp.where(column == row_target, 1.0, 0.0).astype(jnp.bfloat16)
        block = piece[...]
        rows = rows + lax.dot_general(chosen, block, NT, preferred_element_type=jnp.float32)
        turned = turned + lax.dot_general(block[:LAT], chosen, NT, preferred_element_type=jnp.float32)
    encoded = []
    scales = []
    for b in range(NBLK):
        values = rows[:, b * BLOCK:(b + 1) * BLOCK]
        scale = jnp.max(jnp.abs(values), axis=1, keepdims=True) + amax_epsilon
        scale = scale.astype(jnp.bfloat16).astype(jnp.float32)
        encoded.append((values / scale).astype(jnp.bfloat16))
        scales.append(jnp.max(jnp.abs(turned[b * BLOCK:(b + 1) * BLOCK]), axis=0, keepdims=True))
    encoded.append(rows[:, LAT:].astype(jnp.bfloat16))
    scales = jnp.concatenate(scales, axis=0) + amax_epsilon
    scales = (scales * lane_valid).astype(jnp.bfloat16)
    for c in range(slot_count):
        for b, values in enumerate(encoded):
            page_cache[c, :, b * BLOCK:b * BLOCK + values.shape[1]] = values[c * PAGE:(c + 1) * PAGE]
        page_scales[c] = scales[:, c * PAGE:(c + 1) * PAGE]


def earlier_kernel(n_cp, count, group, prompt_pages, combined, summed, stats, value_expand, *rest):
    pieces = rest[:count]
    attended, keys, values, bias = rest[count:]
    rows = attended.shape[0]

    @pl.when(pl.program_id(0) == 0)
    def _():
        for b in range(count):
            block = pieces[b][...]
            keys[:, b * rows:(b + 1) * rows] = block
            values[b * rows:(b + 1) * rows, :] = block[:LAT].T
            bias[:, b * rows:(b + 1) * rows] = visible_bias(prompt_pages, rows, swap_pair(jnp.int32(b + 1), n_cp))

    scores = jnp.dot(combined[...], keys[...], preferred_element_type=jnp.float32)
    scores = (scores.reshape(group, rows, count * rows) + bias[...][None]).reshape(group * rows, count * rows)
    old_peak = stats[:, 0:1]
    peak = jnp.maximum(old_peak, jnp.max(scores, axis=1, keepdims=True))
    weights = jnp.exp2((scores - peak) * exp2_scale)
    factor = jnp.exp2((old_peak - peak) * exp2_scale)
    total = stats[:, 1:2] * factor + jnp.sum(weights, axis=1, keepdims=True)
    added = jnp.dot(weights.astype(jnp.bfloat16), values[...], preferred_element_type=jnp.float32)
    mixed = ((summed[...] * factor + added) * (1.0 / total)).astype(jnp.bfloat16)
    for h in range(group):
        result = jnp.dot(mixed[h * rows:(h + 1) * rows], value_expand[h], preferred_element_type=jnp.float32)
        attended[:, h * VDIM:(h + 1) * VDIM] = result.astype(jnp.bfloat16)


def fetch(own, n_cp, n_dec):
    blocks = []
    for step in range(1, n_cp - 1, 2):
        pairs = [(c * n_dec + e, (c + step + e % 2) % n_cp * n_dec + e) for c in range(n_cp) for e in range(n_dec)]
        blocks.append(lax.ppermute(own, ("cp", "dec"), pairs))
    last = []
    if n_cp % 2 == 0:
        last.append(lax.ppermute(own, "cp", [(c, (c + n_cp - 1) % n_cp) for c in range(n_cp)]))
    return blocks, last


def swap(blocks, n_dec):
    pieces = []
    for block in blocks:
        pieces += [block, lax.ppermute(block, "dec", [(e, e ^ 1) for e in range(n_dec)])]
    return pieces


def on_device(queries, latent_rows, key_absorb, value_expand, prompt_pages, decode_owner, slot_offset):
    n_cp = lax.axis_size("cp")
    dec_count = lax.axis_size("dec")
    heads = key_absorb.shape[0]
    rows = latent_rows.shape[0]
    prompts, width = decode_owner.shape
    slot_count = 3 * (rows // PAGE) // (2 * dec_count)
    reach = width * dec_count * slot_count * PAGE
    count = -(-reach // rows) - (1 if prompts == 2 else 0)
    count = min(n_cp - 1, count + count % 2)
    own = latent_rows.T
    blocks, last = fetch(own, n_cp, dec_count)

    smem = pl.BlockSpec(memory_space=pltpu.SMEM)
    vmem = pl.BlockSpec(memory_space=pltpu.VMEM)
    hbm = pl.BlockSpec(memory_space=pltpu.HBM)
    params = pltpu.CompilerParams(vmem_limit_bytes=32 * 2**20)
    group = 4
    combined, summed, stats = pl.pallas_call(
        functools.partial(own_kernel, group),
        in_specs=[smem, hbm, hbm, vmem],
        out_specs=[vmem, vmem, vmem],
        out_shape=[
            jax.ShapeDtypeStruct((heads * rows, ROW), jnp.bfloat16),
            jax.ShapeDtypeStruct((heads * rows, LAT), jnp.float32),
            jax.ShapeDtypeStruct((heads * rows, 2), jnp.float32),
        ],
        scratch_shapes=[
            pltpu.VMEM((rows, heads * HEAD), jnp.bfloat16),
            pltpu.VMEM((heads, NOPE, LAT), jnp.bfloat16),
            pltpu.SemaphoreType.DMA((2, heads // group)),
            pltpu.VMEM((rows, LAT), jnp.bfloat16),
        ],
        cost_estimate=pl.CostEstimate(
            flops=2 * rows * heads * (NOPE * LAT + rows * (ROW + LAT)),
            bytes_accessed=2 * (queries.size + key_absorb.size + heads * rows * ROW),
            transcendentals=rows * heads * rows,
        ),
        compiler_params=params,
        name="own",
    )(prompt_pages, *[pltpu.with_memory_space_constraint(x, pltpu.HBM) for x in (queries, key_absorb)], own)
    blocks, combined = lax.optimization_barrier((blocks, combined))
    pieces = swap(blocks, dec_count)

    group = 4 if count <= 4 else 1
    attended = pl.pallas_call(
        functools.partial(earlier_kernel, n_cp, count, group),
        grid=(heads // group,),
        in_specs=[
            smem,
            pl.BlockSpec((group * rows, ROW), lambda g: (g, 0)),
            pl.BlockSpec((group * rows, LAT), lambda g: (g, 0)),
            pl.BlockSpec((group * rows, 2), lambda g: (g, 0)),
            pl.BlockSpec((group, LAT, VDIM), lambda g: (g, 0, 0)),
        ] + [pl.BlockSpec((ROW, rows), lambda g: (0, 0))] * count,
        out_specs=pl.BlockSpec((rows, group * VDIM), lambda g: (0, g)),
        out_shape=jax.ShapeDtypeStruct((rows, heads * VDIM), jnp.bfloat16),
        scratch_shapes=[
            pltpu.VMEM((ROW, count * rows), jnp.bfloat16),
            pltpu.VMEM((count * rows, LAT), jnp.bfloat16),
            pltpu.VMEM((rows, count * rows), jnp.float32),
        ],
        cost_estimate=pl.CostEstimate(
            flops=2 * rows * heads * (count * rows * (ROW + LAT) + LAT * VDIM),
            bytes_accessed=2 * (heads * rows * (ROW + VDIM) + value_expand.size),
            transcendentals=rows * heads * count * rows,
        ),
        compiler_params=params,
        name="earlier",
    )(prompt_pages, combined, summed, stats, value_expand, *pieces[:count])

    last, attended = lax.optimization_barrier((last, attended))
    pieces += last
    page_cache, page_scales = pl.pallas_call(
        functools.partial(cache_kernel, n_cp, slot_count),
        in_specs=[smem, smem, smem] + [vmem] * n_cp,
        out_specs=[vmem, vmem],
        out_shape=[
            jax.ShapeDtypeStruct((slot_count, PAGE, ROW), jnp.bfloat16),
            jax.ShapeDtypeStruct((slot_count, NBLK, PAGE), jnp.bfloat16),
        ],
        cost_estimate=pl.CostEstimate(
            flops=4 * n_cp * rows * slot_count * PAGE * ROW,
            bytes_accessed=2 * n_cp * rows * ROW,
            transcendentals=0,
        ),
        compiler_params=params,
        name="cache",
    )(prompt_pages, decode_owner, slot_offset, own, *pieces)
    page_cache = page_cache.reshape(1, 1, slot_count, PAGE, ROW)
    page_scales = page_scales.transpose(0, 2, 1).reshape(1, 1, slot_count, PAGE, NBLK)
    return attended, page_cache, page_scales


def solution(mesh):
    return jax.shard_map(
        on_device,
        mesh=mesh,
        in_specs=(
            P(("grp", "cp"), "dec"),
            P(("grp", "cp"), None),
            P("dec", None, None),
            P("dec", None, None),
            P("grp"),
            P("grp", None),
            P("grp"),
        ),
        out_specs=(
            P(("grp", "cp"), "dec"),
            P(("grp", "cp"), "dec", None, None, None),
            P(("grp", "cp"), "dec", None, None, None),
        ),
        check_vma=False,
    )
```

time: 25.1 us -> 28.3 us (1.13)
  Pallas kernels: 7.79 us -> 20 us
  waiting for transfers between devices: 7.61 us -> 0.01 us
  local copies, waits for them, and re-layouts: 2.74 us -> 1.61 us
    pallas_call x2 -> x3, Pallas kernels: 7.79 us -> 20 us  [the longest x1 12.7 us: on_device(): pl.pallas_call(functools.partial(earlier_kernel, n_cp, count, group), gri...]
    ppermute x3, waiting for transfers between devices: 7.61 us -> 0.01 us  [the longest x1 0.01 us: fetch(): blocks.append(lax.ppermute(own, ('cp', 'dec'), pairs))]
    unnamed x14 -> x10, local copies, waits for them, and re-layouts: 2.74 us -> 1.61 us
  transfers between devices with their start and end apart: 3 -> 3, of which waited for: 1 -> 0; matrix products, arithmetic and copies ran while one was open for 0% -> 0% of each run, Pallas kernels for 5% -> 65%
where the time goes in v2:
time: 28.3 us; the launch traced here: 28.1 us
  Pallas kernels  20 us (71%)
  starting transfers between devices  5.86 us (21%)
  local copies, waits for them, and re-layouts  1.61 us (6%)
  between operations  0.67 us (2%)
    pallas_call x1, Pallas kernels, on_device(): pl.pallas_call(functools.partial(earlier_kernel, n_cp, count, group), gri...  12.7 us
    pallas_call x1, Pallas kernels, on_device(): pl.pallas_call(functools.partial(own_kernel, group), in_specs=[smem, hbm,...  5.55 us
    ppermute x1, starting transfers between devices, fetch(): blocks.append(lax.ppermute(own, ('cp', 'dec'), pairs))  3.08 us
    ppermute x1, starting transfers between devices, fetch(): lax.ppermute(own, 'cp', [(c, (c + n_cp - 1) % n_cp) for c in range(n_cp)])  2.15 us
    pallas_call x1, Pallas kernels, on_device(): pl.pallas_call(functools.partial(cache_kernel, n_cp, slot_count), in_spec...  1.7 us
    unnamed x10, local copies, waits for them, and re-layouts  1.61 us
    ppermute x1, starting transfers between devices, swap(): lax.ppermute(block, 'dec', [(e, e ^ 1) for e in range(n_dec)])  0.63 us
  transfers between devices with their start and end apart: 3, of which 0 were waited for; matrix products, arithmetic and copies ran while one was open for 0% of the time, Pallas kernels for 65%

profile of v2, /device:TPU:0, one launch (start us, length us, event | category | flops | bytes accessed | tf_op | source)
XLA Modules:
  0.0 28.1 jit_solution(11360704425066275803)
XLA Ops:
  0.6 0.0 copy-start
  0.6 3.1 %collective-permute-start.1 = (bf16[576,128]{1,0:T(8,128)(2,1)}, bf16[576,128]{1,0:T(8,128)(2,1)S(1)}, u32[]{:S(2)}, u32[]{:S(2)}) collective-permute-start(bf16[576,128]{1,0:T(8,128)(2,1)} %bitcast.5), channel_id=1, source_target_pairs={{0,4},{1,9},{2,6},{3,11},{4,8},{5,13},{6,10},{7,15},{8,12},{9,1},{... | collective-permute-start | bytes 442376 | tf_op jit(solution)/shard_map/ppermute | solution.py:177
  3.7 0.0 copy-start.1
  3.7 0.9 %copy-done.1 = bf16[128,576]{0,1:T(8,128)(2,1)S(1)} copy-done((bf16[128,576]{0,1:T(8,128)(2,1)S(1)}, bf16[128,576]{0,1:T(8,128)(2,1)}, u32[]{:S(2)}) %copy-start.1) | copy-done | bytes 147480
  4.7 0.0 copy-start.2
  4.7 0.7 %copy-done.2 = s32[2]{0:T(128)S(1)} copy-done((s32[2]{0:T(128)S(1)}, s32[2]{0:T(128)}, u32[]{:S(2)}) %copy-start.2) | copy-done | bytes 32
  5.3 5.5 %own.1 = (bf16[2048,576]{1,0:T(8,128)(2,1)S(1)}, f32[2048,512]{1,0:T(8,128)S(1)}, f32[2048,2]{1,0:T(8,128)S(1)}) custom-call(s32[2]{0:T(128)S(1)} %copy-done.2, bf16[128,3072]{1,0:T(8,128)(2,1)} %queries.1, bf16[16,128,512]{2,1,0:T(8,128)(2,1)} %key_absorb.1, bf16[576,128]{1,0:T(8,128)(2,1)S(1)} %bitcast.6), custom_call_target="tpu_custom_call" | custom-call | flops 838860800 | bytes 5242880 | tf_op jit(solution)/shard_map/own/pallas_call | solution.py:209
  10.9 0.0 collective-permute-done.1.rest_0_.rest_1_
  10.9 0.6 %collective-permute-start.2 = (bf16[576,128]{1,0:T(8,128)(2,1)S(1)}, bf16[576,128]{1,0:T(8,128)(2,1)S(1)}, u32[]{:S(2)}, u32[]{:S(2)}) collective-permute-start(bf16[576,128]{1,0:T(8,128)(2,1)S(1)} %collective-permute-done.1.rest_0_.rest_1_), channel_id=1, source_target_pairs={{0,1},{1,0},{2,3},{3,2},{4,5},{5,4},{6,7},{7,6},{8,9},{9,8},{10,11... | collective-permute-start | bytes 442376 | tf_op jit(solution)/shard_map/ppermute | solution.py:187
  11.5 2.2 %collective-permute-start = (bf16[576,128]{1,0:T(8,128)(2,1)S(1)}, bf16[576,128]{1,0:T(8,128)(2,1)S(1)}, u32[]{:S(2)}, u32[]{:S(2)}) collective-permute-start(bf16[576,128]{1,0:T(8,128)(2,1)S(1)} %bitcast.7), channel_id=1, source_target_pairs={{0,12},{4,0},{8,4},{12,8},{1,13},{5,1},{9,5},{13,9},{2,14},{6,2},{... | collective-permute-start | bytes 442376 | tf_op jit(solution)/shard_map/ppermute | solution.py:180
  13.7 0.0 collective-permute-done.2.rest_1_.rest_2_
  13.7 0.0 copy-done
  13.7 0.0 copy-start.3
  13.7 0.0 copy-start.4
  13.7 12.7 %earlier.1 = bf16[128,2048]{1,0:T(8,128)(2,1)} custom-call(s32[2]{0:T(128)S(1)} %copy-done.2, bf16[2048,576]{1,0:T(8,128)(2,1)S(1)} %get-tuple-element.13.combined, f32[2048,512]{1,0:T(8,128)S(1)} %get-tuple-element.14.summed, f32[2048,2]{1,0:T(8,128)S(1)} %get-tuple-element.15.stats, bf16[16,512,128]{2,1,0:T(8,128)(2,1)S(1)} %copy-done, ...), custom_call_target="tpu_custom_call" | custom-call | flops 1409286144 | bytes 4980736 | tf_op jit(solution)/shard_map/earlier/pallas_call | solution.py:236
  26.4 0.0 collective-permute-done.rest_3_
  26.4 0.0 copy-done.3
  26.4 0.0 copy-done.4
  26.4 1.7 %cache.1 = (bf16[3,16,576]{2,1,0:T(8,128)(2,1)}, bf16[3,4,16]{2,1,0:T(4,128)(2,1)}) custom-call(s32[2]{0:T(128)S(1)} %copy-done.2, s32[2,2]{1,0:T(2,128)S(1)} %copy-done.3, s32[2]{0:T(128)S(1)} %copy-done.4, bf16[576,128]{1,0:T(8,128)(2,1)S(1)} %bitcast.8, bf16[576,128]{1,0:T(8,128)(2,1)S(1)} %collective-permute-done.1.rest_0_.rest_1_, ...), custom_call_target="tpu_custom_call" | custom-call | flops 56623104 | bytes 589824 | tf_op jit(solution)/shard_map/cache/pallas_call | solution.py:264
Async XLA Ops:
  0.6 13.0 %copy-start = (bf16[16,512,128]{2,1,0:T(8,128)(2,1)S(1)}, bf16[16,512,128]{2,1,0:T(8,128)(2,1)}, u32[]{:S(2)}) copy-start(bf16[16,512,128]{2,1,0:T(8,128)(2,1)} %value_expand.1) | copy-start | bytes 6291460
  0.6 10.2 %collective-permute-start.1 = (bf16[576,128]{1,0:T(8,128)(2,1)}, bf16[576,128]{1,0:T(8,128)(2,1)S(1)}, u32[]{:S(2)}, u32[]{:S(2)}) collective-permute-start(bf16[576,128]{1,0:T(8,128)(2,1)} %bitcast.5), channel_id=1, source_target_pairs={{0,4},{1,9},{2,6},{3,11},{4,8},{5,13},{6,10},{7,15},{8,12},{9,1},{... | collective-permute-start | bytes 442376 | tf_op jit(solution)/shard_map/ppermute | solution.py:177
  3.7 0.9 %copy-start.1 = (bf16[128,576]{0,1:T(8,128)(2,1)S(1)}, bf16[128,576]{0,1:T(8,128)(2,1)}, u32[]{:S(2)}) copy-start(bf16[128,576]{0,1:T(8,128)(2,1)} %param.8) | copy-start | bytes 442372
  4.7 0.7 %copy-start.2 = (s32[2]{0:T(128)S(1)}, s32[2]{0:T(128)}, u32[]{:S(2)}) copy-start(s32[2]{0:T(128)} %prompt_pages.5) | copy-start | bytes 28
  10.9 2.8 %collective-permute-start.2 = (bf16[576,128]{1,0:T(8,128)(2,1)S(1)}, bf16[576,128]{1,0:T(8,128)(2,1)S(1)}, u32[]{:S(2)}, u32[]{:S(2)}) collective-permute-start(bf16[576,128]{1,0:T(8,128)(2,1)S(1)} %collective-permute-done.1.rest_0_.rest_1_), channel_id=1, source_target_pairs={{0,1},{1,0},{2,3},{3,2},{4,5},{5,4},{6,7},{7,6},{8,9},{9,8},{10,11... | collective-permute-start | bytes 442376 | tf_op jit(solution)/shard_map/ppermute | solution.py:187
  11.5 14.9 %collective-permute-start = (bf16[576,128]{1,0:T(8,128)(2,1)S(1)}, bf16[576,128]{1,0:T(8,128)(2,1)S(1)}, u32[]{:S(2)}, u32[]{:S(2)}) collective-permute-start(bf16[576,128]{1,0:T(8,128)(2,1)S(1)} %bitcast.7), channel_id=1, source_target_pairs={{0,12},{4,0},{8,4},{12,8},{1,13},{5,1},{9,5},{13,9},{2,14},{6,2},{... | collective-permute-start | bytes 442376 | tf_op jit(solution)/shard_map/ppermute | solution.py:180
  13.7 12.7 %copy-start.3 = (s32[2,2]{1,0:T(2,128)S(1)}, s32[2,2]{1,0:T(2,128)}, u32[]{:S(2)}) copy-start(s32[2,2]{1,0:T(2,128)} %decode_owner.1) | copy-start | bytes 52
  13.7 12.7 %copy-start.4 = (s32[2]{0:T(128)S(1)}, s32[2]{0:T(128)}, u32[]{:S(2)}) copy-start(s32[2]{0:T(128)} %slot_offset.1) | copy-start | bytes 28

commit v3 on v2

v3 whole, which is shorter than its diff:
```python
import functools
import math

import jax
import jax.numpy as jnp
from jax import lax
from jax.experimental import pallas as pl
from jax.experimental.pallas import tpu as pltpu
from jax.sharding import PartitionSpec as P

LAT = 512
ROPE = 64
NOPE = 128
VDIM = 128
PAGE = 16
BLOCK = 128
NBLK = LAT // BLOCK
ROW = LAT + ROPE
HEAD = NOPE + ROPE
LANES = 128

masked_fill = -1e30
amax_epsilon = 1e-06
exp2_scale = math.log2(math.e) / math.sqrt(HEAD)

NT = (((1,), (1,)), ((), ()))


def prompt_starts(prompt_pages):
    starts = [jnp.int32(0)]
    for k in range(prompt_pages.shape[0] - 1):
        starts.append(starts[-1] + prompt_pages[k])
    return starts


def visible_bias(prompt_pages, rows, steps_back):
    first = lax.axis_index("cp") * rows
    token = first + lax.broadcasted_iota(jnp.int32, (rows, 1), 0)
    begin = jnp.zeros((rows, 1), jnp.int32)
    for start in prompt_starts(prompt_pages):
        begin = jnp.maximum(begin, jnp.where(start * PAGE <= token, start * PAGE, 0))
    spot = first - steps_back * rows + lax.broadcasted_iota(jnp.int32, (1, rows), 1)
    return jnp.where((spot >= begin) & (spot <= token), 0.0, masked_fill)


def swap_pair(position, n_cp):
    odd = lax.rem(lax.axis_index("dec"), 2)
    within = lax.rem(position + 1, 2)
    swapped = position - within + lax.rem(within + odd, 2)
    paired = (position >= 1) & (position <= (n_cp - 1) // 2 * 2)
    return jnp.where(paired, swapped, position)


def slot_pages(owner, slot_count, prompt_pages, decode_owner, slot_offset):
    prompts, width = decode_owner.shape
    cycle = width * lax.axis_size("dec") * slot_count
    starts = prompt_starts(prompt_pages)
    pages, start, offset, place = jnp.int32(0), jnp.int32(0), jnp.int32(0), jnp.int32(0)
    for k in range(prompts):
        for p in range(width):
            mine = decode_owner[k, p] == owner
            pages = jnp.where(mine, prompt_pages[k], pages)
            start = jnp.where(mine, starts[k], start)
            offset = jnp.where(mine, slot_offset[k], offset)
            place = jnp.where(mine, p, place)
    result = []
    for c in range(slot_count):
        turn = width * (lax.axis_index("dec") * slot_count + c) + place
        page = lax.rem(turn - offset + 2 * cycle, cycle)
        result.append((page < pages, start + page))
    return result


def row_picker(targets, columns):
    kept = len(targets) * PAGE
    row = lax.broadcasted_iota(jnp.int32, (kept, 1), 0)
    target = jnp.full((kept, 1), -1, jnp.int32)
    for c, column in enumerate(targets):
        target = jnp.where(row // PAGE == c, column + row % PAGE, target)
    column = lax.broadcasted_iota(jnp.int32, (1, columns), 1)
    return jnp.where(column == target, 1.0, 0.0).astype(jnp.bfloat16)


def own_kernel(n_cp, count, group, slot_count, *refs):
    inputs, refs = refs[:6], refs[6:]
    combined, summed, peaks, totals, bias, picked, kept_rows, sent_rows, filled = refs[:9]
    buffers, sems, values = refs[9:15], refs[15], refs[16]
    pages_hbm, owner_hbm, offset_hbm, own_hbm, queries_hbm, absorb_hbm = inputs
    prompt_pages, decode_owner, slot_offset, own, queries, key_absorb = buffers
    rows = own.shape[1]
    heads = key_absorb.shape[0]
    wide = group * HEAD
    small = [pltpu.make_async_copy(inputs[i], buffers[i], sems.at[i]) for i in range(4)]
    large = []
    for g in range(heads // group):
        at = 4 + 2 * g
        large.append((
            pltpu.make_async_copy(queries_hbm.at[:, pl.ds(g * wide, wide)], queries.at[:, pl.ds(g * wide, wide)], sems.at[at]),
            pltpu.make_async_copy(absorb_hbm.at[pl.ds(g * group, group)], key_absorb.at[pl.ds(g * group, group)], sems.at[at + 1]),
        ))
    for copy in small:
        copy.start()
    for pair in large:
        for copy in pair:
            copy.start()
    for copy in small:
        copy.wait()
    block = own[...]
    values[...] = block[:LAT].T
    own_bias = visible_bias(prompt_pages, rows, 0)
    for b in range(count):
        bias[:, b * rows:(b + 1) * rows] = visible_bias(prompt_pages, rows, swap_pair(jnp.int32(b + 1), n_cp))

    me = lax.axis_index("cp")
    targets = []
    lane = lax.broadcasted_iota(jnp.int32, filled.shape, 1)
    lane_filled = jnp.zeros(filled.shape, jnp.float32)
    for c, (valid, page) in enumerate(slot_pages(me, slot_count, prompt_pages, decode_owner, slot_offset)):
        source = page * PAGE // rows
        column = swap_pair(lax.rem(me - source + n_cp, n_cp), n_cp) * rows + lax.rem(page * PAGE, rows)
        targets.append(jnp.where(valid, column, -PAGE))
        lane_filled = jnp.where(lane // PAGE == c, valid.astype(jnp.float32), lane_filled)
    filled[...] = lane_filled
    choice = row_picker(targets, (n_cp - 1) * rows)
    picked[...] = choice
    kept_rows[...] = lax.dot_general(choice[:, :rows], block, NT, preferred_element_type=jnp.float32).astype(jnp.bfloat16)
    targets = []
    behind = lax.rem(me + n_cp - 1, n_cp)
    for valid, page in slot_pages(behind, slot_count, prompt_pages, decode_owner, slot_offset):
        here = valid & (page * PAGE // rows == me)
        targets.append(jnp.where(here, lax.rem(page * PAGE, rows), -PAGE))
    choice = row_picker(targets, rows)
    sent_rows[...] = lax.dot_general(choice, block, NT, preferred_element_type=jnp.float32).astype(jnp.bfloat16)

    for g in range(heads // group):
        for copy in large[g]:
            copy.wait()
        for h in range(g * group, (g + 1) * group):
            at = h * HEAD
            absorbed = jnp.dot(queries[:, at:at + NOPE], key_absorb[h], preferred_element_type=jnp.float32)
            combined[h * rows:(h + 1) * rows, :LAT] = absorbed.astype(jnp.bfloat16)
            combined[h * rows:(h + 1) * rows, LAT:] = queries[:, at + NOPE:at + HEAD]
        span = pl.ds(g * group * rows, group * rows)
        scores = jnp.dot(combined[span, :], block, preferred_element_type=jnp.float32)
        scores = (scores.reshape(group, rows, rows) + own_bias[None]).reshape(group * rows, rows)
        peak = jnp.max(scores, axis=1, keepdims=True)
        weights = jnp.exp2((scores - peak) * exp2_scale)
        total = jnp.sum(weights, axis=1, keepdims=True)
        summed[span, :] = jnp.dot(weights.astype(jnp.bfloat16), values[...], preferred_element_type=jnp.float32)
        peaks[span, :] = jnp.broadcast_to(peak, (group * rows, LANES))
        totals[span, :] = jnp.broadcast_to(total, (group * rows, LANES))


def write_cache(rows, filled, page_cache, page_scales):
    slot_count = page_cache.shape[0]
    scales = []
    for b in range(NBLK):
        values = rows[:, b * BLOCK:(b + 1) * BLOCK]
        scale = jnp.max(jnp.abs(values), axis=1, keepdims=True) + amax_epsilon
        scale = scale.astype(jnp.bfloat16).astype(jnp.float32)
        encoded = (values / scale).astype(jnp.bfloat16)
        for c in range(slot_count):
            page_cache[c, :, b * BLOCK:(b + 1) * BLOCK] = encoded[c * PAGE:(c + 1) * PAGE]
        scales.append(scale)
    kept = rows.shape[0]
    which = lax.broadcasted_iota(jnp.int32, (kept, LANES), 1)
    table = jnp.zeros((kept, LANES), jnp.float32)
    for b, scale in enumerate(scales):
        table = jnp.where(which == b, scale, table)
    table = (table.T[:NBLK] * filled[:1, :kept]).astype(jnp.bfloat16)
    for c in range(slot_count):
        page_cache[c, :, LAT:] = rows[c * PAGE:(c + 1) * PAGE, LAT:].astype(jnp.bfloat16)
        page_scales[c] = table[:, c * PAGE:(c + 1) * PAGE]


def earlier_kernel(n_cp, count, group, *refs):
    combined, summed, peaks, totals, value_expand, bias, picked, kept_rows, sent_rows, filled = refs[:10]
    pieces = refs[10:8 + n_cp]
    attended, page_cache, page_scales, keys, values, result, sems = refs[8 + n_cp:]
    rows = attended.shape[0]
    heads = value_expand.shape[0]
    width = count * rows
    for b in range(count):
        block = pieces[b][...]
        keys[:, b * rows:(b + 1) * rows] = block
        values[b * rows:(b + 1) * rows, :] = block[:LAT].T

    def one_group(g, _):
        span = pl.ds(pl.multiple_of(g * group * rows, group * rows), group * rows)
        scores = jnp.dot(combined[span, :], keys[...], preferred_element_type=jnp.float32)
        scores = (scores.reshape(group, rows, width) + bias[...][None]).reshape(group * rows, width)
        old_peak = peaks[span, :]
        peak = jnp.maximum(old_peak, jnp.max(scores, axis=1, keepdims=True))
        total = jnp.zeros((group * rows, 1), jnp.float32)
        weights = []
        for b in range(count):
            part = jnp.exp2((scores[:, b * rows:(b + 1) * rows] - peak) * exp2_scale)
            total = total + jnp.sum(part, axis=1, keepdims=True)
            weights.append(part.astype(jnp.bfloat16))
        factor = jnp.exp2((old_peak - peak) * exp2_scale)
        inverse = 1.0 / (totals[span, :] * factor + total)
        factor = factor * inverse
        added = jnp.dot(jnp.concatenate(weights, axis=1), values[...], preferred_element_type=jnp.float32)
        mixed = []
        for b in range(NBLK):
            part = slice(b * BLOCK, (b + 1) * BLOCK)
            mixed.append((summed[span, part] * factor + added[:, part] * inverse).astype(jnp.bfloat16))
        mixed = jnp.concatenate(mixed, axis=1)
        for h in range(group):
            out = jnp.dot(mixed[h * rows:(h + 1) * rows], value_expand[g * group + h], preferred_element_type=jnp.float32)
            at = pl.ds(pl.multiple_of((g * group + h) * VDIM, VDIM), VDIM)
            result[:, at] = out.astype(jnp.bfloat16)
        send(g).start()
        return 0

    def send(g):
        at = pl.ds(pl.multiple_of(g * group * VDIM, group * VDIM), group * VDIM)
        return pltpu.make_async_copy(result.at[:, at], attended.at[:, at], sems.at[g])

    if count <= 4:
        for g in range(heads // group):
            one_group(g, 0)
    else:
        lax.fori_loop(0, heads // group, one_group, 0)
    found = kept_rows[...].astype(jnp.float32) + sent_rows[...].astype(jnp.float32)
    for b, piece in enumerate(pieces):
        choice = picked[:, (b + 1) * rows:(b + 2) * rows]
        found = found + lax.dot_general(choice, piece[...], NT, preferred_element_type=jnp.float32)
    write_cache(found, filled, page_cache, page_scales)
    for g in range(heads // group):
        send(g).wait()


def fetch(own, n_cp, n_dec):
    blocks = []
    for step in range(1, n_cp - 1, 2):
        pairs = [(c * n_dec + e, (c + step + e % 2) % n_cp * n_dec + e) for c in range(n_cp) for e in range(n_dec)]
        blocks.append(lax.ppermute(own, ("cp", "dec"), pairs))
    return blocks


def swap(blocks, n_dec):
    pieces = []
    for block in blocks:
        pieces += [block, lax.ppermute(block, "dec", [(e, e ^ 1) for e in range(n_dec)])]
    return pieces


def on_device(queries, latent_rows, key_absorb, value_expand, prompt_pages, decode_owner, slot_offset):
    n_cp = lax.axis_size("cp")
    dec_count = lax.axis_size("dec")
    heads = key_absorb.shape[0]
    rows = latent_rows.shape[0]
    prompts, width = decode_owner.shape
    slot_count = 3 * (rows // PAGE) // (2 * dec_count)
    kept = slot_count * PAGE
    reach = width * dec_count * slot_count * PAGE
    count = -(-reach // rows) - (1 if prompts == 2 else 0)
    count = min(n_cp - 2, count + count % 2)
    own = latent_rows.T
    blocks = fetch(own, n_cp, dec_count)

    vmem = pl.BlockSpec(memory_space=pltpu.VMEM)
    hbm = pl.BlockSpec(memory_space=pltpu.HBM)
    params = pltpu.CompilerParams(vmem_limit_bytes=32 * 2**20)
    group = 8
    inputs = (prompt_pages, decode_owner, slot_offset, own, queries, key_absorb)
    (combined, summed, peaks, totals, bias, picked, kept_rows, sent_rows, filled) = pl.pallas_call(
        functools.partial(own_kernel, n_cp, count, group, slot_count),
        in_specs=[hbm] * 6,
        out_specs=[vmem] * 9,
        out_shape=[
            jax.ShapeDtypeStruct((heads * rows, ROW), jnp.bfloat16),
            jax.ShapeDtypeStruct((heads * rows, LAT), jnp.float32),
            jax.ShapeDtypeStruct((heads * rows, LANES), jnp.float32),
            jax.ShapeDtypeStruct((heads * rows, LANES), jnp.float32),
            jax.ShapeDtypeStruct((rows, count * rows), jnp.float32),
            jax.ShapeDtypeStruct((kept, (n_cp - 1) * rows), jnp.bfloat16),
            jax.ShapeDtypeStruct((kept, ROW), jnp.bfloat16),
            jax.ShapeDtypeStruct((kept, ROW), jnp.bfloat16),
            jax.ShapeDtypeStruct((8, LANES), jnp.float32),
        ],
        scratch_shapes=[
            pltpu.SMEM(prompt_pages.shape, jnp.int32),
            pltpu.SMEM(decode_owner.shape, jnp.int32),
            pltpu.SMEM(slot_offset.shape, jnp.int32),
            pltpu.VMEM((ROW, rows), jnp.bfloat16),
            pltpu.VMEM((rows, heads * HEAD), jnp.bfloat16),
            pltpu.VMEM((heads, NOPE, LAT), jnp.bfloat16),
            pltpu.SemaphoreType.DMA((4 + 2 * (heads // group),)),
            pltpu.VMEM((rows, LAT), jnp.bfloat16),
        ],
        cost_estimate=pl.CostEstimate(
            flops=2 * rows * heads * (NOPE * LAT + rows * (ROW + LAT)),
            bytes_accessed=2 * (queries.size + key_absorb.size + heads * rows * ROW),
            transcendentals=rows * heads * rows,
        ),
        compiler_params=params,
        name="own",
    )(*[pltpu.with_memory_space_constraint(x, pltpu.HBM) for x in inputs])
    blocks, combined = lax.optimization_barrier((blocks, combined))
    pieces = swap(blocks, dec_count)
    sent_rows = lax.ppermute(sent_rows, "cp", [(c, (c + n_cp - 1) % n_cp) for c in range(n_cp)])

    group = 8 if count <= 4 else 1
    operands = (combined, summed, peaks, totals, value_expand, bias, picked, kept_rows, sent_rows, filled, *pieces)
    attended, page_cache, page_scales = pl.pallas_call(
        functools.partial(earlier_kernel, n_cp, count, group),
        in_specs=[vmem] * len(operands),
        out_specs=[hbm, vmem, vmem],
        out_shape=[
            jax.ShapeDtypeStruct((rows, heads * VDIM), jnp.bfloat16),
            jax.ShapeDtypeStruct((slot_count, PAGE, ROW), jnp.bfloat16),
            jax.ShapeDtypeStruct((slot_count, NBLK, PAGE), jnp.bfloat16),
        ],
        scratch_shapes=[
            pltpu.VMEM((ROW, count * rows), jnp.bfloat16),
            pltpu.VMEM((count * rows, LAT), jnp.bfloat16),
            pltpu.VMEM((rows, heads * VDIM), jnp.bfloat16),
            pltpu.SemaphoreType.DMA((heads // group,)),
        ],
        cost_estimate=pl.CostEstimate(
            flops=2 * rows * heads * (count * rows * (ROW + LAT) + LAT * VDIM),
            bytes_accessed=2 * (heads * rows * (ROW + VDIM) + value_expand.size),
            transcendentals=rows * heads * count * rows,
        ),
        compiler_params=params,
        name="earlier",
    )(*operands)
    page_cache = page_cache.reshape(1, 1, slot_count, PAGE, ROW)
    page_scales = page_scales.transpose(0, 2, 1).reshape(1, 1, slot_count, PAGE, NBLK)
    return attended, page_cache, page_scales


def solution(mesh):
    return jax.shard_map(
        on_device,
        mesh=mesh,
        in_specs=(
            P(("grp", "cp"), "dec"),
            P(("grp", "cp"), None),
            P("dec", None, None),
            P("dec", None, None),
            P("grp"),
            P("grp", None),
            P("grp"),
        ),
        out_specs=(
            P(("grp", "cp"), "dec"),
            P(("grp", "cp"), "dec", None, None, None),
            P(("grp", "cp"), "dec", None, None, None),
        ),
        check_vma=False,
    )
```

time: 28.3 us -> 20.4 us (0.72)
  Pallas kernels: 20 us -> 9.51 us
  waiting for transfers between devices: 0.01 us -> 3.26 us
  local copies, waits for them, and re-layouts: 1.61 us -> 0.01 us
  starting transfers between devices: 5.86 us -> 6.79 us
    pallas_call x3 -> x2, Pallas kernels: 20 us -> 9.51 us  [the longest x1 4.84 us: on_device(): pl.pallas_call(functools.partial(own_kernel, n_cp, count, group, slot_cou...]
    ppermute x1, waiting for transfers between devices: 0.01 us -> 1.87 us  [on_device(): lax.ppermute(sent_rows, 'cp', [(c, (c + n_cp - 1) % n_cp) for c in range(...]
    unnamed x10 -> x2, local copies, waits for them, and re-layouts: 1.61 us -> 0.01 us
    ppermute x1, waiting for transfers between devices: 0.01 us -> 1.39 us  [fetch(): blocks.append(lax.ppermute(own, ('cp', 'dec'), pairs))]
    ppermute x1, starting transfers between devices: 2.15 us -> 3.48 us  [on_device(): lax.ppermute(sent_rows, 'cp', [(c, (c + n_cp - 1) % n_cp) for c in range(...]
    ppermute x1, starting transfers between devices: 0.63 us -> 0.24 us  [swap(): lax.ppermute(block, 'dec', [(e, e ^ 1) for e in range(n_dec)])]
  transfers between devices with their start and end apart: 3 -> 3, of which waited for: 0 -> 2; matrix products, arithmetic and copies ran while one was open for 0% -> 0% of each run, Pallas kernels for 65% -> 24%
where the time goes in v3:
time: 20.4 us; the launch traced here: 20.2 us
  Pallas kernels  9.51 us (47%)
  starting transfers between devices  6.79 us (33%)
  waiting for transfers between devices  3.26 us (16%)
  between operations  0.65 us (3%)
    pallas_call x1, Pallas kernels, on_device(): pl.pallas_call(functools.partial(own_kernel, n_cp, count, group, slot_cou...  4.84 us
    pallas_call x1, Pallas kernels, on_device(): pl.pallas_call(functools.partial(earlier_kernel, n_cp, count, group), in_...  4.67 us
    ppermute x1, starting transfers between devices, on_device(): lax.ppermute(sent_rows, 'cp', [(c, (c + n_cp - 1) % n_cp) for c in range(...  3.48 us
    ppermute x1, starting transfers between devices, fetch(): blocks.append(lax.ppermute(own, ('cp', 'dec'), pairs))  3.08 us
    ppermute x1, waiting for transfers between devices, on_device(): lax.ppermute(sent_rows, 'cp', [(c, (c + n_cp - 1) % n_cp) for c in range(...  1.87 us
    ppermute x1, waiting for transfers between devices, fetch(): blocks.append(lax.ppermute(own, ('cp', 'dec'), pairs))  1.39 us
  transfers between devices with their start and end apart: 3, of which 2 were waited for; matrix products, arithmetic and copies ran while one was open for 0% of the time, Pallas kernels for 24%

profile of v3, /device:TPU:0, one launch (start us, length us, event | category | flops | bytes accessed | tf_op | source)
XLA Modules:
  0.0 20.2 jit_solution(5717065099382188024)
XLA Ops:
  0.6 0.0 copy-start
  0.6 3.1 %collective-permute-start = (bf16[576,128]{1,0:T(8,128)(2,1)}, bf16[576,128]{1,0:T(8,128)(2,1)S(1)}, u32[]{:S(2)}, u32[]{:S(2)}) collective-permute-start(bf16[576,128]{1,0:T(8,128)(2,1)} %bitcast.5), channel_id=1, source_target_pairs={{0,4},{1,9},{2,6},{3,11},{4,8},{5,13},{6,10},{7,15},{8,12},{9,1},{... | collective-permute-start | bytes 442376 | tf_op jit(solution)/shard_map/ppermute | solution.py:238
  3.7 4.8 %own.1 = (bf16[2048,576]{1,0:T(8,128)(2,1)S(1)}, f32[2048,512]{1,0:T(8,128)S(1)}, f32[2048,128]{1,0:T(8,128)S(1)}, f32[2048,128]{1,0:T(8,128)S(1)}, f32[128,256]...) custom-call(s32[2]{0:T(128)} %refs_0_.1, ...), custom_call_target="tpu_custom_call" | custom-call | flops 838860800 | bytes 5242880 | tf_op jit(solution)/shard_map/own/pallas_call | solution.py:268
  8.6 1.4 %collective-permute-done.refs_10_ = bf16[576,128]{1,0:T(8,128)(2,1)S(1)} collective-permute-done((bf16[576,128]{1,0:T(8,128)(2,1)}, bf16[576,128]{1,0:T(8,128)(2,1)S(1)}, u32[]{:S(2)}, u32[]{:S(2)}) %collective-permute-start) | collective-permute-done | bytes 147488 | tf_op jit(solution)/shard_map/ppermute | solution.py:238
  10.0 0.2 %collective-permute-start.2 = (bf16[576,128]{1,0:T(8,128)(2,1)S(1)}, bf16[576,128]{1,0:T(8,128)(2,1)S(1)}, u32[]{:S(2)}, u32[]{:S(2)}) collective-permute-start(bf16[576,128]{1,0:T(8,128)(2,1)S(1)} %collective-permute-done.refs_10_), channel_id=1, source_target_pairs={{0,1},{1,0},{2,3},{3,2},{4,5},{5,4},{6,7},{7,6},{8,9},{9,8},{10,11... | collective-permute-start | bytes 442376 | tf_op jit(solution)/shard_map/ppermute | solution.py:245
  10.2 3.5 %collective-permute-start.1 = (bf16[48,576]{1,0:T(8,128)(2,1)S(1)}, bf16[48,576]{1,0:T(8,128)(2,1)S(1)}, u32[]{:S(2)}, u32[]{:S(2)}) collective-permute-start(bf16[48,576]{1,0:T(8,128)(2,1)S(1)} %get-tuple-element.25), channel_id=1, source_target_pairs={{0,12},{4,0},{8,4},{12,8},{1,13},{5,1},{9,5},{13,9},{2,14},{6,2},{... | collective-permute-start | bytes 165896 | tf_op jit(solution)/shard_map/ppermute | solution.py:303
  13.7 1.9 %collective-permute-done.1.refs_8_ = bf16[48,576]{1,0:T(8,128)(2,1)S(1)} collective-permute-done((bf16[48,576]{1,0:T(8,128)(2,1)S(1)}, bf16[48,576]{1,0:T(8,128)(2,1)S(1)}, u32[]{:S(2)}, u32[]{:S(2)}) %collective-permute-start.1) | collective-permute-done | bytes 55328 | tf_op jit(solution)/shard_map/ppermute | solution.py:303
  15.5 0.0 collective-permute-done.2.refs_11_
  15.5 0.0 copy-done
  15.5 4.7 %earlier.1 = (bf16[128,2048]{1,0:T(8,128)(2,1)}, bf16[3,16,576]{2,1,0:T(8,128)(2,1)}, bf16[3,4,16]{2,1,0:T(4,128)(2,1)}) custom-call(bf16[2048,576]{1,0:T(8,128)(2,1)S(1)} %get-tuple-element.18.refs_0_, f32[2048,512]{1,0:T(8,128)S(1)} %get-tuple-element.19.refs_1_, f32[2048,128]{1,0:T(8,128)S(1)} %get-tuple-element.20.refs_2_, ...), custom_call_target="tpu_custom_call" | custom-call | flops 1409286144 | bytes 4980736 | tf_op jit(solution)/shard_map/earlier/pallas_call | solution.py:307
Async XLA Ops:
  0.6 14.9 %copy-start = (bf16[16,512,128]{2,1,0:T(8,128)(2,1)S(1)}, bf16[16,512,128]{2,1,0:T(8,128)(2,1)}, u32[]{:S(2)}) copy-start(bf16[16,512,128]{2,1,0:T(8,128)(2,1)} %refs_4_.3) | copy-start | bytes 6291460
  0.6 9.3 %collective-permute-start = (bf16[576,128]{1,0:T(8,128)(2,1)}, bf16[576,128]{1,0:T(8,128)(2,1)S(1)}, u32[]{:S(2)}, u32[]{:S(2)}) collective-permute-start(bf16[576,128]{1,0:T(8,128)(2,1)} %bitcast.5), channel_id=1, source_target_pairs={{0,4},{1,9},{2,6},{3,11},{4,8},{5,13},{6,10},{7,15},{8,12},{9,1},{... | collective-permute-start | bytes 442376 | tf_op jit(solution)/shard_map/ppermute | solution.py:238
  10.0 5.6 %collective-permute-start.2 = (bf16[576,128]{1,0:T(8,128)(2,1)S(1)}, bf16[576,128]{1,0:T(8,128)(2,1)S(1)}, u32[]{:S(2)}, u32[]{:S(2)}) collective-permute-start(bf16[576,128]{1,0:T(8,128)(2,1)S(1)} %collective-permute-done.refs_10_), channel_id=1, source_target_pairs={{0,1},{1,0},{2,3},{3,2},{4,5},{5,4},{6,7},{7,6},{8,9},{9,8},{10,11... | collective-permute-start | bytes 442376 | tf_op jit(solution)/shard_map/ppermute | solution.py:245
  10.2 5.3 %collective-permute-start.1 = (bf16[48,576]{1,0:T(8,128)(2,1)S(1)}, bf16[48,576]{1,0:T(8,128)(2,1)S(1)}, u32[]{:S(2)}, u32[]{:S(2)}) collective-permute-start(bf16[48,576]{1,0:T(8,128)(2,1)S(1)} %get-tuple-element.25), channel_id=1, source_target_pairs={{0,12},{4,0},{8,4},{12,8},{1,13},{5,1},{9,5},{13,9},{2,14},{6,2},{... | collective-permute-start | bytes 165896 | tf_op jit(solution)/shard_map/ppermute | solution.py:303

commit v4 on v3

--- a/solution.py
+++ b/solution.py
@@ -83,8 +83,8 @@
 
 def own_kernel(n_cp, count, group, slot_count, *refs):
     inputs, refs = refs[:6], refs[6:]
-    combined, summed, peaks, totals, bias, picked, kept_rows, sent_rows, filled = refs[:9]
-    buffers, sems, values = refs[9:15], refs[15], refs[16]
+    combined, summed, peaks, totals, bias, picked, kept_rows, filled = refs[:8]
+    buffers, sems, values = refs[8:14], refs[14], refs[15]
     pages_hbm, owner_hbm, offset_hbm, own_hbm, queries_hbm, absorb_hbm = inputs
     prompt_pages, decode_owner, slot_offset, own, queries, key_absorb = buffers
     rows = own.shape[1]
@@ -98,43 +98,22 @@
             pltpu.make_async_copy(queries_hbm.at[:, pl.ds(g * wide, wide)], queries.at[:, pl.ds(g * wide, wide)], sems.at[at]),
             pltpu.make_async_copy(absorb_hbm.at[pl.ds(g * group, group)], key_absorb.at[pl.ds(g * group, group)], sems.at[at + 1]),
         ))
-    for copy in small:
-        copy.start()
+    small[3].start()
     for pair in large:
         for copy in pair:
             copy.start()
-    for copy in small:
-        copy.wait()
+    for copy in small[:3]:
+        copy.start()
+    small[3].wait()
     block = own[...]
     values[...] = block[:LAT].T
-    own_bias = visible_bias(prompt_pages, rows, 0)
-    for b in range(count):
-        bias[:, b * rows:(b + 1) * rows] = visible_bias(prompt_pages, rows, swap_pair(jnp.int32(b + 1), n_cp))
-
-    me = lax.axis_index("cp")
-    targets = []
-    lane = lax.broadcasted_iota(jnp.int32, filled.shape, 1)
-    lane_filled = jnp.zeros(filled.shape, jnp.float32)
-    for c, (valid, page) in enumerate(slot_pages(me, slot_count, prompt_pages, decode_owner, slot_offset)):
-        source = page * PAGE // rows
-        column = swap_pair(lax.rem(me - source + n_cp, n_cp), n_cp) * rows + lax.rem(page * PAGE, rows)
-        targets.append(jnp.where(valid, column, -PAGE))
-        lane_filled = jnp.where(lane // PAGE == c, valid.astype(jnp.float32), lane_filled)
-    filled[...] = lane_filled
-    choice = row_picker(targets, (n_cp - 1) * rows)
-    picked[...] = choice
-    kept_rows[...] = lax.dot_general(choice[:, :rows], block, NT, preferred_element_type=jnp.float32).astype(jnp.bfloat16)
-    targets = []
-    behind = lax.rem(me + n_cp - 1, n_cp)
-    for valid, page in slot_pages(behind, slot_count, prompt_pages, decode_owner, slot_offset):
-        here = valid & (page * PAGE // rows == me)
-        targets.append(jnp.where(here, lax.rem(page * PAGE, rows), -PAGE))
-    choice = row_picker(targets, rows)
-    sent_rows[...] = lax.dot_general(choice, block, NT, preferred_element_type=jnp.float32).astype(jnp.bfloat16)
-
     for g in range(heads // group):
         for copy in large[g]:
             copy.wait()
+        if g == 0:
+            for copy in small[:3]:
+                copy.wait()
+            own_bias = visible_bias(prompt_pages, rows, 0)
         for h in range(g * group, (g + 1) * group):
             at = h * HEAD
             absorbed = jnp.dot(queries[:, at:at + NOPE], key_absorb[h], preferred_element_type=jnp.float32)
@@ -149,6 +128,22 @@
         summed[span, :] = jnp.dot(weights.astype(jnp.bfloat16), values[...], preferred_element_type=jnp.float32)
         peaks[span, :] = jnp.broadcast_to(peak, (group * rows, LANES))
         totals[span, :] = jnp.broadcast_to(total, (group * rows, LANES))
+
+    for b in range(count):
+        bias[:, b * rows:(b + 1) * rows] = visible_bias(prompt_pages, rows, swap_pair(jnp.int32(b + 1), n_cp))
+    me = lax.axis_index("cp")
+    targets = []
+    lane = lax.broadcasted_iota(jnp.int32, filled.shape, 1)
+    lane_filled = jnp.zeros(filled.shape, jnp.float32)
+    for c, (valid, page) in enumerate(slot_pages(me, slot_count, prompt_pages, decode_owner, slot_offset)):
+        source = page * PAGE // rows
+        column = swap_pair(lax.rem(me - source + n_cp, n_cp), n_cp) * rows + lax.rem(page * PAGE, rows)
+        targets.append(jnp.where(valid, column, -PAGE))
+        lane_filled = jnp.where(lane // PAGE == c, valid.astype(jnp.float32), lane_filled)
+    filled[...] = lane_filled
+    choice = row_picker(targets, n_cp * rows)
+    picked[...] = choice
+    kept_rows[...] = lax.dot_general(choice[:, :rows], block, NT, preferred_element_type=jnp.float32).astype(jnp.bfloat16)
 
 
 def write_cache(rows, filled, page_cache, page_scales):
@@ -174,8 +169,8 @@
 
 
 def earlier_kernel(n_cp, count, group, *refs):
-    combined, summed, peaks, totals, value_expand, bias, picked, kept_rows, sent_rows, filled = refs[:10]
-    pieces = refs[10:8 + n_cp]
+    combined, summed, peaks, totals, value_expand, bias, picked, kept_rows, filled = refs[:9]
+    pieces = refs[9:8 + n_cp]
     attended, page_cache, page_scales, keys, values, result, sems = refs[8 + n_cp:]
     rows = attended.shape[0]
     heads = value_expand.shape[0]
@@ -222,7 +217,7 @@
             one_group(g, 0)
     else:
         lax.fori_loop(0, heads // group, one_group, 0)
-    found = kept_rows[...].astype(jnp.float32) + sent_rows[...].astype(jnp.float32)
+    found = kept_rows[...].astype(jnp.float32)
     for b, piece in enumerate(pieces):
         choice = picked[:, (b + 1) * rows:(b + 2) * rows]
         found = found + lax.dot_general(choice, piece[...], NT, preferred_element_type=jnp.float32)
@@ -236,7 +231,8 @@
     for step in range(1, n_cp - 1, 2):
         pairs = [(c * n_dec + e, (c + step + e % 2) % n_cp * n_dec + e) for c in range(n_cp) for e in range(n_dec)]
         blocks.append(lax.ppermute(own, ("cp", "dec"), pairs))
-    return blocks
+    last = lax.ppermute(own, "cp", [(c, (c + n_cp - 1) % n_cp) for c in range(n_cp)])
+    return blocks, last
 
 
 def swap(blocks, n_dec):
@@ -258,25 +254,24 @@
     count = -(-reach // rows) - (1 if prompts == 2 else 0)
     count = min(n_cp - 2, count + count % 2)
     own = latent_rows.T
-    blocks = fetch(own, n_cp, dec_count)
+    blocks, last = fetch(own, n_cp, dec_count)
 
     vmem = pl.BlockSpec(memory_space=pltpu.VMEM)
     hbm = pl.BlockSpec(memory_space=pltpu.HBM)
     params = pltpu.CompilerParams(vmem_limit_bytes=32 * 2**20)
-    group = 8
+    group = 4
     inputs = (prompt_pages, decode_owner, slot_offset, own, queries, key_absorb)
-    (combined, summed, peaks, totals, bias, picked, kept_rows, sent_rows, filled) = pl.pallas_call(
+    (combined, summed, peaks, totals, bias, picked, kept_rows, filled) = pl.pallas_call(
         functools.partial(own_kernel, n_cp, count, group, slot_count),
         in_specs=[hbm] * 6,
-        out_specs=[vmem] * 9,
+        out_specs=[vmem] * 8,
         out_shape=[
             jax.ShapeDtypeStruct((heads * rows, ROW), jnp.bfloat16),
             jax.ShapeDtypeStruct((heads * rows, LAT), jnp.float32),
             jax.ShapeDtypeStruct((heads * rows, LANES), jnp.float32),
             jax.ShapeDtypeStruct((heads * rows, LANES), jnp.float32),
             jax.ShapeDtypeStruct((rows, count * rows), jnp.float32),
-            jax.ShapeDtypeStruct((kept, (n_cp - 1) * rows), jnp.bfloat16),
-            jax.ShapeDtypeStruct((kept, ROW), jnp.bfloat16),
+            jax.ShapeDtypeStruct((kept, n_cp * rows), jnp.bfloat16),
             jax.ShapeDtypeStruct((kept, ROW), jnp.bfloat16),
             jax.ShapeDtypeStruct((8, LANES), jnp.float32),
         ],
@@ -299,11 +294,10 @@
         name="own",
     )(*[pltpu.with_memory_space_constraint(x, pltpu.HBM) for x in inputs])
     blocks, combined = lax.optimization_barrier((blocks, combined))
-    pieces = swap(blocks, dec_count)
-    sent_rows = lax.ppermute(sent_rows, "cp", [(c, (c + n_cp - 1) % n_cp) for c in range(n_cp)])
+    pieces = swap(blocks, dec_count) + [last]
 
     group = 8 if count <= 4 else 1
-    operands = (combined, summed, peaks, totals, value_expand, bias, picked, kept_rows, sent_rows, filled, *pieces)
+    operands = (combined, summed, peaks, totals, value_expand, bias, picked, kept_rows, filled, *pieces)
     attended, page_cache, page_scales = pl.pallas_call(
         functools.partial(earlier_kernel, n_cp, count, group),
         in_specs=[vmem] * len(operands),

time: 20.4 us -> 18.6 us (0.912)
  the two profiles are of different devices: /device:TPU:0 before, /device:TPU:17 now
where the time goes in v4:
time: 18.6 us; the launch traced here: 18.5 us
  Pallas kernels  9.76 us (52%)
  starting transfers between devices  7.03 us (38%)
  waiting for transfers between devices  1.01 us (5%)
  between operations  0.67 us (4%)
    pallas_call x1, Pallas kernels, on_device(): pl.pallas_call(functools.partial(own_kernel, n_cp, count, group, slot_cou...  5.11 us
    pallas_call x1, Pallas kernels, on_device(): pl.pallas_call(functools.partial(earlier_kernel, n_cp, count, group), in_...  4.65 us
    ppermute x1, starting transfers between devices, swap(): lax.ppermute(block, 'dec', [(e, e ^ 1) for e in range(n_dec)])  4.5 us
    ppermute x1, starting transfers between devices, fetch(): lax.ppermute(own, 'cp', [(c, (c + n_cp - 1) % n_cp) for c in range(n_cp)])  2.47 us
    ppermute x1, waiting for transfers between devices, swap(): lax.ppermute(block, 'dec', [(e, e ^ 1) for e in range(n_dec)])  1 us
  transfers between devices with their start and end apart: 3, of which 1 were waited for; matrix products, arithmetic and copies ran while one was open for 0% of the time, Pallas kernels for 28%

profile of v4, /device:TPU:17, one launch (start us, length us, event | category | flops | bytes accessed | tf_op | source)
XLA Modules:
  0.0 18.5 jit_solution(13138374519931738339)
XLA Ops:
  0.6 0.0 copy-start
  0.6 0.1 collective-permute-start
  0.7 2.5 %collective-permute-start.2 = (bf16[576,128]{1,0:T(8,128)(2,1)}, bf16[576,128]{1,0:T(8,128)(2,1)S(1)}, u32[]{:S(2)}, u32[]{:S(2)}) collective-permute-start(bf16[576,128]{1,0:T(8,128)(2,1)} %bitcast.6), channel_id=1, source_target_pairs={{0,12},{4,0},{8,4},{12,8},{1,13},{5,1},{9,5},{13,9},{2,14},{6,2},{... | collective-permute-start | bytes 442376 | tf_op jit(solution)/shard_map/ppermute | solution.py:234
  3.2 5.1 %own.1 = (bf16[2048,576]{1,0:T(8,128)(2,1)S(1)}, f32[2048,512]{1,0:T(8,128)S(1)}, f32[2048,128]{1,0:T(8,128)S(1)}, f32[2048,128]{1,0:T(8,128)S(1)}, f32[128,256]...) custom-call(s32[2]{0:T(128)} %refs_0_.1, s32[2,2]{1,0:T(2,128)} %refs_1_.1, ...), custom_call_target="tpu_custom_call" | custom-call | flops 838860800 | bytes 5242880 | tf_op jit(solution)/shard_map/own/pallas_call | solution.py:264
  8.3 0.0 collective-permute-done.refs_9_
  8.3 4.5 %collective-permute-start.1 = (bf16[576,128]{1,0:T(8,128)(2,1)S(1)}, bf16[576,128]{1,0:T(8,128)(2,1)S(1)}, u32[]{:S(2)}, u32[]{:S(2)}) collective-permute-start(bf16[576,128]{1,0:T(8,128)(2,1)S(1)} %collective-permute-done.refs_9_), channel_id=1, source_target_pairs={{0,1},{1,0},{2,3},{3,2},{4,5},{5,4},{6,7},{7,6},{8,9},{9,8},{10,11... | collective-permute-start | bytes 442376 | tf_op jit(solution)/shard_map/ppermute | solution.py:241
  12.8 0.0 collective-permute-done.2.refs_11_
  12.8 1.0 %collective-permute-done.1.refs_10_ = bf16[576,128]{1,0:T(8,128)(2,1)S(1)} collective-permute-done((bf16[576,128]{1,0:T(8,128)(2,1)S(1)}, bf16[576,128]{1,0:T(8,128)(2,1)S(1)}, u32[]{:S(2)}, u32[]{:S(2)}) %collective-permute-start.1) | collective-permute-done | bytes 147488 | tf_op jit(solution)/shard_map/ppermute | solution.py:241
  13.8 0.0 copy-done
  13.8 4.6 %earlier.1 = (bf16[128,2048]{1,0:T(8,128)(2,1)}, bf16[3,16,576]{2,1,0:T(8,128)(2,1)}, bf16[3,4,16]{2,1,0:T(4,128)(2,1)}) custom-call(bf16[2048,576]{1,0:T(8,128)(2,1)S(1)} %get-tuple-element.17.refs_0_, f32[2048,512]{1,0:T(8,128)S(1)} %get-tuple-element.18.refs_1_, f32[2048,128]{1,0:T(8,128)S(1)} %get-tuple-element.19.refs_2_, ...), custom_call_target="tpu_custom_call" | custom-call | flops 1409286144 | bytes 4980736 | tf_op jit(solution)/shard_map/earlier/pallas_call | solution.py:301
Async XLA Ops:
  0.6 13.2 %copy-start = (bf16[16,512,128]{2,1,0:T(8,128)(2,1)S(1)}, bf16[16,512,128]{2,1,0:T(8,128)(2,1)}, u32[]{:S(2)}) copy-start(bf16[16,512,128]{2,1,0:T(8,128)(2,1)} %refs_4_.3) | copy-start | bytes 6291460
  0.6 7.7 %collective-permute-start = (bf16[576,128]{1,0:T(8,128)(2,1)}, bf16[576,128]{1,0:T(8,128)(2,1)S(1)}, u32[]{:S(2)}, u32[]{:S(2)}) collective-permute-start(bf16[576,128]{1,0:T(8,128)(2,1)} %bitcast.5), channel_id=1, source_target_pairs={{0,4},{1,9},{2,6},{3,11},{4,8},{5,13},{6,10},{7,15},{8,12},{9,1},{... | collective-permute-start | bytes 442376 | tf_op jit(solution)/shard_map/ppermute | solution.py:233
  0.7 12.1 %collective-permute-start.2 = (bf16[576,128]{1,0:T(8,128)(2,1)}, bf16[576,128]{1,0:T(8,128)(2,1)S(1)}, u32[]{:S(2)}, u32[]{:S(2)}) collective-permute-start(bf16[576,128]{1,0:T(8,128)(2,1)} %bitcast.6), channel_id=1, source_target_pairs={{0,12},{4,0},{8,4},{12,8},{1,13},{5,1},{9,5},{13,9},{2,14},{6,2},{... | collective-permute-start | bytes 442376 | tf_op jit(solution)/shard_map/ppermute | solution.py:234
  8.3 5.5 %collective-permute-start.1 = (bf16[576,128]{1,0:T(8,128)(2,1)S(1)}, bf16[576,128]{1,0:T(8,128)(2,1)S(1)}, u32[]{:S(2)}, u32[]{:S(2)}) collective-permute-start(bf16[576,128]{1,0:T(8,128)(2,1)S(1)} %collective-permute-done.refs_9_), channel_id=1, source_target_pairs={{0,1},{1,0},{2,3},{3,2},{4,5},{5,4},{6,7},{7,6},{8,9},{9,8},{10,11... | collective-permute-start | bytes 442376 | tf_op jit(solution)/shard_map/ppermute | solution.py:241

commit v5 on v4

--- a/solution.py
+++ b/solution.py
@@ -18,6 +18,7 @@
 ROW = LAT + ROPE
 HEAD = NOPE + ROPE
 LANES = 128
+SWAP = 3
 
 masked_fill = -1e30
 amax_epsilon = 1e-06
@@ -81,10 +82,15 @@
     return jnp.where(column == target, 1.0, 0.0).astype(jnp.bfloat16)
 
 
-def own_kernel(n_cp, count, group, slot_count, *refs):
-    inputs, refs = refs[:6], refs[6:]
-    combined, summed, peaks, totals, bias, picked, kept_rows, filled = refs[:8]
-    buffers, sems, values = refs[8:14], refs[14], refs[15]
+def head_values(latents, value_expand, h):
+    both = jnp.concatenate([value_expand[h], value_expand[h + 1]], axis=1)
+    return jnp.dot(latents, both, preferred_element_type=jnp.float32).astype(jnp.bfloat16)
+
+
+def own_kernel(n_cp, group, slot_count, *refs):
+    inputs, expand_hbm, refs = refs[:6], refs[6], refs[7:]
+    combined, result, peaks, totals, sent_rows, value_expand = refs[:6]
+    buffers, sems, latents = refs[6:12], refs[12], refs[13]
     pages_hbm, owner_hbm, offset_hbm, own_hbm, queries_hbm, absorb_hbm = inputs
     prompt_pages, decode_owner, slot_offset, own, queries, key_absorb = buffers
     rows = own.shape[1]
@@ -93,20 +99,21 @@
     small = [pltpu.make_async_copy(inputs[i], buffers[i], sems.at[i]) for i in range(4)]
     large = []
     for g in range(heads // group):
-        at = 4 + 2 * g
+        at = 4 + 3 * g
+        some = pl.ds(g * group, group)
         large.append((
             pltpu.make_async_copy(queries_hbm.at[:, pl.ds(g * wide, wide)], queries.at[:, pl.ds(g * wide, wide)], sems.at[at]),
-            pltpu.make_async_copy(absorb_hbm.at[pl.ds(g * group, group)], key_absorb.at[pl.ds(g * group, group)], sems.at[at + 1]),
+            pltpu.make_async_copy(absorb_hbm.at[some], key_absorb.at[some], sems.at[at + 1]),
+            pltpu.make_async_copy(expand_hbm.at[some], value_expand.at[some], sems.at[at + 2]),
         ))
-    small[3].start()
+    for copy in small:
+        copy.start()
     for pair in large:
         for copy in pair:
             copy.start()
-    for copy in small[:3]:
-        copy.start()
     small[3].wait()
     block = own[...]
-    values[...] = block[:LAT].T
+    latents[...] = block[:LAT].T
     for g in range(heads // group):
         for copy in large[g]:
             copy.wait()
@@ -114,6 +121,16 @@
             for copy in small[:3]:
                 copy.wait()
             own_bias = visible_bias(prompt_pages, rows, 0)
+            me = lax.axis_index("cp")
+            behind = lax.rem(me + n_cp - 1, n_cp)
+            targets = []
+            for valid, page in slot_pages(behind, slot_count, prompt_pages, decode_owner, slot_offset):
+                here = valid & (page * PAGE // rows == me)
+                targets.append(jnp.where(here, lax.rem(page * PAGE, rows), -PAGE))
+            choice = row_picker(targets, rows)
+            sent = lax.dot_general(choice, block, NT, preferred_element_type=jnp.float32)
+            sent_rows[:, :ROW] = sent.astype(jnp.bfloat16)
+            sent_rows[:, ROW:] = jnp.zeros((choice.shape[0], sent_rows.shape[1] - ROW), jnp.bfloat16)
         for h in range(g * group, (g + 1) * group):
             at = h * HEAD
             absorbed = jnp.dot(queries[:, at:at + NOPE], key_absorb[h], preferred_element_type=jnp.float32)
@@ -125,10 +142,28 @@
         peak = jnp.max(scores, axis=1, keepdims=True)
         weights = jnp.exp2((scores - peak) * exp2_scale)
         total = jnp.sum(weights, axis=1, keepdims=True)
-        summed[span, :] = jnp.dot(weights.astype(jnp.bfloat16), values[...], preferred_element_type=jnp.float32)
+        weights = weights.astype(jnp.bfloat16)
+        for i in range(0, group, 2):
+            both = head_values(latents[...], value_expand, g * group + i)
+            for j in range(2):
+                h = i + j
+                out = jnp.dot(weights[h * rows:(h + 1) * rows], both[:, j * VDIM:(j + 1) * VDIM], preferred_element_type=jnp.float32)
+                result[(g * group + h) * rows:(g * group + h + 1) * rows, :] = out
         peaks[span, :] = jnp.broadcast_to(peak, (group * rows, LANES))
         totals[span, :] = jnp.broadcast_to(total, (group * rows, LANES))
 
+
+def index_kernel(n_cp, count, slot_count, *refs):
+    inputs, refs = refs[:4], refs[4:]
+    bias, picked, kept_rows, filled = refs[:4]
+    buffers, sems = refs[4:8], refs[8]
+    prompt_pages, decode_owner, slot_offset, own = buffers
+    rows = own.shape[1]
+    copies = [pltpu.make_async_copy(inputs[i], buffers[i], sems.at[i]) for i in range(4)]
+    for copy in copies:
+        copy.start()
+    for copy in copies:
+        copy.wait()
     for b in range(count):
         bias[:, b * rows:(b + 1) * rows] = visible_bias(prompt_pages, rows, swap_pair(jnp.int32(b + 1), n_cp))
     me = lax.axis_index("cp")
@@ -141,9 +176,9 @@
         targets.append(jnp.where(valid, column, -PAGE))
         lane_filled = jnp.where(lane // PAGE == c, valid.astype(jnp.float32), lane_filled)
     filled[...] = lane_filled
-    choice = row_picker(targets, n_cp * rows)
+    choice = row_picker(targets, (n_cp - 1) * rows)
     picked[...] = choice
-    kept_rows[...] = lax.dot_general(choice[:, :rows], block, NT, preferred_element_type=jnp.float32).astype(jnp.bfloat16)
+    kept_rows[...] = lax.dot_general(choice[:, :rows], own[...], NT, preferred_element_type=jnp.float32).astype(jnp.bfloat16)
 
 
 def write_cache(rows, filled, page_cache, page_scales):
@@ -169,16 +204,20 @@
 
 
 def earlier_kernel(n_cp, count, group, *refs):
-    combined, summed, peaks, totals, value_expand, bias, picked, kept_rows, filled = refs[:9]
-    pieces = refs[9:8 + n_cp]
-    attended, page_cache, page_scales, keys, values, result, sems = refs[8 + n_cp:]
+    combined, own_result, peaks, totals, value_expand, bias, picked, kept_rows, sent_rows, filled = refs[:10]
+    arrived, refs = refs[10:10 + (n_cp - 2) // 2 * (1 + SWAP)], refs[10 + (n_cp - 2) // 2 * (1 + SWAP):]
+    attended, page_cache, page_scales, keys, latents, result, sems = refs
+    pieces = []
+    for at in range(0, len(arrived), 1 + SWAP):
+        pieces.append(arrived[at][...])
+        pieces.append(jnp.concatenate([part[...] for part in arrived[at + 1:at + 1 + SWAP]], axis=0))
     rows = attended.shape[0]
     heads = value_expand.shape[0]
     width = count * rows
     for b in range(count):
-        block = pieces[b][...]
+        block = pieces[b]
         keys[:, b * rows:(b + 1) * rows] = block
-        values[b * rows:(b + 1) * rows, :] = block[:LAT].T
+        latents[b * rows:(b + 1) * rows, :] = block[:LAT].T
 
     def one_group(g, _):
         span = pl.ds(pl.multiple_of(g * group * rows, group * rows), group * rows)
@@ -192,19 +231,17 @@
             part = jnp.exp2((scores[:, b * rows:(b + 1) * rows] - peak) * exp2_scale)
             total = total + jnp.sum(part, axis=1, keepdims=True)
             weights.append(part.astype(jnp.bfloat16))
+        weights = jnp.concatenate(weights, axis=1)
         factor = jnp.exp2((old_peak - peak) * exp2_scale)
         inverse = 1.0 / (totals[span, :] * factor + total)
-        factor = factor * inverse
-        added = jnp.dot(jnp.concatenate(weights, axis=1), values[...], preferred_element_type=jnp.float32)
-        mixed = []
-        for b in range(NBLK):
-            part = slice(b * BLOCK, (b + 1) * BLOCK)
-            mixed.append((summed[span, part] * factor + added[:, part] * inverse).astype(jnp.bfloat16))
-        mixed = jnp.concatenate(mixed, axis=1)
-        for h in range(group):
-            out = jnp.dot(mixed[h * rows:(h + 1) * rows], value_expand[g * group + h], preferred_element_type=jnp.float32)
-            at = pl.ds(pl.multiple_of((g * group + h) * VDIM, VDIM), VDIM)
-            result[:, at] = out.astype(jnp.bfloat16)
+        old = own_result[span, :] * (factor * inverse)
+        for i in range(0, group, 2):
+            both = head_values(latents[...], value_expand, g * group + i)
+            for j in range(2):
+                part = slice((i + j) * rows, (i + j + 1) * rows)
+                out = jnp.dot(weights[part], both[:, j * VDIM:(j + 1) * VDIM], preferred_element_type=jnp.float32)
+                at = pl.ds(pl.multiple_of((g * group + i + j) * VDIM, VDIM), VDIM)
+                result[:, at] = (old[part] + out * inverse[part]).astype(jnp.bfloat16)
         send(g).start()
         return 0
 
@@ -217,10 +254,10 @@
             one_group(g, 0)
     else:
         lax.fori_loop(0, heads // group, one_group, 0)
-    found = kept_rows[...].astype(jnp.float32)
+    found = kept_rows[...].astype(jnp.float32) + sent_rows[:, :ROW].astype(jnp.float32)
     for b, piece in enumerate(pieces):
         choice = picked[:, (b + 1) * rows:(b + 2) * rows]
-        found = found + lax.dot_general(choice, piece[...], NT, preferred_element_type=jnp.float32)
+        found = found + lax.dot_general(choice, piece, NT, preferred_element_type=jnp.float32)
     write_cache(found, filled, page_cache, page_scales)
     for g in range(heads // group):
         send(g).wait()
@@ -231,14 +268,14 @@
     for step in range(1, n_cp - 1, 2):
         pairs = [(c * n_dec + e, (c + step + e % 2) % n_cp * n_dec + e) for c in range(n_cp) for e in range(n_dec)]
         blocks.append(lax.ppermute(own, ("cp", "dec"), pairs))
-    last = lax.ppermute(own, "cp", [(c, (c + n_cp - 1) % n_cp) for c in range(n_cp)])
-    return blocks, last
+    return blocks
 
 
 def swap(blocks, n_dec):
     pieces = []
     for block in blocks:
-        pieces += [block, lax.ppermute(block, "dec", [(e, e ^ 1) for e in range(n_dec)])]
+        parts = [block[at:at + ROW // SWAP] for at in range(0, ROW, ROW // SWAP)]
+        pieces += [block] + [lax.ppermute(part, "dec", [(e, e ^ 1) for e in range(n_dec)]) for part in parts]
     return pieces
 
 
@@ -254,50 +291,67 @@
     count = -(-reach // rows) - (1 if prompts == 2 else 0)
     count = min(n_cp - 2, count + count % 2)
     own = latent_rows.T
-    blocks, last = fetch(own, n_cp, dec_count)
+    blocks = fetch(own, n_cp, dec_count)
 
     vmem = pl.BlockSpec(memory_space=pltpu.VMEM)
     hbm = pl.BlockSpec(memory_space=pltpu.HBM)
     params = pltpu.CompilerParams(vmem_limit_bytes=32 * 2**20)
     group = 4
-    inputs = (prompt_pages, decode_owner, slot_offset, own, queries, key_absorb)
-    (combined, summed, peaks, totals, bias, picked, kept_rows, filled) = pl.pallas_call(
-        functools.partial(own_kernel, n_cp, count, group, slot_count),
-        in_specs=[hbm] * 6,
-        out_specs=[vmem] * 8,
+    inputs = [pltpu.with_memory_space_constraint(x, pltpu.HBM) for x in (prompt_pages, decode_owner, slot_offset, own, queries, key_absorb)]
+    small_scratch = [
+        pltpu.SMEM(prompt_pages.shape, jnp.int32),
+        pltpu.SMEM(decode_owner.shape, jnp.int32),
+        pltpu.SMEM(slot_offset.shape, jnp.int32),
+        pltpu.VMEM((ROW, rows), jnp.bfloat16),
+    ]
+    combined, result, peaks, totals, sent_rows, value_copy = pl.pallas_call(
+        functools.partial(own_kernel, n_cp, group, slot_count),
+        in_specs=[hbm] * 7,
+        out_specs=[vmem] * 6,
         out_shape=[
             jax.ShapeDtypeStruct((heads * rows, ROW), jnp.bfloat16),
-            jax.ShapeDtypeStruct((heads * rows, LAT), jnp.float32),
+            jax.ShapeDtypeStruct((heads * rows, VDIM), jnp.float32),
             jax.ShapeDtypeStruct((heads * rows, LANES), jnp.float32),
             jax.ShapeDtypeStruct((heads * rows, LANES), jnp.float32),
-            jax.ShapeDtypeStruct((rows, count * rows), jnp.float32),
-            jax.ShapeDtypeStruct((kept, n_cp * rows), jnp.bfloat16),
-            jax.ShapeDtypeStruct((kept, ROW), jnp.bfloat16),
-            jax.ShapeDtypeStruct((8, LANES), jnp.float32),
+            jax.ShapeDtypeStruct((kept, -(-ROW // LANES) * LANES), jnp.bfloat16),
+            jax.ShapeDtypeStruct(value_expand.shape, jnp.bfloat16),
         ],
-        scratch_shapes=[
-            pltpu.SMEM(prompt_pages.shape, jnp.int32),
-            pltpu.SMEM(decode_owner.shape, jnp.int32),
-            pltpu.SMEM(slot_offset.shape, jnp.int32),
-            pltpu.VMEM((ROW, rows), jnp.bfloat16),
+        scratch_shapes=small_scratch + [
             pltpu.VMEM((rows, heads * HEAD), jnp.bfloat16),
             pltpu.VMEM((heads, NOPE, LAT), jnp.bfloat16),
-            pltpu.SemaphoreType.DMA((4 + 2 * (heads // group),)),
+            pltpu.SemaphoreType.DMA((4 + 3 * (heads // group),)),
             pltpu.VMEM((rows, LAT), jnp.bfloat16),
         ],
         cost_estimate=pl.CostEstimate(
-            flops=2 * rows * heads * (NOPE * LAT + rows * (ROW + LAT)),
+            flops=2 * rows * heads * (2 * NOPE * LAT + rows * (ROW + VDIM)),
             bytes_accessed=2 * (queries.size + key_absorb.size + heads * rows * ROW),
             transcendentals=rows * heads * rows,
         ),
         compiler_params=params,
         name="own",
-    )(*[pltpu.with_memory_space_constraint(x, pltpu.HBM) for x in inputs])
-    blocks, combined = lax.optimization_barrier((blocks, combined))
-    pieces = swap(blocks, dec_count) + [last]
-
-    group = 8 if count <= 4 else 1
-    operands = (combined, summed, peaks, totals, value_expand, bias, picked, kept_rows, filled, *pieces)
+    )(*inputs, pltpu.with_memory_space_constraint(value_expand, pltpu.HBM))
+    sent_rows = lax.ppermute(sent_rows, "cp", [(c, (c + n_cp - 1) % n_cp) for c in range(n_cp)])
+    *inputs, combined = lax.optimization_barrier((*inputs[:4], combined))
+    bias, picked, kept_rows, filled = pl.pallas_call(
+        functools.partial(index_kernel, n_cp, count, slot_count),
+        in_specs=[hbm] * 4,
+        out_specs=[vmem] * 4,
+        out_shape=[
+            jax.ShapeDtypeStruct((rows, count * rows), jnp.float32),
+            jax.ShapeDtypeStruct((kept, (n_cp - 1) * rows), jnp.bfloat16),
+            jax.ShapeDtypeStruct((kept, ROW), jnp.bfloat16),
+            jax.ShapeDtypeStruct((8, LANES), jnp.float32),
+        ],
+        scratch_shapes=small_scratch + [pltpu.SemaphoreType.DMA((4,))],
+        cost_estimate=pl.CostEstimate(flops=2**27, bytes_accessed=2**20, transcendentals=0),
+        compiler_params=params,
+        name="index",
+    )(*inputs)
+    blocks, bias = lax.optimization_barrier((blocks, bias))
+    pieces = swap(blocks, dec_count)
+
+    group = 8 if count <= 4 else 2
+    operands = (combined, result, peaks, totals, value_copy, bias, picked, kept_rows, sent_rows, filled, *pieces)
     attended, page_cache, page_scales = pl.pallas_call(
         functools.partial(earlier_kernel, n_cp, count, group),
         in_specs=[vmem] * len(operands),
@@ -314,7 +368,7 @@
             pltpu.SemaphoreType.DMA((heads // group,)),
         ],
         cost_estimate=pl.CostEstimate(
-            flops=2 * rows * heads * (count * rows * (ROW + LAT) + LAT * VDIM),
+            flops=2 * heads * count * rows * (rows * (ROW + VDIM) + LAT * VDIM),
             bytes_accessed=2 * (heads * rows * (ROW + VDIM) + value_expand.size),
             transcendentals=rows * heads * count * rows,
         ),

time: 18.6 us -> 19.4 us (1.043)
  the two profiles are of different devices: /device:TPU:17 before, /device:TPU:0 now
where the time goes in v5:
time: 19.4 us; the launch traced here: 19.3 us
  Pallas kernels  11.6 us (60%)
  starting transfers between devices  5.81 us (30%)
  waiting for transfers between devices  1.15 us (6%)
  between operations  0.67 us (3%)
    pallas_call x1, Pallas kernels, on_device(): pl.pallas_call(functools.partial(own_kernel, n_cp, group, slot_count), in...  5.32 us
    pallas_call x1, Pallas kernels, on_device(): pl.pallas_call(functools.partial(earlier_kernel, n_cp, count, group), in_...  5.14 us
    ppermute x1, starting transfers between devices, fetch(): blocks.append(lax.ppermute(own, ('cp', 'dec'), pairs))  3.08 us
    ppermute x1, starting transfers between devices, on_device(): lax.ppermute(sent_rows, 'cp', [(c, (c + n_cp - 1) % n_cp) for c in range(...  2.09 us
    pallas_call x1, Pallas kernels, on_device(): pl.pallas_call(functools.partial(index_kernel, n_cp, count, slot_count),...  1.17 us
    ppermute x3, starting transfers between devices, swap(): lax.ppermute(part, 'dec', [(e, e ^ 1) for e in range(n_dec)])  0.65 us
    ppermute x1, waiting for transfers between devices, on_device(): lax.ppermute(sent_rows, 'cp', [(c, (c + n_cp - 1) % n_cp) for c in range(...  0.59 us
    ppermute x3, waiting for transfers between devices, swap(): lax.ppermute(part, 'dec', [(e, e ^ 1) for e in range(n_dec)])  0.57 us
  transfers between devices with their start and end apart: 5, of which 4 were waited for; matrix products, arithmetic and copies ran while one was open for 0% of the time, Pallas kernels for 34%

profile of v5, /device:TPU:0, one launch (start us, length us, event | category | flops | bytes accessed | tf_op | source)
XLA Modules:
  0.0 19.3 jit_solution(17750657292741860571)
XLA Ops:
  0.6 3.1 %collective-permute-start = (bf16[576,128]{1,0:T(8,128)(2,1)}, bf16[576,128]{1,0:T(8,128)(2,1)S(1)}, u32[]{:S(2)}, u32[]{:S(2)}) collective-permute-start(bf16[576,128]{1,0:T(8,128)(2,1)} %bitcast.5), channel_id=1, source_target_pairs={{0,4},{1,9},{2,6},{3,11},{4,8},{5,13},{6,10},{7,15},{8,12},{9,1},{... | collective-permute-start | bytes 442376 | tf_op jit(solution)/shard_map/ppermute | solution.py:270
  3.7 5.3 %own.1 = (bf16[2048,576]{1,0:T(8,128)(2,1)S(1)}, f32[2048,128]{1,0:T(8,128)S(1)}, f32[2048,128]{1,0:T(8,128)S(1)}, f32[2048,128]{1,0:T(8,128)S(1)}, bf16[48,640]...) custom-call(s32[2]{0:T(128)} %refs_0_.2, s32[2,2]{1,0:T(2,128)} %refs_1_.2, s32[2]{0:T(128)} %refs_2_.2, ...), custom_call_target="tpu_custom_call" | custom-call | flops 905969664 | bytes 5242880 | tf_op jit(solution)/shard_map/own/pallas_call | solution.py:307
  9.0 2.1 %collective-permute-start.1 = (bf16[48,640]{1,0:T(8,128)(2,1)S(1)}, bf16[48,640]{1,0:T(8,128)(2,1)S(1)}, u32[]{:S(2)}, u32[]{:S(2)}) collective-permute-start(bf16[48,640]{1,0:T(8,128)(2,1)S(1)} %get-tuple-element.37), channel_id=1, source_target_pairs={{0,12},{4,0},{8,4},{12,8},{1,13},{5,1},{9,5},{13,9},{2,14},{6,2},{... | collective-permute-start | bytes 184328 | tf_op jit(solution)/shard_map/ppermute | solution.py:333
  11.1 1.2 %index.1 = (f32[128,256]{1,0:T(8,128)S(1)}, bf16[48,384]{1,0:T(8,128)(2,1)S(1)}, bf16[48,576]{1,0:T(8,128)(2,1)S(1)}, f32[8,128]{1,0:T(8,128)S(1)}) custom-call(s32[2]{0:T(128)} %refs_0_.2, s32[2,2]{1,0:T(2,128)} %refs_1_.2, s32[2]{0:T(128)} %refs_2_.2, bf16[576,128]{1,0:T(8,128)(2,1)} %bitcast.7), custom_call_target="tpu_custom_call" | custom-call | flops 134217728 | bytes 1048576 | tf_op jit(solution)/shard_map/index/pallas_call | solution.py:335
  12.3 0.0 collective-permute-done.refs_10_
  12.3 0.1 collective-permute-start.4
  12.4 0.5 %collective-permute-start.3 = (bf16[192,128]{1,0:T(8,128)(2,1)S(1)}, bf16[192,128]{1,0:T(8,128)(2,1)S(1)}, u32[]{:S(2)}, u32[]{:S(2)}) collective-permute-start(bf16[192,128]{1,0:T(8,128)(2,1)S(1)} %get-tuple-element.44), channel_id=1, source_target_pairs={{0,1},{1,0},{2,3},{3,2},{4,5},{5,4},{6,7},{7,6},{8,9},{9,8},{10,11... | collective-permute-start | bytes 147464 | tf_op jit(solution)/shard_map/ppermute | solution.py:278
  12.9 0.1 collective-permute-start.2
  13.0 0.6 %collective-permute-done.1.refs_8_ = bf16[48,640]{1,0:T(8,128)(2,1)S(1)} collective-permute-done((bf16[48,640]{1,0:T(8,128)(2,1)S(1)}, bf16[48,640]{1,0:T(8,128)(2,1)S(1)}, u32[]{:S(2)}, u32[]{:S(2)}) %collective-permute-start.1) | collective-permute-done | bytes 61472 | tf_op jit(solution)/shard_map/ppermute | solution.py:333
  13.6 0.1 collective-permute-done.4.refs_13_
  13.6 0.2 collective-permute-done.3.refs_12_
  13.8 0.3 %collective-permute-done.2.refs_11_ = bf16[192,128]{1,0:T(8,128)(2,1)S(1)} collective-permute-done((bf16[192,128]{1,0:T(8,128)(2,1)S(1)}, bf16[192,128]{1,0:T(8,128)(2,1)S(1)}, u32[]{:S(2)}, u32[]{:S(2)}) %collective-permute-start.2) | collective-permute-done | bytes 49184 | tf_op jit(solution)/shard_map/ppermute | solution.py:278
  14.1 5.1 %earlier.1 = (bf16[128,2048]{1,0:T(8,128)(2,1)}, bf16[3,16,576]{2,1,0:T(8,128)(2,1)}, bf16[3,4,16]{2,1,0:T(4,128)(2,1)}) custom-call(bf16[2048,576]{1,0:T(8,128)(2,1)S(1)} %get-tuple-element.24.refs_0_, f32[2048,128]{1,0:T(8,128)S(1)} %get-tuple-element.25.refs_1_, f32[2048,128]{1,0:T(8,128)S(1)} %get-tuple-element.26.refs_2_, ...), custom_call_target="tpu_custom_call" | custom-call | flops 1275068416 | bytes 4980736 | tf_op jit(solution)/shard_map/earlier/pallas_call | solution.py:355
  (1 shorter events, 0.0 us)
Async XLA Ops:
  0.6 11.7 %collective-permute-start = (bf16[576,128]{1,0:T(8,128)(2,1)}, bf16[576,128]{1,0:T(8,128)(2,1)S(1)}, u32[]{:S(2)}, u32[]{:S(2)}) collective-permute-start(bf16[576,128]{1,0:T(8,128)(2,1)} %bitcast.5), channel_id=1, source_target_pairs={{0,4},{1,9},{2,6},{3,11},{4,8},{5,13},{6,10},{7,15},{8,12},{9,1},{... | collective-permute-start | bytes 442376 | tf_op jit(solution)/shard_map/ppermute | solution.py:270
  9.0 4.5 %collective-permute-start.1 = (bf16[48,640]{1,0:T(8,128)(2,1)S(1)}, bf16[48,640]{1,0:T(8,128)(2,1)S(1)}, u32[]{:S(2)}, u32[]{:S(2)}) collective-permute-start(bf16[48,640]{1,0:T(8,128)(2,1)S(1)} %get-tuple-element.37), channel_id=1, source_target_pairs={{0,12},{4,0},{8,4},{12,8},{1,13},{5,1},{9,5},{13,9},{2,14},{6,2},{... | collective-permute-start | bytes 184328 | tf_op jit(solution)/shard_map/ppermute | solution.py:333
  12.3 1.3 %collective-permute-start.4 = (bf16[192,128]{1,0:T(8,128)(2,1)S(1)}, bf16[192,128]{1,0:T(8,128)(2,1)S(1)}, u32[]{:S(2)}, u32[]{:S(2)}) collective-permute-start(bf16[192,128]{1,0:T(8,128)(2,1)S(1)} %get-tuple-element.43), channel_id=1, source_target_pairs={{0,1},{1,0},{2,3},{3,2},{4,5},{5,4},{6,7},{7,6},{8,9},{9,8},{10,11... | collective-permute-start | bytes 147464 | tf_op jit(solution)/shard_map/ppermute | solution.py:278
  12.4 1.4 %collective-permute-start.3 = (bf16[192,128]{1,0:T(8,128)(2,1)S(1)}, bf16[192,128]{1,0:T(8,128)(2,1)S(1)}, u32[]{:S(2)}, u32[]{:S(2)}) collective-permute-start(bf16[192,128]{1,0:T(8,128)(2,1)S(1)} %get-tuple-element.44), channel_id=1, source_target_pairs={{0,1},{1,0},{2,3},{3,2},{4,5},{5,4},{6,7},{7,6},{8,9},{9,8},{10,11... | collective-permute-start | bytes 147464 | tf_op jit(solution)/shard_map/ppermute | solution.py:278
  12.9 1.2 %collective-permute-start.2 = (bf16[192,128]{1,0:T(8,128)(2,1)S(1)}, bf16[192,128]{1,0:T(8,128)(2,1)S(1)}, u32[]{:S(2)}, u32[]{:S(2)}) collective-permute-start(bf16[192,128]{1,0:T(8,128)(2,1)S(1)} %get-tuple-element.45), channel_id=1, source_target_pairs={{0,1},{1,0},{2,3},{3,2},{4,5},{5,4},{6,7},{7,6},{8,9},{9,8},{10,11... | collective-permute-start | bytes 147464 | tf_op jit(solution)/shard_map/ppermute | solution.py:278

commit v6 on v4

v6 whole, which is shorter than its diff:
```python
import functools
import math

import jax
import jax.numpy as jnp
from jax import lax
from jax.experimental import pallas as pl
from jax.experimental.pallas import tpu as pltpu
from jax.sharding import PartitionSpec as P

LAT = 512
ROPE = 64
NOPE = 128
VDIM = 128
PAGE = 16
BLOCK = 128
NBLK = LAT // BLOCK
ROW = LAT + ROPE
HEAD = NOPE + ROPE
LANES = 128
SWAP = 3

masked_fill = -1e30
amax_epsilon = 1e-06
exp2_scale = math.log2(math.e) / math.sqrt(HEAD)

NT = (((1,), (1,)), ((), ()))


def prompt_starts(prompt_pages):
    starts = [jnp.int32(0)]
    for k in range(prompt_pages.shape[0] - 1):
        starts.append(starts[-1] + prompt_pages[k])
    return starts


def visible_bias(prompt_pages, rows, steps_back):
    first = lax.axis_index("cp") * rows
    token = first + lax.broadcasted_iota(jnp.int32, (rows, 1), 0)
    begin = jnp.zeros((rows, 1), jnp.int32)
    for start in prompt_starts(prompt_pages):
        begin = jnp.maximum(begin, jnp.where(start * PAGE <= token, start * PAGE, 0))
    spot = first - steps_back * rows + lax.broadcasted_iota(jnp.int32, (1, rows), 1)
    return jnp.where((spot >= begin) & (spot <= token), 0.0, masked_fill)


def swap_pair(position, n_cp):
    odd = lax.rem(lax.axis_index("dec"), 2)
    within = lax.rem(position + 1, 2)
    swapped = position - within + lax.rem(within + odd, 2)
    paired = (position >= 1) & (position <= (n_cp - 1) // 2 * 2)
    return jnp.where(paired, swapped, position)


def slot_pages(owner, slot_count, prompt_pages, decode_owner, slot_offset):
    prompts, width = decode_owner.shape
    cycle = width * lax.axis_size("dec") * slot_count
    starts = prompt_starts(prompt_pages)
    pages, start, offset, place = jnp.int32(0), jnp.int32(0), jnp.int32(0), jnp.int32(0)
    for k in range(prompts):
        for p in range(width):
            mine = decode_owner[k, p] == owner
            pages = jnp.where(mine, prompt_pages[k], pages)
            start = jnp.where(mine, starts[k], start)
            offset = jnp.where(mine, slot_offset[k], offset)
            place = jnp.where(mine, p, place)
    result = []
    for c in range(slot_count):
        turn = width * (lax.axis_index("dec") * slot_count + c) + place
        page = lax.rem(turn - offset + 2 * cycle, cycle)
        result.append((page < pages, start + page))
    return result


def row_picker(targets, columns):
    kept = len(targets) * PAGE
    row = lax.broadcasted_iota(jnp.int32, (kept, 1), 0)
    target = jnp.full((kept, 1), -1, jnp.int32)
    for c, column in enumerate(targets):
        target = jnp.where(row // PAGE == c, column + row % PAGE, target)
    column = lax.broadcasted_iota(jnp.int32, (1, columns), 1)
    return jnp.where(column == target, 1.0, 0.0).astype(jnp.bfloat16)


def head_values(latents, value_expand, h):
    both = jnp.concatenate([value_expand[h], value_expand[h + 1]], axis=1)
    return jnp.dot(latents, both, preferred_element_type=jnp.float32).astype(jnp.bfloat16)


def own_kernel(n_cp, count, chunk, group, slot_count, *refs):
    inputs, refs = refs[:7], refs[7:]
    combined, result, peaks, totals, sent_rows, bias, picked, filled, own, value_expand = refs[:10]
    prompt_pages, decode_owner, slot_offset, queries, key_absorb, latents, sems = refs[10:]
    pages_hbm, owner_hbm, offset_hbm, own_hbm, queries_hbm, absorb_hbm, expand_hbm = inputs
    rows = own.shape[1]
    heads = key_absorb.shape[0]
    small = [
        pltpu.make_async_copy(source, target, sems.at[i])
        for i, (source, target) in enumerate(zip(inputs[:4], (prompt_pages, decode_owner, slot_offset, own)))
    ]
    large = []
    for g in range(heads // chunk):
        at = 4 + 3 * g
        some = pl.ds(g * chunk, chunk)
        wide = pl.ds(g * chunk * HEAD, chunk * HEAD)
        large.append((
            pltpu.make_async_copy(queries_hbm.at[:, wide], queries.at[:, wide], sems.at[at]),
            pltpu.make_async_copy(absorb_hbm.at[some], key_absorb.at[some], sems.at[at + 1]),
            pltpu.make_async_copy(expand_hbm.at[some], value_expand.at[some], sems.at[at + 2]),
        ))
    for copy in small:
        copy.start()
    for i in range(3):
        for chunk_copies in large:
            if i < 2:
                chunk_copies[i].start()
    for chunk_copies in large:
        chunk_copies[2].start()
    small[3].wait()
    block = own[...]
    latents[...] = block[:LAT].T
    for copy in small[:3]:
        copy.wait()
    own_bias = visible_bias(prompt_pages, rows, 0)
    index_work(n_cp, count, slot_count, prompt_pages, decode_owner, slot_offset, block, sent_rows, bias, picked, filled)

    for g in range(heads // group):
        if g * group % chunk == 0:
            for copy in large[g * group // chunk]:
                copy.wait()
        for h in range(g * group, (g + 1) * group):
            at = h * HEAD
            absorbed = jnp.dot(queries[:, at:at + NOPE], key_absorb[h], preferred_element_type=jnp.float32)
            combined[h * rows:(h + 1) * rows, :LAT] = absorbed.astype(jnp.bfloat16)
            combined[h * rows:(h + 1) * rows, LAT:] = queries[:, at + NOPE:at + HEAD]
        span = pl.ds(g * group * rows, group * rows)
        scores = jnp.dot(combined[span, :], block, preferred_element_type=jnp.float32)
        scores = (scores.reshape(group, rows, rows) + own_bias[None]).reshape(group * rows, rows)
        peak = jnp.max(scores, axis=1, keepdims=True)
        weights = jnp.exp2((scores - peak) * exp2_scale)
        total = jnp.sum(weights, axis=1, keepdims=True)
        weights = weights.astype(jnp.bfloat16)
        for i in range(0, group, 2):
            both = head_values(latents[...], value_expand, g * group + i)
            for j in range(2):
                h = i + j
                out = jnp.dot(weights[h * rows:(h + 1) * rows], both[:, j * VDIM:(j + 1) * VDIM], preferred_element_type=jnp.float32)
                result[(g * group + h) * rows:(g * group + h + 1) * rows, :] = out
        peaks[span, :] = jnp.broadcast_to(peak, (group * rows, LANES))
        totals[span, :] = jnp.broadcast_to(total, (group * rows, LANES))


def index_work(n_cp, count, slot_count, prompt_pages, decode_owner, slot_offset, block, sent_rows, bias, picked, filled):
    rows = block.shape[1]
    me = lax.axis_index("cp")
    behind = lax.rem(me + n_cp - 1, n_cp)
    targets = []
    for valid, page in slot_pages(behind, slot_count, prompt_pages, decode_owner, slot_offset):
        here = valid & (page * PAGE // rows == me)
        targets.append(jnp.where(here, lax.rem(page * PAGE, rows), -PAGE))
    choice = row_picker(targets, rows)
    sent = lax.dot_general(choice, block, NT, preferred_element_type=jnp.float32)
    sent_rows[:, :ROW] = sent.astype(jnp.bfloat16)
    sent_rows[:, ROW:] = jnp.zeros((choice.shape[0], sent_rows.shape[1] - ROW), jnp.bfloat16)
    for b in range(count):
        bias[:, b * rows:(b + 1) * rows] = visible_bias(prompt_pages, rows, swap_pair(jnp.int32(b + 1), n_cp))
    targets = []
    lane = lax.broadcasted_iota(jnp.int32, filled.shape, 1)
    lane_filled = jnp.zeros(filled.shape, jnp.float32)
    for c, (valid, page) in enumerate(slot_pages(me, slot_count, prompt_pages, decode_owner, slot_offset)):
        source = page * PAGE // rows
        column = swap_pair(lax.rem(me - source + n_cp, n_cp), n_cp) * rows + lax.rem(page * PAGE, rows)
        targets.append(jnp.where(valid, column, -PAGE))
        lane_filled = jnp.where(lane // PAGE == c, valid.astype(jnp.float32), lane_filled)
    filled[...] = lane_filled
    picked[...] = row_picker(targets, (n_cp - 1) * rows)


def keep_kernel(picked, own, kept_rows):
    choice = picked[:, :own.shape[1]]
    kept_rows[...] = lax.dot_general(choice, own[...], NT, preferred_element_type=jnp.float32)


def arrived_kernel(picked, kept_rows, *refs):
    half = (len(refs) - 2)
    blocks, found, latents = refs[:half], refs[half], refs[half + 1]
    rows = blocks[0].shape[1]
    total = kept_rows[...]
    for i, block in enumerate(blocks):
        at = (1 + 2 * i) * rows
        total = total + lax.dot_general(picked[:, at:at + rows], block[...], NT, preferred_element_type=jnp.float32)
        latents[i * rows:(i + 1) * rows, :] = block[:LAT, :].T
    found[...] = total


def write_cache(rows, filled, page_cache, page_scales):
    slot_count = page_cache.shape[0]
    scales = []
    for b in range(NBLK):
        values = rows[:, b * BLOCK:(b + 1) * BLOCK]
        scale = jnp.max(jnp.abs(values), axis=1, keepdims=True) + amax_epsilon
        scale = scale.astype(jnp.bfloat16).astype(jnp.float32)
        encoded = (values / scale).astype(jnp.bfloat16)
        for c in range(slot_count):
            page_cache[c, :, b * BLOCK:(b + 1) * BLOCK] = encoded[c * PAGE:(c + 1) * PAGE]
        scales.append(scale)
    kept = rows.shape[0]
    which = lax.broadcasted_iota(jnp.int32, (kept, LANES), 1)
    table = jnp.zeros((kept, LANES), jnp.float32)
    for b, scale in enumerate(scales):
        table = jnp.where(which == b, scale, table)
    table = (table.T[:NBLK] * filled[:1, :kept]).astype(jnp.bfloat16)
    for c in range(slot_count):
        page_cache[c, :, LAT:] = rows[c * PAGE:(c + 1) * PAGE, LAT:].astype(jnp.bfloat16)
        page_scales[c] = table[:, c * PAGE:(c + 1) * PAGE]


def earlier_kernel(n_cp, count, group, *refs):
    combined, own_result, peaks, totals, value_expand, bias, picked, found, sent_rows, filled, fetched_latents = refs[:11]
    arrived, refs = refs[11:11 + (n_cp - 2) // 2 * (1 + SWAP)], refs[11 + (n_cp - 2) // 2 * (1 + SWAP):]
    attended, page_cache, page_scales, keys, latents, result, cache_buf, scale_buf, sems = refs
    rows = attended.shape[0]
    heads = value_expand.shape[0]
    width = count * rows
    steps = heads // group
    found_rows = found[...] + sent_rows[:, :ROW].astype(jnp.float32)
    for i in range((n_cp - 2) // 2):
        at = i * (1 + SWAP)
        swapped = jnp.concatenate([part[...] for part in arrived[at + 1:at + 1 + SWAP]], axis=0)
        b = 2 * i + 1
        choice = picked[:, (b + 1) * rows:(b + 2) * rows]
        found_rows = found_rows + lax.dot_general(choice, swapped, NT, preferred_element_type=jnp.float32)
        if b < count:
            keys[:, (b - 1) * rows:b * rows] = arrived[at][...]
            keys[:, b * rows:(b + 1) * rows] = swapped
            latents[(b - 1) * rows:b * rows, :] = fetched_latents[i * rows:(i + 1) * rows, :]
            latents[b * rows:(b + 1) * rows, :] = swapped[:LAT].T

    def span(g):
        return slice(g * group * rows, (g + 1) * group * rows)

    def score(g):
        scores = jnp.dot(combined[span(g), :], keys[...], preferred_element_type=jnp.float32)
        return (scores.reshape(group, rows, width) + bias[...][None]).reshape(group * rows, width)

    def weigh(g, scores):
        old_peak = peaks[span(g), :]
        parts = [scores[:, b * rows:(b + 1) * rows] for b in range(count)]
        peak = jnp.maximum(old_peak, jnp.max(functools.reduce(jnp.maximum, parts), axis=1, keepdims=True))
        parts = [jnp.exp2((part - peak) * exp2_scale) for part in parts]
        total = jnp.sum(functools.reduce(jnp.add, parts), axis=1, keepdims=True)
        factor = jnp.exp2((old_peak - peak) * exp2_scale)
        inverse = 1.0 / (totals[span(g), :] * factor + total)
        weights = jnp.concatenate([part.astype(jnp.bfloat16) for part in parts], axis=1)
        return weights, factor * inverse, inverse

    def mix(g, weights):
        return jnp.dot(weights, latents[...], preferred_element_type=jnp.float32).astype(jnp.bfloat16)

    def finish(g, mixed, factor, inverse):
        for i in range(group):
            part = slice(i * rows, (i + 1) * rows)
            h = g * group + i
            out = jnp.dot(mixed[part], value_expand[h], preferred_element_type=jnp.float32)
            out = own_result[h * rows:(h + 1) * rows, :] * factor[part] + out * inverse[part]
            result[:, h * VDIM:(h + 1) * VDIM] = out.astype(jnp.bfloat16)
        send(g).start()

    def send(g):
        at = pl.ds(g * group * VDIM, group * VDIM)
        return pltpu.make_async_copy(result.at[:, at], attended.at[:, at], sems.at[g])

    scores, weights, mixed = {}, {}, {}
    for step in range(steps + 2):
        if step < steps:
            scores[step] = score(step)
        if step == 0:
            write_cache(found_rows, filled, cache_buf, scale_buf)
            cache_copies = [
                pltpu.make_async_copy(cache_buf, page_cache, sems.at[steps]),
                pltpu.make_async_copy(scale_buf, page_scales, sems.at[steps + 1]),
            ]
            for copy in cache_copies:
                copy.start()
        if 0 <= step - 2:
            finish(step - 2, mixed.pop(step - 2), *weights.pop(step - 2)[1:])
        if 0 <= step - 1 < steps:
            weights[step - 1] = weigh(step - 1, scores.pop(step - 1))
            mixed[step - 1] = mix(step - 1, weights[step - 1][0])
    for g in range(steps):
        send(g).wait()
    for copy in cache_copies:
        copy.wait()


def fetch(own, n_cp, n_dec):
    blocks = []
    for step in range(1, n_cp - 1, 2):
        pairs = [(c * n_dec + e, (c + step + e % 2) % n_cp * n_dec + e) for c in range(n_cp) for e in range(n_dec)]
        blocks.append(lax.ppermute(own, ("cp", "dec"), pairs))
    return blocks


def swap(blocks, n_dec):
    pieces = []
    for block in blocks:
        parts = [block[at:at + ROW // SWAP] for at in range(0, ROW, ROW // SWAP)]
        pieces += [block] + [lax.ppermute(part, "dec", [(e, e ^ 1) for e in range(n_dec)]) for part in parts]
    return pieces


def on_device(queries, latent_rows, key_absorb, value_expand, prompt_pages, decode_owner, slot_offset):
    n_cp = lax.axis_size("cp")
    dec_count = lax.axis_size("dec")
    heads = key_absorb.shape[0]
    rows = latent_rows.shape[0]
    prompts, width = decode_owner.shape
    slot_count = 3 * (rows // PAGE) // (2 * dec_count)
    kept = slot_count * PAGE
    reach = width * dec_count * slot_count * PAGE
    count = -(-reach // rows) - (1 if prompts == 2 else 0)
    count = min(n_cp - 2, count + count % 2)
    own = latent_rows.T
    blocks = fetch(own, n_cp, dec_count)

    vmem = pl.BlockSpec(memory_space=pltpu.VMEM)
    hbm = pl.BlockSpec(memory_space=pltpu.HBM)
    params = pltpu.CompilerParams(vmem_limit_bytes=32 * 2**20)
    group, chunk = 2, 4
    inputs = (prompt_pages, decode_owner, slot_offset, own, queries, key_absorb, value_expand)
    combined, result, peaks, totals, sent_rows, bias, picked, filled, own_copy, value_copy = pl.pallas_call(
        functools.partial(own_kernel, n_cp, count, chunk, group, slot_count),
        in_specs=[hbm] * 7,
        out_specs=[vmem] * 10,
        out_shape=[
            jax.ShapeDtypeStruct((heads * rows, ROW), jnp.bfloat16),
            jax.ShapeDtypeStruct((heads * rows, VDIM), jnp.float32),
            jax.ShapeDtypeStruct((heads * rows, LANES), jnp.float32),
            jax.ShapeDtypeStruct((heads * rows, LANES), jnp.float32),
            jax.ShapeDtypeStruct((kept, -(-ROW // LANES) * LANES), jnp.bfloat16),
            jax.ShapeDtypeStruct((rows, count * rows), jnp.float32),
            jax.ShapeDtypeStruct((kept, (n_cp - 1) * rows), jnp.bfloat16),
            jax.ShapeDtypeStruct((8, LANES), jnp.float32),
            jax.ShapeDtypeStruct(own.shape, jnp.bfloat16),
            jax.ShapeDtypeStruct(value_expand.shape, jnp.bfloat16),
        ],
        scratch_shapes=[
            pltpu.SMEM(prompt_pages.shape, jnp.int32),
            pltpu.SMEM(decode_owner.shape, jnp.int32),
            pltpu.SMEM(slot_offset.shape, jnp.int32),
            pltpu.VMEM((rows, heads * HEAD), jnp.bfloat16),
            pltpu.VMEM((heads, NOPE, LAT), jnp.bfloat16),
            pltpu.VMEM((rows, LAT), jnp.bfloat16),
            pltpu.SemaphoreType.DMA((4 + 3 * (heads // chunk),)),
        ],
        cost_estimate=pl.CostEstimate(
            flops=2 * rows * heads * (2 * NOPE * LAT + rows * (ROW + VDIM)),
            bytes_accessed=2 * (queries.size + key_absorb.size + heads * rows * ROW),
            transcendentals=rows * heads * rows,
        ),
        compiler_params=params,
        name="own",
    )(*[pltpu.with_memory_space_constraint(x, pltpu.HBM) for x in inputs])
    sent_rows = lax.ppermute(sent_rows, "cp", [(c, (c + n_cp - 1) % n_cp) for c in range(n_cp)])
    kept_rows = pl.pallas_call(
        keep_kernel,
        in_specs=[vmem] * 2,
        out_specs=vmem,
        out_shape=jax.ShapeDtypeStruct((kept, ROW), jnp.float32),
        cost_estimate=pl.CostEstimate(flops=2**27, bytes_accessed=2**20, transcendentals=0),
        compiler_params=params,
        name="keep",
    )(picked, own_copy)
    blocks, kept_rows = lax.optimization_barrier((blocks, kept_rows))
    pieces = swap(blocks, dec_count)
    found, fetched_latents = pl.pallas_call(
        arrived_kernel,
        in_specs=[vmem] * (2 + len(blocks)),
        out_specs=[vmem] * 2,
        out_shape=[
            jax.ShapeDtypeStruct((kept, ROW), jnp.float32),
            jax.ShapeDtypeStruct((len(blocks) * rows, LAT), jnp.bfloat16),
        ],
        cost_estimate=pl.CostEstimate(flops=2**20, bytes_accessed=2**10, transcendentals=0),
        compiler_params=params,
        name="arrived",
    )(picked, kept_rows, *blocks)

    operands = (combined, result, peaks, totals, value_copy, bias, picked, found, sent_rows, filled, fetched_latents, *pieces)
    attended, page_cache, page_scales = pl.pallas_call(
        functools.partial(earlier_kernel, n_cp, count, group),
        in_specs=[vmem] * len(operands),
        out_specs=[hbm] * 3,
        out_shape=[
            jax.ShapeDtypeStruct((rows, heads * VDIM), jnp.bfloat16),
            jax.ShapeDtypeStruct((slot_count, PAGE, ROW), jnp.bfloat16),
            jax.ShapeDtypeStruct((slot_count, NBLK, PAGE), jnp.bfloat16),
        ],
        scratch_shapes=[
            pltpu.VMEM((ROW, count * rows), jnp.bfloat16),
            pltpu.VMEM((count * rows, LAT), jnp.bfloat16),
            pltpu.VMEM((rows, heads * VDIM), jnp.bfloat16),
            pltpu.VMEM((slot_count, PAGE, ROW), jnp.bfloat16),
            pltpu.VMEM((slot_count, NBLK, PAGE), jnp.bfloat16),
            pltpu.SemaphoreType.DMA((heads // group + 2,)),
        ],
        cost_estimate=pl.CostEstimate(
            flops=2 * rows * heads * (count * rows * (ROW + LAT) + LAT * VDIM),
            bytes_accessed=2 * (heads * rows * (ROW + VDIM) + value_expand.size),
            transcendentals=rows * heads * count * rows,
        ),
        compiler_params=params,
        name="earlier",
    )(*operands)
    page_cache = page_cache.reshape(1, 1, slot_count, PAGE, ROW)
    page_scales = page_scales.transpose(0, 2, 1).reshape(1, 1, slot_count, PAGE, NBLK)
    return attended, page_cache, page_scales


def solution(mesh):
    return jax.shard_map(
        on_device,
        mesh=mesh,
        in_specs=(
            P(("grp", "cp"), "dec"),
            P(("grp", "cp"), None),
            P("dec", None, None),
            P("dec", None, None),
            P("grp"),
            P("grp", None),
            P("grp"),
        ),
        out_specs=(
            P(("grp", "cp"), "dec"),
            P(("grp", "cp"), "dec", None, None, None),
            P(("grp", "cp"), "dec", None, None, None),
        ),
        check_vma=False,
    )
```

time: 18.6 us -> 18.6 us (level)
  the two profiles are of different devices: /device:TPU:17 before, /device:TPU:0 now
where the time goes in v6:
time: 18.6 us; the launch traced here: 18.5 us
  Pallas kernels  10.6 us (57%)
  starting transfers between devices  5.83 us (31%)
  waiting for transfers between devices  1.4 us (8%)
  between operations  0.67 us (4%)
    pallas_call x1, Pallas kernels, on_device(): pl.pallas_call(functools.partial(own_kernel, n_cp, count, chunk, group, s...  6.48 us
    pallas_call x1, Pallas kernels, on_device(): pl.pallas_call(functools.partial(earlier_kernel, n_cp, count, group), in_...  3.74 us
    ppermute x1, starting transfers between devices, fetch(): blocks.append(lax.ppermute(own, ('cp', 'dec'), pairs))  3.08 us
    ppermute x1, starting transfers between devices, on_device(): lax.ppermute(sent_rows, 'cp', [(c, (c + n_cp - 1) % n_cp) for c in range(...  2.11 us
    ppermute x1, waiting for transfers between devices, on_device(): lax.ppermute(sent_rows, 'cp', [(c, (c + n_cp - 1) % n_cp) for c in range(...  1.39 us
    ppermute x3, starting transfers between devices, swap(): lax.ppermute(part, 'dec', [(e, e ^ 1) for e in range(n_dec)])  0.65 us
  transfers between devices with their start and end apart: 5, of which 1 were waited for; matrix products, arithmetic and copies ran while one was open for 0% of the time, Pallas kernels for 37%

profile of v6, /device:TPU:0, one launch (start us, length us, event | category | flops | bytes accessed | tf_op | source)
XLA Modules:
  0.0 18.5 jit_solution(10734429922660078702)
XLA Ops:
  0.6 3.1 %collective-permute-start = (bf16[576,128]{1,0:T(8,128)(2,1)}, bf16[576,128]{1,0:T(8,128)(2,1)S(1)}, u32[]{:S(2)}, u32[]{:S(2)}) collective-permute-start(bf16[576,128]{1,0:T(8,128)(2,1)} %bitcast.5), channel_id=1, source_target_pairs={{0,4},{1,9},{2,6},{3,11},{4,8},{5,13},{6,10},{7,15},{8,12},{9,1},{... | collective-permute-start | bytes 442376 | tf_op jit(solution)/shard_map/ppermute | solution.py:300
  3.7 6.5 %own.1 = (bf16[2048,576]{1,0:T(8,128)(2,1)S(1)}, f32[2048,128]{1,0:T(8,128)S(1)}, f32[2048,128]{1,0:T(8,128)S(1)}, f32[2048,128]{1,0:T(8,128)S(1)}, bf16[48,640]...) custom-call(s32[2]{0:T(128)} %refs_0_.1, ...), custom_call_target="tpu_custom_call" | custom-call | flops 905969664 | bytes 5242880 | tf_op jit(solution)/shard_map/own/pallas_call | solution.py:331
  10.2 2.1 %collective-permute-start.1 = (bf16[48,640]{1,0:T(8,128)(2,1)S(1)}, bf16[48,640]{1,0:T(8,128)(2,1)S(1)}, u32[]{:S(2)}, u32[]{:S(2)}) collective-permute-start(bf16[48,640]{1,0:T(8,128)(2,1)S(1)} %get-tuple-element.31), channel_id=1, source_target_pairs={{0,12},{4,0},{8,4},{12,8},{1,13},{5,1},{9,5},{13,9},{2,14},{6,2},{... | collective-permute-start | bytes 184328 | tf_op jit(solution)/shard_map/ppermute | solution.py:364
  12.3 0.2 keep.1.kept_rows
  12.5 0.0 collective-permute-done.refs_0_.refs_11_
  12.5 0.1 collective-permute-start.4
  12.6 0.5 %collective-permute-start.3 = (bf16[192,128]{1,0:T(8,128)(2,1)S(1)}, bf16[192,128]{1,0:T(8,128)(2,1)S(1)}, u32[]{:S(2)}, u32[]{:S(2)}) collective-permute-start(bf16[192,128]{1,0:T(8,128)(2,1)S(1)} %get-tuple-element.38), channel_id=1, source_target_pairs={{0,1},{1,0},{2,3},{3,2},{4,5},{5,4},{6,7},{7,6},{8,9},{9,8},{10,11... | collective-permute-start | bytes 147464 | tf_op jit(solution)/shard_map/ppermute | solution.py:308
  13.1 0.1 collective-permute-start.2
  13.2 0.2 arrived.1
  13.3 1.4 %collective-permute-done.1.refs_8_ = bf16[48,640]{1,0:T(8,128)(2,1)S(1)} collective-permute-done((bf16[48,640]{1,0:T(8,128)(2,1)S(1)}, bf16[48,640]{1,0:T(8,128)(2,1)S(1)}, u32[]{:S(2)}, u32[]{:S(2)}) %collective-permute-start.1) | collective-permute-done | bytes 61472 | tf_op jit(solution)/shard_map/ppermute | solution.py:364
  14.7 0.0 collective-permute-done.4.refs_14_
  14.7 0.0 collective-permute-done.3.refs_13_
  14.7 0.0 collective-permute-done.2.refs_12_
  14.7 3.7 %earlier.1 = (bf16[128,2048]{1,0:T(8,128)(2,1)}, bf16[3,16,576]{2,1,0:T(8,128)(2,1)}, bf16[3,4,16]{2,1,0:T(4,128)(2,1)}) custom-call(bf16[2048,576]{1,0:T(8,128)(2,1)S(1)} %get-tuple-element.20.refs_0_, f32[2048,128]{1,0:T(8,128)S(1)} %get-tuple-element.21.refs_1_, f32[2048,128]{1,0:T(8,128)S(1)} %get-tuple-element.22.refs_2_, ...), custom_call_target="tpu_custom_call" | custom-call | flops 1409286144 | bytes 4980736 | tf_op jit(solution)/shard_map/earlier/pallas_call | solution.py:390
  (1 shorter events, 0.0 us)
Async XLA Ops:
  0.6 11.8 %collective-permute-start = (bf16[576,128]{1,0:T(8,128)(2,1)}, bf16[576,128]{1,0:T(8,128)(2,1)S(1)}, u32[]{:S(2)}, u32[]{:S(2)}) collective-permute-start(bf16[576,128]{1,0:T(8,128)(2,1)} %bitcast.5), channel_id=1, source_target_pairs={{0,4},{1,9},{2,6},{3,11},{4,8},{5,13},{6,10},{7,15},{8,12},{9,1},{... | collective-permute-start | bytes 442376 | tf_op jit(solution)/shard_map/ppermute | solution.py:300
  10.2 4.5 %collective-permute-start.1 = (bf16[48,640]{1,0:T(8,128)(2,1)S(1)}, bf16[48,640]{1,0:T(8,128)(2,1)S(1)}, u32[]{:S(2)}, u32[]{:S(2)}) collective-permute-start(bf16[48,640]{1,0:T(8,128)(2,1)S(1)} %get-tuple-element.31), channel_id=1, source_target_pairs={{0,12},{4,0},{8,4},{12,8},{1,13},{5,1},{9,5},{13,9},{2,14},{6,2},{... | collective-permute-start | bytes 184328 | tf_op jit(solution)/shard_map/ppermute | solution.py:364
  12.5 2.2 %collective-permute-start.4 = (bf16[192,128]{1,0:T(8,128)(2,1)S(1)}, bf16[192,128]{1,0:T(8,128)(2,1)S(1)}, u32[]{:S(2)}, u32[]{:S(2)}) collective-permute-start(bf16[192,128]{1,0:T(8,128)(2,1)S(1)} %get-tuple-element.37), channel_id=1, source_target_pairs={{0,1},{1,0},{2,3},{3,2},{4,5},{5,4},{6,7},{7,6},{8,9},{9,8},{10,11... | collective-permute-start | bytes 147464 | tf_op jit(solution)/shard_map/ppermute | solution.py:308
  12.6 2.2 %collective-permute-start.3 = (bf16[192,128]{1,0:T(8,128)(2,1)S(1)}, bf16[192,128]{1,0:T(8,128)(2,1)S(1)}, u32[]{:S(2)}, u32[]{:S(2)}) collective-permute-start(bf16[192,128]{1,0:T(8,128)(2,1)S(1)} %get-tuple-element.38), channel_id=1, source_target_pairs={{0,1},{1,0},{2,3},{3,2},{4,5},{5,4},{6,7},{7,6},{8,9},{9,8},{10,11... | collective-permute-start | bytes 147464 | tf_op jit(solution)/shard_map/ppermute | solution.py:308
  13.1 1.7 %collective-permute-start.2 = (bf16[192,128]{1,0:T(8,128)(2,1)S(1)}, bf16[192,128]{1,0:T(8,128)(2,1)S(1)}, u32[]{:S(2)}, u32[]{:S(2)}) collective-permute-start(bf16[192,128]{1,0:T(8,128)(2,1)S(1)} %get-tuple-element.39), channel_id=1, source_target_pairs={{0,1},{1,0},{2,3},{3,2},{4,5},{5,4},{6,7},{7,6},{8,9},{9,8},{10,11... | collective-permute-start | bytes 147464 | tf_op jit(solution)/shard_map/ppermute | solution.py:308

commit v7 on v6

--- a/solution.py
+++ b/solution.py
@@ -110,44 +110,60 @@
         ))
     for copy in small:
         copy.start()
-    for i in range(3):
-        for chunk_copies in large:
-            if i < 2:
-                chunk_copies[i].start()
     for chunk_copies in large:
-        chunk_copies[2].start()
-    small[3].wait()
-    block = own[...]
-    latents[...] = block[:LAT].T
-    for copy in small[:3]:
-        copy.wait()
-    own_bias = visible_bias(prompt_pages, rows, 0)
-    index_work(n_cp, count, slot_count, prompt_pages, decode_owner, slot_offset, block, sent_rows, bias, picked, filled)
-
-    for g in range(heads // group):
+        for copy in chunk_copies:
+            copy.start()
+    steps = heads // group
+
+    def absorb(g):
         if g * group % chunk == 0:
-            for copy in large[g * group // chunk]:
+            for copy in large[g * group // chunk][:2]:
                 copy.wait()
         for h in range(g * group, (g + 1) * group):
             at = h * HEAD
             absorbed = jnp.dot(queries[:, at:at + NOPE], key_absorb[h], preferred_element_type=jnp.float32)
             combined[h * rows:(h + 1) * rows, :LAT] = absorbed.astype(jnp.bfloat16)
             combined[h * rows:(h + 1) * rows, LAT:] = queries[:, at + NOPE:at + HEAD]
-        span = pl.ds(g * group * rows, group * rows)
-        scores = jnp.dot(combined[span, :], block, preferred_element_type=jnp.float32)
+
+    def score(g):
+        return jnp.dot(combined[g * group * rows:(g + 1) * group * rows, :], own[...], preferred_element_type=jnp.float32)
+
+    def value(g):
+        if g * group % chunk == 0:
+            large[g * group // chunk][2].wait()
+        return [head_values(latents[...], value_expand, g * group + i) for i in range(0, group, 2)]
+
+    def finish(g, scores, both):
+        span = slice(g * group * rows, (g + 1) * group * rows)
         scores = (scores.reshape(group, rows, rows) + own_bias[None]).reshape(group * rows, rows)
         peak = jnp.max(scores, axis=1, keepdims=True)
         weights = jnp.exp2((scores - peak) * exp2_scale)
         total = jnp.sum(weights, axis=1, keepdims=True)
         weights = weights.astype(jnp.bfloat16)
-        for i in range(0, group, 2):
-            both = head_values(latents[...], value_expand, g * group + i)
-            for j in range(2):
-                h = i + j
-                out = jnp.dot(weights[h * rows:(h + 1) * rows], both[:, j * VDIM:(j + 1) * VDIM], preferred_element_type=jnp.float32)
-                result[(g * group + h) * rows:(g * group + h + 1) * rows, :] = out
+        for i in range(group):
+            mine = both[i // 2][:, i % 2 * VDIM:(i % 2 + 1) * VDIM]
+            out = jnp.dot(weights[i * rows:(i + 1) * rows], mine, preferred_element_type=jnp.float32)
+            result[(g * group + i) * rows:(g * group + i + 1) * rows, :] = out
         peaks[span, :] = jnp.broadcast_to(peak, (group * rows, LANES))
         totals[span, :] = jnp.broadcast_to(total, (group * rows, LANES))
+
+    scores, both = {}, {}
+    for step in range(steps + 2):
+        if step < steps:
+            absorb(step)
+        if step == 0:
+            small[3].wait()
+            latents[...] = own[:LAT, :].T
+        if step == 1:
+            for copy in small[:3]:
+                copy.wait()
+            own_bias = visible_bias(prompt_pages, rows, 0)
+            index_work(n_cp, count, slot_count, prompt_pages, decode_owner, slot_offset, own[...], sent_rows, bias, picked, filled)
+        if 0 <= step - 1 < steps:
+            scores[step - 1] = score(step - 1)
+            both[step - 1] = value(step - 1)
+        if 0 <= step - 2:
+            finish(step - 2, scores.pop(step - 2), both.pop(step - 2))
 
 
 def index_work(n_cp, count, slot_count, prompt_pages, decode_owner, slot_offset, block, sent_rows, bias, picked, filled):

time: 18.6 us -> 17.3 us (0.930)
  Pallas kernels: 10.6 us -> 9.25 us
    pallas_call x1, Pallas kernels: 6.48 us -> 5.16 us  [on_device(): pl.pallas_call(functools.partial(own_kernel, n_cp, count, chunk, group, s...]
  transfers between devices with their start and end apart: 5 -> 5, of which waited for: 1 -> 1; matrix products, arithmetic and copies ran while one was open for 0% -> 0% of each run, Pallas kernels for 37% -> 32%
where the time goes in v7:
time: 17.3 us; the launch traced here: 17.2 us
  Pallas kernels  9.25 us (53%)
  starting transfers between devices  5.83 us (34%)
  waiting for transfers between devices  1.4 us (8%)
  between operations  0.67 us (4%)
    pallas_call x1, Pallas kernels, on_device(): pl.pallas_call(functools.partial(own_kernel, n_cp, count, chunk, group, s...  5.16 us
    pallas_call x1, Pallas kernels, on_device(): pl.pallas_call(functools.partial(earlier_kernel, n_cp, count, group), in_...  3.74 us
    ppermute x1, starting transfers between devices, fetch(): blocks.append(lax.ppermute(own, ('cp', 'dec'), pairs))  3.08 us
    ppermute x1, starting transfers between devices, on_device(): lax.ppermute(sent_rows, 'cp', [(c, (c + n_cp - 1) % n_cp) for c in range(...  2.11 us
    ppermute x1, waiting for transfers between devices, on_device(): lax.ppermute(sent_rows, 'cp', [(c, (c + n_cp - 1) % n_cp) for c in range(...  1.39 us
    ppermute x3, starting transfers between devices, swap(): lax.ppermute(part, 'dec', [(e, e ^ 1) for e in range(n_dec)])  0.65 us
  transfers between devices with their start and end apart: 5, of which 1 were waited for; matrix products, arithmetic and copies ran while one was open for 0% of the time, Pallas kernels for 32%

profile of v7, /device:TPU:0, one launch (start us, length us, event | category | flops | bytes accessed | tf_op | source)
XLA Modules:
  0.0 17.2 jit_solution(10655049206401180011)
XLA Ops:
  0.6 3.1 %collective-permute-start = (bf16[576,128]{1,0:T(8,128)(2,1)}, bf16[576,128]{1,0:T(8,128)(2,1)S(1)}, u32[]{:S(2)}, u32[]{:S(2)}) collective-permute-start(bf16[576,128]{1,0:T(8,128)(2,1)} %bitcast.5), channel_id=1, source_target_pairs={{0,4},{1,9},{2,6},{3,11},{4,8},{5,13},{6,10},{7,15},{8,12},{9,1},{... | collective-permute-start | bytes 442376 | tf_op jit(solution)/shard_map/ppermute | solution.py:316
  3.7 5.2 %own.1 = (bf16[2048,576]{1,0:T(8,128)(2,1)S(1)}, f32[2048,128]{1,0:T(8,128)S(1)}, f32[2048,128]{1,0:T(8,128)S(1)}, f32[2048,128]{1,0:T(8,128)S(1)}, bf16[48,640]...) custom-call(s32[2]{0:T(128)} %refs_0_.1, ...), custom_call_target="tpu_custom_call" | custom-call | flops 905969664 | bytes 5242880 | tf_op jit(solution)/shard_map/own/pallas_call | solution.py:347
  8.9 2.1 %collective-permute-start.1 = (bf16[48,640]{1,0:T(8,128)(2,1)S(1)}, bf16[48,640]{1,0:T(8,128)(2,1)S(1)}, u32[]{:S(2)}, u32[]{:S(2)}) collective-permute-start(bf16[48,640]{1,0:T(8,128)(2,1)S(1)} %get-tuple-element.31), channel_id=1, source_target_pairs={{0,12},{4,0},{8,4},{12,8},{1,13},{5,1},{9,5},{13,9},{2,14},{6,2},{... | collective-permute-start | bytes 184328 | tf_op jit(solution)/shard_map/ppermute | solution.py:380
  11.0 0.2 %keep.1.kept_rows = f32[48,576]{1,0:T(8,128)S(1)} custom-call(bf16[48,384]{1,0:T(8,128)(2,1)S(1)} %get-tuple-element.26.picked.refs_6_, bf16[576,128]{1,0:T(8,128)(2,1)S(1)} %get-tuple-element.27.own), custom_call_target="tpu_custom_call" | custom-call | flops 134217728 | bytes 1048576 | tf_op jit(solution)/shard_map/keep/pallas_call | solution.py:381
  11.2 0.0 collective-permute-done.refs_0_.refs_11_
  11.2 0.1 collective-permute-start.4
  11.3 0.5 %collective-permute-start.3 = (bf16[192,128]{1,0:T(8,128)(2,1)S(1)}, bf16[192,128]{1,0:T(8,128)(2,1)S(1)}, u32[]{:S(2)}, u32[]{:S(2)}) collective-permute-start(bf16[192,128]{1,0:T(8,128)(2,1)S(1)} %get-tuple-element.38), channel_id=1, source_target_pairs={{0,1},{1,0},{2,3},{3,2},{4,5},{5,4},{6,7},{7,6},{8,9},{9,8},{10,11... | collective-permute-start | bytes 147464 | tf_op jit(solution)/shard_map/ppermute | solution.py:324
  11.8 0.1 collective-permute-start.2
  11.8 0.2 %arrived.1 = (f32[48,576]{1,0:T(8,128)S(1)}, bf16[128,512]{1,0:T(8,128)(2,1)S(1)}) custom-call(bf16[48,384]{1,0:T(8,128)(2,1)S(1)} %get-tuple-element.26.picked.refs_6_, f32[48,576]{1,0:T(8,128)S(1)} %keep.1.kept_rows, bf16[576,128]{1,0:T(8,128)(2,1)S(1)} %collective-permute-done.refs_0_.refs_11_), custom_call_target="tpu_custom_call" | custom-call | flops 1048576 | bytes 1024 | tf_op jit(solution)/shard_map/arrived/pallas_call | solution.py:392
  12.0 1.4 %collective-permute-done.1.refs_8_ = bf16[48,640]{1,0:T(8,128)(2,1)S(1)} collective-permute-done((bf16[48,640]{1,0:T(8,128)(2,1)S(1)}, bf16[48,640]{1,0:T(8,128)(2,1)S(1)}, u32[]{:S(2)}, u32[]{:S(2)}) %collective-permute-start.1) | collective-permute-done | bytes 61472 | tf_op jit(solution)/shard_map/ppermute | solution.py:380
  13.4 0.0 collective-permute-done.4.refs_14_
  13.4 0.0 collective-permute-done.3.refs_13_
  13.4 0.0 collective-permute-done.2.refs_12_
  13.4 3.7 %earlier.1 = (bf16[128,2048]{1,0:T(8,128)(2,1)}, bf16[3,16,576]{2,1,0:T(8,128)(2,1)}, bf16[3,4,16]{2,1,0:T(4,128)(2,1)}) custom-call(bf16[2048,576]{1,0:T(8,128)(2,1)S(1)} %get-tuple-element.20.refs_0_, f32[2048,128]{1,0:T(8,128)S(1)} %get-tuple-element.21.refs_1_, f32[2048,128]{1,0:T(8,128)S(1)} %get-tuple-element.22.refs_2_, ...), custom_call_target="tpu_custom_call" | custom-call | flops 1409286144 | bytes 4980736 | tf_op jit(solution)/shard_map/earlier/pallas_call | solution.py:406
  (1 shorter events, 0.0 us)
Async XLA Ops:
  0.6 10.5 %collective-permute-start = (bf16[576,128]{1,0:T(8,128)(2,1)}, bf16[576,128]{1,0:T(8,128)(2,1)S(1)}, u32[]{:S(2)}, u32[]{:S(2)}) collective-permute-start(bf16[576,128]{1,0:T(8,128)(2,1)} %bitcast.5), channel_id=1, source_target_pairs={{0,4},{1,9},{2,6},{3,11},{4,8},{5,13},{6,10},{7,15},{8,12},{9,1},{... | collective-permute-start | bytes 442376 | tf_op jit(solution)/shard_map/ppermute | solution.py:316
  8.9 4.5 %collective-permute-start.1 = (bf16[48,640]{1,0:T(8,128)(2,1)S(1)}, bf16[48,640]{1,0:T(8,128)(2,1)S(1)}, u32[]{:S(2)}, u32[]{:S(2)}) collective-permute-start(bf16[48,640]{1,0:T(8,128)(2,1)S(1)} %get-tuple-element.31), channel_id=1, source_target_pairs={{0,12},{4,0},{8,4},{12,8},{1,13},{5,1},{9,5},{13,9},{2,14},{6,2},{... | collective-permute-start | bytes 184328 | tf_op jit(solution)/shard_map/ppermute | solution.py:380
  11.2 2.2 %collective-permute-start.4 = (bf16[192,128]{1,0:T(8,128)(2,1)S(1)}, bf16[192,128]{1,0:T(8,128)(2,1)S(1)}, u32[]{:S(2)}, u32[]{:S(2)}) collective-permute-start(bf16[192,128]{1,0:T(8,128)(2,1)S(1)} %get-tuple-element.37), channel_id=1, source_target_pairs={{0,1},{1,0},{2,3},{3,2},{4,5},{5,4},{6,7},{7,6},{8,9},{9,8},{10,11... | collective-permute-start | bytes 147464 | tf_op jit(solution)/shard_map/ppermute | solution.py:324
  11.3 2.2 %collective-permute-start.3 = (bf16[192,128]{1,0:T(8,128)(2,1)S(1)}, bf16[192,128]{1,0:T(8,128)(2,1)S(1)}, u32[]{:S(2)}, u32[]{:S(2)}) collective-permute-start(bf16[192,128]{1,0:T(8,128)(2,1)S(1)} %get-tuple-element.38), channel_id=1, source_target_pairs={{0,1},{1,0},{2,3},{3,2},{4,5},{5,4},{6,7},{7,6},{8,9},{9,8},{10,11... | collective-permute-start | bytes 147464 | tf_op jit(solution)/shard_map/ppermute | solution.py:324
  11.8 1.7 %collective-permute-start.2 = (bf16[192,128]{1,0:T(8,128)(2,1)S(1)}, bf16[192,128]{1,0:T(8,128)(2,1)S(1)}, u32[]{:S(2)}, u32[]{:S(2)}) collective-permute-start(bf16[192,128]{1,0:T(8,128)(2,1)S(1)} %get-tuple-element.39), channel_id=1, source_target_pairs={{0,1},{1,0},{2,3},{3,2},{4,5},{5,4},{6,7},{7,6},{8,9},{9,8},{10,11... | collective-permute-start | bytes 147464 | tf_op jit(solution)/shard_map/ppermute | solution.py:324

commit v8 on v7

v8 whole, which is shorter than its diff:
```python
import functools
import math

import jax
import jax.numpy as jnp
from jax import lax
from jax.experimental import pallas as pl
from jax.experimental.pallas import tpu as pltpu
from jax.sharding import PartitionSpec as P

LAT = 512
ROPE = 64
NOPE = 128
VDIM = 128
PAGE = 16
BLOCK = 128
NBLK = LAT // BLOCK
ROW = LAT + ROPE
HEAD = NOPE + ROPE
LANES = 128

masked_fill = -1e30
amax_epsilon = 1e-06
exp2_scale = math.log2(math.e) / math.sqrt(HEAD)

NT = (((1,), (1,)), ((), ()))


def prompt_starts(prompt_pages):
    starts = [jnp.int32(0)]
    for k in range(prompt_pages.shape[0] - 1):
        starts.append(starts[-1] + prompt_pages[k])
    return starts


def visible_bias(prompt_pages, rows, steps_back):
    first = lax.axis_index("cp") * rows
    token = first + lax.broadcasted_iota(jnp.int32, (rows, 1), 0)
    begin = jnp.zeros((rows, 1), jnp.int32)
    for start in prompt_starts(prompt_pages):
        begin = jnp.maximum(begin, jnp.where(start * PAGE <= token, start * PAGE, 0))
    spot = first - steps_back * rows + lax.broadcasted_iota(jnp.int32, (1, rows), 1)
    return jnp.where((spot >= begin) & (spot <= token), 0.0, masked_fill)


def piece_of(source, me):
    distance = jnp.abs(me - source)
    other = lax.rem(lax.rem(lax.axis_index("dec"), 2) + (source > me).astype(jnp.int32), 2)
    return jnp.where(distance == 0, 0, 2 * distance - 1 + other)


def slot_pages(owner, slot_count, prompt_pages, decode_owner, slot_offset):
    prompts, width = decode_owner.shape
    cycle = width * lax.axis_size("dec") * slot_count
    starts = prompt_starts(prompt_pages)
    pages, start, offset, place = jnp.int32(0), jnp.int32(0), jnp.int32(0), jnp.int32(0)
    for k in range(prompts):
        for p in range(width):
            mine = decode_owner[k, p] == owner
            pages = jnp.where(mine, prompt_pages[k], pages)
            start = jnp.where(mine, starts[k], start)
            offset = jnp.where(mine, slot_offset[k], offset)
            place = jnp.where(mine, p, place)
    result = []
    for c in range(slot_count):
        turn = width * (lax.axis_index("dec") * slot_count + c) + place
        page = lax.rem(turn - offset + 2 * cycle, cycle)
        result.append((page < pages, start + page))
    return result


def row_picker(targets, columns):
    kept = len(targets) * PAGE
    row = lax.broadcasted_iota(jnp.int32, (kept, 1), 0)
    target = jnp.full((kept, 1), -1, jnp.int32)
    for c, column in enumerate(targets):
        target = jnp.where(row // PAGE == c, column + row % PAGE, target)
    column = lax.broadcasted_iota(jnp.int32, (1, columns), 1)
    return jnp.where(column == target, 1.0, 0.0).astype(jnp.bfloat16)


def head_values(latents, value_expand, h):
    both = jnp.concatenate([value_expand[h], value_expand[h + 1]], axis=1)
    return jnp.dot(latents, both, preferred_element_type=jnp.float32).astype(jnp.bfloat16)


def own_steps(heads, group, before, queries, key_absorb, value_expand, own, latents, own_bias, outputs):
    combined, result, peaks, totals = outputs
    rows = own.shape[1]
    steps = heads // group

    def absorb(g):
        for h in range(g * group, (g + 1) * group):
            at = h * HEAD
            absorbed = jnp.dot(queries[:, at:at + NOPE], key_absorb[h], preferred_element_type=jnp.float32)
            combined[h * rows:(h + 1) * rows, :LAT] = absorbed.astype(jnp.bfloat16)
            combined[h * rows:(h + 1) * rows, LAT:] = queries[:, at + NOPE:at + HEAD]

    def score(g):
        return jnp.dot(combined[g * group * rows:(g + 1) * group * rows, :], own[...], preferred_element_type=jnp.float32)

    def value(g):
        return [head_values(latents[...], value_expand, g * group + i) for i in range(0, group, 2)]

    def finish(g, scores, both):
        span = slice(g * group * rows, (g + 1) * group * rows)
        scores = (scores.reshape(group, rows, rows) + own_bias[...][None]).reshape(group * rows, rows)
        peak = jnp.max(scores, axis=1, keepdims=True)
        weights = jnp.exp2((scores - peak) * exp2_scale)
        total = jnp.sum(weights, axis=1, keepdims=True)
        weights = weights.astype(jnp.bfloat16)
        for i in range(group):
            mine = both[i // 2][:, i % 2 * VDIM:(i % 2 + 1) * VDIM]
            out = jnp.dot(weights[i * rows:(i + 1) * rows], mine, preferred_element_type=jnp.float32)
            result[(g * group + i) * rows:(g * group + i + 1) * rows, :] = out
        peaks[span, :] = jnp.broadcast_to(peak, (group * rows, LANES))
        totals[span, :] = jnp.broadcast_to(total, (group * rows, LANES))

    scores, both = {}, {}
    for step in range(steps + 2):
        before(step)
        if step < steps:
            absorb(step)
        if 0 <= step - 1 < steps:
            scores[step - 1] = score(step - 1)
            both[step - 1] = value(step - 1)
        if 0 <= step - 2:
            finish(step - 2, scores.pop(step - 2), both.pop(step - 2))


def own_first_kernel(heads, group, *refs):
    pages_hbm, own_hbm, queries_hbm, absorb_hbm, expand_hbm = refs[:5]
    outputs, (own, latents, own_bias, late_queries, late_absorb, value_expand) = refs[5:9], refs[9:15]
    prompt_pages, queries, key_absorb, sems = refs[15:]
    rows = own.shape[1]
    total = value_expand.shape[0]
    some, wide = pl.ds(0, heads), pl.ds(0, heads * HEAD)
    rest, wide_rest = pl.ds(heads, total - heads), pl.ds(heads * HEAD, (total - heads) * HEAD)
    copies = [
        pltpu.make_async_copy(source, target, sems.at[i])
        for i, (source, target) in enumerate((
            (own_hbm, own),
            (pages_hbm, prompt_pages),
            (queries_hbm.at[:, wide], queries),
            (absorb_hbm.at[some], key_absorb),
            (expand_hbm.at[some], value_expand.at[some]),
            (queries_hbm.at[:, wide_rest], late_queries),
            (absorb_hbm.at[rest], late_absorb),
            (expand_hbm.at[rest], value_expand.at[rest]),
        ))
    ]
    for copy in copies:
        copy.start()

    def before(step):
        if step == 0:
            copies[2].wait()
            copies[3].wait()
        if step == 1:
            copies[0].wait()
            latents[...] = own[:LAT, :].T
            copies[1].wait()
            own_bias[...] = visible_bias(prompt_pages, rows, 0)
            copies[4].wait()

    own_steps(heads, group, before, queries, key_absorb, value_expand, own, latents, own_bias, outputs)
    for copy in copies[5:]:
        copy.wait()


def own_second_kernel(n_cp, count, heads, group, slot_count, *refs):
    small_hbm, (own, latents, own_bias, queries, key_absorb, value_expand) = refs[:3], refs[3:9]
    outputs, (sent_rows, bias, picked, filled) = refs[9:13], refs[13:17]
    prompt_pages, decode_owner, slot_offset, sems = refs[17:]
    copies = [
        pltpu.make_async_copy(source, target, sems.at[i])
        for i, (source, target) in enumerate(zip(small_hbm, (prompt_pages, decode_owner, slot_offset)))
    ]
    for copy in copies:
        copy.start()

    def before(step):
        if step == 2:
            for copy in copies:
                copy.wait()
            index_work(n_cp, count, slot_count, prompt_pages, decode_owner, slot_offset, own[...], sent_rows, bias, picked, filled)

    mine = value_expand.at[pl.ds(value_expand.shape[0] - heads, heads)]
    own_steps(heads, group, before, queries, key_absorb, mine, own, latents, own_bias, outputs)


def index_work(n_cp, count, slot_count, prompt_pages, decode_owner, slot_offset, block, sent_rows, bias, picked, filled):
    rows = block.shape[1]
    me = lax.axis_index("cp")
    targets = []
    for valid, page in slot_pages(n_cp - 1 - me, slot_count, prompt_pages, decode_owner, slot_offset):
        here = valid & (page * PAGE // rows == me)
        targets.append(jnp.where(here, lax.rem(page * PAGE, rows), -PAGE))
    choice = row_picker(targets, rows)
    sent = lax.dot_general(choice, block, NT, preferred_element_type=jnp.float32)
    sent_rows[:, :ROW] = sent.astype(jnp.bfloat16)
    sent_rows[:, ROW:] = jnp.zeros((choice.shape[0], sent_rows.shape[1] - ROW), jnp.bfloat16)
    for b in range(count):
        bias[:, b * rows:(b + 1) * rows] = visible_bias(prompt_pages, rows, b + 1)
    targets = []
    lane = lax.broadcasted_iota(jnp.int32, filled.shape, 1)
    lane_filled = jnp.zeros(filled.shape, jnp.float32)
    for c, (valid, page) in enumerate(slot_pages(me, slot_count, prompt_pages, decode_owner, slot_offset)):
        source = page * PAGE // rows
        here = valid & (jnp.abs(me - source) < n_cp - 1)
        column = piece_of(source, me) * rows + lax.rem(page * PAGE, rows)
        targets.append(jnp.where(here, column, -PAGE))
        lane_filled = jnp.where(lane // PAGE == c, valid.astype(jnp.float32), lane_filled)
    filled[...] = lane_filled
    picked[...] = row_picker(targets, picked.shape[1])


def pick_rows(picked, index, block):
    rows = block.shape[1]
    return lax.dot_general(picked[:, index * rows:(index + 1) * rows], block, NT, preferred_element_type=jnp.float32)


def lower_block(mine, others):
    odd = lax.rem(lax.axis_index("dec"), 2) == 1
    return jnp.where(odd, others, mine)


def arrived_kernel(ready, picked, *refs):
    blocks, (found, keys, latents) = refs[:-3], refs[-3:]
    rows = blocks[0].shape[1]
    total = pick_rows(picked, 0, blocks[0][...])
    for i, block in enumerate(blocks[1:]):
        total = total + pick_rows(picked, i + 1, block[...])
    found[...] = total
    for b in range(ready):
        block = lower_block(blocks[2 * b + 1][...], blocks[2 * b + 2][...])
        keys[:, b * rows:(b + 1) * rows] = block
        latents[b * rows:(b + 1) * rows, :] = block[:LAT].T


def cache_kernel(last, picked, found, filled, sent_rows, block, page_cache, page_scales):
    rows = found[...] + sent_rows[:, :ROW].astype(jnp.float32) + pick_rows(picked, last, block[...])
    write_cache(rows, filled, page_cache, page_scales)


def write_cache(rows, filled, page_cache, page_scales):
    slot_count = page_cache.shape[0]
    scales = []
    for b in range(NBLK):
        values = rows[:, b * BLOCK:(b + 1) * BLOCK]
        scale = jnp.max(jnp.abs(values), axis=1, keepdims=True) + amax_epsilon
        scale = scale.astype(jnp.bfloat16).astype(jnp.float32)
        encoded = (values / scale).astype(jnp.bfloat16)
        for c in range(slot_count):
            page_cache[c, :, b * BLOCK:(b + 1) * BLOCK] = encoded[c * PAGE:(c + 1) * PAGE]
        scales.append(scale)
    kept = rows.shape[0]
    which = lax.broadcasted_iota(jnp.int32, (kept, LANES), 1)
    table = jnp.zeros((kept, LANES), jnp.float32)
    for b, scale in enumerate(scales):
        table = jnp.where(which == b, scale, table)
    table = (table.T[:NBLK] * filled[:1, :kept]).astype(jnp.bfloat16)
    for c in range(slot_count):
        page_cache[c, :, LAT:] = rows[c * PAGE:(c + 1) * PAGE, LAT:].astype(jnp.bfloat16)
        page_scales[c] = table[:, c * PAGE:(c + 1) * PAGE]


def earlier_kernel(count, ready, group, *refs):
    halves = (refs[:4], refs[4:8])
    value_expand, bias, ready_keys, ready_latents, fetched, swapped = refs[8:14]
    attended, keys, latents, result, sems = refs[14:]
    rows = attended.shape[0]
    heads = value_expand.shape[0]
    width = count * rows
    steps = heads // group
    keys[:, :ready * rows] = ready_keys[...]
    latents[:ready * rows, :] = ready_latents[...]
    if ready < count:
        block = lower_block(fetched[...], swapped[...])
        keys[:, ready * rows:] = block
        latents[ready * rows:, :] = block[:LAT].T

    def part_of(i, g):
        first = halves[0][i].shape[0]
        at = g * group * rows
        half = halves[0][i] if at < first else halves[1][i]
        at = at % first
        return half[at:at + group * rows, :]

    def score(g):
        scores = jnp.dot(part_of(0, g), keys[...], preferred_element_type=jnp.float32)
        return (scores.reshape(group, rows, width) + bias[...][None]).reshape(group * rows, width)

    def weigh(g, scores):
        old_peak = part_of(2, g)
        parts = [scores[:, b * rows:(b + 1) * rows] for b in range(count)]
        peak = jnp.maximum(old_peak, jnp.max(functools.reduce(jnp.maximum, parts), axis=1, keepdims=True))
        parts = [jnp.exp2((part - peak) * exp2_scale) for part in parts]
        total = jnp.sum(functools.reduce(jnp.add, parts), axis=1, keepdims=True)
        factor = jnp.exp2((old_peak - peak) * exp2_scale)
        inverse = 1.0 / (part_of(3, g) * factor + total)
        weights = jnp.concatenate([part.astype(jnp.bfloat16) for part in parts], axis=1)
        return weights, factor * inverse, inverse

    def mix(g, weights):
        return jnp.dot(weights, latents[...], preferred_element_type=jnp.float32).astype(jnp.bfloat16)

    def finish(g, mixed, factor, inverse):
        own_result = part_of(1, g)
        for i in range(group):
            part = slice(i * rows, (i + 1) * rows)
            h = g * group + i
            out = jnp.dot(mixed[part], value_expand[h], preferred_element_type=jnp.float32)
            out = own_result[part] * factor[part] + out * inverse[part]
            result[:, h * VDIM:(h + 1) * VDIM] = out.astype(jnp.bfloat16)
        send(g).start()

    def send(g):
        at = pl.ds(g * group * VDIM, group * VDIM)
        return pltpu.make_async_copy(result.at[:, at], attended.at[:, at], sems.at[g])

    scores, weights, mixed = {}, {}, {}
    for step in range(steps + 2):
        if step < steps:
            scores[step] = score(step)
        if 0 <= step - 2:
            finish(step - 2, mixed.pop(step - 2), *weights.pop(step - 2)[1:])
        if 0 <= step - 1 < steps:
            weights[step - 1] = weigh(step - 1, scores.pop(step - 1))
            mixed[step - 1] = mix(step - 1, weights[step - 1][0])
    for g in range(steps):
        send(g).wait()


def pass_on(block, n_cp, n_dec):
    pairs = []
    for c in range(n_cp):
        for e in range(n_dec):
            target = c - 1 if e % 2 else c + 1
            if 0 <= target < n_cp:
                pairs.append((c * n_dec + e, target * n_dec + e))
    return lax.ppermute(block, ("cp", "dec"), pairs)


def swap(block, n_dec):
    return lax.ppermute(block, "dec", [(e, e ^ 1) for e in range(n_dec)])


def on_device(queries, latent_rows, key_absorb, value_expand, prompt_pages, decode_owner, slot_offset):
    n_cp = lax.axis_size("cp")
    dec_count = lax.axis_size("dec")
    heads = key_absorb.shape[0]
    rows = latent_rows.shape[0]
    prompts, width = decode_owner.shape
    slot_count = 3 * (rows // PAGE) // (2 * dec_count)
    kept = slot_count * PAGE
    reach = width * dec_count * slot_count * PAGE
    count = min(n_cp - 2, -(-reach // rows) - (1 if prompts == 2 else 0))
    ready = min(count, n_cp - 3)
    own = latent_rows.T
    fetched = [pass_on(own, n_cp, dec_count)]

    vmem = pl.BlockSpec(memory_space=pltpu.VMEM)
    hbm = pl.BlockSpec(memory_space=pltpu.HBM)
    params = pltpu.CompilerParams(vmem_limit_bytes=32 * 2**20)
    group, first_heads = 2, heads // 2

    def in_hbm(*arrays):
        return [pltpu.with_memory_space_constraint(x, pltpu.HBM) for x in arrays]

    def own_cost(some):
        return pl.CostEstimate(
            flops=2 * rows * some * (2 * NOPE * LAT + rows * (ROW + VDIM)),
            bytes_accessed=2 * (queries.size + key_absorb.size + some * rows * ROW),
            transcendentals=rows * some * rows,
        )

    def own_shapes(some):
        return [
            jax.ShapeDtypeStruct((some * rows, ROW), jnp.bfloat16),
            jax.ShapeDtypeStruct((some * rows, VDIM), jnp.float32),
            jax.ShapeDtypeStruct((some * rows, LANES), jnp.float32),
            jax.ShapeDtypeStruct((some * rows, LANES), jnp.float32),
        ]

    late_heads = heads - first_heads
    *first, own_copy, latents, own_bias, late_queries, late_absorb, value_copy = pl.pallas_call(
        functools.partial(own_first_kernel, first_heads, group),
        in_specs=[hbm] * 5,
        out_specs=[vmem] * 10,
        out_shape=own_shapes(first_heads) + [
            jax.ShapeDtypeStruct(own.shape, jnp.bfloat16),
            jax.ShapeDtypeStruct((rows, LAT), jnp.bfloat16),
            jax.ShapeDtypeStruct((rows, rows), jnp.float32),
            jax.ShapeDtypeStruct((rows, late_heads * HEAD), jnp.bfloat16),
            jax.ShapeDtypeStruct((late_heads, NOPE, LAT), jnp.bfloat16),
            jax.ShapeDtypeStruct(value_expand.shape, jnp.bfloat16),
        ],
        scratch_shapes=[
            pltpu.SMEM(prompt_pages.shape, jnp.int32),
            pltpu.VMEM((rows, first_heads * HEAD), jnp.bfloat16),
            pltpu.VMEM((first_heads, NOPE, LAT), jnp.bfloat16),
            pltpu.SemaphoreType.DMA((8,)),
        ],
        cost_estimate=own_cost(first_heads),
        compiler_params=params,
        name="own_first",
    )(*in_hbm(prompt_pages, own, queries, key_absorb, value_expand))
    fetched[0], own_copy = lax.optimization_barrier((fetched[0], own_copy))

    pieces = 2 * (n_cp - 2) + 1
    late = (own_copy, latents, own_bias, late_queries, late_absorb, value_copy)
    *second, sent_rows, bias, picked, filled = pl.pallas_call(
        functools.partial(own_second_kernel, n_cp, count, late_heads, group, slot_count),
        in_specs=[hbm] * 3 + [vmem] * len(late),
        out_specs=[vmem] * 8,
        out_shape=own_shapes(late_heads) + [
            jax.ShapeDtypeStruct((kept, -(-ROW // LANES) * LANES), jnp.bfloat16),
            jax.ShapeDtypeStruct((rows, count * rows), jnp.float32),
            jax.ShapeDtypeStruct((kept, pieces * rows), jnp.bfloat16),
            jax.ShapeDtypeStruct((8, LANES), jnp.float32),
        ],
        scratch_shapes=[
            pltpu.SMEM(prompt_pages.shape, jnp.int32),
            pltpu.SMEM(decode_owner.shape, jnp.int32),
            pltpu.SMEM(slot_offset.shape, jnp.int32),
            pltpu.SemaphoreType.DMA((3,)),
        ],
        cost_estimate=own_cost(late_heads),
        compiler_params=params,
        name="own_second",
    )(*in_hbm(prompt_pages, decode_owner, slot_offset), *late)
    for _ in range(n_cp - 3):
        fetched.append(pass_on(fetched[-1], n_cp, dec_count))
    fetched[-1], bias = lax.optimization_barrier((fetched[-1], bias))
    swapped = [swap(block, dec_count) for block in fetched]
    sent_rows = lax.ppermute(sent_rows, "cp", [(0, n_cp - 1), (n_cp - 1, 0)])

    arrived = [own_copy] + [block for pair in zip(fetched, swapped) for block in pair][:-1]
    found, ready_keys, ready_latents = pl.pallas_call(
        functools.partial(arrived_kernel, ready),
        in_specs=[vmem] * (1 + len(arrived)),
        out_specs=[vmem] * 3,
        out_shape=[
            jax.ShapeDtypeStruct((kept, ROW), jnp.float32),
            jax.ShapeDtypeStruct((ROW, ready * rows), jnp.bfloat16),
            jax.ShapeDtypeStruct((ready * rows, LAT), jnp.bfloat16),
        ],
        cost_estimate=pl.CostEstimate(flops=2**20, bytes_accessed=2**10, transcendentals=0),
        compiler_params=params,
        name="arrived",
    )(picked, *arrived)

    operands = (*first, *second, value_copy, bias, ready_keys, ready_latents, fetched[-1], swapped[-1])
    attended = pl.pallas_call(
        functools.partial(earlier_kernel, count, ready, group),
        in_specs=[vmem] * len(operands),
        out_specs=hbm,
        out_shape=jax.ShapeDtypeStruct((rows, heads * VDIM), jnp.bfloat16),
        scratch_shapes=[
            pltpu.VMEM((ROW, count * rows), jnp.bfloat16),
            pltpu.VMEM((count * rows, LAT), jnp.bfloat16),
            pltpu.VMEM((rows, heads * VDIM), jnp.bfloat16),
            pltpu.SemaphoreType.DMA((heads // group,)),
        ],
        cost_estimate=pl.CostEstimate(
            flops=2 * rows * heads * (count * rows * (ROW + LAT) + LAT * VDIM),
            bytes_accessed=2 * (heads * rows * (ROW + VDIM) + value_expand.size),
            transcendentals=rows * heads * count * rows,
        ),
        compiler_params=params,
        name="earlier",
    )(*operands)
    sent_rows, attended = lax.optimization_barrier((sent_rows, attended))
    page_cache, page_scales = pl.pallas_call(
        functools.partial(cache_kernel, pieces - 1),
        in_specs=[vmem] * 5,
        out_specs=[vmem] * 2,
        out_shape=[
            jax.ShapeDtypeStruct((slot_count, PAGE, ROW), jnp.bfloat16),
            jax.ShapeDtypeStruct((slot_count, NBLK, PAGE), jnp.bfloat16),
        ],
        cost_estimate=pl.CostEstimate(flops=2**20, bytes_accessed=2**10, transcendentals=0),
        compiler_params=params,
        name="cache",
    )(picked, found, filled, sent_rows, swapped[-1])
    page_cache = page_cache.reshape(1, 1, slot_count, PAGE, ROW)
    page_scales = page_scales.transpose(0, 2, 1).reshape(1, 1, slot_count, PAGE, NBLK)
    return attended, page_cache, page_scales


def solution(mesh):
    return jax.shard_map(
        on_device,
        mesh=mesh,
        in_specs=(
            P(("grp", "cp"), "dec"),
            P(("grp", "cp"), None),
            P("dec", None, None),
            P("dec", None, None),
            P("grp"),
            P("grp", None),
            P("grp"),
        ),
        out_specs=(
            P(("grp", "cp"), "dec"),
            P(("grp", "cp"), "dec", None, None, None),
            P(("grp", "cp"), "dec", None, None, None),
        ),
        check_vma=False,
    )
```

time: 17.3 us -> 26.9 us (1.55)
  starting transfers between devices: 5.83 us -> 15.6 us
  waiting for transfers between devices: 1.4 us -> 0.83 us
    ppermute x5, starting transfers between devices: 5.83 us -> 15.6 us  [the longest x2 9.18 us: pass_on(): return lax.ppermute(block, ('cp', 'dec'), pairs)]
    ppermute x5, waiting for transfers between devices: 1.4 us -> 0.83 us  [the longest x2 0.82 us: pass_on(): return lax.ppermute(block, ('cp', 'dec'), pairs)]
    pallas_call x4 -> x5, Pallas kernels: 9.25 us -> 9.46 us  [the longest x1 3.47 us: on_device(): pl.pallas_call(functools.partial(earlier_kernel, count, ready, group), in...]
where the time goes in v8:
time: 26.9 us; the launch traced here: 26.7 us
  starting transfers between devices  15.6 us (58%)
  Pallas kernels  9.46 us (35%)
  waiting for transfers between devices  0.83 us (3%)
  between operations  0.73 us (3%)
    ppermute x2, starting transfers between devices, pass_on(): return lax.ppermute(block, ('cp', 'dec'), pairs)  9.18 us
    ppermute x1, starting transfers between devices, on_device(): sent_rows = lax.ppermute(sent_rows, 'cp', [(0, n_cp - 1), (n_cp - 1, 0)])  6.39 us
    pallas_call x1, Pallas kernels, on_device(): pl.pallas_call(functools.partial(earlier_kernel, count, ready, group), in...  3.47 us
    pallas_call x1, Pallas kernels, on_device(): pl.pallas_call(functools.partial(own_first_kernel, first_heads, group), i...  2.96 us
    pallas_call x1, Pallas kernels, on_device(): pl.pallas_call(functools.partial(own_second_kernel, n_cp, count, late_hea...  1.74 us
    pallas_call x1, Pallas kernels, on_device(): pl.pallas_call(functools.partial(cache_kernel, pieces - 1), in_specs=[vme...  0.97 us
    ppermute x2, waiting for transfers between devices, pass_on(): return lax.ppermute(block, ('cp', 'dec'), pairs)  0.82 us
  transfers between devices with their start and end apart: 5, of which 1 were waited for; matrix products, arithmetic and copies ran while one was open for 0% of the time, Pallas kernels for 32%

profile of v8, /device:TPU:0, one launch (start us, length us, event | category | flops | bytes accessed | tf_op | source)
XLA Modules:
  0.0 26.7 jit_solution(4360737920529987645)
XLA Ops:
  0.6 4.9 %collective-permute-start = (bf16[576,128]{1,0:T(8,128)(2,1)}, bf16[576,128]{1,0:T(8,128)(2,1)S(1)}, u32[]{:S(2)}, u32[]{:S(2)}) collective-permute-start(bf16[576,128]{1,0:T(8,128)(2,1)} %bitcast.5), channel_id=1, source_target_pairs={{0,4},{2,6},{4,8},{5,1},{6,10},{7,3},{8,12},{9,5},{10,14},{11,7},{... | collective-permute-start | bytes 442376 | tf_op jit(solution)/shard_map/ppermute | solution.py:342
  5.6 3.0 %own_first.1 = (bf16[1024,576]{1,0:T(8,128)(2,1)S(1)}, f32[1024,128]{1,0:T(8,128)S(1)}, f32[1024,128]{1,0:T(8,128)S(1)}, f32[1024,128]{1,0:T(8,128)S(1)}, bf16[5...) custom-call(s32[2]{0:T(128)} %refs_0_.3, ...), custom_call_target="tpu_custom_call" | custom-call | flops 452984832 | bytes 4063232 | tf_op jit(solution)/shard_map/own_first/pallas_call | solution.py:387
  8.5 0.0 collective-permute-done.refs_1_
  8.6 4.2 %collective-permute-start.2 = (bf16[576,128]{1,0:T(8,128)(2,1)S(1)}, bf16[576,128]{1,0:T(8,128)(2,1)S(1)}, u32[]{:S(2)}, u32[]{:S(2)}) collective-permute-start(bf16[576,128]{1,0:T(8,128)(2,1)S(1)} %collective-permute-done.refs_1_), channel_id=1, source_target_pairs={{0,4},{2,6},{4,8},{5,1},{6,10},{7,3},{8,12},{9,5},{10,14},{11,7},{... | collective-permute-start | bytes 442376 | tf_op jit(solution)/shard_map/ppermute | solution.py:342
  12.8 0.1 collective-permute-start.3
  12.9 1.7 %own_second.1 = (bf16[1024,576]{1,0:T(8,128)(2,1)S(1)}, f32[1024,128]{1,0:T(8,128)S(1)}, f32[1024,128]{1,0:T(8,128)S(1)}, f32[1024,128]{1,0:T(8,128)S(1)}, bf16[...) custom-call(s32[2]{0:T(128)} %refs_0_.3, ...), custom_call_target="tpu_custom_call" | custom-call | flops 452984832 | bytes 4063232 | tf_op jit(solution)/shard_map/own_second/pallas_call | solution.py:413
  14.6 0.8 %collective-permute-done.2.refs_3_.refs_12_ = bf16[576,128]{1,0:T(8,128)(2,1)S(1)} collective-permute-done((bf16[576,128]{1,0:T(8,128)(2,1)S(1)}, bf16[576,128]{1,0:T(8,128)(2,1)S(1)}, u32[]{:S(2)}, u32[]{:S(2)}) %collective-permute-start.2) | collective-permute-done | bytes 147488 | tf_op jit(solution)/shard_map/ppermute | solution.py:342
  15.5 0.0 collective-permute-start.4
  15.5 6.4 %collective-permute-start.1 = (bf16[48,640]{1,0:T(8,128)(2,1)S(1)}, bf16[48,640]{1,0:T(8,128)(2,1)S(1)}, u32[]{:S(2)}, u32[]{:S(2)}) collective-permute-start(bf16[48,640]{1,0:T(8,128)(2,1)S(1)} %get-tuple-element.39), channel_id=1, source_target_pairs={{0,12},{12,0},{1,13},{13,1},{2,14},{14,2},{3,15},{15,3},{16,28},{2... | collective-permute-start | bytes 184328 | tf_op jit(solution)/shard_map/ppermute | solution.py:437
  21.9 0.0 collective-permute-done.3.refs_2_
  21.9 0.3 %arrived.1 = (f32[48,576]{1,0:T(8,128)S(1)}, bf16[576,128]{1,0:T(8,128)(2,1)S(1)}, bf16[128,512]{1,0:T(8,128)(2,1)S(1)}) custom-call(bf16[48,640]{1,0:T(8,128)(2,1)S(1)} %get-tuple-element.51.picked, bf16[576,128]{1,0:T(8,128)(2,1)S(1)} %get-tuple-element.33.refs_3_.refs_0_, bf16[576,128]{1,0:T(8,128)(2,1)S(1)} %collective-permute-done.refs_1_, ...), custom_call_target="tpu_custom_call" | custom-call | flops 1048576 | bytes 1024 | tf_op jit(solution)/shard_map/arrived/pallas_call | solution.py:440
  22.2 0.0 collective-permute-done.4.refs_13_.block
  22.2 3.5 %earlier.1 = bf16[128,2048]{1,0:T(8,128)(2,1)} custom-call(bf16[1024,576]{1,0:T(8,128)(2,1)S(1)} %get-tuple-element.40.refs_0_, f32[1024,128]{1,0:T(8,128)S(1)} %get-tuple-element.41.refs_1_, f32[1024,128]{1,0:T(8,128)S(1)} %get-tuple-element.42.refs_2_, f32[1024,128]{1,0:T(8,128)S(1)} %get-tuple-element.43.refs_3_, ...), custom_call_target="tpu_custom_call" | custom-call | flops 1409286144 | bytes 4980736 | tf_op jit(solution)/shard_map/earlier/pallas_call | solution.py:455
  25.7 0.0 collective-permute-done.1.sent_rows
  25.7 1.0 %cache.1 = (bf16[3,16,576]{2,1,0:T(8,128)(2,1)}, bf16[3,4,16]{2,1,0:T(4,128)(2,1)}) custom-call(bf16[48,640]{1,0:T(8,128)(2,1)S(1)} %get-tuple-element.51.picked, f32[48,576]{1,0:T(8,128)S(1)} %get-tuple-element.56.found, f32[8,128]{1,0:T(8,128)S(1)} %get-tuple-element.57.filled, bf16[48,640]{1,0:T(8,128)(2,1)S(1)} %collective-permute-done.1.sent_rows, ...), custom_call_target="tpu_custom_call" | custom-call | flops 1048576 | bytes 1024 | tf_op jit(solution)/shard_map/cache/pallas_call | solution.py:475
Async XLA Ops:
  0.6 7.9 %collective-permute-start = (bf16[576,128]{1,0:T(8,128)(2,1)}, bf16[576,128]{1,0:T(8,128)(2,1)S(1)}, u32[]{:S(2)}, u32[]{:S(2)}) collective-permute-start(bf16[576,128]{1,0:T(8,128)(2,1)} %bitcast.5), channel_id=1, source_target_pairs={{0,4},{2,6},{4,8},{5,1},{6,10},{7,3},{8,12},{9,5},{10,14},{11,7},{... | collective-permute-start | bytes 442376 | tf_op jit(solution)/shard_map/ppermute | solution.py:342
  8.6 6.9 %collective-permute-start.2 = (bf16[576,128]{1,0:T(8,128)(2,1)S(1)}, bf16[576,128]{1,0:T(8,128)(2,1)S(1)}, u32[]{:S(2)}, u32[]{:S(2)}) collective-permute-start(bf16[576,128]{1,0:T(8,128)(2,1)S(1)} %collective-permute-done.refs_1_), channel_id=1, source_target_pairs={{0,4},{2,6},{4,8},{5,1},{6,10},{7,3},{8,12},{9,5},{10,14},{11,7},{... | collective-permute-start | bytes 442376 | tf_op jit(solution)/shard_map/ppermute | solution.py:342
  12.8 9.1 %collective-permute-start.3 = (bf16[576,128]{1,0:T(8,128)(2,1)S(1)}, bf16[576,128]{1,0:T(8,128)(2,1)S(1)}, u32[]{:S(2)}, u32[]{:S(2)}) collective-permute-start(bf16[576,128]{1,0:T(8,128)(2,1)S(1)} %collective-permute-done.refs_1_), channel_id=1, source_target_pairs={{0,1},{1,0},{2,3},{3,2},{4,5},{5,4},{6,7},{7,6},{8,9},{9,8},{10,11... | collective-permute-start | bytes 442376 | tf_op jit(solution)/shard_map/ppermute | solution.py:346
  15.5 6.7 %collective-permute-start.4 = (bf16[576,128]{1,0:T(8,128)(2,1)S(1)}, bf16[576,128]{1,0:T(8,128)(2,1)S(1)}, u32[]{:S(2)}, u32[]{:S(2)}) collective-permute-start(bf16[576,128]{1,0:T(8,128)(2,1)S(1)} %collective-permute-done.2.refs_3_.refs_12_), channel_id=1, source_target_pairs={{0,1},{1,0},{2,3},{3,2},{4,5},{5,4},{6,7},{7,6},{8,9},{9,8},{10,11... | collective-permute-start | bytes 442376 | tf_op jit(solution)/shard_map/ppermute | solution.py:346
  15.5 10.2 %collective-permute-start.1 = (bf16[48,640]{1,0:T(8,128)(2,1)S(1)}, bf16[48,640]{1,0:T(8,128)(2,1)S(1)}, u32[]{:S(2)}, u32[]{:S(2)}) collective-permute-start(bf16[48,640]{1,0:T(8,128)(2,1)S(1)} %get-tuple-element.39), channel_id=1, source_target_pairs={{0,12},{12,0},{1,13},{13,1},{2,14},{14,2},{3,15},{15,3},{16,28},{2... | collective-permute-start | bytes 184328 | tf_op jit(solution)/shard_map/ppermute | solution.py:437

commit v9 on v8

--- a/solution.py
+++ b/solution.py
@@ -193,8 +193,9 @@
     rows = block.shape[1]
     me = lax.axis_index("cp")
     targets = []
+    at_end = (me == 0) | (me == n_cp - 1)
     for valid, page in slot_pages(n_cp - 1 - me, slot_count, prompt_pages, decode_owner, slot_offset):
-        here = valid & (page * PAGE // rows == me)
+        here = valid & at_end & (page * PAGE // rows == me)
         targets.append(jnp.where(here, lax.rem(page * PAGE, rows), -PAGE))
     choice = row_picker(targets, rows)
     sent = lax.dot_general(choice, block, NT, preferred_element_type=jnp.float32)
@@ -337,8 +338,17 @@
     for c in range(n_cp):
         for e in range(n_dec):
             target = c - 1 if e % 2 else c + 1
-            if 0 <= target < n_cp:
-                pairs.append((c * n_dec + e, target * n_dec + e))
+            at = (target, e) if 0 <= target < n_cp else (c, e ^ 1)
+            pairs.append((c * n_dec + e, at[0] * n_dec + at[1]))
+    return lax.ppermute(block, ("cp", "dec"), pairs)
+
+
+def end_to_end(block, n_cp, n_dec):
+    pairs = []
+    for c in range(n_cp):
+        for e in range(n_dec):
+            at = (n_cp - 1 - c, e) if c in (0, n_cp - 1) else (c, e ^ 1)
+            pairs.append((c * n_dec + e, at[0] * n_dec + at[1]))
     return lax.ppermute(block, ("cp", "dec"), pairs)
 
 
@@ -434,7 +444,7 @@
         fetched.append(pass_on(fetched[-1], n_cp, dec_count))
     fetched[-1], bias = lax.optimization_barrier((fetched[-1], bias))
     swapped = [swap(block, dec_count) for block in fetched]
-    sent_rows = lax.ppermute(sent_rows, "cp", [(0, n_cp - 1), (n_cp - 1, 0)])
+    sent_rows = end_to_end(sent_rows, n_cp, dec_count)
 
     arrived = [own_copy] + [block for pair in zip(fetched, swapped) for block in pair][:-1]
     found, ready_keys, ready_latents = pl.pallas_call(

time: 26.9 us -> 21.1 us (0.78)
  starting transfers between devices: 15.6 us -> 9.9 us
    ppermute x2, starting transfers between devices: 9.18 us -> 5.4 us  [pass_on(): return lax.ppermute(block, ('cp', 'dec'), pairs)]
    ppermute x1, starting transfers between devices: 6.39 us -> 4.49 us  [end_to_end(): return lax.ppermute(block, ('cp', 'dec'), pairs)]
  transfers between devices with their start and end apart: 5 -> 5, of which waited for: 1 -> 1; matrix products, arithmetic and copies ran while one was open for 0% -> 0% of each run, Pallas kernels for 32% -> 40%
where the time goes in v9:
time: 21.1 us; the launch traced here: 21 us
  starting transfers between devices  9.9 us (47%)
  Pallas kernels  9.43 us (45%)
  waiting for transfers between devices  0.97 us (5%)
  between operations  0.68 us (3%)
    ppermute x2, starting transfers between devices, pass_on(): return lax.ppermute(block, ('cp', 'dec'), pairs)  5.4 us
    ppermute x1, starting transfers between devices, end_to_end(): return lax.ppermute(block, ('cp', 'dec'), pairs)  4.49 us
    pallas_call x1, Pallas kernels, on_device(): pl.pallas_call(functools.partial(earlier_kernel, count, ready, group), in...  3.47 us
    pallas_call x1, Pallas kernels, on_device(): pl.pallas_call(functools.partial(own_first_kernel, first_heads, group), i...  2.95 us
    pallas_call x1, Pallas kernels, on_device(): pl.pallas_call(functools.partial(own_second_kernel, n_cp, count, late_hea...  1.74 us
    pallas_call x1, Pallas kernels, on_device(): pl.pallas_call(functools.partial(cache_kernel, pieces - 1), in_specs=[vme...  0.97 us
    ppermute x2, waiting for transfers between devices, pass_on(): return lax.ppermute(block, ('cp', 'dec'), pairs)  0.96 us
  transfers between devices with their start and end apart: 5, of which 1 were waited for; matrix products, arithmetic and copies ran while one was open for 0% of the time, Pallas kernels for 40%

profile of v9, /device:TPU:0, one launch (start us, length us, event | category | flops | bytes accessed | tf_op | source)
XLA Modules:
  0.0 21.0 jit_solution(4084306564253888533)
XLA Ops:
  0.6 3.0 %collective-permute-start = (bf16[576,128]{1,0:T(8,128)(2,1)}, bf16[576,128]{1,0:T(8,128)(2,1)S(1)}, u32[]{:S(2)}, u32[]{:S(2)}) collective-permute-start(bf16[576,128]{1,0:T(8,128)(2,1)} %bitcast.5), channel_id=1, source_target_pairs={{0,4},{1,0},{2,6},{3,2},{4,8},{5,1},{6,10},{7,3},{8,12},{9,5},{10,... | collective-permute-start | bytes 442376 | tf_op jit(solution)/shard_map/ppermute | solution.py:343
  3.7 2.9 %own_first.1 = (bf16[1024,576]{1,0:T(8,128)(2,1)S(1)}, f32[1024,128]{1,0:T(8,128)S(1)}, f32[1024,128]{1,0:T(8,128)S(1)}, f32[1024,128]{1,0:T(8,128)S(1)}, bf16[5...) custom-call(s32[2]{0:T(128)} %refs_0_.3, ...), custom_call_target="tpu_custom_call" | custom-call | flops 452984832 | bytes 4063232 | tf_op jit(solution)/shard_map/own_first/pallas_call | solution.py:397
  6.6 0.0 collective-permute-done.refs_1_
  6.7 2.4 %collective-permute-start.2 = (bf16[576,128]{1,0:T(8,128)(2,1)S(1)}, bf16[576,128]{1,0:T(8,128)(2,1)S(1)}, u32[]{:S(2)}, u32[]{:S(2)}) collective-permute-start(bf16[576,128]{1,0:T(8,128)(2,1)S(1)} %collective-permute-done.refs_1_), channel_id=1, source_target_pairs={{0,4},{1,0},{2,6},{3,2},{4,8},{5,1},{6,10},{7,3},{8,12},{9,5},{10,... | collective-permute-start | bytes 442376 | tf_op jit(solution)/shard_map/ppermute | solution.py:343
  9.0 0.0 collective-permute-start.3
  9.0 1.7 %own_second.1 = (bf16[1024,576]{1,0:T(8,128)(2,1)S(1)}, f32[1024,128]{1,0:T(8,128)S(1)}, f32[1024,128]{1,0:T(8,128)S(1)}, f32[1024,128]{1,0:T(8,128)S(1)}, bf16[...) custom-call(s32[2]{0:T(128)} %refs_0_.3, ...), custom_call_target="tpu_custom_call" | custom-call | flops 452984832 | bytes 4063232 | tf_op jit(solution)/shard_map/own_second/pallas_call | solution.py:423
  10.8 0.9 %collective-permute-done.2.refs_3_.refs_12_ = bf16[576,128]{1,0:T(8,128)(2,1)S(1)} collective-permute-done((bf16[576,128]{1,0:T(8,128)(2,1)S(1)}, bf16[576,128]{1,0:T(8,128)(2,1)S(1)}, u32[]{:S(2)}, u32[]{:S(2)}) %collective-permute-start.2) | collective-permute-done | bytes 147488 | tf_op jit(solution)/shard_map/ppermute | solution.py:343
  11.7 0.0 collective-permute-start.4
  11.7 4.5 %collective-permute-start.1 = (bf16[48,640]{1,0:T(8,128)(2,1)S(1)}, bf16[48,640]{1,0:T(8,128)(2,1)S(1)}, u32[]{:S(2)}, u32[]{:S(2)}) collective-permute-start(bf16[48,640]{1,0:T(8,128)(2,1)S(1)} %get-tuple-element.39), channel_id=1, source_target_pairs={{0,12},{1,13},{2,14},{3,15},{4,5},{5,4},{6,7},{7,6},{8,9},{9,8},{1... | collective-permute-start | bytes 184328 | tf_op jit(solution)/shard_map/ppermute | solution.py:352
  16.2 0.0 collective-permute-done.3.refs_2_
  16.2 0.3 %arrived.1 = (f32[48,576]{1,0:T(8,128)S(1)}, bf16[576,128]{1,0:T(8,128)(2,1)S(1)}, bf16[128,512]{1,0:T(8,128)(2,1)S(1)}) custom-call(bf16[48,640]{1,0:T(8,128)(2,1)S(1)} %get-tuple-element.51.picked, bf16[576,128]{1,0:T(8,128)(2,1)S(1)} %get-tuple-element.33.refs_3_.refs_0_, bf16[576,128]{1,0:T(8,128)(2,1)S(1)} %collective-permute-done.refs_1_, ...), custom_call_target="tpu_custom_call" | custom-call | flops 1048576 | bytes 1024 | tf_op jit(solution)/shard_map/arrived/pallas_call | solution.py:450
  16.5 0.0 collective-permute-done.4.refs_13_.block
  16.5 3.5 %earlier.1 = bf16[128,2048]{1,0:T(8,128)(2,1)} custom-call(bf16[1024,576]{1,0:T(8,128)(2,1)S(1)} %get-tuple-element.40.refs_0_, f32[1024,128]{1,0:T(8,128)S(1)} %get-tuple-element.41.refs_1_, f32[1024,128]{1,0:T(8,128)S(1)} %get-tuple-element.42.refs_2_, f32[1024,128]{1,0:T(8,128)S(1)} %get-tuple-element.43.refs_3_, ...), custom_call_target="tpu_custom_call" | custom-call | flops 1409286144 | bytes 4980736 | tf_op jit(solution)/shard_map/earlier/pallas_call | solution.py:465
  20.0 0.0 collective-permute-done.1.sent_rows
  20.0 1.0 %cache.1 = (bf16[3,16,576]{2,1,0:T(8,128)(2,1)}, bf16[3,4,16]{2,1,0:T(4,128)(2,1)}) custom-call(bf16[48,640]{1,0:T(8,128)(2,1)S(1)} %get-tuple-element.51.picked, f32[48,576]{1,0:T(8,128)S(1)} %get-tuple-element.56.found, f32[8,128]{1,0:T(8,128)S(1)} %get-tuple-element.57.filled, bf16[48,640]{1,0:T(8,128)(2,1)S(1)} %collective-permute-done.1.sent_rows, ...), custom_call_target="tpu_custom_call" | custom-call | flops 1048576 | bytes 1024 | tf_op jit(solution)/shard_map/cache/pallas_call | solution.py:485
Async XLA Ops:
  0.6 6.0 %collective-permute-start = (bf16[576,128]{1,0:T(8,128)(2,1)}, bf16[576,128]{1,0:T(8,128)(2,1)S(1)}, u32[]{:S(2)}, u32[]{:S(2)}) collective-permute-start(bf16[576,128]{1,0:T(8,128)(2,1)} %bitcast.5), channel_id=1, source_target_pairs={{0,4},{1,0},{2,6},{3,2},{4,8},{5,1},{6,10},{7,3},{8,12},{9,5},{10,... | collective-permute-start | bytes 442376 | tf_op jit(solution)/shard_map/ppermute | solution.py:343
  6.7 5.0 %collective-permute-start.2 = (bf16[576,128]{1,0:T(8,128)(2,1)S(1)}, bf16[576,128]{1,0:T(8,128)(2,1)S(1)}, u32[]{:S(2)}, u32[]{:S(2)}) collective-permute-start(bf16[576,128]{1,0:T(8,128)(2,1)S(1)} %collective-permute-done.refs_1_), channel_id=1, source_target_pairs={{0,4},{1,0},{2,6},{3,2},{4,8},{5,1},{6,10},{7,3},{8,12},{9,5},{10,... | collective-permute-start | bytes 442376 | tf_op jit(solution)/shard_map/ppermute | solution.py:343
  9.0 7.2 %collective-permute-start.3 = (bf16[576,128]{1,0:T(8,128)(2,1)S(1)}, bf16[576,128]{1,0:T(8,128)(2,1)S(1)}, u32[]{:S(2)}, u32[]{:S(2)}) collective-permute-start(bf16[576,128]{1,0:T(8,128)(2,1)S(1)} %collective-permute-done.refs_1_), channel_id=1, source_target_pairs={{0,1},{1,0},{2,3},{3,2},{4,5},{5,4},{6,7},{7,6},{8,9},{9,8},{10,11... | collective-permute-start | bytes 442376 | tf_op jit(solution)/shard_map/ppermute | solution.py:356
  11.7 4.8 %collective-permute-start.4 = (bf16[576,128]{1,0:T(8,128)(2,1)S(1)}, bf16[576,128]{1,0:T(8,128)(2,1)S(1)}, u32[]{:S(2)}, u32[]{:S(2)}) collective-permute-start(bf16[576,128]{1,0:T(8,128)(2,1)S(1)} %collective-permute-done.2.refs_3_.refs_12_), channel_id=1, source_target_pairs={{0,1},{1,0},{2,3},{3,2},{4,5},{5,4},{6,7},{7,6},{8,9},{9,8},{10,11... | collective-permute-start | bytes 442376 | tf_op jit(solution)/shard_map/ppermute | solution.py:356
  11.7 8.3 %collective-permute-start.1 = (bf16[48,640]{1,0:T(8,128)(2,1)S(1)}, bf16[48,640]{1,0:T(8,128)(2,1)S(1)}, u32[]{:S(2)}, u32[]{:S(2)}) collective-permute-start(bf16[48,640]{1,0:T(8,128)(2,1)S(1)} %get-tuple-element.39), channel_id=1, source_target_pairs={{0,12},{1,13},{2,14},{3,15},{4,5},{5,4},{6,7},{7,6},{8,9},{9,8},{1... | collective-permute-start | bytes 184328 | tf_op jit(solution)/shard_map/ppermute | solution.py:352

commit v10 on v8

--- a/solution.py
+++ b/solution.py
@@ -41,12 +41,6 @@
         begin = jnp.maximum(begin, jnp.where(start * PAGE <= token, start * PAGE, 0))
     spot = first - steps_back * rows + lax.broadcasted_iota(jnp.int32, (1, rows), 1)
     return jnp.where((spot >= begin) & (spot <= token), 0.0, masked_fill)
-
-
-def piece_of(source, me):
-    distance = jnp.abs(me - source)
-    other = lax.rem(lax.rem(lax.axis_index("dec"), 2) + (source > me).astype(jnp.int32), 2)
-    return jnp.where(distance == 0, 0, 2 * distance - 1 + other)
 
 
 def slot_pages(owner, slot_count, prompt_pages, decode_owner, slot_offset):
@@ -193,7 +187,8 @@
     rows = block.shape[1]
     me = lax.axis_index("cp")
     targets = []
-    for valid, page in slot_pages(n_cp - 1 - me, slot_count, prompt_pages, decode_owner, slot_offset):
+    behind = lax.rem(me + n_cp - 1, n_cp)
+    for valid, page in slot_pages(behind, slot_count, prompt_pages, decode_owner, slot_offset):
         here = valid & (page * PAGE // rows == me)
         targets.append(jnp.where(here, lax.rem(page * PAGE, rows), -PAGE))
     choice = row_picker(targets, rows)
@@ -207,9 +202,8 @@
     lane_filled = jnp.zeros(filled.shape, jnp.float32)
     for c, (valid, page) in enumerate(slot_pages(me, slot_count, prompt_pages, decode_owner, slot_offset)):
         source = page * PAGE // rows
-        here = valid & (jnp.abs(me - source) < n_cp - 1)
-        column = piece_of(source, me) * rows + lax.rem(page * PAGE, rows)
-        targets.append(jnp.where(here, column, -PAGE))
+        column = lax.rem(me - source + n_cp, n_cp) * rows + lax.rem(page * PAGE, rows)
+        targets.append(jnp.where(valid, column, -PAGE))
         lane_filled = jnp.where(lane // PAGE == c, valid.astype(jnp.float32), lane_filled)
     filled[...] = lane_filled
     picked[...] = row_picker(targets, picked.shape[1])
@@ -220,26 +214,27 @@
     return lax.dot_general(picked[:, index * rows:(index + 1) * rows], block, NT, preferred_element_type=jnp.float32)
 
 
-def lower_block(mine, others):
+def whole_block(mine, others):
     odd = lax.rem(lax.axis_index("dec"), 2) == 1
-    return jnp.where(odd, others, mine)
-
-
-def arrived_kernel(ready, picked, *refs):
-    blocks, (found, keys, latents) = refs[:-3], refs[-3:]
-    rows = blocks[0].shape[1]
-    total = pick_rows(picked, 0, blocks[0][...])
-    for i, block in enumerate(blocks[1:]):
-        total = total + pick_rows(picked, i + 1, block[...])
+    mine, others = mine[...], others[...]
+    return jnp.concatenate([jnp.where(odd, others, mine), jnp.where(odd, mine, others)], axis=0)
+
+
+def arrived_kernel(ready, picked, own, *refs):
+    halves, (found, keys, latents) = refs[:-3], refs[-3:]
+    rows = own.shape[1]
+    total = pick_rows(picked, 0, own[...])
+    for i in range(len(halves) // 2):
+        block = whole_block(halves[2 * i], halves[2 * i + 1])
+        total = total + pick_rows(picked, i + 1, block)
+        if i < ready:
+            keys[:, i * rows:(i + 1) * rows] = block
+            latents[i * rows:(i + 1) * rows, :] = block[:LAT].T
     found[...] = total
-    for b in range(ready):
-        block = lower_block(blocks[2 * b + 1][...], blocks[2 * b + 2][...])
-        keys[:, b * rows:(b + 1) * rows] = block
-        latents[b * rows:(b + 1) * rows, :] = block[:LAT].T
-
-
-def cache_kernel(last, picked, found, filled, sent_rows, block, page_cache, page_scales):
-    rows = found[...] + sent_rows[:, :ROW].astype(jnp.float32) + pick_rows(picked, last, block[...])
+
+
+def cache_kernel(last, picked, found, filled, sent_rows, fetched, swapped, page_cache, page_scales):
+    rows = found[...] + sent_rows[:, :ROW].astype(jnp.float32) + pick_rows(picked, last, whole_block(fetched, swapped))
     write_cache(rows, filled, page_cache, page_scales)
 
 
@@ -276,7 +271,7 @@
     keys[:, :ready * rows] = ready_keys[...]
     latents[:ready * rows, :] = ready_latents[...]
     if ready < count:
-        block = lower_block(fetched[...], swapped[...])
+        block = whole_block(fetched, swapped)
         keys[:, ready * rows:] = block
         latents[ready * rows:, :] = block[:LAT].T
 
@@ -332,14 +327,8 @@
         send(g).wait()
 
 
-def pass_on(block, n_cp, n_dec):
-    pairs = []
-    for c in range(n_cp):
-        for e in range(n_dec):
-            target = c - 1 if e % 2 else c + 1
-            if 0 <= target < n_cp:
-                pairs.append((c * n_dec + e, target * n_dec + e))
-    return lax.ppermute(block, ("cp", "dec"), pairs)
+def shift(block, n_cp, steps):
+    return lax.ppermute(block, "cp", [(c, (c + steps) % n_cp) for c in range(n_cp)])
 
 
 def swap(block, n_dec):
@@ -358,7 +347,9 @@
     count = min(n_cp - 2, -(-reach // rows) - (1 if prompts == 2 else 0))
     ready = min(count, n_cp - 3)
     own = latent_rows.T
-    fetched = [pass_on(own, n_cp, dec_count)]
+    half = ROW // 2
+    mine = lax.dynamic_slice_in_dim(own, lax.rem(lax.axis_index("dec"), 2) * half, half, 0)
+    fetched = [shift(mine, n_cp, 1)]
 
     vmem = pl.BlockSpec(memory_space=pltpu.VMEM)
     hbm = pl.BlockSpec(memory_space=pltpu.HBM)
@@ -408,7 +399,7 @@
     )(*in_hbm(prompt_pages, own, queries, key_absorb, value_expand))
     fetched[0], own_copy = lax.optimization_barrier((fetched[0], own_copy))
 
-    pieces = 2 * (n_cp - 2) + 1
+    pieces = n_cp - 1
     late = (own_copy, latents, own_bias, late_queries, late_absorb, value_copy)
     *second, sent_rows, bias, picked, filled = pl.pallas_call(
         functools.partial(own_second_kernel, n_cp, count, late_heads, group, slot_count),
@@ -431,12 +422,12 @@
         name="own_second",
     )(*in_hbm(prompt_pages, decode_owner, slot_offset), *late)
     for _ in range(n_cp - 3):
-        fetched.append(pass_on(fetched[-1], n_cp, dec_count))
+        fetched.append(shift(fetched[-1], n_cp, 1))
     fetched[-1], bias = lax.optimization_barrier((fetched[-1], bias))
     swapped = [swap(block, dec_count) for block in fetched]
-    sent_rows = lax.ppermute(sent_rows, "cp", [(0, n_cp - 1), (n_cp - 1, 0)])
-
-    arrived = [own_copy] + [block for pair in zip(fetched, swapped) for block in pair][:-1]
+    sent_rows = shift(sent_rows, n_cp, -1)
+
+    arrived = [own_copy] + [block for pair in zip(fetched[:-1], swapped[:-1]) for block in pair]
     found, ready_keys, ready_latents = pl.pallas_call(
         functools.partial(arrived_kernel, ready),
         in_specs=[vmem] * (1 + len(arrived)),
@@ -474,7 +465,7 @@
     sent_rows, attended = lax.optimization_barrier((sent_rows, attended))
     page_cache, page_scales = pl.pallas_call(
         functools.partial(cache_kernel, pieces - 1),
-        in_specs=[vmem] * 5,
+        in_specs=[vmem] * 6,
         out_specs=[vmem] * 2,
         out_shape=[
             jax.ShapeDtypeStruct((slot_count, PAGE, ROW), jnp.bfloat16),
@@ -483,7 +474,7 @@
         cost_estimate=pl.CostEstimate(flops=2**20, bytes_accessed=2**10, transcendentals=0),
         compiler_params=params,
         name="cache",
-    )(picked, found, filled, sent_rows, swapped[-1])
+    )(picked, found, filled, sent_rows, fetched[-1], swapped[-1])
     page_cache = page_cache.reshape(1, 1, slot_count, PAGE, ROW)
     page_scales = page_scales.transpose(0, 2, 1).reshape(1, 1, slot_count, PAGE, NBLK)
     return attended, page_cache, page_scales

time: 26.9 us -> 20.9 us (0.78)
  starting transfers between devices: 15.6 us -> 3.51 us
  waiting for transfers between devices: 0.83 us -> 6.32 us
  local copies, waits for them, and re-layouts: 0 us -> 0.89 us
    ppermute x3, starting transfers between devices: 15.6 us -> 3.51 us  [shift(): lax.ppermute(block, 'cp', [(c, (c + steps) % n_cp) for c in range(n_cp)])]
    ppermute x3, waiting for transfers between devices: 0.83 us -> 5.52 us  [shift(): lax.ppermute(block, 'cp', [(c, (c + steps) % n_cp) for c in range(n_cp)])]
    dynamic_slice x0 -> x1, local copies, waits for them, and re-layouts: none -> 0.89 us  [on_device(): lax.dynamic_slice_in_dim(own, lax.rem(lax.axis_index('dec'), 2) * half, h...]
    ppermute x2, waiting for transfers between devices: 0.01 us -> 0.8 us  [swap(): return lax.ppermute(block, 'dec', [(e, e ^ 1) for e in range(n_dec)])]
  transfers between devices with their start and end apart: 5 -> 5, of which waited for: 1 -> 3; matrix products, arithmetic and copies ran while one was open for 0% -> 0% of each run, Pallas kernels for 32% -> 40%
where the time goes in v10:
time: 20.9 us; the launch traced here: 20.7 us
  Pallas kernels  9.33 us (45%)
  waiting for transfers between devices  6.32 us (30%)
  starting transfers between devices  3.51 us (17%)
  local copies, waits for them, and re-layouts  0.89 us (4%)
  between operations  0.68 us (3%)
    ppermute x3, waiting for transfers between devices, shift(): lax.ppermute(block, 'cp', [(c, (c + steps) % n_cp) for c in range(n_cp)])  5.52 us
    ppermute x3, starting transfers between devices, shift(): lax.ppermute(block, 'cp', [(c, (c + steps) % n_cp) for c in range(n_cp)])  3.51 us
    pallas_call x1, Pallas kernels, on_device(): pl.pallas_call(functools.partial(earlier_kernel, count, ready, group), in...  3.41 us
    pallas_call x1, Pallas kernels, on_device(): pl.pallas_call(functools.partial(own_first_kernel, first_heads, group), i...  2.97 us
    pallas_call x1, Pallas kernels, on_device(): pl.pallas_call(functools.partial(own_second_kernel, n_cp, count, late_hea...  1.74 us
    pallas_call x1, Pallas kernels, on_device(): pl.pallas_call(functools.partial(cache_kernel, pieces - 1), in_specs=[vme...  0.98 us
    dynamic_slice x1, local copies, waits for them, and re-layouts, on_device(): lax.dynamic_slice_in_dim(own, lax.rem(lax.axis_index('dec'), 2) * half, h...  0.89 us
    ppermute x2, waiting for transfers between devices, swap(): return lax.ppermute(block, 'dec', [(e, e ^ 1) for e in range(n_dec)])  0.8 us
  transfers between devices with their start and end apart: 5, of which 3 were waited for; matrix products, arithmetic and copies ran while one was open for 0% of the time, Pallas kernels for 40%

profile of v10, /device:TPU:0, one launch (start us, length us, event | category | flops | bytes accessed | tf_op | source)
XLA Modules:
  0.0 20.7 jit_solution(7811025637300367195)
XLA Ops:
  0.6 0.9 %dynamic-slice_bitcast_fusion = bf16[288,128]{1,0:T(8,128)(2,1)S(1)} fusion(bf16[128,576]{0,1:T(8,128)(2,1)} %param.8, s32[]{:T(128)S(6)} %select_n.3), kind=kLoop, calls=%fused_computation | loop fusion | bytes 147460 | tf_op jit(solution)/shard_map/dynamic_slice | solution.py:351
  1.5 3.0 %collective-permute-start = (bf16[288,128]{1,0:T(8,128)(2,1)S(1)}, bf16[288,128]{1,0:T(8,128)(2,1)S(1)}, u32[]{:S(2)}, u32[]{:S(2)}) collective-permute-start(bf16[288,128]{1,0:T(8,128)(2,1)S(1)} %dynamic-slice_bitcast_fusion), channel_id=1, source_target_pairs={{0,4},{4,8},{8,12},{12,0},{1,5},{5,9},{9,13},{13,1},{2,6},{6,10},{... | collective-permute-start | bytes 221192 | tf_op jit(solution)/shard_map/ppermute | solution.py:331
  4.6 3.0 %own_first.1 = (bf16[1024,576]{1,0:T(8,128)(2,1)S(1)}, f32[1024,128]{1,0:T(8,128)S(1)}, f32[1024,128]{1,0:T(8,128)S(1)}, f32[1024,128]{1,0:T(8,128)S(1)}, bf16[5...) custom-call(s32[2]{0:T(128)} %refs_0_.3, ...), custom_call_target="tpu_custom_call" | custom-call | flops 452984832 | bytes 4063232 | tf_op jit(solution)/shard_map/own_first/pallas_call | solution.py:378
  7.5 1.4 %collective-permute-done.refs_0_ = bf16[288,128]{1,0:T(8,128)(2,1)S(1)} collective-permute-done((bf16[288,128]{1,0:T(8,128)(2,1)S(1)}, bf16[288,128]{1,0:T(8,128)(2,1)S(1)}, u32[]{:S(2)}, u32[]{:S(2)}) %collective-permute-start) | collective-permute-done | bytes 73760 | tf_op jit(solution)/shard_map/ppermute | solution.py:331
  8.9 0.3 %collective-permute-start.2 = (bf16[288,128]{1,0:T(8,128)(2,1)S(1)}, bf16[288,128]{1,0:T(8,128)(2,1)S(1)}, u32[]{:S(2)}, u32[]{:S(2)}) collective-permute-start(bf16[288,128]{1,0:T(8,128)(2,1)S(1)} %collective-permute-done.refs_0_), channel_id=1, source_target_pairs={{0,4},{4,8},{8,12},{12,0},{1,5},{5,9},{9,13},{13,1},{2,6},{6,10},{... | collective-permute-start | bytes 221192 | tf_op jit(solution)/shard_map/ppermute | solution.py:331
  9.2 0.0 collective-permute-start.3
  9.2 1.7 %own_second.1 = (bf16[1024,576]{1,0:T(8,128)(2,1)S(1)}, f32[1024,128]{1,0:T(8,128)S(1)}, f32[1024,128]{1,0:T(8,128)S(1)}, f32[1024,128]{1,0:T(8,128)S(1)}, bf16[...) custom-call(s32[2]{0:T(128)} %refs_0_.3, ...), custom_call_target="tpu_custom_call" | custom-call | flops 452984832 | bytes 4063232 | tf_op jit(solution)/shard_map/own_second/pallas_call | solution.py:404
  10.9 4.1 %collective-permute-done.2.refs_12_.fetched = bf16[288,128]{1,0:T(8,128)(2,1)S(1)} collective-permute-done((bf16[288,128]{1,0:T(8,128)(2,1)S(1)}, bf16[288,128]{1,0:T(8,128)(2,1)S(1)}, u32[]{:S(2)}, u32[]{:S(2)}) %collective-permute-start.2) | collective-permute-done | bytes 73760 | tf_op jit(solution)/shard_map/ppermute | solution.py:331
  15.1 0.0 collective-permute-start.4
  15.1 0.2 %collective-permute-start.1 = (bf16[48,640]{1,0:T(8,128)(2,1)S(1)}, bf16[48,640]{1,0:T(8,128)(2,1)S(1)}, u32[]{:S(2)}, u32[]{:S(2)}) collective-permute-start(bf16[48,640]{1,0:T(8,128)(2,1)S(1)} %get-tuple-element.39), channel_id=1, source_target_pairs={{0,12},{4,0},{8,4},{12,8},{1,13},{5,1},{9,5},{13,9},{2,14},{6,2},{... | collective-permute-start | bytes 184328 | tf_op jit(solution)/shard_map/ppermute | solution.py:331
  15.3 0.0 collective-permute-done.3.refs_1_
  15.3 0.2 %arrived.1 = (f32[48,576]{1,0:T(8,128)S(1)}, bf16[576,128]{1,0:T(8,128)(2,1)S(1)}, bf16[128,512]{1,0:T(8,128)(2,1)S(1)}) custom-call(bf16[48,384]{1,0:T(8,128)(2,1)S(1)} %get-tuple-element.51.picked, bf16[576,128]{1,0:T(8,128)(2,1)S(1)} %get-tuple-element.33.refs_3_.own, bf16[288,128]{1,0:T(8,128)(2,1)S(1)} %collective-permute-done.refs_0_, ...), custom_call_target="tpu_custom_call" | custom-call | flops 1048576 | bytes 1024 | tf_op jit(solution)/shard_map/arrived/pallas_call | solution.py:431
  15.5 0.8 %collective-permute-done.4.refs_13_.swapped = bf16[288,128]{1,0:T(8,128)(2,1)S(1)} collective-permute-done((bf16[288,128]{1,0:T(8,128)(2,1)S(1)}, bf16[288,128]{1,0:T(8,128)(2,1)S(1)}, u32[]{:S(2)}, u32[]{:S(2)}) %collective-permute-start.4) | collective-permute-done | bytes 73760 | tf_op jit(solution)/shard_map/ppermute | solution.py:335
  16.3 3.4 %earlier.1 = bf16[128,2048]{1,0:T(8,128)(2,1)} custom-call(bf16[1024,576]{1,0:T(8,128)(2,1)S(1)} %get-tuple-element.40.refs_0_, f32[1024,128]{1,0:T(8,128)S(1)} %get-tuple-element.41.refs_1_, f32[1024,128]{1,0:T(8,128)S(1)} %get-tuple-element.42.refs_2_, f32[1024,128]{1,0:T(8,128)S(1)} %get-tuple-element.43.refs_3_, ...), custom_call_target="tpu_custom_call" | custom-call | flops 1409286144 | bytes 4980736 | tf_op jit(solution)/shard_map/earlier/pallas_call | solution.py:446
  19.8 0.0 collective-permute-done.1.sent_rows
  19.8 1.0 %cache.1 = (bf16[3,16,576]{2,1,0:T(8,128)(2,1)}, bf16[3,4,16]{2,1,0:T(4,128)(2,1)}) custom-call(bf16[48,384]{1,0:T(8,128)(2,1)S(1)} %get-tuple-element.51.picked, f32[48,576]{1,0:T(8,128)S(1)} %get-tuple-element.56.found, f32[8,128]{1,0:T(8,128)S(1)} %get-tuple-element.57.filled, bf16[48,640]{1,0:T(8,128)(2,1)S(1)} %collective-permute-done.1.sent_rows, ...), custom_call_target="tpu_custom_call" | custom-call | flops 1048576 | bytes 1024 | tf_op jit(solution)/shard_map/cache/pallas_call | solution.py:466
Async XLA Ops:
  1.5 7.4 %collective-permute-start = (bf16[288,128]{1,0:T(8,128)(2,1)S(1)}, bf16[288,128]{1,0:T(8,128)(2,1)S(1)}, u32[]{:S(2)}, u32[]{:S(2)}) collective-permute-start(bf16[288,128]{1,0:T(8,128)(2,1)S(1)} %dynamic-slice_bitcast_fusion), channel_id=1, source_target_pairs={{0,4},{4,8},{8,12},{12,0},{1,5},{5,9},{9,13},{13,1},{2,6},{6,10},{... | collective-permute-start | bytes 221192 | tf_op jit(solution)/shard_map/ppermute | solution.py:331
  8.9 6.2 %collective-permute-start.2 = (bf16[288,128]{1,0:T(8,128)(2,1)S(1)}, bf16[288,128]{1,0:T(8,128)(2,1)S(1)}, u32[]{:S(2)}, u32[]{:S(2)}) collective-permute-start(bf16[288,128]{1,0:T(8,128)(2,1)S(1)} %collective-permute-done.refs_0_), channel_id=1, source_target_pairs={{0,4},{4,8},{8,12},{12,0},{1,5},{5,9},{9,13},{13,1},{2,6},{6,10},{... | collective-permute-start | bytes 221192 | tf_op jit(solution)/shard_map/ppermute | solution.py:331
  9.2 6.1 %collective-permute-start.3 = (bf16[288,128]{1,0:T(8,128)(2,1)S(1)}, bf16[288,128]{1,0:T(8,128)(2,1)S(1)}, u32[]{:S(2)}, u32[]{:S(2)}) collective-permute-start(bf16[288,128]{1,0:T(8,128)(2,1)S(1)} %collective-permute-done.refs_0_), channel_id=1, source_target_pairs={{0,1},{1,0},{2,3},{3,2},{4,5},{5,4},{6,7},{7,6},{8,9},{9,8},{10,11... | collective-permute-start | bytes 221192 | tf_op jit(solution)/shard_map/ppermute | solution.py:335
  15.1 1.3 %collective-permute-start.4 = (bf16[288,128]{1,0:T(8,128)(2,1)S(1)}, bf16[288,128]{1,0:T(8,128)(2,1)S(1)}, u32[]{:S(2)}, u32[]{:S(2)}) collective-permute-start(bf16[288,128]{1,0:T(8,128)(2,1)S(1)} %collective-permute-done.2.refs_12_.fetched), channel_id=1, source_target_pairs={{0,1},{1,0},{2,3},{3,2},{4,5},{5,4},{6,7},{7,6},{8,9},{9,8},{10,11... | collective-permute-start | bytes 221192 | tf_op jit(solution)/shard_map/ppermute | solution.py:335
  15.1 4.7 %collective-permute-start.1 = (bf16[48,640]{1,0:T(8,128)(2,1)S(1)}, bf16[48,640]{1,0:T(8,128)(2,1)S(1)}, u32[]{:S(2)}, u32[]{:S(2)}) collective-permute-start(bf16[48,640]{1,0:T(8,128)(2,1)S(1)} %get-tuple-element.39), channel_id=1, source_target_pairs={{0,12},{4,0},{8,4},{12,8},{1,13},{5,1},{9,5},{13,9},{2,14},{6,2},{... | collective-permute-start | bytes 184328 | tf_op jit(solution)/shard_map/ppermute | solution.py:331

commit v11 on v7

--- a/solution.py
+++ b/solution.py
@@ -18,7 +18,6 @@
 ROW = LAT + ROPE
 HEAD = NOPE + ROPE
 LANES = 128
-SWAP = 3
 
 masked_fill = -1e30
 amax_epsilon = 1e-06
@@ -192,19 +191,17 @@
     picked[...] = row_picker(targets, (n_cp - 1) * rows)
 
 
-def keep_kernel(picked, own, kept_rows):
-    choice = picked[:, :own.shape[1]]
-    kept_rows[...] = lax.dot_general(choice, own[...], NT, preferred_element_type=jnp.float32)
-
-
-def arrived_kernel(picked, kept_rows, *refs):
-    half = (len(refs) - 2)
-    blocks, found, latents = refs[:half], refs[half], refs[half + 1]
-    rows = blocks[0].shape[1]
-    total = kept_rows[...]
+def pick_rows(picked, index, block):
+    rows = block.shape[1]
+    return lax.dot_general(picked[:, index * rows:(index + 1) * rows], block, NT, preferred_element_type=jnp.float32)
+
+
+def arrived_kernel(picked, own, *refs):
+    blocks, (found, latents) = refs[:-2], refs[-2:]
+    rows = own.shape[1]
+    total = pick_rows(picked, 0, own[...])
     for i, block in enumerate(blocks):
-        at = (1 + 2 * i) * rows
-        total = total + lax.dot_general(picked[:, at:at + rows], block[...], NT, preferred_element_type=jnp.float32)
+        total = total + pick_rows(picked, 1 + 2 * i, block[...])
         latents[i * rows:(i + 1) * rows, :] = block[:LAT, :].T
     found[...] = total
 
@@ -231,29 +228,19 @@
         page_scales[c] = table[:, c * PAGE:(c + 1) * PAGE]
 
 
-def earlier_kernel(n_cp, count, group, *refs):
-    combined, own_result, peaks, totals, value_expand, bias, picked, found, sent_rows, filled, fetched_latents = refs[:11]
-    arrived, refs = refs[11:11 + (n_cp - 2) // 2 * (1 + SWAP)], refs[11 + (n_cp - 2) // 2 * (1 + SWAP):]
-    attended, page_cache, page_scales, keys, latents, result, cache_buf, scale_buf, sems = refs
-    rows = attended.shape[0]
-    heads = value_expand.shape[0]
-    width = count * rows
+def earlier_heads(first_head, heads, group, inputs, keys, latents, attended, result, sems, beside):
+    combined, own_result, peaks, totals, value_expand, bias = inputs
+    rows, width = bias.shape
     steps = heads // group
-    found_rows = found[...] + sent_rows[:, :ROW].astype(jnp.float32)
-    for i in range((n_cp - 2) // 2):
-        at = i * (1 + SWAP)
-        swapped = jnp.concatenate([part[...] for part in arrived[at + 1:at + 1 + SWAP]], axis=0)
-        b = 2 * i + 1
-        choice = picked[:, (b + 1) * rows:(b + 2) * rows]
-        found_rows = found_rows + lax.dot_general(choice, swapped, NT, preferred_element_type=jnp.float32)
-        if b < count:
-            keys[:, (b - 1) * rows:b * rows] = arrived[at][...]
-            keys[:, b * rows:(b + 1) * rows] = swapped
-            latents[(b - 1) * rows:b * rows, :] = fetched_latents[i * rows:(i + 1) * rows, :]
-            latents[b * rows:(b + 1) * rows, :] = swapped[:LAT].T
 
     def span(g):
-        return slice(g * group * rows, (g + 1) * group * rows)
+        at = (first_head + g * group) * rows
+        return slice(at, at + group * rows)
+
+    def send(g):
+        at = pl.ds((first_head + g * group) * VDIM, group * VDIM)
+        here = pl.ds(g * group * VDIM, group * VDIM)
+        return pltpu.make_async_copy(result.at[:, here], attended.at[:, at], sems.at[g])
 
     def score(g):
         scores = jnp.dot(combined[span(g), :], keys[...], preferred_element_type=jnp.float32)
@@ -261,7 +248,7 @@
 
     def weigh(g, scores):
         old_peak = peaks[span(g), :]
-        parts = [scores[:, b * rows:(b + 1) * rows] for b in range(count)]
+        parts = [scores[:, b:b + LANES] for b in range(0, width, LANES)]
         peak = jnp.maximum(old_peak, jnp.max(functools.reduce(jnp.maximum, parts), axis=1, keepdims=True))
         parts = [jnp.exp2((part - peak) * exp2_scale) for part in parts]
         total = jnp.sum(functools.reduce(jnp.add, parts), axis=1, keepdims=True)
@@ -276,35 +263,73 @@
     def finish(g, mixed, factor, inverse):
         for i in range(group):
             part = slice(i * rows, (i + 1) * rows)
-            h = g * group + i
+            h = first_head + g * group + i
             out = jnp.dot(mixed[part], value_expand[h], preferred_element_type=jnp.float32)
             out = own_result[h * rows:(h + 1) * rows, :] * factor[part] + out * inverse[part]
-            result[:, h * VDIM:(h + 1) * VDIM] = out.astype(jnp.bfloat16)
+            at = (g * group + i) * VDIM
+            result[:, at:at + VDIM] = out.astype(jnp.bfloat16)
         send(g).start()
 
-    def send(g):
-        at = pl.ds(g * group * VDIM, group * VDIM)
-        return pltpu.make_async_copy(result.at[:, at], attended.at[:, at], sems.at[g])
-
-    scores, weights, mixed = {}, {}, {}
-    for step in range(steps + 2):
-        if step < steps:
-            scores[step] = score(step)
-        if step == 0:
-            write_cache(found_rows, filled, cache_buf, scale_buf)
-            cache_copies = [
-                pltpu.make_async_copy(cache_buf, page_cache, sems.at[steps]),
-                pltpu.make_async_copy(scale_buf, page_scales, sems.at[steps + 1]),
-            ]
-            for copy in cache_copies:
-                copy.start()
-        if 0 <= step - 2:
-            finish(step - 2, mixed.pop(step - 2), *weights.pop(step - 2)[1:])
-        if 0 <= step - 1 < steps:
-            weights[step - 1] = weigh(step - 1, scores.pop(step - 1))
-            mixed[step - 1] = mix(step - 1, weights[step - 1][0])
+    @pl.when(lax.axis_index("cp") == 0)
+    def _():
+        beside()
+        for g in range(steps):
+            for i in range(group):
+                h = first_head + g * group + i
+                at = (g * group + i) * VDIM
+                part = slice(h * rows, (h + 1) * rows)
+                result[:, at:at + VDIM] = (own_result[part, :] / totals[part, :]).astype(jnp.bfloat16)
+            send(g).start()
+
+    @pl.when(lax.axis_index("cp") > 0)
+    def _():
+        scores, weights, mixed = {}, {}, {}
+        for step in range(steps + 2):
+            if step < steps:
+                scores[step] = score(step)
+            if step == 0:
+                beside()
+            if 0 <= step - 2:
+                finish(step - 2, mixed.pop(step - 2), *weights.pop(step - 2)[1:])
+            if 0 <= step - 1 < steps:
+                weights[step - 1] = weigh(step - 1, scores.pop(step - 1))
+                mixed[step - 1] = mix(step - 1, weights[step - 1][0])
+
     for g in range(steps):
         send(g).wait()
+
+
+def earlier_first_kernel(count, heads, group, *refs):
+    inputs, fetched_latents, refs = refs[:6], refs[6], refs[7:]
+    arrived, (attended, keys, latents, result, sems) = refs[:-5], refs[-5:]
+    rows = arrived[0].shape[1]
+    for b in range(count):
+        keys[:, b * rows:(b + 1) * rows] = arrived[b][...]
+        if b % 2:
+            latents[b * rows:(b + 1) * rows, :] = arrived[b][:LAT, :].T
+        else:
+            latents[b * rows:(b + 1) * rows, :] = fetched_latents[b // 2 * rows:(b // 2 + 1) * rows, :]
+    earlier_heads(0, heads, group, inputs, keys, latents, attended, result, sems, lambda: None)
+
+
+def earlier_last_kernel(first_head, heads, group, *refs):
+    inputs, (keys, latents, picked, found, sent_rows, filled), refs = refs[:6], refs[6:12], refs[12:]
+    swapped, refs = refs[:-8], refs[-7:]
+    attended, page_cache, page_scales, result, cache_buf, scale_buf, sems = refs
+    cache_copies = [
+        pltpu.make_async_copy(cache_buf, page_cache, sems.at[heads // group]),
+        pltpu.make_async_copy(scale_buf, page_scales, sems.at[heads // group + 1]),
+    ]
+
+    def cache():
+        rows = found[...] + sent_rows[:, :ROW].astype(jnp.float32)
+        for i, block in enumerate(swapped):
+            rows = rows + pick_rows(picked, 2 + 2 * i, block[...])
+        write_cache(rows, filled, cache_buf, scale_buf)
+        for copy in cache_copies:
+            copy.start()
+
+    earlier_heads(first_head, heads, group, inputs, keys, latents, attended, result, sems, cache)
     for copy in cache_copies:
         copy.wait()
 
@@ -320,8 +345,7 @@
 def swap(blocks, n_dec):
     pieces = []
     for block in blocks:
-        parts = [block[at:at + ROW // SWAP] for at in range(0, ROW, ROW // SWAP)]
-        pieces += [block] + [lax.ppermute(part, "dec", [(e, e ^ 1) for e in range(n_dec)]) for part in parts]
+        pieces += [block, lax.ppermute(block, "dec", [(e, e ^ 1) for e in range(n_dec)])]
     return pieces
 
 
@@ -378,16 +402,7 @@
         name="own",
     )(*[pltpu.with_memory_space_constraint(x, pltpu.HBM) for x in inputs])
     sent_rows = lax.ppermute(sent_rows, "cp", [(c, (c + n_cp - 1) % n_cp) for c in range(n_cp)])
-    kept_rows = pl.pallas_call(
-        keep_kernel,
-        in_specs=[vmem] * 2,
-        out_specs=vmem,
-        out_shape=jax.ShapeDtypeStruct((kept, ROW), jnp.float32),
-        cost_estimate=pl.CostEstimate(flops=2**27, bytes_accessed=2**20, transcendentals=0),
-        compiler_params=params,
-        name="keep",
-    )(picked, own_copy)
-    blocks, kept_rows = lax.optimization_barrier((blocks, kept_rows))
+    blocks, picked = lax.optimization_barrier((blocks, picked))
     pieces = swap(blocks, dec_count)
     found, fetched_latents = pl.pallas_call(
         arrived_kernel,
@@ -400,33 +415,60 @@
         cost_estimate=pl.CostEstimate(flops=2**20, bytes_accessed=2**10, transcendentals=0),
         compiler_params=params,
         name="arrived",
-    )(picked, kept_rows, *blocks)
-
-    operands = (combined, result, peaks, totals, value_copy, bias, picked, found, sent_rows, filled, fetched_latents, *pieces)
+    )(picked, own_copy, *blocks)
+
+    def earlier_cost(some):
+        return pl.CostEstimate(
+            flops=2 * rows * some * (count * rows * (ROW + LAT) + LAT * VDIM),
+            bytes_accessed=2 * (some * rows * (ROW + VDIM) + value_expand.size),
+            transcendentals=rows * some * count * rows,
+        )
+
+    attended_shape = jax.ShapeDtypeStruct((rows, heads * VDIM), jnp.bfloat16)
+    last_heads = heads // 4
+    first_heads = heads - last_heads
+    group = 4 if count <= 4 else 2
+    inputs = (combined, result, peaks, totals, value_copy, bias)
+    operands = (*inputs, fetched_latents, *pieces[:count])
+    attended, keys, latents = pl.pallas_call(
+        functools.partial(earlier_first_kernel, count, first_heads, group),
+        in_specs=[vmem] * len(operands),
+        out_specs=[hbm, vmem, vmem],
+        out_shape=[
+            attended_shape,
+            jax.ShapeDtypeStruct((ROW, count * rows), jnp.bfloat16),
+            jax.ShapeDtypeStruct((count * rows, LAT), jnp.bfloat16),
+        ],
+        scratch_shapes=[
+            pltpu.VMEM((rows, first_heads * VDIM), jnp.bfloat16),
+            pltpu.SemaphoreType.DMA((first_heads // group,)),
+        ],
+        cost_estimate=earlier_cost(first_heads),
+        compiler_params=params,
+        name="earlier_first",
+    )(*operands)
+    sent_rows, keys = lax.optimization_barrier((sent_rows, keys))
+    group = 2
+    operands = (*inputs, keys, latents, picked, found, sent_rows, filled, *pieces[1::2], attended)
     attended, page_cache, page_scales = pl.pallas_call(
-        functools.partial(earlier_kernel, n_cp, count, group),
-        in_specs=[vmem] * len(operands),
+        functools.partial(earlier_last_kernel, first_heads, last_heads, group),
+        in_specs=[vmem] * (len(operands) - 1) + [hbm],
         out_specs=[hbm] * 3,
         out_shape=[
-            jax.ShapeDtypeStruct((rows, heads * VDIM), jnp.bfloat16),
+            attended_shape,
             jax.ShapeDtypeStruct((slot_count, PAGE, ROW), jnp.bfloat16),
             jax.ShapeDtypeStruct((slot_count, NBLK, PAGE), jnp.bfloat16),
         ],
         scratch_shapes=[
-            pltpu.VMEM((ROW, count * rows), jnp.bfloat16),
-            pltpu.VMEM((count * rows, LAT), jnp.bfloat16),
-            pltpu.VMEM((rows, heads * VDIM), jnp.bfloat16),
+            pltpu.VMEM((rows, last_heads * VDIM), jnp.bfloat16),
             pltpu.VMEM((slot_count, PAGE, ROW), jnp.bfloat16),
             pltpu.VMEM((slot_count, NBLK, PAGE), jnp.bfloat16),
-            pltpu.SemaphoreType.DMA((heads // group + 2,)),
-        ],
-        cost_estimate=pl.CostEstimate(
-            flops=2 * rows * heads * (count * rows * (ROW + LAT) + LAT * VDIM),
-            bytes_accessed=2 * (heads * rows * (ROW + VDIM) + value_expand.size),
-            transcendentals=rows * heads * count * rows,
-        ),
+            pltpu.SemaphoreType.DMA((last_heads // group + 2,)),
+        ],
+        input_output_aliases={len(operands) - 1: 0},
+        cost_estimate=earlier_cost(last_heads),
         compiler_params=params,
-        name="earlier",
+        name="earlier_last",
     )(*operands)
     page_cache = page_cache.reshape(1, 1, slot_count, PAGE, ROW)
     page_scales = page_scales.transpose(0, 2, 1).reshape(1, 1, slot_count, PAGE, NBLK)

time: 17.3 us -> 16.8 us (0.971)
  Pallas kernels: 9.25 us -> 7.34 us
  starting transfers between devices: 5.83 us -> 6.79 us
  waiting for transfers between devices: 1.4 us -> 1.81 us
    pallas_call x2, Pallas kernels: 3.91 us -> 1.97 us  [the longest x1 1.08 us: on_device(): pl.pallas_call(functools.partial(earlier_last_kernel, first_heads, last_h...]
    ppermute x1, starting transfers between devices: 2.11 us -> 3.48 us  [on_device(): lax.ppermute(sent_rows, 'cp', [(c, (c + n_cp - 1) % n_cp) for c in range(...]
    ppermute x1, waiting for transfers between devices: 0.01 us -> 1.07 us  [fetch(): blocks.append(lax.ppermute(own, ('cp', 'dec'), pairs))]
    ppermute x1, waiting for transfers between devices: 1.39 us -> 0.74 us  [on_device(): lax.ppermute(sent_rows, 'cp', [(c, (c + n_cp - 1) % n_cp) for c in range(...]
    ppermute x3 -> x1, starting transfers between devices: 0.65 us -> 0.24 us  [swap(): lax.ppermute(block, 'dec', [(e, e ^ 1) for e in range(n_dec)])]
  transfers between devices with their start and end apart: 5 -> 3, of which waited for: 1 -> 2; matrix products, arithmetic and copies ran while one was open for 0% -> 0% of each run, Pallas kernels for 32% -> 38%
where the time goes in v11:
time: 16.8 us; the launch traced here: 16.6 us
  Pallas kernels  7.34 us (44%)
  starting transfers between devices  6.79 us (40%)
  waiting for transfers between devices  1.81 us (11%)
  between operations  0.67 us (4%)
    pallas_call x1, Pallas kernels, on_device(): pl.pallas_call(functools.partial(own_kernel, n_cp, count, chunk, group, s...  5.15 us
    ppermute x1, starting transfers between devices, on_device(): lax.ppermute(sent_rows, 'cp', [(c, (c + n_cp - 1) % n_cp) for c in range(...  3.48 us
    ppermute x1, starting transfers between devices, fetch(): blocks.append(lax.ppermute(own, ('cp', 'dec'), pairs))  3.08 us
    pallas_call x1, Pallas kernels, on_device(): pl.pallas_call(functools.partial(earlier_last_kernel, first_heads, last_h...  1.08 us
    ppermute x1, waiting for transfers between devices, fetch(): blocks.append(lax.ppermute(own, ('cp', 'dec'), pairs))  1.07 us
    pallas_call x1, Pallas kernels, on_device(): pl.pallas_call(functools.partial(earlier_first_kernel, count, first_heads...  0.89 us
    ppermute x1, waiting for transfers between devices, on_device(): lax.ppermute(sent_rows, 'cp', [(c, (c + n_cp - 1) % n_cp) for c in range(...  0.74 us
  transfers between devices with their start and end apart: 3, of which 2 were waited for; matrix products, arithmetic and copies ran while one was open for 0% of the time, Pallas kernels for 38%

profile of v11, /device:TPU:0, one launch (start us, length us, event | category | flops | bytes accessed | tf_op | source)
XLA Modules:
  0.0 16.6 jit_solution(8122780052109024744)
XLA Ops:
  0.6 3.1 %collective-permute-start.1 = (bf16[576,128]{1,0:T(8,128)(2,1)}, bf16[576,128]{1,0:T(8,128)(2,1)S(1)}, u32[]{:S(2)}, u32[]{:S(2)}) collective-permute-start(bf16[576,128]{1,0:T(8,128)(2,1)} %bitcast.5), channel_id=1, source_target_pairs={{0,4},{1,9},{2,6},{3,11},{4,8},{5,13},{6,10},{7,15},{8,12},{9,1},{... | collective-permute-start | bytes 442376 | tf_op jit(solution)/shard_map/ppermute | solution.py:341
  3.7 5.2 %own.1 = (bf16[2048,576]{1,0:T(8,128)(2,1)S(1)}, f32[2048,128]{1,0:T(8,128)S(1)}, f32[2048,128]{1,0:T(8,128)S(1)}, f32[2048,128]{1,0:T(8,128)S(1)}, bf16[48,640]...) custom-call(s32[2]{0:T(128)} %refs_0_.1, ...), custom_call_target="tpu_custom_call" | custom-call | flops 905969664 | bytes 5242880 | tf_op jit(solution)/shard_map/own/pallas_call | solution.py:371
  8.9 1.1 %collective-permute-done.1.refs_0_.refs_7_ = bf16[576,128]{1,0:T(8,128)(2,1)S(1)} collective-permute-done((bf16[576,128]{1,0:T(8,128)(2,1)}, bf16[576,128]{1,0:T(8,128)(2,1)S(1)}, u32[]{:S(2)}, u32[]{:S(2)}) %collective-permute-start.1) | collective-permute-done | bytes 147488 | tf_op jit(solution)/shard_map/ppermute | solution.py:341
  9.9 0.2 %collective-permute-start.2 = (bf16[576,128]{1,0:T(8,128)(2,1)S(1)}, bf16[576,128]{1,0:T(8,128)(2,1)S(1)}, u32[]{:S(2)}, u32[]{:S(2)}) collective-permute-start(bf16[576,128]{1,0:T(8,128)(2,1)S(1)} %collective-permute-done.1.refs_0_.refs_7_), channel_id=1, source_target_pairs={{0,1},{1,0},{2,3},{3,2},{4,5},{5,4},{6,7},{7,6},{8,9},{9,8},{10,11... | collective-permute-start | bytes 442376 | tf_op jit(solution)/shard_map/ppermute | solution.py:348
  10.2 3.5 %collective-permute-start = (bf16[48,640]{1,0:T(8,128)(2,1)S(1)}, bf16[48,640]{1,0:T(8,128)(2,1)S(1)}, u32[]{:S(2)}, u32[]{:S(2)}) collective-permute-start(bf16[48,640]{1,0:T(8,128)(2,1)S(1)} %get-tuple-element.31), channel_id=1, source_target_pairs={{0,12},{4,0},{8,4},{12,8},{1,13},{5,1},{9,5},{13,9},{2,14},{6,2},{... | collective-permute-start | bytes 184328 | tf_op jit(solution)/shard_map/ppermute | solution.py:404
  13.7 0.2 %arrived.1 = (f32[48,576]{1,0:T(8,128)S(1)}, bf16[128,512]{1,0:T(8,128)(2,1)S(1)}) custom-call(bf16[48,384]{1,0:T(8,128)(2,1)S(1)} %get-tuple-element.33.picked.refs_8_, bf16[576,128]{1,0:T(8,128)(2,1)S(1)} %get-tuple-element.34.own, bf16[576,128]{1,0:T(8,128)(2,1)S(1)} %collective-permute-done.1.refs_0_.refs_7_), custom_call_target="tpu_custom_call" | custom-call | flops 1048576 | bytes 1024 | tf_op jit(solution)/shard_map/arrived/pallas_call | solution.py:407
  13.9 0.0 collective-permute-done.2.refs_8_.refs_12_
  13.9 0.9 %earlier_first.1 = (bf16[128,2048]{1,0:T(8,128)(2,1)}, bf16[576,256]{1,0:T(8,128)(2,1)S(1)}, bf16[256,512]{1,0:T(8,128)(2,1)S(1)}) custom-call(bf16[2048,576]{1,0:T(8,128)(2,1)S(1)} %get-tuple-element.25.refs_0_, f32[2048,128]{1,0:T(8,128)S(1)} %get-tuple-element.26.refs_1_, f32[2048,128]{1,0:T(8,128)S(1)} %get-tuple-element.27.refs_2_, ...), custom_call_target="tpu_custom_call" | custom-call | flops 1056964608 | bytes 4259840 | tf_op jit(solution)/shard_map/earlier_first/pallas_call | solution.py:433
  14.8 0.7 %collective-permute-done.refs_10_ = bf16[48,640]{1,0:T(8,128)(2,1)S(1)} collective-permute-done((bf16[48,640]{1,0:T(8,128)(2,1)S(1)}, bf16[48,640]{1,0:T(8,128)(2,1)S(1)}, u32[]{:S(2)}, u32[]{:S(2)}) %collective-permute-start) | collective-permute-done | bytes 61472 | tf_op jit(solution)/shard_map/ppermute | solution.py:404
  15.5 1.1 %earlier_last.1 = (bf16[128,2048]{1,0:T(8,128)(2,1)}, bf16[3,16,576]{2,1,0:T(8,128)(2,1)}, bf16[3,4,16]{2,1,0:T(4,128)(2,1)}) custom-call(bf16[2048,576]{1,0:T(8,128)(2,1)S(1)} %get-tuple-element.25.refs_0_, f32[2048,128]{1,0:T(8,128)S(1)} %get-tuple-element.26.refs_1_, f32[2048,128]{1,0:T(8,128)S(1)} %get-tuple-element.27.refs_2_, ...), custom_call_target="tpu_custom_call", output_to_operand_aliasing={{0}: (13, {})} | custom-call | flops 352321536 | bytes 2818048 | tf_op jit(solution)/shard_map/earlier_last/pallas_call | solution.py:453
Async XLA Ops:
  0.6 9.3 %collective-permute-start.1 = (bf16[576,128]{1,0:T(8,128)(2,1)}, bf16[576,128]{1,0:T(8,128)(2,1)S(1)}, u32[]{:S(2)}, u32[]{:S(2)}) collective-permute-start(bf16[576,128]{1,0:T(8,128)(2,1)} %bitcast.5), channel_id=1, source_target_pairs={{0,4},{1,9},{2,6},{3,11},{4,8},{5,13},{6,10},{7,15},{8,12},{9,1},{... | collective-permute-start | bytes 442376 | tf_op jit(solution)/shard_map/ppermute | solution.py:341
  9.9 3.9 %collective-permute-start.2 = (bf16[576,128]{1,0:T(8,128)(2,1)S(1)}, bf16[576,128]{1,0:T(8,128)(2,1)S(1)}, u32[]{:S(2)}, u32[]{:S(2)}) collective-permute-start(bf16[576,128]{1,0:T(8,128)(2,1)S(1)} %collective-permute-done.1.refs_0_.refs_7_), channel_id=1, source_target_pairs={{0,1},{1,0},{2,3},{3,2},{4,5},{5,4},{6,7},{7,6},{8,9},{9,8},{10,11... | collective-permute-start | bytes 442376 | tf_op jit(solution)/shard_map/ppermute | solution.py:348
  10.2 5.3 %collective-permute-start = (bf16[48,640]{1,0:T(8,128)(2,1)S(1)}, bf16[48,640]{1,0:T(8,128)(2,1)S(1)}, u32[]{:S(2)}, u32[]{:S(2)}) collective-permute-start(bf16[48,640]{1,0:T(8,128)(2,1)S(1)} %get-tuple-element.31), channel_id=1, source_target_pairs={{0,12},{4,0},{8,4},{12,8},{1,13},{5,1},{9,5},{13,9},{2,14},{6,2},{... | collective-permute-start | bytes 184328 | tf_op jit(solution)/shard_map/ppermute | solution.py:404

commit v12 on v11

--- a/solution.py
+++ b/solution.py
@@ -18,6 +18,7 @@
 ROW = LAT + ROPE
 HEAD = NOPE + ROPE
 LANES = 128
+SWAP = 3
 
 masked_fill = -1e30
 amax_epsilon = 1e-06
@@ -303,12 +304,14 @@
     inputs, fetched_latents, refs = refs[:6], refs[6], refs[7:]
     arrived, (attended, keys, latents, result, sems) = refs[:-5], refs[-5:]
     rows = arrived[0].shape[1]
-    for b in range(count):
-        keys[:, b * rows:(b + 1) * rows] = arrived[b][...]
-        if b % 2:
-            latents[b * rows:(b + 1) * rows, :] = arrived[b][:LAT, :].T
-        else:
-            latents[b * rows:(b + 1) * rows, :] = fetched_latents[b // 2 * rows:(b // 2 + 1) * rows, :]
+    for i in range(count // 2):
+        fetched, *parts = arrived[i * (1 + SWAP):(i + 1) * (1 + SWAP)]
+        swapped = jnp.concatenate([part[...] for part in parts], axis=0)
+        at = 2 * i * rows
+        keys[:, at:at + rows] = fetched[...]
+        keys[:, at + rows:at + 2 * rows] = swapped
+        latents[at:at + rows, :] = fetched_latents[i * rows:(i + 1) * rows, :]
+        latents[at + rows:at + 2 * rows, :] = swapped[:LAT].T
     earlier_heads(0, heads, group, inputs, keys, latents, attended, result, sems, lambda: None)
 
 
@@ -323,8 +326,9 @@
 
     def cache():
         rows = found[...] + sent_rows[:, :ROW].astype(jnp.float32)
-        for i, block in enumerate(swapped):
-            rows = rows + pick_rows(picked, 2 + 2 * i, block[...])
+        for i in range(len(swapped) // SWAP):
+            block = jnp.concatenate([part[...] for part in swapped[i * SWAP:(i + 1) * SWAP]], axis=0)
+            rows = rows + pick_rows(picked, 2 + 2 * i, block)
         write_cache(rows, filled, cache_buf, scale_buf)
         for copy in cache_copies:
             copy.start()
@@ -345,7 +349,8 @@
 def swap(blocks, n_dec):
     pieces = []
     for block in blocks:
-        pieces += [block, lax.ppermute(block, "dec", [(e, e ^ 1) for e in range(n_dec)])]
+        parts = [block[at:at + ROW // SWAP] for at in range(0, ROW, ROW // SWAP)]
+        pieces += [block] + [lax.ppermute(part, "dec", [(e, e ^ 1) for e in range(n_dec)]) for part in parts]
     return pieces
 
 
@@ -429,7 +434,7 @@
     first_heads = heads - last_heads
     group = 4 if count <= 4 else 2
     inputs = (combined, result, peaks, totals, value_copy, bias)
-    operands = (*inputs, fetched_latents, *pieces[:count])
+    operands = (*inputs, fetched_latents, *pieces[:count // 2 * (1 + SWAP)])
     attended, keys, latents = pl.pallas_call(
         functools.partial(earlier_first_kernel, count, first_heads, group),
         in_specs=[vmem] * len(operands),
@@ -443,13 +448,13 @@
             pltpu.VMEM((rows, first_heads * VDIM), jnp.bfloat16),
             pltpu.SemaphoreType.DMA((first_heads // group,)),
         ],
-        cost_estimate=earlier_cost(first_heads),
+        cost_estimate=pl.CostEstimate(flops=2**20, bytes_accessed=2**10, transcendentals=0),
         compiler_params=params,
         name="earlier_first",
     )(*operands)
     sent_rows, keys = lax.optimization_barrier((sent_rows, keys))
     group = 2
-    operands = (*inputs, keys, latents, picked, found, sent_rows, filled, *pieces[1::2], attended)
+    operands = (*inputs, keys, latents, picked, found, sent_rows, filled, *[part for i, part in enumerate(pieces) if i % (1 + SWAP)], attended)
     attended, page_cache, page_scales = pl.pallas_call(
         functools.partial(earlier_last_kernel, first_heads, last_heads, group),
         in_specs=[vmem] * (len(operands) - 1) + [hbm],

time: 16.8 us -> 15.8 us (0.940)
  the two profiles are of different devices: /device:TPU:0 before, /device:TPU:21 now
where the time goes in v12:
time: 15.8 us; the launch traced here: 15.7 us
  Pallas kernels  9.91 us (63%)
  starting transfers between devices  4.42 us (28%)
  waiting for transfers between devices  0.67 us (4%)
  between operations  0.67 us (4%)
    pallas_call x1, Pallas kernels, on_device(): pl.pallas_call(functools.partial(own_kernel, n_cp, count, chunk, group, s...  5.15 us
    pallas_call x1, Pallas kernels, on_device(): pl.pallas_call(functools.partial(earlier_first_kernel, count, first_heads...  2.87 us
    ppermute x1, starting transfers between devices, on_device(): lax.ppermute(sent_rows, 'cp', [(c, (c + n_cp - 1) % n_cp) for c in range(...  2.47 us
    ppermute x3, starting transfers between devices, swap(): lax.ppermute(part, 'dec', [(e, e ^ 1) for e in range(n_dec)])  1.84 us
    pallas_call x1, Pallas kernels, on_device(): pl.pallas_call(functools.partial(earlier_last_kernel, first_heads, last_h...  1.68 us
    ppermute x3, waiting for transfers between devices, swap(): lax.ppermute(part, 'dec', [(e, e ^ 1) for e in range(n_dec)])  0.66 us
  transfers between devices with their start and end apart: 5, of which 3 were waited for; matrix products, arithmetic and copies ran while one was open for 0% of the time, Pallas kernels for 52%

profile of v12, /device:TPU:21, one launch (start us, length us, event | category | flops | bytes accessed | tf_op | source)
XLA Modules:
  0.0 15.7 jit_solution(2427211738549631284)
XLA Ops:
  0.6 0.1 collective-permute-start.1
  0.7 5.2 %own.1 = (bf16[2048,576]{1,0:T(8,128)(2,1)S(1)}, f32[2048,128]{1,0:T(8,128)S(1)}, f32[2048,128]{1,0:T(8,128)S(1)}, f32[2048,128]{1,0:T(8,128)S(1)}, bf16[48,640]...) custom-call(s32[2]{0:T(128)} %refs_0_.1, ...), custom_call_target="tpu_custom_call" | custom-call | flops 905969664 | bytes 5242880 | tf_op jit(solution)/shard_map/own/pallas_call | solution.py:376
  5.9 2.5 %collective-permute-start = (bf16[48,640]{1,0:T(8,128)(2,1)S(1)}, bf16[48,640]{1,0:T(8,128)(2,1)S(1)}, u32[]{:S(2)}, u32[]{:S(2)}) collective-permute-start(bf16[48,640]{1,0:T(8,128)(2,1)S(1)} %get-tuple-element.31), channel_id=1, source_target_pairs={{0,12},{4,0},{8,4},{12,8},{1,13},{5,1},{9,5},{13,9},{2,14},{6,2},{... | collective-permute-start | bytes 184328 | tf_op jit(solution)/shard_map/ppermute | solution.py:409
  8.4 0.0 collective-permute-done.1.refs_0_.refs_7_
  8.4 1.3 %collective-permute-start.4 = (bf16[192,128]{1,0:T(8,128)(2,1)S(1)}, bf16[192,128]{1,0:T(8,128)(2,1)S(1)}, u32[]{:S(2)}, u32[]{:S(2)}) collective-permute-start(bf16[192,128]{1,0:T(8,128)(2,1)S(1)} %get-tuple-element.47), channel_id=1, source_target_pairs={{0,1},{1,0},{2,3},{3,2},{4,5},{5,4},{6,7},{7,6},{8,9},{9,8},{10,11... | collective-permute-start | bytes 147464 | tf_op jit(solution)/shard_map/ppermute | solution.py:353
  9.7 0.1 collective-permute-start.3
  9.8 0.4 %collective-permute-start.2 = (bf16[192,128]{1,0:T(8,128)(2,1)S(1)}, bf16[192,128]{1,0:T(8,128)(2,1)S(1)}, u32[]{:S(2)}, u32[]{:S(2)}) collective-permute-start(bf16[192,128]{1,0:T(8,128)(2,1)S(1)} %get-tuple-element.49), channel_id=1, source_target_pairs={{0,1},{1,0},{2,3},{3,2},{4,5},{5,4},{6,7},{7,6},{8,9},{9,8},{10,11... | collective-permute-start | bytes 147464 | tf_op jit(solution)/shard_map/ppermute | solution.py:353
  10.2 0.2 %arrived.1 = (f32[48,576]{1,0:T(8,128)S(1)}, bf16[128,512]{1,0:T(8,128)(2,1)S(1)}) custom-call(bf16[48,384]{1,0:T(8,128)(2,1)S(1)} %get-tuple-element.33.picked.refs_8_, bf16[576,128]{1,0:T(8,128)(2,1)S(1)} %get-tuple-element.34.own, bf16[576,128]{1,0:T(8,128)(2,1)S(1)} %collective-permute-done.1.refs_0_.refs_7_), custom_call_target="tpu_custom_call" | custom-call | flops 1048576 | bytes 1024 | tf_op jit(solution)/shard_map/arrived/pallas_call | solution.py:412
  10.4 0.2 collective-permute-done.4.refs_10_.refs_14_
  10.6 0.3 %collective-permute-done.3.refs_9_.refs_13_ = bf16[192,128]{1,0:T(8,128)(2,1)S(1)} collective-permute-done((bf16[192,128]{1,0:T(8,128)(2,1)S(1)}, bf16[192,128]{1,0:T(8,128)(2,1)S(1)}, u32[]{:S(2)}, u32[]{:S(2)}) %collective-permute-start.3) | collective-permute-done | bytes 49184 | tf_op jit(solution)/shard_map/ppermute | solution.py:353
  10.9 0.2 %collective-permute-done.2.refs_8_.refs_12_ = bf16[192,128]{1,0:T(8,128)(2,1)S(1)} collective-permute-done((bf16[192,128]{1,0:T(8,128)(2,1)S(1)}, bf16[192,128]{1,0:T(8,128)(2,1)S(1)}, u32[]{:S(2)}, u32[]{:S(2)}) %collective-permute-start.2) | collective-permute-done | bytes 49184 | tf_op jit(solution)/shard_map/ppermute | solution.py:353
  11.1 2.9 %earlier_first.1 = (bf16[128,2048]{1,0:T(8,128)(2,1)}, bf16[576,256]{1,0:T(8,128)(2,1)S(1)}, bf16[256,512]{1,0:T(8,128)(2,1)S(1)}) custom-call(bf16[2048,576]{1,0:T(8,128)(2,1)S(1)} %get-tuple-element.25.refs_0_, f32[2048,128]{1,0:T(8,128)S(1)} %get-tuple-element.26.refs_1_, f32[2048,128]{1,0:T(8,128)S(1)} %get-tuple-element.27.refs_2_, ...), custom_call_target="tpu_custom_call" | custom-call | flops 1048576 | bytes 1024 | tf_op jit(solution)/shard_map/earlier_first/pallas_call | solution.py:438
  14.0 0.0 collective-permute-done.refs_10_
  14.0 1.7 %earlier_last.1 = (bf16[128,2048]{1,0:T(8,128)(2,1)}, bf16[3,16,576]{2,1,0:T(8,128)(2,1)}, bf16[3,4,16]{2,1,0:T(4,128)(2,1)}) custom-call(bf16[2048,576]{1,0:T(8,128)(2,1)S(1)} %get-tuple-element.25.refs_0_, f32[2048,128]{1,0:T(8,128)S(1)} %get-tuple-element.26.refs_1_, f32[2048,128]{1,0:T(8,128)S(1)} %get-tuple-element.27.refs_2_, ...), custom_call_target="tpu_custom_call", output_to_operand_aliasing={{0}: (15, {})} | custom-call | flops 352321536 | bytes 2818048 | tf_op jit(solution)/shard_map/earlier_last/pallas_call | solution.py:458
  (1 shorter events, 0.0 us)
Async XLA Ops:
  0.6 7.7 %collective-permute-start.1 = (bf16[576,128]{1,0:T(8,128)(2,1)}, bf16[576,128]{1,0:T(8,128)(2,1)S(1)}, u32[]{:S(2)}, u32[]{:S(2)}) collective-permute-start(bf16[576,128]{1,0:T(8,128)(2,1)} %bitcast.5), channel_id=1, source_target_pairs={{0,4},{1,9},{2,6},{3,11},{4,8},{5,13},{6,10},{7,15},{8,12},{9,1},{... | collective-permute-start | bytes 442376 | tf_op jit(solution)/shard_map/ppermute | solution.py:345
  5.9 8.1 %collective-permute-start = (bf16[48,640]{1,0:T(8,128)(2,1)S(1)}, bf16[48,640]{1,0:T(8,128)(2,1)S(1)}, u32[]{:S(2)}, u32[]{:S(2)}) collective-permute-start(bf16[48,640]{1,0:T(8,128)(2,1)S(1)} %get-tuple-element.31), channel_id=1, source_target_pairs={{0,12},{4,0},{8,4},{12,8},{1,13},{5,1},{9,5},{13,9},{2,14},{6,2},{... | collective-permute-start | bytes 184328 | tf_op jit(solution)/shard_map/ppermute | solution.py:409
  8.4 2.2 %collective-permute-start.4 = (bf16[192,128]{1,0:T(8,128)(2,1)S(1)}, bf16[192,128]{1,0:T(8,128)(2,1)S(1)}, u32[]{:S(2)}, u32[]{:S(2)}) collective-permute-start(bf16[192,128]{1,0:T(8,128)(2,1)S(1)} %get-tuple-element.47), channel_id=1, source_target_pairs={{0,1},{1,0},{2,3},{3,2},{4,5},{5,4},{6,7},{7,6},{8,9},{9,8},{10,11... | collective-permute-start | bytes 147464 | tf_op jit(solution)/shard_map/ppermute | solution.py:353
  9.7 1.2 %collective-permute-start.3 = (bf16[192,128]{1,0:T(8,128)(2,1)S(1)}, bf16[192,128]{1,0:T(8,128)(2,1)S(1)}, u32[]{:S(2)}, u32[]{:S(2)}) collective-permute-start(bf16[192,128]{1,0:T(8,128)(2,1)S(1)} %get-tuple-element.48), channel_id=1, source_target_pairs={{0,1},{1,0},{2,3},{3,2},{4,5},{5,4},{6,7},{7,6},{8,9},{9,8},{10,11... | collective-permute-start | bytes 147464 | tf_op jit(solution)/shard_map/ppermute | solution.py:353
  9.8 1.3 %collective-permute-start.2 = (bf16[192,128]{1,0:T(8,128)(2,1)S(1)}, bf16[192,128]{1,0:T(8,128)(2,1)S(1)}, u32[]{:S(2)}, u32[]{:S(2)}) collective-permute-start(bf16[192,128]{1,0:T(8,128)(2,1)S(1)} %get-tuple-element.49), channel_id=1, source_target_pairs={{0,1},{1,0},{2,3},{3,2},{4,5},{5,4},{6,7},{7,6},{8,9},{9,8},{10,11... | collective-permute-start | bytes 147464 | tf_op jit(solution)/shard_map/ppermute | solution.py:353

commit v13 on v12

--- a/solution.py
+++ b/solution.py
@@ -18,7 +18,7 @@
 ROW = LAT + ROPE
 HEAD = NOPE + ROPE
 LANES = 128
-SWAP = 3
+SWAP = 2
 
 masked_fill = -1e30
 amax_epsilon = 1e-06
@@ -87,7 +87,7 @@
     return jnp.dot(latents, both, preferred_element_type=jnp.float32).astype(jnp.bfloat16)
 
 
-def own_kernel(n_cp, count, chunk, group, slot_count, *refs):
+def own_kernel(n_cp, count, chunks, group, slot_count, *refs):
     inputs, refs = refs[:7], refs[7:]
     combined, result, peaks, totals, sent_rows, bias, picked, filled, own, value_expand = refs[:10]
     prompt_pages, decode_owner, slot_offset, queries, key_absorb, latents, sems = refs[10:]
@@ -98,27 +98,28 @@
         pltpu.make_async_copy(source, target, sems.at[i])
         for i, (source, target) in enumerate(zip(inputs[:4], (prompt_pages, decode_owner, slot_offset, own)))
     ]
-    large = []
-    for g in range(heads // chunk):
-        at = 4 + 3 * g
-        some = pl.ds(g * chunk, chunk)
-        wide = pl.ds(g * chunk * HEAD, chunk * HEAD)
-        large.append((
+    large = {}
+    first = 0
+    for chunk in chunks:
+        at = 4 + 3 * len(large)
+        some = pl.ds(first, chunk)
+        wide = pl.ds(first * HEAD, chunk * HEAD)
+        large[first] = (
             pltpu.make_async_copy(queries_hbm.at[:, wide], queries.at[:, wide], sems.at[at]),
             pltpu.make_async_copy(absorb_hbm.at[some], key_absorb.at[some], sems.at[at + 1]),
             pltpu.make_async_copy(expand_hbm.at[some], value_expand.at[some], sems.at[at + 2]),
-        ))
+        )
+        first += chunk
     for copy in small:
         copy.start()
-    for chunk_copies in large:
+    for chunk_copies in large.values():
         for copy in chunk_copies:
             copy.start()
     steps = heads // group
 
     def absorb(g):
-        if g * group % chunk == 0:
-            for copy in large[g * group // chunk][:2]:
-                copy.wait()
+        for copy in large.get(g * group, ())[:2]:
+            copy.wait()
         for h in range(g * group, (g + 1) * group):
             at = h * HEAD
             absorbed = jnp.dot(queries[:, at:at + NOPE], key_absorb[h], preferred_element_type=jnp.float32)
@@ -129,8 +130,8 @@
         return jnp.dot(combined[g * group * rows:(g + 1) * group * rows, :], own[...], preferred_element_type=jnp.float32)
 
     def value(g):
-        if g * group % chunk == 0:
-            large[g * group // chunk][2].wait()
+        for copy in large.get(g * group, ())[2:]:
+            copy.wait()
         return [head_values(latents[...], value_expand, g * group + i) for i in range(0, group, 2)]
 
     def finish(g, scores, both):
@@ -176,8 +177,9 @@
         targets.append(jnp.where(here, lax.rem(page * PAGE, rows), -PAGE))
     choice = row_picker(targets, rows)
     sent = lax.dot_general(choice, block, NT, preferred_element_type=jnp.float32)
-    sent_rows[:, :ROW] = sent.astype(jnp.bfloat16)
-    sent_rows[:, ROW:] = jnp.zeros((choice.shape[0], sent_rows.shape[1] - ROW), jnp.bfloat16)
+    kept = choice.shape[0]
+    sent_rows[...] = jnp.zeros(sent_rows.shape, jnp.bfloat16)
+    sent_rows[:kept, :ROW] = sent.astype(jnp.bfloat16)
     for b in range(count):
         bias[:, b * rows:(b + 1) * rows] = visible_bias(prompt_pages, rows, swap_pair(jnp.int32(b + 1), n_cp))
     targets = []
@@ -229,19 +231,16 @@
         page_scales[c] = table[:, c * PAGE:(c + 1) * PAGE]
 
 
-def earlier_heads(first_head, heads, group, inputs, keys, latents, attended, result, sems, beside):
-    combined, own_result, peaks, totals, value_expand, bias = inputs
+def earlier_kernel(count, group, *refs):
+    combined, own_result, peaks, totals, value_expand, bias, fetched_latents = refs[:7]
+    arrived, (result, keys, latents) = refs[7:-3], refs[-3:]
     rows, width = bias.shape
+    heads = value_expand.shape[0]
     steps = heads // group
 
     def span(g):
-        at = (first_head + g * group) * rows
+        at = g * group * rows
         return slice(at, at + group * rows)
-
-    def send(g):
-        at = pl.ds((first_head + g * group) * VDIM, group * VDIM)
-        here = pl.ds(g * group * VDIM, group * VDIM)
-        return pltpu.make_async_copy(result.at[:, here], attended.at[:, at], sems.at[g])
 
     def score(g):
         scores = jnp.dot(combined[span(g), :], keys[...], preferred_element_type=jnp.float32)
@@ -264,77 +263,53 @@
     def finish(g, mixed, factor, inverse):
         for i in range(group):
             part = slice(i * rows, (i + 1) * rows)
-            h = first_head + g * group + i
+            h = g * group + i
             out = jnp.dot(mixed[part], value_expand[h], preferred_element_type=jnp.float32)
             out = own_result[h * rows:(h + 1) * rows, :] * factor[part] + out * inverse[part]
-            at = (g * group + i) * VDIM
-            result[:, at:at + VDIM] = out.astype(jnp.bfloat16)
-        send(g).start()
+            result[:, h * VDIM:(h + 1) * VDIM] = out.astype(jnp.bfloat16)
 
     @pl.when(lax.axis_index("cp") == 0)
     def _():
-        beside()
-        for g in range(steps):
-            for i in range(group):
-                h = first_head + g * group + i
-                at = (g * group + i) * VDIM
-                part = slice(h * rows, (h + 1) * rows)
-                result[:, at:at + VDIM] = (own_result[part, :] / totals[part, :]).astype(jnp.bfloat16)
-            send(g).start()
+        for h in range(heads):
+            part = slice(h * rows, (h + 1) * rows)
+            result[:, h * VDIM:(h + 1) * VDIM] = (own_result[part, :] / totals[part, :]).astype(jnp.bfloat16)
 
     @pl.when(lax.axis_index("cp") > 0)
     def _():
+        for i in range(count // 2):
+            fetched, *parts = arrived[i * (1 + SWAP):(i + 1) * (1 + SWAP)]
+            swapped = jnp.concatenate([part[...] for part in parts], axis=0)
+            at = 2 * i * rows
+            keys[:, at:at + rows] = fetched[...]
+            keys[:, at + rows:at + 2 * rows] = swapped
+            latents[at:at + rows, :] = fetched_latents[i * rows:(i + 1) * rows, :]
+            latents[at + rows:at + 2 * rows, :] = swapped[:LAT].T
         scores, weights, mixed = {}, {}, {}
         for step in range(steps + 2):
             if step < steps:
                 scores[step] = score(step)
-            if step == 0:
-                beside()
             if 0 <= step - 2:
                 finish(step - 2, mixed.pop(step - 2), *weights.pop(step - 2)[1:])
             if 0 <= step - 1 < steps:
                 weights[step - 1] = weigh(step - 1, scores.pop(step - 1))
                 mixed[step - 1] = mix(step - 1, weights[step - 1][0])
 
-    for g in range(steps):
-        send(g).wait()
-
-
-def earlier_first_kernel(count, heads, group, *refs):
-    inputs, fetched_latents, refs = refs[:6], refs[6], refs[7:]
-    arrived, (attended, keys, latents, result, sems) = refs[:-5], refs[-5:]
-    rows = arrived[0].shape[1]
-    for i in range(count // 2):
-        fetched, *parts = arrived[i * (1 + SWAP):(i + 1) * (1 + SWAP)]
-        swapped = jnp.concatenate([part[...] for part in parts], axis=0)
-        at = 2 * i * rows
-        keys[:, at:at + rows] = fetched[...]
-        keys[:, at + rows:at + 2 * rows] = swapped
-        latents[at:at + rows, :] = fetched_latents[i * rows:(i + 1) * rows, :]
-        latents[at + rows:at + 2 * rows, :] = swapped[:LAT].T
-    earlier_heads(0, heads, group, inputs, keys, latents, attended, result, sems, lambda: None)
-
-
-def earlier_last_kernel(first_head, heads, group, *refs):
-    inputs, (keys, latents, picked, found, sent_rows, filled), refs = refs[:6], refs[6:12], refs[12:]
-    swapped, refs = refs[:-8], refs[-7:]
-    attended, page_cache, page_scales, result, cache_buf, scale_buf, sems = refs
-    cache_copies = [
-        pltpu.make_async_copy(cache_buf, page_cache, sems.at[heads // group]),
-        pltpu.make_async_copy(scale_buf, page_scales, sems.at[heads // group + 1]),
+
+def store_kernel(result, picked, found, sent_rows, filled, *refs):
+    swapped, (attended, page_cache, page_scales, cache_buf, scale_buf, sems) = refs[:-6], refs[-6:]
+    copies = [
+        pltpu.make_async_copy(source, target, sems.at[i])
+        for i, (source, target) in enumerate(((result, attended), (cache_buf, page_cache), (scale_buf, page_scales)))
     ]
-
-    def cache():
-        rows = found[...] + sent_rows[:, :ROW].astype(jnp.float32)
-        for i in range(len(swapped) // SWAP):
-            block = jnp.concatenate([part[...] for part in swapped[i * SWAP:(i + 1) * SWAP]], axis=0)
-            rows = rows + pick_rows(picked, 2 + 2 * i, block)
-        write_cache(rows, filled, cache_buf, scale_buf)
-        for copy in cache_copies:
-            copy.start()
-
-    earlier_heads(first_head, heads, group, inputs, keys, latents, attended, result, sems, cache)
-    for copy in cache_copies:
+    copies[0].start()
+    rows = found[...] + sent_rows[:found.shape[0], :ROW].astype(jnp.float32)
+    for i in range(len(swapped) // SWAP):
+        block = jnp.concatenate([part[...] for part in swapped[i * SWAP:(i + 1) * SWAP]], axis=0)
+        rows = rows + pick_rows(picked, 2 + 2 * i, block)
+    write_cache(rows, filled, cache_buf, scale_buf)
+    for copy in copies[1:]:
+        copy.start()
+    for copy in copies:
         copy.wait()
 
 
@@ -371,10 +346,10 @@
     vmem = pl.BlockSpec(memory_space=pltpu.VMEM)
     hbm = pl.BlockSpec(memory_space=pltpu.HBM)
     params = pltpu.CompilerParams(vmem_limit_bytes=32 * 2**20)
-    group, chunk = 2, 4
+    group, chunks = 2, (heads // 8, heads // 8, heads // 4, heads // 2)
     inputs = (prompt_pages, decode_owner, slot_offset, own, queries, key_absorb, value_expand)
     combined, result, peaks, totals, sent_rows, bias, picked, filled, own_copy, value_copy = pl.pallas_call(
-        functools.partial(own_kernel, n_cp, count, chunk, group, slot_count),
+        functools.partial(own_kernel, n_cp, count, chunks, group, slot_count),
         in_specs=[hbm] * 7,
         out_specs=[vmem] * 10,
         out_shape=[
@@ -382,7 +357,7 @@
             jax.ShapeDtypeStruct((heads * rows, VDIM), jnp.float32),
             jax.ShapeDtypeStruct((heads * rows, LANES), jnp.float32),
             jax.ShapeDtypeStruct((heads * rows, LANES), jnp.float32),
-            jax.ShapeDtypeStruct((kept, -(-ROW // LANES) * LANES), jnp.bfloat16),
+            jax.ShapeDtypeStruct((kept + PAGE, -(-ROW // LANES) * LANES), jnp.bfloat16),
             jax.ShapeDtypeStruct((rows, count * rows), jnp.float32),
             jax.ShapeDtypeStruct((kept, (n_cp - 1) * rows), jnp.bfloat16),
             jax.ShapeDtypeStruct((8, LANES), jnp.float32),
@@ -396,7 +371,7 @@
             pltpu.VMEM((rows, heads * HEAD), jnp.bfloat16),
             pltpu.VMEM((heads, NOPE, LAT), jnp.bfloat16),
             pltpu.VMEM((rows, LAT), jnp.bfloat16),
-            pltpu.SemaphoreType.DMA((4 + 3 * (heads // chunk),)),
+            pltpu.SemaphoreType.DMA((4 + 3 * len(chunks),)),
         ],
         cost_estimate=pl.CostEstimate(
             flops=2 * rows * heads * (2 * NOPE * LAT + rows * (ROW + VDIM)),
@@ -422,58 +397,40 @@
         name="arrived",
     )(picked, own_copy, *blocks)
 
-    def earlier_cost(some):
-        return pl.CostEstimate(
-            flops=2 * rows * some * (count * rows * (ROW + LAT) + LAT * VDIM),
-            bytes_accessed=2 * (some * rows * (ROW + VDIM) + value_expand.size),
-            transcendentals=rows * some * count * rows,
-        )
-
-    attended_shape = jax.ShapeDtypeStruct((rows, heads * VDIM), jnp.bfloat16)
-    last_heads = heads // 4
-    first_heads = heads - last_heads
     group = 4 if count <= 4 else 2
-    inputs = (combined, result, peaks, totals, value_copy, bias)
-    operands = (*inputs, fetched_latents, *pieces[:count // 2 * (1 + SWAP)])
-    attended, keys, latents = pl.pallas_call(
-        functools.partial(earlier_first_kernel, count, first_heads, group),
+    operands = (combined, result, peaks, totals, value_copy, bias, fetched_latents, *pieces[:count // 2 * (1 + SWAP)])
+    attended = pl.pallas_call(
+        functools.partial(earlier_kernel, count, group),
         in_specs=[vmem] * len(operands),
-        out_specs=[hbm, vmem, vmem],
-        out_shape=[
-            attended_shape,
-            jax.ShapeDtypeStruct((ROW, count * rows), jnp.bfloat16),
-            jax.ShapeDtypeStruct((count * rows, LAT), jnp.bfloat16),
-        ],
+        out_specs=vmem,
+        out_shape=jax.ShapeDtypeStruct((rows, heads * VDIM), jnp.bfloat16),
         scratch_shapes=[
-            pltpu.VMEM((rows, first_heads * VDIM), jnp.bfloat16),
-            pltpu.SemaphoreType.DMA((first_heads // group,)),
+            pltpu.VMEM((ROW, count * rows), jnp.bfloat16),
+            pltpu.VMEM((count * rows, LAT), jnp.bfloat16),
         ],
         cost_estimate=pl.CostEstimate(flops=2**20, bytes_accessed=2**10, transcendentals=0),
         compiler_params=params,
-        name="earlier_first",
+        name="earlier",
     )(*operands)
-    sent_rows, keys = lax.optimization_barrier((sent_rows, keys))
-    group = 2
-    operands = (*inputs, keys, latents, picked, found, sent_rows, filled, *[part for i, part in enumerate(pieces) if i % (1 + SWAP)], attended)
+    sent_rows, attended = lax.optimization_barrier((sent_rows, attended))
+    operands = (attended, picked, found, sent_rows, filled, *[part for i, part in enumerate(pieces) if i % (1 + SWAP)])
     attended, page_cache, page_scales = pl.pallas_call(
-        functools.partial(earlier_last_kernel, first_heads, last_heads, group),
-        in_specs=[vmem] * (len(operands) - 1) + [hbm],
+        store_kernel,
+        in_specs=[vmem] * len(operands),
         out_specs=[hbm] * 3,
         out_shape=[
-            attended_shape,
+            jax.ShapeDtypeStruct((rows, heads * VDIM), jnp.bfloat16),
             jax.ShapeDtypeStruct((slot_count, PAGE, ROW), jnp.bfloat16),
             jax.ShapeDtypeStruct((slot_count, NBLK, PAGE), jnp.bfloat16),
         ],
         scratch_shapes=[
-            pltpu.VMEM((rows, last_heads * VDIM), jnp.bfloat16),
             pltpu.VMEM((slot_count, PAGE, ROW), jnp.bfloat16),
             pltpu.VMEM((slot_count, NBLK, PAGE), jnp.bfloat16),
-            pltpu.SemaphoreType.DMA((last_heads // group + 2,)),
-        ],
-        input_output_aliases={len(operands) - 1: 0},
-        cost_estimate=earlier_cost(last_heads),
+            pltpu.SemaphoreType.DMA((3,)),
+        ],
+        cost_estimate=pl.CostEstimate(flops=2**20, bytes_accessed=2**10, transcendentals=0),
         compiler_params=params,
-        name="earlier_last",
+        name="store",
     )(*operands)
     page_cache = page_cache.reshape(1, 1, slot_count, PAGE, ROW)
     page_scales = page_scales.transpose(0, 2, 1).reshape(1, 1, slot_count, PAGE, NBLK)

time: 15.8 us -> 14.8 us (0.937)
  the two profiles are of different devices: /device:TPU:21 before, /device:TPU:0 now
where the time goes in v13:
time: 14.8 us; the launch traced here: 14.6 us
  Pallas kernels  6.23 us (42%)
  starting transfers between devices  5.76 us (39%)
  waiting for transfers between devices  1.89 us (13%)
  between operations  0.67 us (5%)
    pallas_call x1, Pallas kernels, on_device(): pl.pallas_call(functools.partial(own_kernel, n_cp, count, chunks, group,...  4.88 us
    ppermute x1, starting transfers between devices, fetch(): blocks.append(lax.ppermute(own, ('cp', 'dec'), pairs))  3.08 us
    ppermute x1, starting transfers between devices, on_device(): lax.ppermute(sent_rows, 'cp', [(c, (c + n_cp - 1) % n_cp) for c in range(...  2.11 us
    ppermute x1, waiting for transfers between devices, on_device(): lax.ppermute(sent_rows, 'cp', [(c, (c + n_cp - 1) % n_cp) for c in range(...  1.19 us
    pallas_call x1, Pallas kernels, on_device(): pl.pallas_call(store_kernel, in_specs=[vmem] * len(operands), out_specs=[...  0.99 us
    ppermute x2, waiting for transfers between devices, swap(): lax.ppermute(part, 'dec', [(e, e ^ 1) for e in range(n_dec)])  0.69 us
    ppermute x2, starting transfers between devices, swap(): lax.ppermute(part, 'dec', [(e, e ^ 1) for e in range(n_dec)])  0.57 us
  transfers between devices with their start and end apart: 4, of which 3 were waited for; matrix products, arithmetic and copies ran while one was open for 0% of the time, Pallas kernels for 36%

profile of v13, /device:TPU:0, one launch (start us, length us, event | category | flops | bytes accessed | tf_op | source)
XLA Modules:
  0.0 14.6 jit_solution(12619503312221736800)
XLA Ops:
  0.6 3.1 %collective-permute-start.1 = (bf16[576,128]{1,0:T(8,128)(2,1)}, bf16[576,128]{1,0:T(8,128)(2,1)S(1)}, u32[]{:S(2)}, u32[]{:S(2)}) collective-permute-start(bf16[576,128]{1,0:T(8,128)(2,1)} %bitcast.5), channel_id=1, source_target_pairs={{0,4},{1,9},{2,6},{3,11},{4,8},{5,13},{6,10},{7,15},{8,12},{9,1},{... | collective-permute-start | bytes 442376 | tf_op jit(solution)/shard_map/ppermute | solution.py:320
  3.7 4.9 %own.1 = (bf16[2048,576]{1,0:T(8,128)(2,1)S(1)}, f32[2048,128]{1,0:T(8,128)S(1)}, f32[2048,128]{1,0:T(8,128)S(1)}, f32[2048,128]{1,0:T(8,128)S(1)}, bf16[64,640]...) custom-call(s32[2]{0:T(128)} %refs_0_.1, ...), custom_call_target="tpu_custom_call" | custom-call | flops 905969664 | bytes 5242880 | tf_op jit(solution)/shard_map/own/pallas_call | solution.py:351
  8.6 2.1 %collective-permute-start = (bf16[64,640]{1,0:T(8,128)(2,1)S(1)}, bf16[64,640]{1,0:T(8,128)(2,1)S(1)}, u32[]{:S(2)}, u32[]{:S(2)}) collective-permute-start(bf16[64,640]{1,0:T(8,128)(2,1)S(1)} %get-tuple-element.22), channel_id=1, source_target_pairs={{0,12},{4,0},{8,4},{12,8},{1,13},{5,1},{9,5},{13,9},{2,14},{6,2},{... | collective-permute-start | bytes 245768 | tf_op jit(solution)/shard_map/ppermute | solution.py:384
  10.7 0.0 collective-permute-done.1.refs_0_.refs_7_
  10.7 0.1 collective-permute-start.3
  10.8 0.5 %collective-permute-start.2 = (bf16[288,128]{1,0:T(8,128)(2,1)S(1)}, bf16[288,128]{1,0:T(8,128)(2,1)S(1)}, u32[]{:S(2)}, u32[]{:S(2)}) collective-permute-start(bf16[288,128]{1,0:T(8,128)(2,1)S(1)} %get-tuple-element.42), channel_id=1, source_target_pairs={{0,1},{1,0},{2,3},{3,2},{4,5},{5,4},{6,7},{7,6},{8,9},{9,8},{10,11... | collective-permute-start | bytes 221192 | tf_op jit(solution)/shard_map/ppermute | solution.py:328
  11.3 0.2 %arrived.1 = (f32[48,576]{1,0:T(8,128)S(1)}, bf16[128,512]{1,0:T(8,128)(2,1)S(1)}) custom-call(bf16[48,384]{1,0:T(8,128)(2,1)S(1)} %get-tuple-element.30.picked, bf16[576,128]{1,0:T(8,128)(2,1)S(1)} %get-tuple-element.31.own, bf16[576,128]{1,0:T(8,128)(2,1)S(1)} %collective-permute-done.1.refs_0_.refs_7_), custom_call_target="tpu_custom_call" | custom-call | flops 1048576 | bytes 1024 | tf_op jit(solution)/shard_map/arrived/pallas_call | solution.py:387
  11.5 0.5 %collective-permute-done.3.refs_9_.refs_1_ = bf16[288,128]{1,0:T(8,128)(2,1)S(1)} collective-permute-done((bf16[288,128]{1,0:T(8,128)(2,1)S(1)}, bf16[288,128]{1,0:T(8,128)(2,1)S(1)}, u32[]{:S(2)}, u32[]{:S(2)}) %collective-permute-start.3) | collective-permute-done | bytes 73760 | tf_op jit(solution)/shard_map/ppermute | solution.py:328
  12.1 0.2 %collective-permute-done.2.refs_8_.refs_0_ = bf16[288,128]{1,0:T(8,128)(2,1)S(1)} collective-permute-done((bf16[288,128]{1,0:T(8,128)(2,1)S(1)}, bf16[288,128]{1,0:T(8,128)(2,1)S(1)}, u32[]{:S(2)}, u32[]{:S(2)}) %collective-permute-start.2) | collective-permute-done | bytes 73760 | tf_op jit(solution)/shard_map/ppermute | solution.py:328
  12.2 0.1 %earlier.1.result = bf16[128,2048]{1,0:T(8,128)(2,1)S(1)} custom-call(bf16[2048,576]{1,0:T(8,128)(2,1)S(1)} %get-tuple-element.23.refs_0_, f32[2048,128]{1,0:T(8,128)S(1)} %get-tuple-element.24.refs_1_, f32[2048,128]{1,0:T(8,128)S(1)} %get-tuple-element.25.refs_2_, f32[2048,128]{1,0:T(8,128)S(1)} %get-tuple-element.26.refs_3_, ...), custom_call_target="tpu_custom_call" | custom-call | flops 1048576 | bytes 1024 | tf_op jit(solution)/shard_map/earlier/pallas_call | solution.py:402
  12.4 1.2 %collective-permute-done.sent_rows = bf16[64,640]{1,0:T(8,128)(2,1)S(1)} collective-permute-done((bf16[64,640]{1,0:T(8,128)(2,1)S(1)}, bf16[64,640]{1,0:T(8,128)(2,1)S(1)}, u32[]{:S(2)}, u32[]{:S(2)}) %collective-permute-start) | collective-permute-done | bytes 81952 | tf_op jit(solution)/shard_map/ppermute | solution.py:384
  13.6 1.0 %store.1 = (bf16[128,2048]{1,0:T(8,128)(2,1)}, bf16[3,16,576]{2,1,0:T(8,128)(2,1)}, bf16[3,4,16]{2,1,0:T(4,128)(2,1)}) custom-call(bf16[128,2048]{1,0:T(8,128)(2,1)S(1)} %earlier.1.result, bf16[48,384]{1,0:T(8,128)(2,1)S(1)} %get-tuple-element.30.picked, f32[48,576]{1,0:T(8,128)S(1)} %get-tuple-element.35.found, ...), custom_call_target="tpu_custom_call" | custom-call | flops 1048576 | bytes 1024 | tf_op jit(solution)/shard_map/store/pallas_call | solution.py:417
  (1 shorter events, 0.0 us)
Async XLA Ops:
  0.6 10.1 %collective-permute-start.1 = (bf16[576,128]{1,0:T(8,128)(2,1)}, bf16[576,128]{1,0:T(8,128)(2,1)S(1)}, u32[]{:S(2)}, u32[]{:S(2)}) collective-permute-start(bf16[576,128]{1,0:T(8,128)(2,1)} %bitcast.5), channel_id=1, source_target_pairs={{0,4},{1,9},{2,6},{3,11},{4,8},{5,13},{6,10},{7,15},{8,12},{9,1},{... | collective-permute-start | bytes 442376 | tf_op jit(solution)/shard_map/ppermute | solution.py:320
  8.6 5.0 %collective-permute-start = (bf16[64,640]{1,0:T(8,128)(2,1)S(1)}, bf16[64,640]{1,0:T(8,128)(2,1)S(1)}, u32[]{:S(2)}, u32[]{:S(2)}) collective-permute-start(bf16[64,640]{1,0:T(8,128)(2,1)S(1)} %get-tuple-element.22), channel_id=1, source_target_pairs={{0,12},{4,0},{8,4},{12,8},{1,13},{5,1},{9,5},{13,9},{2,14},{6,2},{... | collective-permute-start | bytes 245768 | tf_op jit(solution)/shard_map/ppermute | solution.py:384
  10.7 1.3 %collective-permute-start.3 = (bf16[288,128]{1,0:T(8,128)(2,1)S(1)}, bf16[288,128]{1,0:T(8,128)(2,1)S(1)}, u32[]{:S(2)}, u32[]{:S(2)}) collective-permute-start(bf16[288,128]{1,0:T(8,128)(2,1)S(1)} %get-tuple-element.41), channel_id=1, source_target_pairs={{0,1},{1,0},{2,3},{3,2},{4,5},{5,4},{6,7},{7,6},{8,9},{9,8},{10,11... | collective-permute-start | bytes 221192 | tf_op jit(solution)/shard_map/ppermute | solution.py:328
  10.8 1.4 %collective-permute-start.2 = (bf16[288,128]{1,0:T(8,128)(2,1)S(1)}, bf16[288,128]{1,0:T(8,128)(2,1)S(1)}, u32[]{:S(2)}, u32[]{:S(2)}) collective-permute-start(bf16[288,128]{1,0:T(8,128)(2,1)S(1)} %get-tuple-element.42), channel_id=1, source_target_pairs={{0,1},{1,0},{2,3},{3,2},{4,5},{5,4},{6,7},{7,6},{8,9},{9,8},{10,11... | collective-permute-start | bytes 221192 | tf_op jit(solution)/shard_map/ppermute | solution.py:328

commit v14 on v13

--- a/solution.py
+++ b/solution.py
@@ -232,8 +232,8 @@
 
 
 def earlier_kernel(count, group, *refs):
-    combined, own_result, peaks, totals, value_expand, bias, fetched_latents = refs[:7]
-    arrived, (result, keys, latents) = refs[7:-3], refs[-3:]
+    combined, own_result, peaks, totals, value_expand, bias, fetched_latents, picked, found = refs[:9]
+    arrived, (result, found_more, keys, latents) = refs[9:-4], refs[-4:]
     rows, width = bias.shape
     heads = value_expand.shape[0]
     steps = heads // group
@@ -268,8 +268,16 @@
             out = own_result[h * rows:(h + 1) * rows, :] * factor[part] + out * inverse[part]
             result[:, h * VDIM:(h + 1) * VDIM] = out.astype(jnp.bfloat16)
 
+    def pick_swapped():
+        total = found[...]
+        for i in range(len(arrived) // (1 + SWAP)):
+            parts = arrived[i * (1 + SWAP) + 1:(i + 1) * (1 + SWAP)]
+            total = total + pick_rows(picked, 2 + 2 * i, jnp.concatenate([part[...] for part in parts], axis=0))
+        found_more[...] = total
+
     @pl.when(lax.axis_index("cp") == 0)
     def _():
+        pick_swapped()
         for h in range(heads):
             part = slice(h * rows, (h + 1) * rows)
             result[:, h * VDIM:(h + 1) * VDIM] = (own_result[part, :] / totals[part, :]).astype(jnp.bfloat16)
@@ -288,6 +296,8 @@
         for step in range(steps + 2):
             if step < steps:
                 scores[step] = score(step)
+            if step == 1:
+                pick_swapped()
             if 0 <= step - 2:
                 finish(step - 2, mixed.pop(step - 2), *weights.pop(step - 2)[1:])
             if 0 <= step - 1 < steps:
@@ -295,20 +305,19 @@
                 mixed[step - 1] = mix(step - 1, weights[step - 1][0])
 
 
-def store_kernel(result, picked, found, sent_rows, filled, *refs):
-    swapped, (attended, page_cache, page_scales, cache_buf, scale_buf, sems) = refs[:-6], refs[-6:]
-    copies = [
-        pltpu.make_async_copy(source, target, sems.at[i])
-        for i, (source, target) in enumerate(((result, attended), (cache_buf, page_cache), (scale_buf, page_scales)))
-    ]
-    copies[0].start()
+def store_kernel(result, found, sent_rows, filled, attended, page_cache, page_scales, cache_buf, scale_buf, sems):
+    count = sems.shape[0] - 2
+    wide = result.shape[1] // count
+    copies = []
+    for i in range(count):
+        some = pl.ds(i * wide, wide)
+        copies.append(pltpu.make_async_copy(result.at[:, some], attended.at[:, some], sems.at[i]))
+        copies[-1].start()
     rows = found[...] + sent_rows[:found.shape[0], :ROW].astype(jnp.float32)
-    for i in range(len(swapped) // SWAP):
-        block = jnp.concatenate([part[...] for part in swapped[i * SWAP:(i + 1) * SWAP]], axis=0)
-        rows = rows + pick_rows(picked, 2 + 2 * i, block)
     write_cache(rows, filled, cache_buf, scale_buf)
-    for copy in copies[1:]:
-        copy.start()
+    for i, (source, target) in enumerate(((cache_buf, page_cache), (scale_buf, page_scales))):
+        copies.append(pltpu.make_async_copy(source, target, sems.at[count + i]))
+        copies[-1].start()
     for copy in copies:
         copy.wait()
 
@@ -346,7 +355,7 @@
     vmem = pl.BlockSpec(memory_space=pltpu.VMEM)
     hbm = pl.BlockSpec(memory_space=pltpu.HBM)
     params = pltpu.CompilerParams(vmem_limit_bytes=32 * 2**20)
-    group, chunks = 2, (heads // 8, heads // 8, heads // 4, heads // 2)
+    group, chunks = 4, (heads // 4, heads // 4, heads // 2)
     inputs = (prompt_pages, decode_owner, slot_offset, own, queries, key_absorb, value_expand)
     combined, result, peaks, totals, sent_rows, bias, picked, filled, own_copy, value_copy = pl.pallas_call(
         functools.partial(own_kernel, n_cp, count, chunks, group, slot_count),
@@ -397,13 +406,16 @@
         name="arrived",
     )(picked, own_copy, *blocks)
 
-    group = 4 if count <= 4 else 2
-    operands = (combined, result, peaks, totals, value_copy, bias, fetched_latents, *pieces[:count // 2 * (1 + SWAP)])
-    attended = pl.pallas_call(
+    group = 8 if count <= 4 else 2
+    operands = (combined, result, peaks, totals, value_copy, bias, fetched_latents, picked, found, *pieces)
+    attended, found = pl.pallas_call(
         functools.partial(earlier_kernel, count, group),
         in_specs=[vmem] * len(operands),
-        out_specs=vmem,
-        out_shape=jax.ShapeDtypeStruct((rows, heads * VDIM), jnp.bfloat16),
+        out_specs=[vmem] * 2,
+        out_shape=[
+            jax.ShapeDtypeStruct((rows, heads * VDIM), jnp.bfloat16),
+            jax.ShapeDtypeStruct((kept, ROW), jnp.float32),
+        ],
         scratch_shapes=[
             pltpu.VMEM((ROW, count * rows), jnp.bfloat16),
             pltpu.VMEM((count * rows, LAT), jnp.bfloat16),
@@ -413,7 +425,7 @@
         name="earlier",
     )(*operands)
     sent_rows, attended = lax.optimization_barrier((sent_rows, attended))
-    operands = (attended, picked, found, sent_rows, filled, *[part for i, part in enumerate(pieces) if i % (1 + SWAP)])
+    operands = (attended, found, sent_rows, filled)
     attended, page_cache, page_scales = pl.pallas_call(
         store_kernel,
         in_specs=[vmem] * len(operands),
@@ -426,7 +438,7 @@
         scratch_shapes=[
             pltpu.VMEM((slot_count, PAGE, ROW), jnp.bfloat16),
             pltpu.VMEM((slot_count, NBLK, PAGE), jnp.bfloat16),
-            pltpu.SemaphoreType.DMA((3,)),
+            pltpu.SemaphoreType.DMA((4 + 2,)),
         ],
         cost_estimate=pl.CostEstimate(flops=2**20, bytes_accessed=2**10, transcendentals=0),
         compiler_params=params,

time: 14.8 us -> 14.9 us (level)
  the two profiles are of different devices: /device:TPU:0 before, /device:TPU:19 now
where the time goes in v14:
time: 14.9 us; the launch traced here: 14.7 us
  Pallas kernels  8.78 us (59%)
  starting transfers between devices  4.27 us (29%)
  waiting for transfers between devices  0.97 us (7%)
  between operations  0.67 us (4%)
    pallas_call x1, Pallas kernels, on_device(): pl.pallas_call(functools.partial(own_kernel, n_cp, count, chunks, group,...  4.87 us
    pallas_call x1, Pallas kernels, on_device(): pl.pallas_call(functools.partial(earlier_kernel, count, group), in_specs=...  2.83 us
    ppermute x1, starting transfers between devices, on_device(): lax.ppermute(sent_rows, 'cp', [(c, (c + n_cp - 1) % n_cp) for c in range(...  2.47 us
    ppermute x2, starting transfers between devices, swap(): lax.ppermute(part, 'dec', [(e, e ^ 1) for e in range(n_dec)])  1.69 us
    ppermute x2, waiting for transfers between devices, swap(): lax.ppermute(part, 'dec', [(e, e ^ 1) for e in range(n_dec)])  0.97 us
    pallas_call x1, Pallas kernels, on_device(): pl.pallas_call(store_kernel, in_specs=[vmem] * len(operands), out_specs=[...  0.87 us
  transfers between devices with their start and end apart: 4, of which 2 were waited for; matrix products, arithmetic and copies ran while one was open for 0% of the time, Pallas kernels for 54%

profile of v14, /device:TPU:19, one launch (start us, length us, event | category | flops | bytes accessed | tf_op | source)
XLA Modules:
  0.0 14.7 jit_solution(9031960895706845663)
XLA Ops:
  0.6 0.1 collective-permute-start.1
  0.7 4.9 %own.1 = (bf16[2048,576]{1,0:T(8,128)(2,1)S(1)}, f32[2048,128]{1,0:T(8,128)S(1)}, f32[2048,128]{1,0:T(8,128)S(1)}, f32[2048,128]{1,0:T(8,128)S(1)}, bf16[64,640]...) custom-call(s32[2]{0:T(128)} %refs_0_.1, ...), custom_call_target="tpu_custom_call" | custom-call | flops 905969664 | bytes 5242880 | tf_op jit(solution)/shard_map/own/pallas_call | solution.py:360
  5.6 2.5 %collective-permute-start = (bf16[64,640]{1,0:T(8,128)(2,1)S(1)}, bf16[64,640]{1,0:T(8,128)(2,1)S(1)}, u32[]{:S(2)}, u32[]{:S(2)}) collective-permute-start(bf16[64,640]{1,0:T(8,128)(2,1)S(1)} %get-tuple-element.24), channel_id=1, source_target_pairs={{0,12},{4,0},{8,4},{12,8},{1,13},{5,1},{9,5},{13,9},{2,14},{6,2},{... | collective-permute-start | bytes 245768 | tf_op jit(solution)/shard_map/ppermute | solution.py:393
  8.1 0.0 collective-permute-done.1.refs_0_.refs_9_
  8.1 1.6 %collective-permute-start.3 = (bf16[288,128]{1,0:T(8,128)(2,1)S(1)}, bf16[288,128]{1,0:T(8,128)(2,1)S(1)}, u32[]{:S(2)}, u32[]{:S(2)}) collective-permute-start(bf16[288,128]{1,0:T(8,128)(2,1)S(1)} %get-tuple-element.45), channel_id=1, source_target_pairs={{0,1},{1,0},{2,3},{3,2},{4,5},{5,4},{6,7},{7,6},{8,9},{9,8},{10,11... | collective-permute-start | bytes 221192 | tf_op jit(solution)/shard_map/ppermute | solution.py:337
  9.7 0.1 collective-permute-start.2
  9.8 0.2 %arrived.1 = (f32[48,576]{1,0:T(8,128)S(1)}, bf16[128,512]{1,0:T(8,128)(2,1)S(1)}) custom-call(bf16[48,384]{1,0:T(8,128)(2,1)S(1)} %get-tuple-element.32.picked.refs_7_, bf16[576,128]{1,0:T(8,128)(2,1)S(1)} %get-tuple-element.33.own, bf16[576,128]{1,0:T(8,128)(2,1)S(1)} %collective-permute-done.1.refs_0_.refs_9_), custom_call_target="tpu_custom_call" | custom-call | flops 1048576 | bytes 1024 | tf_op jit(solution)/shard_map/arrived/pallas_call | solution.py:396
  10.0 0.6 %collective-permute-done.3.refs_11_ = bf16[288,128]{1,0:T(8,128)(2,1)S(1)} collective-permute-done((bf16[288,128]{1,0:T(8,128)(2,1)S(1)}, bf16[288,128]{1,0:T(8,128)(2,1)S(1)}, u32[]{:S(2)}, u32[]{:S(2)}) %collective-permute-start.3) | collective-permute-done | bytes 73760 | tf_op jit(solution)/shard_map/ppermute | solution.py:337
  10.6 0.4 %collective-permute-done.2.refs_10_ = bf16[288,128]{1,0:T(8,128)(2,1)S(1)} collective-permute-done((bf16[288,128]{1,0:T(8,128)(2,1)S(1)}, bf16[288,128]{1,0:T(8,128)(2,1)S(1)}, u32[]{:S(2)}, u32[]{:S(2)}) %collective-permute-start.2) | collective-permute-done | bytes 73760 | tf_op jit(solution)/shard_map/ppermute | solution.py:337
  11.0 2.8 %earlier.1 = (bf16[128,2048]{1,0:T(8,128)(2,1)S(1)}, f32[48,576]{1,0:T(8,128)S(1)}) custom-call(bf16[2048,576]{1,0:T(8,128)(2,1)S(1)} %get-tuple-element.25.refs_0_, f32[2048,128]{1,0:T(8,128)S(1)} %get-tuple-element.26.refs_1_, f32[2048,128]{1,0:T(8,128)S(1)} %get-tuple-element.27.refs_2_, f32[2048,128]{1,0:T(8,128)S(1)} %get-tuple-element.28.refs_3_, ...), custom_call_target="tpu_custom_call" | custom-call | flops 1048576 | bytes 1024 | tf_op jit(solution)/shard_map/earlier/pallas_call | solution.py:411
  13.8 0.0 collective-permute-done.sent_rows
  13.8 0.9 %store.1 = (bf16[128,2048]{1,0:T(8,128)(2,1)}, bf16[3,16,576]{2,1,0:T(8,128)(2,1)}, bf16[3,4,16]{2,1,0:T(4,128)(2,1)}) custom-call(bf16[128,2048]{1,0:T(8,128)(2,1)S(1)} %get-tuple-element.38.result, f32[48,576]{1,0:T(8,128)S(1)} %get-tuple-element.39.found, bf16[64,640]{1,0:T(8,128)(2,1)S(1)} %collective-permute-done.sent_rows, ...), custom_call_target="tpu_custom_call" | custom-call | flops 1048576 | bytes 1024 | tf_op jit(solution)/shard_map/store/pallas_call | solution.py:429
  (1 shorter events, 0.0 us)
Async XLA Ops:
  0.6 7.5 %collective-permute-start.1 = (bf16[576,128]{1,0:T(8,128)(2,1)}, bf16[576,128]{1,0:T(8,128)(2,1)S(1)}, u32[]{:S(2)}, u32[]{:S(2)}) collective-permute-start(bf16[576,128]{1,0:T(8,128)(2,1)} %bitcast.5), channel_id=1, source_target_pairs={{0,4},{1,9},{2,6},{3,11},{4,8},{5,13},{6,10},{7,15},{8,12},{9,1},{... | collective-permute-start | bytes 442376 | tf_op jit(solution)/shard_map/ppermute | solution.py:329
  5.6 8.2 %collective-permute-start = (bf16[64,640]{1,0:T(8,128)(2,1)S(1)}, bf16[64,640]{1,0:T(8,128)(2,1)S(1)}, u32[]{:S(2)}, u32[]{:S(2)}) collective-permute-start(bf16[64,640]{1,0:T(8,128)(2,1)S(1)} %get-tuple-element.24), channel_id=1, source_target_pairs={{0,12},{4,0},{8,4},{12,8},{1,13},{5,1},{9,5},{13,9},{2,14},{6,2},{... | collective-permute-start | bytes 245768 | tf_op jit(solution)/shard_map/ppermute | solution.py:393
  8.1 2.5 %collective-permute-start.3 = (bf16[288,128]{1,0:T(8,128)(2,1)S(1)}, bf16[288,128]{1,0:T(8,128)(2,1)S(1)}, u32[]{:S(2)}, u32[]{:S(2)}) collective-permute-start(bf16[288,128]{1,0:T(8,128)(2,1)S(1)} %get-tuple-element.45), channel_id=1, source_target_pairs={{0,1},{1,0},{2,3},{3,2},{4,5},{5,4},{6,7},{7,6},{8,9},{9,8},{10,11... | collective-permute-start | bytes 221192 | tf_op jit(solution)/shard_map/ppermute | solution.py:337
  9.7 1.3 %collective-permute-start.2 = (bf16[288,128]{1,0:T(8,128)(2,1)S(1)}, bf16[288,128]{1,0:T(8,128)(2,1)S(1)}, u32[]{:S(2)}, u32[]{:S(2)}) collective-permute-start(bf16[288,128]{1,0:T(8,128)(2,1)S(1)} %get-tuple-element.46), channel_id=1, source_target_pairs={{0,1},{1,0},{2,3},{3,2},{4,5},{5,4},{6,7},{7,6},{8,9},{9,8},{10,11... | collective-permute-start | bytes 221192 | tf_op jit(solution)/shard_map/ppermute | solution.py:337

commit v15 on v14

--- a/solution.py
+++ b/solution.py
@@ -148,18 +148,15 @@
         peaks[span, :] = jnp.broadcast_to(peak, (group * rows, LANES))
         totals[span, :] = jnp.broadcast_to(total, (group * rows, LANES))
 
+    for copy in small:
+        copy.wait()
+    latents[...] = own[:LAT, :].T
+    own_bias = visible_bias(prompt_pages, rows, 0)
+    index_work(n_cp, count, slot_count, prompt_pages, decode_owner, slot_offset, own[...], sent_rows, bias, picked, filled)
     scores, both = {}, {}
     for step in range(steps + 2):
         if step < steps:
             absorb(step)
-        if step == 0:
-            small[3].wait()
-            latents[...] = own[:LAT, :].T
-        if step == 1:
-            for copy in small[:3]:
-                copy.wait()
-            own_bias = visible_bias(prompt_pages, rows, 0)
-            index_work(n_cp, count, slot_count, prompt_pages, decode_owner, slot_offset, own[...], sent_rows, bias, picked, filled)
         if 0 <= step - 1 < steps:
             scores[step - 1] = score(step - 1)
             both[step - 1] = value(step - 1)
@@ -406,7 +403,7 @@
         name="arrived",
     )(picked, own_copy, *blocks)
 
-    group = 8 if count <= 4 else 2
+    group = 4 if count <= 4 else 2
     operands = (combined, result, peaks, totals, value_copy, bias, fetched_latents, picked, found, *pieces)
     attended, found = pl.pallas_call(
         functools.partial(earlier_kernel, count, group),

time: 14.9 us -> 14.8 us (level)
  Pallas kernels: 8.78 us -> 8.44 us
  starting transfers between devices: 4.27 us -> 4.55 us
    pallas_call x1, Pallas kernels: 4.87 us -> 4.59 us  [on_device(): pl.pallas_call(functools.partial(own_kernel, n_cp, count, chunks, group,...]
    ppermute x2, starting transfers between devices: 1.69 us -> 1.97 us  [swap(): lax.ppermute(part, 'dec', [(e, e ^ 1) for e in range(n_dec)])]
  transfers between devices with their start and end apart: 4 -> 4, of which waited for: 2 -> 2; matrix products, arithmetic and copies ran while one was open for 0% -> 0% of each run, Pallas kernels for 54% -> 52%
where the time goes in v15:
time: 14.8 us; the launch traced here: 14.6 us
  Pallas kernels  8.44 us (57%)
  starting transfers between devices  4.55 us (31%)
  waiting for transfers between devices  0.97 us (7%)
  between operations  0.67 us (5%)
    pallas_call x1, Pallas kernels, on_device(): pl.pallas_call(functools.partial(own_kernel, n_cp, count, chunks, group,...  4.59 us
    pallas_call x1, Pallas kernels, on_device(): pl.pallas_call(functools.partial(earlier_kernel, count, group), in_specs=...  2.77 us
    ppermute x1, starting transfers between devices, on_device(): lax.ppermute(sent_rows, 'cp', [(c, (c + n_cp - 1) % n_cp) for c in range(...  2.47 us
    ppermute x2, starting transfers between devices, swap(): lax.ppermute(part, 'dec', [(e, e ^ 1) for e in range(n_dec)])  1.97 us
    ppermute x2, waiting for transfers between devices, swap(): lax.ppermute(part, 'dec', [(e, e ^ 1) for e in range(n_dec)])  0.97 us
    pallas_call x1, Pallas kernels, on_device(): pl.pallas_call(store_kernel, in_specs=[vmem] * len(operands), out_specs=[...  0.87 us
  transfers between devices with their start and end apart: 4, of which 2 were waited for; matrix products, arithmetic and copies ran while one was open for 0% of the time, Pallas kernels for 52%

profile of v15, /device:TPU:19, one launch (start us, length us, event | category | flops | bytes accessed | tf_op | source)
XLA Modules:
  0.0 14.6 jit_solution(14996034342127083237)
XLA Ops:
  0.6 0.1 collective-permute-start.1
  0.7 4.6 %own.1 = (bf16[2048,576]{1,0:T(8,128)(2,1)S(1)}, f32[2048,128]{1,0:T(8,128)S(1)}, f32[2048,128]{1,0:T(8,128)S(1)}, f32[2048,128]{1,0:T(8,128)S(1)}, bf16[64,640]...) custom-call(s32[2]{0:T(128)} %refs_0_.1, ...), custom_call_target="tpu_custom_call" | custom-call | flops 905969664 | bytes 5242880 | tf_op jit(solution)/shard_map/own/pallas_call | solution.py:357
  5.3 2.5 %collective-permute-start = (bf16[64,640]{1,0:T(8,128)(2,1)S(1)}, bf16[64,640]{1,0:T(8,128)(2,1)S(1)}, u32[]{:S(2)}, u32[]{:S(2)}) collective-permute-start(bf16[64,640]{1,0:T(8,128)(2,1)S(1)} %get-tuple-element.24), channel_id=1, source_target_pairs={{0,12},{4,0},{8,4},{12,8},{1,13},{5,1},{9,5},{13,9},{2,14},{6,2},{... | collective-permute-start | bytes 245768 | tf_op jit(solution)/shard_map/ppermute | solution.py:390
  7.8 0.0 collective-permute-done.1.refs_0_.refs_9_
  7.8 1.9 %collective-permute-start.3 = (bf16[288,128]{1,0:T(8,128)(2,1)S(1)}, bf16[288,128]{1,0:T(8,128)(2,1)S(1)}, u32[]{:S(2)}, u32[]{:S(2)}) collective-permute-start(bf16[288,128]{1,0:T(8,128)(2,1)S(1)} %get-tuple-element.45), channel_id=1, source_target_pairs={{0,1},{1,0},{2,3},{3,2},{4,5},{5,4},{6,7},{7,6},{8,9},{9,8},{10,11... | collective-permute-start | bytes 221192 | tf_op jit(solution)/shard_map/ppermute | solution.py:334
  9.7 0.1 collective-permute-start.2
  9.8 0.2 %arrived.1 = (f32[48,576]{1,0:T(8,128)S(1)}, bf16[128,512]{1,0:T(8,128)(2,1)S(1)}) custom-call(bf16[48,384]{1,0:T(8,128)(2,1)S(1)} %get-tuple-element.32.picked.refs_7_, bf16[576,128]{1,0:T(8,128)(2,1)S(1)} %get-tuple-element.33.own, bf16[576,128]{1,0:T(8,128)(2,1)S(1)} %collective-permute-done.1.refs_0_.refs_9_), custom_call_target="tpu_custom_call" | custom-call | flops 1048576 | bytes 1024 | tf_op jit(solution)/shard_map/arrived/pallas_call | solution.py:393
  10.0 0.6 %collective-permute-done.3.refs_11_ = bf16[288,128]{1,0:T(8,128)(2,1)S(1)} collective-permute-done((bf16[288,128]{1,0:T(8,128)(2,1)S(1)}, bf16[288,128]{1,0:T(8,128)(2,1)S(1)}, u32[]{:S(2)}, u32[]{:S(2)}) %collective-permute-start.3) | collective-permute-done | bytes 73760 | tf_op jit(solution)/shard_map/ppermute | solution.py:334
  10.6 0.4 %collective-permute-done.2.refs_10_ = bf16[288,128]{1,0:T(8,128)(2,1)S(1)} collective-permute-done((bf16[288,128]{1,0:T(8,128)(2,1)S(1)}, bf16[288,128]{1,0:T(8,128)(2,1)S(1)}, u32[]{:S(2)}, u32[]{:S(2)}) %collective-permute-start.2) | collective-permute-done | bytes 73760 | tf_op jit(solution)/shard_map/ppermute | solution.py:334
  11.0 2.8 %earlier.1 = (bf16[128,2048]{1,0:T(8,128)(2,1)S(1)}, f32[48,576]{1,0:T(8,128)S(1)}) custom-call(bf16[2048,576]{1,0:T(8,128)(2,1)S(1)} %get-tuple-element.25.refs_0_, f32[2048,128]{1,0:T(8,128)S(1)} %get-tuple-element.26.refs_1_, f32[2048,128]{1,0:T(8,128)S(1)} %get-tuple-element.27.refs_2_, f32[2048,128]{1,0:T(8,128)S(1)} %get-tuple-element.28.refs_3_, ...), custom_call_target="tpu_custom_call" | custom-call | flops 1048576 | bytes 1024 | tf_op jit(solution)/shard_map/earlier/pallas_call | solution.py:408
  13.8 0.0 collective-permute-done.sent_rows
  13.8 0.9 %store.1 = (bf16[128,2048]{1,0:T(8,128)(2,1)}, bf16[3,16,576]{2,1,0:T(8,128)(2,1)}, bf16[3,4,16]{2,1,0:T(4,128)(2,1)}) custom-call(bf16[128,2048]{1,0:T(8,128)(2,1)S(1)} %get-tuple-element.38.result, f32[48,576]{1,0:T(8,128)S(1)} %get-tuple-element.39.found, bf16[64,640]{1,0:T(8,128)(2,1)S(1)} %collective-permute-done.sent_rows, ...), custom_call_target="tpu_custom_call" | custom-call | flops 1048576 | bytes 1024 | tf_op jit(solution)/shard_map/store/pallas_call | solution.py:426
  (1 shorter events, 0.0 us)
Async XLA Ops:
  0.6 7.2 %collective-permute-start.1 = (bf16[576,128]{1,0:T(8,128)(2,1)}, bf16[576,128]{1,0:T(8,128)(2,1)S(1)}, u32[]{:S(2)}, u32[]{:S(2)}) collective-permute-start(bf16[576,128]{1,0:T(8,128)(2,1)} %bitcast.5), channel_id=1, source_target_pairs={{0,4},{1,9},{2,6},{3,11},{4,8},{5,13},{6,10},{7,15},{8,12},{9,1},{... | collective-permute-start | bytes 442376 | tf_op jit(solution)/shard_map/ppermute | solution.py:326
  5.3 8.4 %collective-permute-start = (bf16[64,640]{1,0:T(8,128)(2,1)S(1)}, bf16[64,640]{1,0:T(8,128)(2,1)S(1)}, u32[]{:S(2)}, u32[]{:S(2)}) collective-permute-start(bf16[64,640]{1,0:T(8,128)(2,1)S(1)} %get-tuple-element.24), channel_id=1, source_target_pairs={{0,12},{4,0},{8,4},{12,8},{1,13},{5,1},{9,5},{13,9},{2,14},{6,2},{... | collective-permute-start | bytes 245768 | tf_op jit(solution)/shard_map/ppermute | solution.py:390
  7.8 2.8 %collective-permute-start.3 = (bf16[288,128]{1,0:T(8,128)(2,1)S(1)}, bf16[288,128]{1,0:T(8,128)(2,1)S(1)}, u32[]{:S(2)}, u32[]{:S(2)}) collective-permute-start(bf16[288,128]{1,0:T(8,128)(2,1)S(1)} %get-tuple-element.45), channel_id=1, source_target_pairs={{0,1},{1,0},{2,3},{3,2},{4,5},{5,4},{6,7},{7,6},{8,9},{9,8},{10,11... | collective-permute-start | bytes 221192 | tf_op jit(solution)/shard_map/ppermute | solution.py:334
  9.7 1.3 %collective-permute-start.2 = (bf16[288,128]{1,0:T(8,128)(2,1)S(1)}, bf16[288,128]{1,0:T(8,128)(2,1)S(1)}, u32[]{:S(2)}, u32[]{:S(2)}) collective-permute-start(bf16[288,128]{1,0:T(8,128)(2,1)S(1)} %get-tuple-element.46), channel_id=1, source_target_pairs={{0,1},{1,0},{2,3},{3,2},{4,5},{5,4},{6,7},{7,6},{8,9},{9,8},{10,11... | collective-permute-start | bytes 221192 | tf_op jit(solution)/shard_map/ppermute | solution.py:334

commit v16 on v15

--- a/solution.py
+++ b/solution.py
@@ -196,13 +196,16 @@
     return lax.dot_general(picked[:, index * rows:(index + 1) * rows], block, NT, preferred_element_type=jnp.float32)
 
 
-def arrived_kernel(picked, own, *refs):
-    blocks, (found, latents) = refs[:-2], refs[-2:]
+def arrived_kernel(used, picked, own, value_expand, *refs):
+    blocks, (found, values) = refs[:-2], refs[-2:]
     rows = own.shape[1]
+    for i in range(used):
+        latents = blocks[i][:LAT, :].T
+        for h in range(0, value_expand.shape[0], 2):
+            values[i * rows:(i + 1) * rows, h * VDIM:(h + 2) * VDIM] = head_values(latents, value_expand, h)
     total = pick_rows(picked, 0, own[...])
     for i, block in enumerate(blocks):
         total = total + pick_rows(picked, 1 + 2 * i, block[...])
-        latents[i * rows:(i + 1) * rows, :] = block[:LAT, :].T
     found[...] = total
 
 
@@ -229,8 +232,8 @@
 
 
 def earlier_kernel(count, group, *refs):
-    combined, own_result, peaks, totals, value_expand, bias, fetched_latents, picked, found = refs[:9]
-    arrived, (result, found_more, keys, latents) = refs[9:-4], refs[-4:]
+    combined, own_result, peaks, totals, value_expand, bias, fetched_values = refs[:7]
+    arrived, (result, keys, latents) = refs[7:-3], refs[-3:]
     rows, width = bias.shape
     heads = value_expand.shape[0]
     steps = heads // group
@@ -254,27 +257,26 @@
         weights = jnp.concatenate([part.astype(jnp.bfloat16) for part in parts], axis=1)
         return weights, factor * inverse, inverse
 
-    def mix(g, weights):
-        return jnp.dot(weights, latents[...], preferred_element_type=jnp.float32).astype(jnp.bfloat16)
-
-    def finish(g, mixed, factor, inverse):
+    def value(g):
+        return [
+            [head_values(latents[i * rows:(i + 1) * rows, :], value_expand, h) for h in range(g * group, (g + 1) * group, 2)]
+            for i in range(count // 2)
+        ]
+
+    def finish(g, weights, factor, inverse, swapped):
         for i in range(group):
             part = slice(i * rows, (i + 1) * rows)
             h = g * group + i
-            out = jnp.dot(mixed[part], value_expand[h], preferred_element_type=jnp.float32)
+            values = []
+            for b in range(count // 2):
+                values.append(fetched_values[b * rows:(b + 1) * rows, h * VDIM:(h + 1) * VDIM])
+                values.append(swapped[b][i // 2][:, i % 2 * VDIM:(i % 2 + 1) * VDIM])
+            out = jnp.dot(weights[part], jnp.concatenate(values, axis=0), preferred_element_type=jnp.float32)
             out = own_result[h * rows:(h + 1) * rows, :] * factor[part] + out * inverse[part]
             result[:, h * VDIM:(h + 1) * VDIM] = out.astype(jnp.bfloat16)
 
-    def pick_swapped():
-        total = found[...]
-        for i in range(len(arrived) // (1 + SWAP)):
-            parts = arrived[i * (1 + SWAP) + 1:(i + 1) * (1 + SWAP)]
-            total = total + pick_rows(picked, 2 + 2 * i, jnp.concatenate([part[...] for part in parts], axis=0))
-        found_more[...] = total
-
     @pl.when(lax.axis_index("cp") == 0)
     def _():
-        pick_swapped()
         for h in range(heads):
             part = slice(h * rows, (h + 1) * rows)
             result[:, h * VDIM:(h + 1) * VDIM] = (own_result[part, :] / totals[part, :]).astype(jnp.bfloat16)
@@ -287,22 +289,20 @@
             at = 2 * i * rows
             keys[:, at:at + rows] = fetched[...]
             keys[:, at + rows:at + 2 * rows] = swapped
-            latents[at:at + rows, :] = fetched_latents[i * rows:(i + 1) * rows, :]
-            latents[at + rows:at + 2 * rows, :] = swapped[:LAT].T
-        scores, weights, mixed = {}, {}, {}
+            latents[i * rows:(i + 1) * rows, :] = swapped[:LAT].T
+        scores, values, weights = {}, {}, {}
         for step in range(steps + 2):
             if step < steps:
                 scores[step] = score(step)
-            if step == 1:
-                pick_swapped()
             if 0 <= step - 2:
-                finish(step - 2, mixed.pop(step - 2), *weights.pop(step - 2)[1:])
+                finish(step - 2, *weights.pop(step - 2), values.pop(step - 2))
             if 0 <= step - 1 < steps:
+                values[step - 1] = value(step - 1)
                 weights[step - 1] = weigh(step - 1, scores.pop(step - 1))
-                mixed[step - 1] = mix(step - 1, weights[step - 1][0])
-
-
-def store_kernel(result, found, sent_rows, filled, attended, page_cache, page_scales, cache_buf, scale_buf, sems):
+
+
+def store_kernel(result, picked, found, sent_rows, filled, *refs):
+    swapped, (attended, page_cache, page_scales, cache_buf, scale_buf, sems) = refs[:-6], refs[-6:]
     count = sems.shape[0] - 2
     wide = result.shape[1] // count
     copies = []
@@ -311,6 +311,9 @@
         copies.append(pltpu.make_async_copy(result.at[:, some], attended.at[:, some], sems.at[i]))
         copies[-1].start()
     rows = found[...] + sent_rows[:found.shape[0], :ROW].astype(jnp.float32)
+    for i in range(len(swapped) // SWAP):
+        block = jnp.concatenate([part[...] for part in swapped[i * SWAP:(i + 1) * SWAP]], axis=0)
+        rows = rows + pick_rows(picked, 2 + 2 * i, block)
     write_cache(rows, filled, cache_buf, scale_buf)
     for i, (source, target) in enumerate(((cache_buf, page_cache), (scale_buf, page_scales))):
         copies.append(pltpu.make_async_copy(source, target, sems.at[count + i]))
@@ -390,39 +393,36 @@
     sent_rows = lax.ppermute(sent_rows, "cp", [(c, (c + n_cp - 1) % n_cp) for c in range(n_cp)])
     blocks, picked = lax.optimization_barrier((blocks, picked))
     pieces = swap(blocks, dec_count)
-    found, fetched_latents = pl.pallas_call(
-        arrived_kernel,
-        in_specs=[vmem] * (2 + len(blocks)),
+    found, fetched_values = pl.pallas_call(
+        functools.partial(arrived_kernel, count // 2),
+        in_specs=[vmem] * (3 + len(blocks)),
         out_specs=[vmem] * 2,
         out_shape=[
             jax.ShapeDtypeStruct((kept, ROW), jnp.float32),
-            jax.ShapeDtypeStruct((len(blocks) * rows, LAT), jnp.bfloat16),
+            jax.ShapeDtypeStruct((count // 2 * rows, heads * VDIM), jnp.bfloat16),
         ],
         cost_estimate=pl.CostEstimate(flops=2**20, bytes_accessed=2**10, transcendentals=0),
         compiler_params=params,
         name="arrived",
-    )(picked, own_copy, *blocks)
+    )(picked, own_copy, value_copy, *blocks)
 
     group = 4 if count <= 4 else 2
-    operands = (combined, result, peaks, totals, value_copy, bias, fetched_latents, picked, found, *pieces)
-    attended, found = pl.pallas_call(
+    operands = (combined, result, peaks, totals, value_copy, bias, fetched_values, *pieces[:count // 2 * (1 + SWAP)])
+    attended = pl.pallas_call(
         functools.partial(earlier_kernel, count, group),
         in_specs=[vmem] * len(operands),
-        out_specs=[vmem] * 2,
-        out_shape=[
-            jax.ShapeDtypeStruct((rows, heads * VDIM), jnp.bfloat16),
-            jax.ShapeDtypeStruct((kept, ROW), jnp.float32),
-        ],
+        out_specs=vmem,
+        out_shape=jax.ShapeDtypeStruct((rows, heads * VDIM), jnp.bfloat16),
         scratch_shapes=[
             pltpu.VMEM((ROW, count * rows), jnp.bfloat16),
-            pltpu.VMEM((count * rows, LAT), jnp.bfloat16),
+            pltpu.VMEM((count // 2 * rows, LAT), jnp.bfloat16),
         ],
         cost_estimate=pl.CostEstimate(flops=2**20, bytes_accessed=2**10, transcendentals=0),
         compiler_params=params,
         name="earlier",
     )(*operands)
     sent_rows, attended = lax.optimization_barrier((sent_rows, attended))
-    operands = (attended, found, sent_rows, filled)
+    operands = (attended, picked, found, sent_rows, filled, *[part for i, part in enumerate(pieces) if i % (1 + SWAP)])
     attended, page_cache, page_scales = pl.pallas_call(
         store_kernel,
         in_specs=[vmem] * len(operands),

time: 14.8 us -> 14.4 us (0.973)
  the two profiles are of different devices: /device:TPU:19 before, /device:TPU:0 now
where the time goes in v16:
time: 14.4 us; the launch traced here: 14.3 us
  Pallas kernels  6.25 us (43%)
  starting transfers between devices  5.74 us (40%)
  waiting for transfers between devices  1.59 us (11%)
  between operations  0.67 us (5%)
    pallas_call x1, Pallas kernels, on_device(): pl.pallas_call(functools.partial(own_kernel, n_cp, count, chunks, group,...  4.55 us
    ppermute x1, starting transfers between devices, fetch(): blocks.append(lax.ppermute(own, ('cp', 'dec'), pairs))  3.08 us
    ppermute x1, starting transfers between devices, on_device(): lax.ppermute(sent_rows, 'cp', [(c, (c + n_cp - 1) % n_cp) for c in range(...  2.1 us
    ppermute x1, waiting for transfers between devices, on_device(): lax.ppermute(sent_rows, 'cp', [(c, (c + n_cp - 1) % n_cp) for c in range(...  1.21 us
    pallas_call x1, Pallas kernels, on_device(): pl.pallas_call(store_kernel, in_specs=[vmem] * len(operands), out_specs=[...  1.02 us
    ppermute x2, starting transfers between devices, swap(): lax.ppermute(part, 'dec', [(e, e ^ 1) for e in range(n_dec)])  0.57 us
    pallas_call x1, Pallas kernels, on_device(): pl.pallas_call(functools.partial(arrived_kernel, count // 2), in_specs=[v...  0.53 us
    ppermute x2, waiting for transfers between devices, swap(): lax.ppermute(part, 'dec', [(e, e ^ 1) for e in range(n_dec)])  0.37 us
  transfers between devices with their start and end apart: 4, of which 3 were waited for; matrix products, arithmetic and copies ran while one was open for 0% of the time, Pallas kernels for 37%

profile of v16, /device:TPU:0, one launch (start us, length us, event | category | flops | bytes accessed | tf_op | source)
XLA Modules:
  0.0 14.3 jit_solution(4181756494221069910)
XLA Ops:
  0.6 3.1 %collective-permute-start.1 = (bf16[576,128]{1,0:T(8,128)(2,1)}, bf16[576,128]{1,0:T(8,128)(2,1)S(1)}, u32[]{:S(2)}, u32[]{:S(2)}) collective-permute-start(bf16[576,128]{1,0:T(8,128)(2,1)} %bitcast.5), channel_id=1, source_target_pairs={{0,4},{1,9},{2,6},{3,11},{4,8},{5,13},{6,10},{7,15},{8,12},{9,1},{... | collective-permute-start | bytes 442376 | tf_op jit(solution)/shard_map/ppermute | solution.py:329
  3.7 4.5 %own.1 = (bf16[2048,576]{1,0:T(8,128)(2,1)S(1)}, f32[2048,128]{1,0:T(8,128)S(1)}, f32[2048,128]{1,0:T(8,128)S(1)}, f32[2048,128]{1,0:T(8,128)S(1)}, bf16[64,640]...) custom-call(s32[2]{0:T(128)} %refs_0_.1, ...), custom_call_target="tpu_custom_call" | custom-call | flops 905969664 | bytes 5242880 | tf_op jit(solution)/shard_map/own/pallas_call | solution.py:360
  8.3 2.1 %collective-permute-start = (bf16[64,640]{1,0:T(8,128)(2,1)S(1)}, bf16[64,640]{1,0:T(8,128)(2,1)S(1)}, u32[]{:S(2)}, u32[]{:S(2)}) collective-permute-start(bf16[64,640]{1,0:T(8,128)(2,1)S(1)} %get-tuple-element.22), channel_id=1, source_target_pairs={{0,12},{4,0},{8,4},{12,8},{1,13},{5,1},{9,5},{13,9},{2,14},{6,2},{... | collective-permute-start | bytes 245768 | tf_op jit(solution)/shard_map/ppermute | solution.py:393
  10.4 0.0 collective-permute-done.1.refs_0_.refs_7_
  10.4 0.1 collective-permute-start.3
  10.5 0.5 %collective-permute-start.2 = (bf16[288,128]{1,0:T(8,128)(2,1)S(1)}, bf16[288,128]{1,0:T(8,128)(2,1)S(1)}, u32[]{:S(2)}, u32[]{:S(2)}) collective-permute-start(bf16[288,128]{1,0:T(8,128)(2,1)S(1)} %get-tuple-element.42), channel_id=1, source_target_pairs={{0,1},{1,0},{2,3},{3,2},{4,5},{5,4},{6,7},{7,6},{8,9},{9,8},{10,11... | collective-permute-start | bytes 221192 | tf_op jit(solution)/shard_map/ppermute | solution.py:337
  11.0 0.5 %arrived.1 = (f32[48,576]{1,0:T(8,128)S(1)}, bf16[128,2048]{1,0:T(8,128)(2,1)S(1)}) custom-call(bf16[48,384]{1,0:T(8,128)(2,1)S(1)} %get-tuple-element.30.picked, bf16[576,128]{1,0:T(8,128)(2,1)S(1)} %get-tuple-element.31.own, bf16[16,512,128]{2,1,0:T(8,128)(2,1)S(1)} %get-tuple-element.27.value_expand.refs_4_, ...), custom_call_target="tpu_custom_call" | custom-call | flops 1048576 | bytes 1024 | tf_op jit(solution)/shard_map/arrived/pallas_call | solution.py:396
  11.5 0.2 %collective-permute-done.3.refs_9_.refs_1_ = bf16[288,128]{1,0:T(8,128)(2,1)S(1)} collective-permute-done((bf16[288,128]{1,0:T(8,128)(2,1)S(1)}, bf16[288,128]{1,0:T(8,128)(2,1)S(1)}, u32[]{:S(2)}, u32[]{:S(2)}) %collective-permute-start.3) | collective-permute-done | bytes 73760 | tf_op jit(solution)/shard_map/ppermute | solution.py:337
  11.7 0.2 %collective-permute-done.2.refs_8_.refs_0_ = bf16[288,128]{1,0:T(8,128)(2,1)S(1)} collective-permute-done((bf16[288,128]{1,0:T(8,128)(2,1)S(1)}, bf16[288,128]{1,0:T(8,128)(2,1)S(1)}, u32[]{:S(2)}, u32[]{:S(2)}) %collective-permute-start.2) | collective-permute-done | bytes 73760 | tf_op jit(solution)/shard_map/ppermute | solution.py:337
  11.9 0.1 %earlier.1.result = bf16[128,2048]{1,0:T(8,128)(2,1)S(1)} custom-call(bf16[2048,576]{1,0:T(8,128)(2,1)S(1)} %get-tuple-element.23.refs_0_, f32[2048,128]{1,0:T(8,128)S(1)} %get-tuple-element.24.refs_1_, f32[2048,128]{1,0:T(8,128)S(1)} %get-tuple-element.25.refs_2_, f32[2048,128]{1,0:T(8,128)S(1)} %get-tuple-element.26.refs_3_, ...), custom_call_target="tpu_custom_call" | custom-call | flops 1048576 | bytes 1024 | tf_op jit(solution)/shard_map/earlier/pallas_call | solution.py:411
  12.0 1.2 %collective-permute-done.sent_rows = bf16[64,640]{1,0:T(8,128)(2,1)S(1)} collective-permute-done((bf16[64,640]{1,0:T(8,128)(2,1)S(1)}, bf16[64,640]{1,0:T(8,128)(2,1)S(1)}, u32[]{:S(2)}, u32[]{:S(2)}) %collective-permute-start) | collective-permute-done | bytes 81952 | tf_op jit(solution)/shard_map/ppermute | solution.py:393
  13.2 1.0 %store.1 = (bf16[128,2048]{1,0:T(8,128)(2,1)}, bf16[3,16,576]{2,1,0:T(8,128)(2,1)}, bf16[3,4,16]{2,1,0:T(4,128)(2,1)}) custom-call(bf16[128,2048]{1,0:T(8,128)(2,1)S(1)} %earlier.1.result, bf16[48,384]{1,0:T(8,128)(2,1)S(1)} %get-tuple-element.30.picked, f32[48,576]{1,0:T(8,128)S(1)} %get-tuple-element.35.found, ...), custom_call_target="tpu_custom_call" | custom-call | flops 1048576 | bytes 1024 | tf_op jit(solution)/shard_map/store/pallas_call | solution.py:426
  (1 shorter events, 0.0 us)
Async XLA Ops:
  0.6 9.7 %collective-permute-start.1 = (bf16[576,128]{1,0:T(8,128)(2,1)}, bf16[576,128]{1,0:T(8,128)(2,1)S(1)}, u32[]{:S(2)}, u32[]{:S(2)}) collective-permute-start(bf16[576,128]{1,0:T(8,128)(2,1)} %bitcast.5), channel_id=1, source_target_pairs={{0,4},{1,9},{2,6},{3,11},{4,8},{5,13},{6,10},{7,15},{8,12},{9,1},{... | collective-permute-start | bytes 442376 | tf_op jit(solution)/shard_map/ppermute | solution.py:329
  8.3 5.0 %collective-permute-start = (bf16[64,640]{1,0:T(8,128)(2,1)S(1)}, bf16[64,640]{1,0:T(8,128)(2,1)S(1)}, u32[]{:S(2)}, u32[]{:S(2)}) collective-permute-start(bf16[64,640]{1,0:T(8,128)(2,1)S(1)} %get-tuple-element.22), channel_id=1, source_target_pairs={{0,12},{4,0},{8,4},{12,8},{1,13},{5,1},{9,5},{13,9},{2,14},{6,2},{... | collective-permute-start | bytes 245768 | tf_op jit(solution)/shard_map/ppermute | solution.py:393
  10.4 1.3 %collective-permute-start.3 = (bf16[288,128]{1,0:T(8,128)(2,1)S(1)}, bf16[288,128]{1,0:T(8,128)(2,1)S(1)}, u32[]{:S(2)}, u32[]{:S(2)}) collective-permute-start(bf16[288,128]{1,0:T(8,128)(2,1)S(1)} %get-tuple-element.41), channel_id=1, source_target_pairs={{0,1},{1,0},{2,3},{3,2},{4,5},{5,4},{6,7},{7,6},{8,9},{9,8},{10,11... | collective-permute-start | bytes 221192 | tf_op jit(solution)/shard_map/ppermute | solution.py:337
  10.5 1.4 %collective-permute-start.2 = (bf16[288,128]{1,0:T(8,128)(2,1)S(1)}, bf16[288,128]{1,0:T(8,128)(2,1)S(1)}, u32[]{:S(2)}, u32[]{:S(2)}) collective-permute-start(bf16[288,128]{1,0:T(8,128)(2,1)S(1)} %get-tuple-element.42), channel_id=1, source_target_pairs={{0,1},{1,0},{2,3},{3,2},{4,5},{5,4},{6,7},{7,6},{8,9},{9,8},{10,11... | collective-permute-start | bytes 221192 | tf_op jit(solution)/shard_map/ppermute | solution.py:337

commit v17 on v16

--- a/solution.py
+++ b/solution.py
@@ -232,8 +232,8 @@
 
 
 def earlier_kernel(count, group, *refs):
-    combined, own_result, peaks, totals, value_expand, bias, fetched_values = refs[:7]
-    arrived, (result, keys, latents) = refs[7:-3], refs[-3:]
+    combined, own_result, peaks, totals, value_expand, bias, fetched_values, picked, found = refs[:9]
+    arrived, (attended, last, found_more, keys, latents, result, sems) = refs[9:-7], refs[-7:]
     rows, width = bias.shape
     heads = value_expand.shape[0]
     steps = heads // group
@@ -273,51 +273,80 @@
                 values.append(swapped[b][i // 2][:, i % 2 * VDIM:(i % 2 + 1) * VDIM])
             out = jnp.dot(weights[part], jnp.concatenate(values, axis=0), preferred_element_type=jnp.float32)
             out = own_result[h * rows:(h + 1) * rows, :] * factor[part] + out * inverse[part]
-            result[:, h * VDIM:(h + 1) * VDIM] = out.astype(jnp.bfloat16)
+            place(h, out)
+
+    def swapped_block(i):
+        return jnp.concatenate([part[...] for part in arrived[i * (1 + SWAP) + 1:(i + 1) * (1 + SWAP)]], axis=0)
+
+    def pick_swapped():
+        total = found[...]
+        latent_rows, rotary_rows = total[:, :LAT], total[:, LAT:]
+        for i in range(len(arrived) // (1 + SWAP)):
+            choice = picked[:, (2 + 2 * i) * rows:(3 + 2 * i) * rows]
+            latent_rows = latent_rows + jnp.dot(choice, latents[i * rows:(i + 1) * rows, :], preferred_element_type=jnp.float32)
+            rotary = swapped_block(i)[LAT:]
+            rotary_rows = rotary_rows + lax.dot_general(choice, rotary, NT, preferred_element_type=jnp.float32)
+        found_more[:, :LAT] = latent_rows
+        found_more[:, LAT:] = rotary_rows
+
+    def send(g):
+        at = pl.ds(g * group * VDIM, group * VDIM)
+        return pltpu.make_async_copy(result.at[:, at], attended.at[:, at], sems.at[g])
+
+    def place(h, values):
+        kept = (steps - 1) * group
+        if h < kept:
+            result[:, h * VDIM:(h + 1) * VDIM] = values.astype(jnp.bfloat16)
+        else:
+            last[:, (h - kept) * VDIM:(h - kept + 1) * VDIM] = values.astype(jnp.bfloat16)
+
+    for i in range(len(arrived) // (1 + SWAP)):
+        latents[i * rows:(i + 1) * rows, :] = swapped_block(i)[:LAT].T
 
     @pl.when(lax.axis_index("cp") == 0)
     def _():
         for h in range(heads):
             part = slice(h * rows, (h + 1) * rows)
-            result[:, h * VDIM:(h + 1) * VDIM] = (own_result[part, :] / totals[part, :]).astype(jnp.bfloat16)
+            place(h, own_result[part, :] / totals[part, :])
+            if (h + 1) % group == 0 and h < heads - group:
+                send(h // group).start()
+        pick_swapped()
 
     @pl.when(lax.axis_index("cp") > 0)
     def _():
         for i in range(count // 2):
-            fetched, *parts = arrived[i * (1 + SWAP):(i + 1) * (1 + SWAP)]
-            swapped = jnp.concatenate([part[...] for part in parts], axis=0)
             at = 2 * i * rows
-            keys[:, at:at + rows] = fetched[...]
-            keys[:, at + rows:at + 2 * rows] = swapped
-            latents[i * rows:(i + 1) * rows, :] = swapped[:LAT].T
+            keys[:, at:at + rows] = arrived[i * (1 + SWAP)][...]
+            keys[:, at + rows:at + 2 * rows] = swapped_block(i)
         scores, values, weights = {}, {}, {}
         for step in range(steps + 2):
             if step < steps:
                 scores[step] = score(step)
+            if step == 1:
+                pick_swapped()
             if 0 <= step - 2:
                 finish(step - 2, *weights.pop(step - 2), values.pop(step - 2))
+                if step - 2 < steps - 1:
+                    send(step - 2).start()
             if 0 <= step - 1 < steps:
                 values[step - 1] = value(step - 1)
                 weights[step - 1] = weigh(step - 1, scores.pop(step - 1))
 
-
-def store_kernel(result, picked, found, sent_rows, filled, *refs):
-    swapped, (attended, page_cache, page_scales, cache_buf, scale_buf, sems) = refs[:-6], refs[-6:]
-    count = sems.shape[0] - 2
-    wide = result.shape[1] // count
-    copies = []
-    for i in range(count):
-        some = pl.ds(i * wide, wide)
-        copies.append(pltpu.make_async_copy(result.at[:, some], attended.at[:, some], sems.at[i]))
-        copies[-1].start()
+    for g in range(steps - 1):
+        send(g).wait()
+
+
+def store_kernel(last, found, sent_rows, filled, _, attended, page_cache, page_scales, cache_buf, scale_buf, sems):
+    at = pl.ds(attended.shape[1] - last.shape[1], last.shape[1])
+    copies = [
+        pltpu.make_async_copy(source, target, sems.at[i])
+        for i, (source, target) in enumerate(((last, attended.at[:, at]), (cache_buf, page_cache), (scale_buf, page_scales)))
+    ]
+    copies[0].start()
     rows = found[...] + sent_rows[:found.shape[0], :ROW].astype(jnp.float32)
-    for i in range(len(swapped) // SWAP):
-        block = jnp.concatenate([part[...] for part in swapped[i * SWAP:(i + 1) * SWAP]], axis=0)
-        rows = rows + pick_rows(picked, 2 + 2 * i, block)
     write_cache(rows, filled, cache_buf, scale_buf)
-    for i, (source, target) in enumerate(((cache_buf, page_cache), (scale_buf, page_scales))):
-        copies.append(pltpu.make_async_copy(source, target, sems.at[count + i]))
-        copies[-1].start()
+    for copy in copies[1:]:
+        copy.start()
     for copy in copies:
         copy.wait()
 
@@ -407,25 +436,32 @@
     )(picked, own_copy, value_copy, *blocks)
 
     group = 4 if count <= 4 else 2
-    operands = (combined, result, peaks, totals, value_copy, bias, fetched_values, *pieces[:count // 2 * (1 + SWAP)])
-    attended = pl.pallas_call(
+    steps = heads // group
+    operands = (combined, result, peaks, totals, value_copy, bias, fetched_values, picked, found, *pieces)
+    attended, last, found = pl.pallas_call(
         functools.partial(earlier_kernel, count, group),
         in_specs=[vmem] * len(operands),
-        out_specs=vmem,
-        out_shape=jax.ShapeDtypeStruct((rows, heads * VDIM), jnp.bfloat16),
+        out_specs=[hbm, vmem, vmem],
+        out_shape=[
+            jax.ShapeDtypeStruct((rows, heads * VDIM), jnp.bfloat16),
+            jax.ShapeDtypeStruct((rows, group * VDIM), jnp.bfloat16),
+            jax.ShapeDtypeStruct((kept, ROW), jnp.float32),
+        ],
         scratch_shapes=[
             pltpu.VMEM((ROW, count * rows), jnp.bfloat16),
-            pltpu.VMEM((count // 2 * rows, LAT), jnp.bfloat16),
+            pltpu.VMEM((len(blocks) * rows, LAT), jnp.bfloat16),
+            pltpu.VMEM((rows, (steps - 1) * group * VDIM), jnp.bfloat16),
+            pltpu.SemaphoreType.DMA((steps - 1,)),
         ],
         cost_estimate=pl.CostEstimate(flops=2**20, bytes_accessed=2**10, transcendentals=0),
         compiler_params=params,
         name="earlier",
     )(*operands)
-    sent_rows, attended = lax.optimization_barrier((sent_rows, attended))
-    operands = (attended, picked, found, sent_rows, filled, *[part for i, part in enumerate(pieces) if i % (1 + SWAP)])
+    sent_rows, last = lax.optimization_barrier((sent_rows, last))
+    operands = (last, found, sent_rows, filled, attended)
     attended, page_cache, page_scales = pl.pallas_call(
         store_kernel,
-        in_specs=[vmem] * len(operands),
+        in_specs=[vmem] * (len(operands) - 1) + [hbm],
         out_specs=[hbm] * 3,
         out_shape=[
             jax.ShapeDtypeStruct((rows, heads * VDIM), jnp.bfloat16),
@@ -435,8 +471,9 @@
         scratch_shapes=[
             pltpu.VMEM((slot_count, PAGE, ROW), jnp.bfloat16),
             pltpu.VMEM((slot_count, NBLK, PAGE), jnp.bfloat16),
-            pltpu.SemaphoreType.DMA((4 + 2,)),
-        ],
+            pltpu.SemaphoreType.DMA((3,)),
+        ],
+        input_output_aliases={len(operands) - 1: 0},
         cost_estimate=pl.CostEstimate(flops=2**20, bytes_accessed=2**10, transcendentals=0),
         compiler_params=params,
         name="store",

time: 14.4 us -> 15 us (1.042)
  the two profiles are of different devices: /device:TPU:0 before, /device:TPU:17 now
where the time goes in v17:
time: 15 us; the launch traced here: 14.8 us
  Pallas kernels  8.92 us (59%)
  starting transfers between devices  4.54 us (30%)
  between operations  0.68 us (5%)
  waiting for transfers between devices  0.65 us (4%)
    pallas_call x1, Pallas kernels, on_device(): pl.pallas_call(functools.partial(own_kernel, n_cp, count, chunks, group,...  4.59 us
    pallas_call x1, Pallas kernels, on_device(): pl.pallas_call(functools.partial(earlier_kernel, count, group), in_specs=...  2.94 us
    ppermute x1, starting transfers between devices, on_device(): lax.ppermute(sent_rows, 'cp', [(c, (c + n_cp - 1) % n_cp) for c in range(...  2.52 us
    ppermute x2, starting transfers between devices, swap(): lax.ppermute(part, 'dec', [(e, e ^ 1) for e in range(n_dec)])  1.96 us
    pallas_call x1, Pallas kernels, on_device(): pl.pallas_call(store_kernel, in_specs=[vmem] * (len(operands) - 1) + [hbm...  0.85 us
    ppermute x2, waiting for transfers between devices, swap(): lax.ppermute(part, 'dec', [(e, e ^ 1) for e in range(n_dec)])  0.64 us
    pallas_call x1, Pallas kernels, on_device(): pl.pallas_call(functools.partial(arrived_kernel, count // 2), in_specs=[v...  0.54 us
  transfers between devices with their start and end apart: 4, of which 2 were waited for; matrix products, arithmetic and copies ran while one was open for 0% of the time, Pallas kernels for 55%

profile of v17, /device:TPU:17, one launch (start us, length us, event | category | flops | bytes accessed | tf_op | source)
XLA Modules:
  0.0 14.8 jit_solution(11426159195126012385)
XLA Ops:
  0.6 0.1 collective-permute-start.1
  0.7 4.6 %own.1 = (bf16[2048,576]{1,0:T(8,128)(2,1)S(1)}, f32[2048,128]{1,0:T(8,128)S(1)}, f32[2048,128]{1,0:T(8,128)S(1)}, f32[2048,128]{1,0:T(8,128)S(1)}, bf16[64,640]...) custom-call(s32[2]{0:T(128)} %refs_0_.1, ...), custom_call_target="tpu_custom_call" | custom-call | flops 905969664 | bytes 5242880 | tf_op jit(solution)/shard_map/own/pallas_call | solution.py:389
  5.3 2.5 %collective-permute-start = (bf16[64,640]{1,0:T(8,128)(2,1)S(1)}, bf16[64,640]{1,0:T(8,128)(2,1)S(1)}, u32[]{:S(2)}, u32[]{:S(2)}) collective-permute-start(bf16[64,640]{1,0:T(8,128)(2,1)S(1)} %get-tuple-element.25), channel_id=1, source_target_pairs={{0,12},{4,0},{8,4},{12,8},{1,13},{5,1},{9,5},{13,9},{2,14},{6,2},{... | collective-permute-start | bytes 245768 | tf_op jit(solution)/shard_map/ppermute | solution.py:422
  7.8 0.0 collective-permute-done.1.refs_0_.refs_9_
  7.8 1.9 %collective-permute-start.3 = (bf16[288,128]{1,0:T(8,128)(2,1)S(1)}, bf16[288,128]{1,0:T(8,128)(2,1)S(1)}, u32[]{:S(2)}, u32[]{:S(2)}) collective-permute-start(bf16[288,128]{1,0:T(8,128)(2,1)S(1)} %get-tuple-element.47), channel_id=1, source_target_pairs={{0,1},{1,0},{2,3},{3,2},{4,5},{5,4},{6,7},{7,6},{8,9},{9,8},{10,11... | collective-permute-start | bytes 221192 | tf_op jit(solution)/shard_map/ppermute | solution.py:366
  9.7 0.1 collective-permute-start.2
  9.8 0.5 %arrived.1 = (f32[48,576]{1,0:T(8,128)S(1)}, bf16[128,2048]{1,0:T(8,128)(2,1)S(1)}) custom-call(bf16[48,384]{1,0:T(8,128)(2,1)S(1)} %get-tuple-element.33.picked.refs_7_, bf16[576,128]{1,0:T(8,128)(2,1)S(1)} %get-tuple-element.34.own, bf16[16,512,128]{2,1,0:T(8,128)(2,1)S(1)} %get-tuple-element.30.value_expand.refs_4_, ...), custom_call_target="tpu_custom_call" | custom-call | flops 1048576 | bytes 1024 | tf_op jit(solution)/shard_map/arrived/pallas_call | solution.py:425
  10.3 0.3 %collective-permute-done.3.refs_11_ = bf16[288,128]{1,0:T(8,128)(2,1)S(1)} collective-permute-done((bf16[288,128]{1,0:T(8,128)(2,1)S(1)}, bf16[288,128]{1,0:T(8,128)(2,1)S(1)}, u32[]{:S(2)}, u32[]{:S(2)}) %collective-permute-start.3) | collective-permute-done | bytes 73760 | tf_op jit(solution)/shard_map/ppermute | solution.py:366
  10.6 0.4 %collective-permute-done.2.refs_10_ = bf16[288,128]{1,0:T(8,128)(2,1)S(1)} collective-permute-done((bf16[288,128]{1,0:T(8,128)(2,1)S(1)}, bf16[288,128]{1,0:T(8,128)(2,1)S(1)}, u32[]{:S(2)}, u32[]{:S(2)}) %collective-permute-start.2) | collective-permute-done | bytes 73760 | tf_op jit(solution)/shard_map/ppermute | solution.py:366
  11.0 2.9 %earlier.1 = (bf16[128,2048]{1,0:T(8,128)(2,1)}, bf16[128,512]{1,0:T(8,128)(2,1)S(1)}, f32[48,576]{1,0:T(8,128)S(1)}) custom-call(bf16[2048,576]{1,0:T(8,128)(2,1)S(1)} %get-tuple-element.26.refs_0_, f32[2048,128]{1,0:T(8,128)S(1)} %get-tuple-element.27.refs_1_, f32[2048,128]{1,0:T(8,128)S(1)} %get-tuple-element.28.refs_2_, ...), custom_call_target="tpu_custom_call" | custom-call | flops 1048576 | bytes 1024 | tf_op jit(solution)/shard_map/earlier/pallas_call | solution.py:441
  13.9 0.0 collective-permute-done.sent_rows
  13.9 0.8 %store.1 = (bf16[128,2048]{1,0:T(8,128)(2,1)}, bf16[3,16,576]{2,1,0:T(8,128)(2,1)}, bf16[3,4,16]{2,1,0:T(4,128)(2,1)}) custom-call(bf16[128,512]{1,0:T(8,128)(2,1)S(1)} %get-tuple-element.39.last, f32[48,576]{1,0:T(8,128)S(1)} %get-tuple-element.40.found, bf16[64,640]{1,0:T(8,128)(2,1)S(1)} %collective-permute-done.sent_rows, ...), custom_call_target="tpu_custom_call", output_to_operand_aliasing={{0}: (4, {})} | custom-call | flops 1048576 | bytes 1024 | tf_op jit(solution)/shard_map/store/pallas_call | solution.py:462
  (1 shorter events, 0.0 us)
Async XLA Ops:
  0.6 7.2 %collective-permute-start.1 = (bf16[576,128]{1,0:T(8,128)(2,1)}, bf16[576,128]{1,0:T(8,128)(2,1)S(1)}, u32[]{:S(2)}, u32[]{:S(2)}) collective-permute-start(bf16[576,128]{1,0:T(8,128)(2,1)} %bitcast.5), channel_id=1, source_target_pairs={{0,4},{1,9},{2,6},{3,11},{4,8},{5,13},{6,10},{7,15},{8,12},{9,1},{... | collective-permute-start | bytes 442376 | tf_op jit(solution)/shard_map/ppermute | solution.py:358
  5.3 8.6 %collective-permute-start = (bf16[64,640]{1,0:T(8,128)(2,1)S(1)}, bf16[64,640]{1,0:T(8,128)(2,1)S(1)}, u32[]{:S(2)}, u32[]{:S(2)}) collective-permute-start(bf16[64,640]{1,0:T(8,128)(2,1)S(1)} %get-tuple-element.25), channel_id=1, source_target_pairs={{0,12},{4,0},{8,4},{12,8},{1,13},{5,1},{9,5},{13,9},{2,14},{6,2},{... | collective-permute-start | bytes 245768 | tf_op jit(solution)/shard_map/ppermute | solution.py:422
  7.8 2.8 %collective-permute-start.3 = (bf16[288,128]{1,0:T(8,128)(2,1)S(1)}, bf16[288,128]{1,0:T(8,128)(2,1)S(1)}, u32[]{:S(2)}, u32[]{:S(2)}) collective-permute-start(bf16[288,128]{1,0:T(8,128)(2,1)S(1)} %get-tuple-element.47), channel_id=1, source_target_pairs={{0,1},{1,0},{2,3},{3,2},{4,5},{5,4},{6,7},{7,6},{8,9},{9,8},{10,11... | collective-permute-start | bytes 221192 | tf_op jit(solution)/shard_map/ppermute | solution.py:366
  9.7 1.3 %collective-permute-start.2 = (bf16[288,128]{1,0:T(8,128)(2,1)S(1)}, bf16[288,128]{1,0:T(8,128)(2,1)S(1)}, u32[]{:S(2)}, u32[]{:S(2)}) collective-permute-start(bf16[288,128]{1,0:T(8,128)(2,1)S(1)} %get-tuple-element.48), channel_id=1, source_target_pairs={{0,1},{1,0},{2,3},{3,2},{4,5},{5,4},{6,7},{7,6},{8,9},{9,8},{10,11... | collective-permute-start | bytes 221192 | tf_op jit(solution)/shard_map/ppermute | solution.py:366

commit v18 on v16

--- a/solution.py
+++ b/solution.py
@@ -168,26 +168,26 @@
     rows = block.shape[1]
     me = lax.axis_index("cp")
     behind = lax.rem(me + n_cp - 1, n_cp)
-    targets = []
+    targets, here = [], []
     for valid, page in slot_pages(behind, slot_count, prompt_pages, decode_owner, slot_offset):
-        here = valid & (page * PAGE // rows == me)
-        targets.append(jnp.where(here, lax.rem(page * PAGE, rows), -PAGE))
+        here.append(valid & (page * PAGE // rows == me))
+        targets.append(jnp.where(here[-1], lax.rem(page * PAGE, rows), -PAGE))
     choice = row_picker(targets, rows)
     sent = lax.dot_general(choice, block, NT, preferred_element_type=jnp.float32)
+    encoded, scales = encode(sent, slot_lanes(here))
     kept = choice.shape[0]
     sent_rows[...] = jnp.zeros(sent_rows.shape, jnp.bfloat16)
-    sent_rows[:kept, :ROW] = sent.astype(jnp.bfloat16)
+    sent_rows[:kept, :ROW] = encoded
+    sent_rows[kept:kept + NBLK, :kept] = scales
     for b in range(count):
         bias[:, b * rows:(b + 1) * rows] = visible_bias(prompt_pages, rows, swap_pair(jnp.int32(b + 1), n_cp))
-    targets = []
-    lane = lax.broadcasted_iota(jnp.int32, filled.shape, 1)
-    lane_filled = jnp.zeros(filled.shape, jnp.float32)
-    for c, (valid, page) in enumerate(slot_pages(me, slot_count, prompt_pages, decode_owner, slot_offset)):
-        source = page * PAGE // rows
-        column = swap_pair(lax.rem(me - source + n_cp, n_cp), n_cp) * rows + lax.rem(page * PAGE, rows)
+    targets, found = [], []
+    for valid, page in slot_pages(me, slot_count, prompt_pages, decode_owner, slot_offset):
+        steps_back = lax.rem(me - page * PAGE // rows + n_cp, n_cp)
+        column = swap_pair(steps_back, n_cp) * rows + lax.rem(page * PAGE, rows)
         targets.append(jnp.where(valid, column, -PAGE))
-        lane_filled = jnp.where(lane // PAGE == c, valid.astype(jnp.float32), lane_filled)
-    filled[...] = lane_filled
+        found.append(valid & (steps_back < n_cp - 1))
+    filled[:1, :] = slot_lanes(found, filled.shape[1])
     picked[...] = row_picker(targets, (n_cp - 1) * rows)
 
 
@@ -209,31 +209,33 @@
     found[...] = total
 
 
-def write_cache(rows, filled, page_cache, page_scales):
-    slot_count = page_cache.shape[0]
-    scales = []
+def slot_lanes(flags, width=None):
+    lane = lax.broadcasted_iota(jnp.int32, (1, width or len(flags) * PAGE), 1)
+    lanes = jnp.zeros(lane.shape, jnp.float32)
+    for c, flag in enumerate(flags):
+        lanes = jnp.where(lane // PAGE == c, flag.astype(jnp.float32), lanes)
+    return lanes
+
+
+def encode(rows, filled):
+    kept = rows.shape[0]
+    which = lax.broadcasted_iota(jnp.int32, (kept, LANES), 1)
+    table = jnp.zeros((kept, LANES), jnp.float32)
+    encoded = []
     for b in range(NBLK):
         values = rows[:, b * BLOCK:(b + 1) * BLOCK]
         scale = jnp.max(jnp.abs(values), axis=1, keepdims=True) + amax_epsilon
         scale = scale.astype(jnp.bfloat16).astype(jnp.float32)
-        encoded = (values / scale).astype(jnp.bfloat16)
-        for c in range(slot_count):
-            page_cache[c, :, b * BLOCK:(b + 1) * BLOCK] = encoded[c * PAGE:(c + 1) * PAGE]
-        scales.append(scale)
-    kept = rows.shape[0]
-    which = lax.broadcasted_iota(jnp.int32, (kept, LANES), 1)
-    table = jnp.zeros((kept, LANES), jnp.float32)
-    for b, scale in enumerate(scales):
+        encoded.append((values / scale).astype(jnp.bfloat16))
         table = jnp.where(which == b, scale, table)
-    table = (table.T[:NBLK] * filled[:1, :kept]).astype(jnp.bfloat16)
-    for c in range(slot_count):
-        page_cache[c, :, LAT:] = rows[c * PAGE:(c + 1) * PAGE, LAT:].astype(jnp.bfloat16)
-        page_scales[c] = table[:, c * PAGE:(c + 1) * PAGE]
+    encoded.append(rows[:, LAT:].astype(jnp.bfloat16))
+    scales = (table.T[:NBLK] * filled).astype(jnp.bfloat16)
+    return jnp.concatenate(encoded, axis=1), scales
 
 
 def earlier_kernel(count, group, *refs):
-    combined, own_result, peaks, totals, value_expand, bias, fetched_values = refs[:7]
-    arrived, (result, keys, latents) = refs[7:-3], refs[-3:]
+    combined, own_result, peaks, totals, value_expand, bias, fetched_values, picked, found, filled = refs[:10]
+    arrived, (result, encoded, scales, keys, latents) = refs[10:-5], refs[-5:]
     rows, width = bias.shape
     heads = value_expand.shape[0]
     steps = heads // group
@@ -275,25 +277,42 @@
             out = own_result[h * rows:(h + 1) * rows, :] * factor[part] + out * inverse[part]
             result[:, h * VDIM:(h + 1) * VDIM] = out.astype(jnp.bfloat16)
 
+    def swapped_block(i):
+        return jnp.concatenate([part[...] for part in arrived[i * (1 + SWAP) + 1:(i + 1) * (1 + SWAP)]], axis=0)
+
+    def encode_found():
+        total = found[...]
+        latent_rows, rotary_rows = total[:, :LAT], total[:, LAT:]
+        for i in range(len(arrived) // (1 + SWAP)):
+            choice = picked[:, (2 + 2 * i) * rows:(3 + 2 * i) * rows]
+            latent_rows = latent_rows + jnp.dot(choice, latents[i * rows:(i + 1) * rows, :], preferred_element_type=jnp.float32)
+            rotary = swapped_block(i)[LAT:]
+            rotary_rows = rotary_rows + lax.dot_general(choice, rotary, NT, preferred_element_type=jnp.float32)
+        every = jnp.concatenate([latent_rows, rotary_rows], axis=1)
+        encoded[...], scales[...] = encode(every, filled[:1, :every.shape[0]])
+
+    for i in range(len(arrived) // (1 + SWAP)):
+        latents[i * rows:(i + 1) * rows, :] = swapped_block(i)[:LAT].T
+
     @pl.when(lax.axis_index("cp") == 0)
     def _():
         for h in range(heads):
             part = slice(h * rows, (h + 1) * rows)
             result[:, h * VDIM:(h + 1) * VDIM] = (own_result[part, :] / totals[part, :]).astype(jnp.bfloat16)
+        encode_found()
 
     @pl.when(lax.axis_index("cp") > 0)
     def _():
         for i in range(count // 2):
-            fetched, *parts = arrived[i * (1 + SWAP):(i + 1) * (1 + SWAP)]
-            swapped = jnp.concatenate([part[...] for part in parts], axis=0)
             at = 2 * i * rows
-            keys[:, at:at + rows] = fetched[...]
-            keys[:, at + rows:at + 2 * rows] = swapped
-            latents[i * rows:(i + 1) * rows, :] = swapped[:LAT].T
+            keys[:, at:at + rows] = arrived[i * (1 + SWAP)][...]
+            keys[:, at + rows:at + 2 * rows] = swapped_block(i)
         scores, values, weights = {}, {}, {}
         for step in range(steps + 2):
             if step < steps:
                 scores[step] = score(step)
+            if step == 2:
+                encode_found()
             if 0 <= step - 2:
                 finish(step - 2, *weights.pop(step - 2), values.pop(step - 2))
             if 0 <= step - 1 < steps:
@@ -301,8 +320,7 @@
                 weights[step - 1] = weigh(step - 1, scores.pop(step - 1))
 
 
-def store_kernel(result, picked, found, sent_rows, filled, *refs):
-    swapped, (attended, page_cache, page_scales, cache_buf, scale_buf, sems) = refs[:-6], refs[-6:]
+def store_kernel(result, encoded, scales, sent_rows, attended, page_cache, page_scales, cache_buf, scale_buf, sems):
     count = sems.shape[0] - 2
     wide = result.shape[1] // count
     copies = []
@@ -310,11 +328,11 @@
         some = pl.ds(i * wide, wide)
         copies.append(pltpu.make_async_copy(result.at[:, some], attended.at[:, some], sems.at[i]))
         copies[-1].start()
-    rows = found[...] + sent_rows[:found.shape[0], :ROW].astype(jnp.float32)
-    for i in range(len(swapped) // SWAP):
-        block = jnp.concatenate([part[...] for part in swapped[i * SWAP:(i + 1) * SWAP]], axis=0)
-        rows = rows + pick_rows(picked, 2 + 2 * i, block)
-    write_cache(rows, filled, cache_buf, scale_buf)
+    kept = encoded.shape[0]
+    for c in range(page_cache.shape[0]):
+        part = slice(c * PAGE, (c + 1) * PAGE)
+        cache_buf[c] = encoded[part, :] + sent_rows[part, :ROW]
+        scale_buf[c] = (scales[...] + sent_rows[kept:kept + NBLK, :kept])[:, part]
     for i, (source, target) in enumerate(((cache_buf, page_cache), (scale_buf, page_scales))):
         copies.append(pltpu.make_async_copy(source, target, sems.at[count + i]))
         copies[-1].start()
@@ -407,22 +425,26 @@
     )(picked, own_copy, value_copy, *blocks)
 
     group = 4 if count <= 4 else 2
-    operands = (combined, result, peaks, totals, value_copy, bias, fetched_values, *pieces[:count // 2 * (1 + SWAP)])
-    attended = pl.pallas_call(
+    operands = (combined, result, peaks, totals, value_copy, bias, fetched_values, picked, found, filled, *pieces)
+    attended, encoded, scales = pl.pallas_call(
         functools.partial(earlier_kernel, count, group),
         in_specs=[vmem] * len(operands),
-        out_specs=vmem,
-        out_shape=jax.ShapeDtypeStruct((rows, heads * VDIM), jnp.bfloat16),
+        out_specs=[vmem] * 3,
+        out_shape=[
+            jax.ShapeDtypeStruct((rows, heads * VDIM), jnp.bfloat16),
+            jax.ShapeDtypeStruct((kept, ROW), jnp.bfloat16),
+            jax.ShapeDtypeStruct((NBLK, kept), jnp.bfloat16),
+        ],
         scratch_shapes=[
             pltpu.VMEM((ROW, count * rows), jnp.bfloat16),
-            pltpu.VMEM((count // 2 * rows, LAT), jnp.bfloat16),
+            pltpu.VMEM((len(blocks) * rows, LAT), jnp.bfloat16),
         ],
         cost_estimate=pl.CostEstimate(flops=2**20, bytes_accessed=2**10, transcendentals=0),
         compiler_params=params,
         name="earlier",
     )(*operands)
     sent_rows, attended = lax.optimization_barrier((sent_rows, attended))
-    operands = (attended, picked, found, sent_rows, filled, *[part for i, part in enumerate(pieces) if i % (1 + SWAP)])
+    operands = (attended, encoded, scales, sent_rows)
     attended, page_cache, page_scales = pl.pallas_call(
         store_kernel,
         in_specs=[vmem] * len(operands),

time: 14.4 us -> 14.3 us (level)
  waiting for transfers between devices: 1.59 us -> 1.25 us
  Pallas kernels: 6.25 us -> 6.46 us
    pallas_call x1, Pallas kernels: 0.14 us -> 0.5 us  [on_device(): pl.pallas_call(functools.partial(earlier_kernel, count, group), in_specs=...]
    ppermute x1, waiting for transfers between devices: 1.21 us -> 0.88 us  [on_device(): lax.ppermute(sent_rows, 'cp', [(c, (c + n_cp - 1) % n_cp) for c in range(...]
    pallas_call x1, Pallas kernels: 1.02 us -> 0.85 us  [on_device(): pl.pallas_call(store_kernel, in_specs=[vmem] * len(operands), out_specs=[...]
  transfers between devices with their start and end apart: 4 -> 4, of which waited for: 3 -> 3; matrix products, arithmetic and copies ran while one was open for 0% -> 0% of each run, Pallas kernels for 37% -> 40%
where the time goes in v18:
time: 14.3 us; the launch traced here: 14.1 us
  Pallas kernels  6.46 us (45%)
  starting transfers between devices  5.73 us (40%)
  waiting for transfers between devices  1.25 us (9%)
  between operations  0.67 us (5%)
    pallas_call x1, Pallas kernels, on_device(): pl.pallas_call(functools.partial(own_kernel, n_cp, count, chunks, group,...  4.57 us
    ppermute x1, starting transfers between devices, fetch(): blocks.append(lax.ppermute(own, ('cp', 'dec'), pairs))  3.08 us
    ppermute x1, starting transfers between devices, on_device(): lax.ppermute(sent_rows, 'cp', [(c, (c + n_cp - 1) % n_cp) for c in range(...  2.08 us
    ppermute x1, waiting for transfers between devices, on_device(): lax.ppermute(sent_rows, 'cp', [(c, (c + n_cp - 1) % n_cp) for c in range(...  0.88 us
    pallas_call x1, Pallas kernels, on_device(): pl.pallas_call(store_kernel, in_specs=[vmem] * len(operands), out_specs=[...  0.85 us
    ppermute x2, starting transfers between devices, swap(): lax.ppermute(part, 'dec', [(e, e ^ 1) for e in range(n_dec)])  0.57 us
    pallas_call x1, Pallas kernels, on_device(): pl.pallas_call(functools.partial(arrived_kernel, count // 2), in_specs=[v...  0.54 us
    pallas_call x1, Pallas kernels, on_device(): pl.pallas_call(functools.partial(earlier_kernel, count, group), in_specs=...  0.5 us
  transfers between devices with their start and end apart: 4, of which 3 were waited for; matrix products, arithmetic and copies ran while one was open for 0% of the time, Pallas kernels for 40%

profile of v18, /device:TPU:0, one launch (start us, length us, event | category | flops | bytes accessed | tf_op | source)
XLA Modules:
  0.0 14.1 jit_solution(16955118938818916573)
XLA Ops:
  0.6 3.1 %collective-permute-start.1 = (bf16[576,128]{1,0:T(8,128)(2,1)}, bf16[576,128]{1,0:T(8,128)(2,1)S(1)}, u32[]{:S(2)}, u32[]{:S(2)}) collective-permute-start(bf16[576,128]{1,0:T(8,128)(2,1)} %bitcast.5), channel_id=1, source_target_pairs={{0,4},{1,9},{2,6},{3,11},{4,8},{5,13},{6,10},{7,15},{8,12},{9,1},{... | collective-permute-start | bytes 442376 | tf_op jit(solution)/shard_map/ppermute | solution.py:347
  3.7 4.6 %own.1 = (bf16[2048,576]{1,0:T(8,128)(2,1)S(1)}, f32[2048,128]{1,0:T(8,128)S(1)}, f32[2048,128]{1,0:T(8,128)S(1)}, f32[2048,128]{1,0:T(8,128)S(1)}, bf16[64,640]...) custom-call(s32[2]{0:T(128)} %refs_0_.1, ...), custom_call_target="tpu_custom_call" | custom-call | flops 905969664 | bytes 5242880 | tf_op jit(solution)/shard_map/own/pallas_call | solution.py:378
  8.3 2.1 %collective-permute-start = (bf16[64,640]{1,0:T(8,128)(2,1)S(1)}, bf16[64,640]{1,0:T(8,128)(2,1)S(1)}, u32[]{:S(2)}, u32[]{:S(2)}) collective-permute-start(bf16[64,640]{1,0:T(8,128)(2,1)S(1)} %get-tuple-element.25), channel_id=1, source_target_pairs={{0,12},{4,0},{8,4},{12,8},{1,13},{5,1},{9,5},{13,9},{2,14},{6,2},{... | collective-permute-start | bytes 245768 | tf_op jit(solution)/shard_map/ppermute | solution.py:411
  10.4 0.0 collective-permute-done.1.refs_0_.refs_10_
  10.4 0.1 collective-permute-start.3
  10.5 0.5 %collective-permute-start.2 = (bf16[288,128]{1,0:T(8,128)(2,1)S(1)}, bf16[288,128]{1,0:T(8,128)(2,1)S(1)}, u32[]{:S(2)}, u32[]{:S(2)}) collective-permute-start(bf16[288,128]{1,0:T(8,128)(2,1)S(1)} %get-tuple-element.48), channel_id=1, source_target_pairs={{0,1},{1,0},{2,3},{3,2},{4,5},{5,4},{6,7},{7,6},{8,9},{9,8},{10,11... | collective-permute-start | bytes 221192 | tf_op jit(solution)/shard_map/ppermute | solution.py:355
  11.0 0.5 %arrived.1 = (f32[48,576]{1,0:T(8,128)S(1)}, bf16[128,2048]{1,0:T(8,128)(2,1)S(1)}) custom-call(bf16[48,384]{1,0:T(8,128)(2,1)S(1)} %get-tuple-element.33.picked.refs_7_, bf16[576,128]{1,0:T(8,128)(2,1)S(1)} %get-tuple-element.34.own, bf16[16,512,128]{2,1,0:T(8,128)(2,1)S(1)} %get-tuple-element.30.value_expand.refs_4_, ...), custom_call_target="tpu_custom_call" | custom-call | flops 1048576 | bytes 1024 | tf_op jit(solution)/shard_map/arrived/pallas_call | solution.py:414
  11.5 0.2 %collective-permute-done.3.refs_12_ = bf16[288,128]{1,0:T(8,128)(2,1)S(1)} collective-permute-done((bf16[288,128]{1,0:T(8,128)(2,1)S(1)}, bf16[288,128]{1,0:T(8,128)(2,1)S(1)}, u32[]{:S(2)}, u32[]{:S(2)}) %collective-permute-start.3) | collective-permute-done | bytes 73760 | tf_op jit(solution)/shard_map/ppermute | solution.py:355
  11.7 0.2 %collective-permute-done.2.refs_11_ = bf16[288,128]{1,0:T(8,128)(2,1)S(1)} collective-permute-done((bf16[288,128]{1,0:T(8,128)(2,1)S(1)}, bf16[288,128]{1,0:T(8,128)(2,1)S(1)}, u32[]{:S(2)}, u32[]{:S(2)}) %collective-permute-start.2) | collective-permute-done | bytes 73760 | tf_op jit(solution)/shard_map/ppermute | solution.py:355
  11.9 0.5 %earlier.1 = (bf16[128,2048]{1,0:T(8,128)(2,1)S(1)}, bf16[48,576]{1,0:T(8,128)(2,1)S(1)}, bf16[4,48]{1,0:T(4,128)(2,1)S(1)}) custom-call(bf16[2048,576]{1,0:T(8,128)(2,1)S(1)} %get-tuple-element.26.refs_0_, f32[2048,128]{1,0:T(8,128)S(1)} %get-tuple-element.27.refs_1_, f32[2048,128]{1,0:T(8,128)S(1)} %get-tuple-element.28.refs_2_, ...), custom_call_target="tpu_custom_call" | custom-call | flops 1048576 | bytes 1024 | tf_op jit(solution)/shard_map/earlier/pallas_call | solution.py:429
  12.4 0.9 %collective-permute-done.sent_rows = bf16[64,640]{1,0:T(8,128)(2,1)S(1)} collective-permute-done((bf16[64,640]{1,0:T(8,128)(2,1)S(1)}, bf16[64,640]{1,0:T(8,128)(2,1)S(1)}, u32[]{:S(2)}, u32[]{:S(2)}) %collective-permute-start) | collective-permute-done | bytes 81952 | tf_op jit(solution)/shard_map/ppermute | solution.py:411
  13.3 0.8 %store.1 = (bf16[128,2048]{1,0:T(8,128)(2,1)}, bf16[3,16,576]{2,1,0:T(8,128)(2,1)}, bf16[3,4,16]{2,1,0:T(4,128)(2,1)}) custom-call(bf16[128,2048]{1,0:T(8,128)(2,1)S(1)} %get-tuple-element.40.result, bf16[48,576]{1,0:T(8,128)(2,1)S(1)} %get-tuple-element.41.encoded, bf16[4,48]{1,0:T(4,128)(2,1)S(1)} %get-tuple-element.42.scales, ...), custom_call_target="tpu_custom_call" | custom-call | flops 1048576 | bytes 1024 | tf_op jit(solution)/shard_map/store/pallas_call | solution.py:448
  (1 shorter events, 0.0 us)
Async XLA Ops:
  0.6 9.7 %collective-permute-start.1 = (bf16[576,128]{1,0:T(8,128)(2,1)}, bf16[576,128]{1,0:T(8,128)(2,1)S(1)}, u32[]{:S(2)}, u32[]{:S(2)}) collective-permute-start(bf16[576,128]{1,0:T(8,128)(2,1)} %bitcast.5), channel_id=1, source_target_pairs={{0,4},{1,9},{2,6},{3,11},{4,8},{5,13},{6,10},{7,15},{8,12},{9,1},{... | collective-permute-start | bytes 442376 | tf_op jit(solution)/shard_map/ppermute | solution.py:347
  8.3 5.0 %collective-permute-start = (bf16[64,640]{1,0:T(8,128)(2,1)S(1)}, bf16[64,640]{1,0:T(8,128)(2,1)S(1)}, u32[]{:S(2)}, u32[]{:S(2)}) collective-permute-start(bf16[64,640]{1,0:T(8,128)(2,1)S(1)} %get-tuple-element.25), channel_id=1, source_target_pairs={{0,12},{4,0},{8,4},{12,8},{1,13},{5,1},{9,5},{13,9},{2,14},{6,2},{... | collective-permute-start | bytes 245768 | tf_op jit(solution)/shard_map/ppermute | solution.py:411
  10.4 1.3 %collective-permute-start.3 = (bf16[288,128]{1,0:T(8,128)(2,1)S(1)}, bf16[288,128]{1,0:T(8,128)(2,1)S(1)}, u32[]{:S(2)}, u32[]{:S(2)}) collective-permute-start(bf16[288,128]{1,0:T(8,128)(2,1)S(1)} %get-tuple-element.47), channel_id=1, source_target_pairs={{0,1},{1,0},{2,3},{3,2},{4,5},{5,4},{6,7},{7,6},{8,9},{9,8},{10,11... | collective-permute-start | bytes 221192 | tf_op jit(solution)/shard_map/ppermute | solution.py:355
  10.5 1.4 %collective-permute-start.2 = (bf16[288,128]{1,0:T(8,128)(2,1)S(1)}, bf16[288,128]{1,0:T(8,128)(2,1)S(1)}, u32[]{:S(2)}, u32[]{:S(2)}) collective-permute-start(bf16[288,128]{1,0:T(8,128)(2,1)S(1)} %get-tuple-element.48), channel_id=1, source_target_pairs={{0,1},{1,0},{2,3},{3,2},{4,5},{5,4},{6,7},{7,6},{8,9},{9,8},{10,11... | collective-permute-start | bytes 221192 | tf_op jit(solution)/shard_map/ppermute | solution.py:355

commit v19 on v18

--- a/solution.py
+++ b/solution.py
@@ -152,7 +152,6 @@
         copy.wait()
     latents[...] = own[:LAT, :].T
     own_bias = visible_bias(prompt_pages, rows, 0)
-    index_work(n_cp, count, slot_count, prompt_pages, decode_owner, slot_offset, own[...], sent_rows, bias, picked, filled)
     scores, both = {}, {}
     for step in range(steps + 2):
         if step < steps:
@@ -160,6 +159,8 @@
         if 0 <= step - 1 < steps:
             scores[step - 1] = score(step - 1)
             both[step - 1] = value(step - 1)
+        if step == 1:
+            index_work(n_cp, count, slot_count, prompt_pages, decode_owner, slot_offset, own[...], sent_rows, bias, picked, filled)
         if 0 <= step - 2:
             finish(step - 2, scores.pop(step - 2), both.pop(step - 2))
 
@@ -424,7 +425,7 @@
         name="arrived",
     )(picked, own_copy, value_copy, *blocks)
 
-    group = 4 if count <= 4 else 2
+    group = 2
     operands = (combined, result, peaks, totals, value_copy, bias, fetched_values, picked, found, filled, *pieces)
     attended, encoded, scales = pl.pallas_call(
         functools.partial(earlier_kernel, count, group),

time: 14.3 us -> 14.8 us (1.035)
  the two profiles are of different devices: /device:TPU:0 before, /device:TPU:19 now
where the time goes in v19:
time: 14.8 us; the launch traced here: 14.7 us
  Pallas kernels  8.95 us (60%)
  starting transfers between devices  4.41 us (30%)
  between operations  0.67 us (5%)
  waiting for transfers between devices  0.65 us (4%)
    pallas_call x1, Pallas kernels, on_device(): pl.pallas_call(functools.partial(own_kernel, n_cp, count, chunks, group,...  4.73 us
    pallas_call x1, Pallas kernels, on_device(): pl.pallas_call(functools.partial(earlier_kernel, count, group), in_specs=...  2.83 us
    ppermute x1, starting transfers between devices, on_device(): lax.ppermute(sent_rows, 'cp', [(c, (c + n_cp - 1) % n_cp) for c in range(...  2.48 us
    ppermute x2, starting transfers between devices, swap(): lax.ppermute(part, 'dec', [(e, e ^ 1) for e in range(n_dec)])  1.82 us
    pallas_call x1, Pallas kernels, on_device(): pl.pallas_call(store_kernel, in_specs=[vmem] * len(operands), out_specs=[...  0.85 us
    ppermute x2, waiting for transfers between devices, swap(): lax.ppermute(part, 'dec', [(e, e ^ 1) for e in range(n_dec)])  0.64 us
    pallas_call x1, Pallas kernels, on_device(): pl.pallas_call(functools.partial(arrived_kernel, count // 2), in_specs=[v...  0.54 us
  transfers between devices with their start and end apart: 4, of which 2 were waited for; matrix products, arithmetic and copies ran while one was open for 0% of the time, Pallas kernels for 55%

profile of v19, /device:TPU:19, one launch (start us, length us, event | category | flops | bytes accessed | tf_op | source)
XLA Modules:
  0.0 14.7 jit_solution(7310297883008461289)
XLA Ops:
  0.6 0.1 collective-permute-start.1
  0.7 4.7 %own.1 = (bf16[2048,576]{1,0:T(8,128)(2,1)S(1)}, f32[2048,128]{1,0:T(8,128)S(1)}, f32[2048,128]{1,0:T(8,128)S(1)}, f32[2048,128]{1,0:T(8,128)S(1)}, bf16[64,640]...) custom-call(s32[2]{0:T(128)} %refs_0_.1, ...), custom_call_target="tpu_custom_call" | custom-call | flops 905969664 | bytes 5242880 | tf_op jit(solution)/shard_map/own/pallas_call | solution.py:379
  5.5 2.5 %collective-permute-start = (bf16[64,640]{1,0:T(8,128)(2,1)S(1)}, bf16[64,640]{1,0:T(8,128)(2,1)S(1)}, u32[]{:S(2)}, u32[]{:S(2)}) collective-permute-start(bf16[64,640]{1,0:T(8,128)(2,1)S(1)} %get-tuple-element.25), channel_id=1, source_target_pairs={{0,12},{4,0},{8,4},{12,8},{1,13},{5,1},{9,5},{13,9},{2,14},{6,2},{... | collective-permute-start | bytes 245768 | tf_op jit(solution)/shard_map/ppermute | solution.py:412
  8.0 0.0 collective-permute-done.1.refs_0_.refs_10_
  8.0 1.7 %collective-permute-start.3 = (bf16[288,128]{1,0:T(8,128)(2,1)S(1)}, bf16[288,128]{1,0:T(8,128)(2,1)S(1)}, u32[]{:S(2)}, u32[]{:S(2)}) collective-permute-start(bf16[288,128]{1,0:T(8,128)(2,1)S(1)} %get-tuple-element.47), channel_id=1, source_target_pairs={{0,1},{1,0},{2,3},{3,2},{4,5},{5,4},{6,7},{7,6},{8,9},{9,8},{10,11... | collective-permute-start | bytes 221192 | tf_op jit(solution)/shard_map/ppermute | solution.py:356
  9.7 0.1 collective-permute-start.2
  9.8 0.5 %arrived.1 = (f32[48,576]{1,0:T(8,128)S(1)}, bf16[128,2048]{1,0:T(8,128)(2,1)S(1)}) custom-call(bf16[48,384]{1,0:T(8,128)(2,1)S(1)} %get-tuple-element.33.picked.refs_7_, bf16[576,128]{1,0:T(8,128)(2,1)S(1)} %get-tuple-element.34.own, bf16[16,512,128]{2,1,0:T(8,128)(2,1)S(1)} %get-tuple-element.30.value_expand.refs_4_, ...), custom_call_target="tpu_custom_call" | custom-call | flops 1048576 | bytes 1024 | tf_op jit(solution)/shard_map/arrived/pallas_call | solution.py:415
  10.3 0.3 %collective-permute-done.3.refs_12_ = bf16[288,128]{1,0:T(8,128)(2,1)S(1)} collective-permute-done((bf16[288,128]{1,0:T(8,128)(2,1)S(1)}, bf16[288,128]{1,0:T(8,128)(2,1)S(1)}, u32[]{:S(2)}, u32[]{:S(2)}) %collective-permute-start.3) | collective-permute-done | bytes 73760 | tf_op jit(solution)/shard_map/ppermute | solution.py:356
  10.6 0.4 %collective-permute-done.2.refs_11_ = bf16[288,128]{1,0:T(8,128)(2,1)S(1)} collective-permute-done((bf16[288,128]{1,0:T(8,128)(2,1)S(1)}, bf16[288,128]{1,0:T(8,128)(2,1)S(1)}, u32[]{:S(2)}, u32[]{:S(2)}) %collective-permute-start.2) | collective-permute-done | bytes 73760 | tf_op jit(solution)/shard_map/ppermute | solution.py:356
  11.0 2.8 %earlier.1 = (bf16[128,2048]{1,0:T(8,128)(2,1)S(1)}, bf16[48,576]{1,0:T(8,128)(2,1)S(1)}, bf16[4,48]{1,0:T(4,128)(2,1)S(1)}) custom-call(bf16[2048,576]{1,0:T(8,128)(2,1)S(1)} %get-tuple-element.26.refs_0_, f32[2048,128]{1,0:T(8,128)S(1)} %get-tuple-element.27.refs_1_, f32[2048,128]{1,0:T(8,128)S(1)} %get-tuple-element.28.refs_2_, ...), custom_call_target="tpu_custom_call" | custom-call | flops 1048576 | bytes 1024 | tf_op jit(solution)/shard_map/earlier/pallas_call | solution.py:430
  13.8 0.0 collective-permute-done.sent_rows
  13.8 0.9 %store.1 = (bf16[128,2048]{1,0:T(8,128)(2,1)}, bf16[3,16,576]{2,1,0:T(8,128)(2,1)}, bf16[3,4,16]{2,1,0:T(4,128)(2,1)}) custom-call(bf16[128,2048]{1,0:T(8,128)(2,1)S(1)} %get-tuple-element.40.result, bf16[48,576]{1,0:T(8,128)(2,1)S(1)} %get-tuple-element.41.encoded, bf16[4,48]{1,0:T(4,128)(2,1)S(1)} %get-tuple-element.42.scales, ...), custom_call_target="tpu_custom_call" | custom-call | flops 1048576 | bytes 1024 | tf_op jit(solution)/shard_map/store/pallas_call | solution.py:449
  (1 shorter events, 0.0 us)
Async XLA Ops:
  0.6 7.3 %collective-permute-start.1 = (bf16[576,128]{1,0:T(8,128)(2,1)}, bf16[576,128]{1,0:T(8,128)(2,1)S(1)}, u32[]{:S(2)}, u32[]{:S(2)}) collective-permute-start(bf16[576,128]{1,0:T(8,128)(2,1)} %bitcast.5), channel_id=1, source_target_pairs={{0,4},{1,9},{2,6},{3,11},{4,8},{5,13},{6,10},{7,15},{8,12},{9,1},{... | collective-permute-start | bytes 442376 | tf_op jit(solution)/shard_map/ppermute | solution.py:348
  5.5 8.3 %collective-permute-start = (bf16[64,640]{1,0:T(8,128)(2,1)S(1)}, bf16[64,640]{1,0:T(8,128)(2,1)S(1)}, u32[]{:S(2)}, u32[]{:S(2)}) collective-permute-start(bf16[64,640]{1,0:T(8,128)(2,1)S(1)} %get-tuple-element.25), channel_id=1, source_target_pairs={{0,12},{4,0},{8,4},{12,8},{1,13},{5,1},{9,5},{13,9},{2,14},{6,2},{... | collective-permute-start | bytes 245768 | tf_op jit(solution)/shard_map/ppermute | solution.py:412
  8.0 2.7 %collective-permute-start.3 = (bf16[288,128]{1,0:T(8,128)(2,1)S(1)}, bf16[288,128]{1,0:T(8,128)(2,1)S(1)}, u32[]{:S(2)}, u32[]{:S(2)}) collective-permute-start(bf16[288,128]{1,0:T(8,128)(2,1)S(1)} %get-tuple-element.47), channel_id=1, source_target_pairs={{0,1},{1,0},{2,3},{3,2},{4,5},{5,4},{6,7},{7,6},{8,9},{9,8},{10,11... | collective-permute-start | bytes 221192 | tf_op jit(solution)/shard_map/ppermute | solution.py:356
  9.7 1.3 %collective-permute-start.2 = (bf16[288,128]{1,0:T(8,128)(2,1)S(1)}, bf16[288,128]{1,0:T(8,128)(2,1)S(1)}, u32[]{:S(2)}, u32[]{:S(2)}) collective-permute-start(bf16[288,128]{1,0:T(8,128)(2,1)S(1)} %get-tuple-element.48), channel_id=1, source_target_pairs={{0,1},{1,0},{2,3},{3,2},{4,5},{5,4},{6,7},{7,6},{8,9},{9,8},{10,11... | collective-permute-start | bytes 221192 | tf_op jit(solution)/shard_map/ppermute | solution.py:356

commit v20 on v18

--- a/solution.py
+++ b/solution.py
@@ -373,7 +373,7 @@
     vmem = pl.BlockSpec(memory_space=pltpu.VMEM)
     hbm = pl.BlockSpec(memory_space=pltpu.HBM)
     params = pltpu.CompilerParams(vmem_limit_bytes=32 * 2**20)
-    group, chunks = 4, (heads // 4, heads // 4, heads // 2)
+    group, chunks = 8, (heads // 2, heads // 2)
     inputs = (prompt_pages, decode_owner, slot_offset, own, queries, key_absorb, value_expand)
     combined, result, peaks, totals, sent_rows, bias, picked, filled, own_copy, value_copy = pl.pallas_call(
         functools.partial(own_kernel, n_cp, count, chunks, group, slot_count),
@@ -424,7 +424,7 @@
         name="arrived",
     )(picked, own_copy, value_copy, *blocks)
 
-    group = 4 if count <= 4 else 2
+    group = 8 if count <= 4 else 2
     operands = (combined, result, peaks, totals, value_copy, bias, fetched_values, picked, found, filled, *pieces)
     attended, encoded, scales = pl.pallas_call(
         functools.partial(earlier_kernel, count, group),

time: 14.3 us -> 14.6 us (1.021)
  Pallas kernels: 6.46 us -> 6.8 us
    pallas_call x1, Pallas kernels: 4.57 us -> 4.91 us  [on_device(): pl.pallas_call(functools.partial(own_kernel, n_cp, count, chunks, group,...]
  transfers between devices with their start and end apart: 4 -> 4, of which waited for: 3 -> 3; matrix products, arithmetic and copies ran while one was open for 0% -> 0% of each run, Pallas kernels for 40% -> 41%
where the time goes in v20:
time: 14.6 us; the launch traced here: 14.4 us
  Pallas kernels  6.8 us (47%)
  starting transfers between devices  5.74 us (39%)
  waiting for transfers between devices  1.23 us (8%)
  between operations  0.67 us (5%)
    pallas_call x1, Pallas kernels, on_device(): pl.pallas_call(functools.partial(own_kernel, n_cp, count, chunks, group,...  4.91 us
    ppermute x1, starting transfers between devices, fetch(): blocks.append(lax.ppermute(own, ('cp', 'dec'), pairs))  3.08 us
    ppermute x1, starting transfers between devices, on_device(): lax.ppermute(sent_rows, 'cp', [(c, (c + n_cp - 1) % n_cp) for c in range(...  2.1 us
    ppermute x1, waiting for transfers between devices, on_device(): lax.ppermute(sent_rows, 'cp', [(c, (c + n_cp - 1) % n_cp) for c in range(...  0.86 us
    pallas_call x1, Pallas kernels, on_device(): pl.pallas_call(store_kernel, in_specs=[vmem] * len(operands), out_specs=[...  0.85 us
    ppermute x2, starting transfers between devices, swap(): lax.ppermute(part, 'dec', [(e, e ^ 1) for e in range(n_dec)])  0.57 us
    pallas_call x1, Pallas kernels, on_device(): pl.pallas_call(functools.partial(arrived_kernel, count // 2), in_specs=[v...  0.54 us
    pallas_call x1, Pallas kernels, on_device(): pl.pallas_call(functools.partial(earlier_kernel, count, group), in_specs=...  0.5 us
  transfers between devices with their start and end apart: 4, of which 3 were waited for; matrix products, arithmetic and copies ran while one was open for 0% of the time, Pallas kernels for 41%

profile of v20, /device:TPU:0, one launch (start us, length us, event | category | flops | bytes accessed | tf_op | source)
XLA Modules:
  0.0 14.4 jit_solution(3818550421240566806)
XLA Ops:
  0.6 3.1 %collective-permute-start.1 = (bf16[576,128]{1,0:T(8,128)(2,1)}, bf16[576,128]{1,0:T(8,128)(2,1)S(1)}, u32[]{:S(2)}, u32[]{:S(2)}) collective-permute-start(bf16[576,128]{1,0:T(8,128)(2,1)} %bitcast.5), channel_id=1, source_target_pairs={{0,4},{1,9},{2,6},{3,11},{4,8},{5,13},{6,10},{7,15},{8,12},{9,1},{... | collective-permute-start | bytes 442376 | tf_op jit(solution)/shard_map/ppermute | solution.py:347
  3.7 4.9 %own.1 = (bf16[2048,576]{1,0:T(8,128)(2,1)S(1)}, f32[2048,128]{1,0:T(8,128)S(1)}, f32[2048,128]{1,0:T(8,128)S(1)}, f32[2048,128]{1,0:T(8,128)S(1)}, bf16[64,640]...) custom-call(s32[2]{0:T(128)} %refs_0_.1, ...), custom_call_target="tpu_custom_call" | custom-call | flops 905969664 | bytes 5242880 | tf_op jit(solution)/shard_map/own/pallas_call | solution.py:378
  8.6 2.1 %collective-permute-start = (bf16[64,640]{1,0:T(8,128)(2,1)S(1)}, bf16[64,640]{1,0:T(8,128)(2,1)S(1)}, u32[]{:S(2)}, u32[]{:S(2)}) collective-permute-start(bf16[64,640]{1,0:T(8,128)(2,1)S(1)} %get-tuple-element.25), channel_id=1, source_target_pairs={{0,12},{4,0},{8,4},{12,8},{1,13},{5,1},{9,5},{13,9},{2,14},{6,2},{... | collective-permute-start | bytes 245768 | tf_op jit(solution)/shard_map/ppermute | solution.py:411
  10.7 0.0 collective-permute-done.1.refs_0_.refs_10_
  10.7 0.1 collective-permute-start.3
  10.8 0.5 %collective-permute-start.2 = (bf16[288,128]{1,0:T(8,128)(2,1)S(1)}, bf16[288,128]{1,0:T(8,128)(2,1)S(1)}, u32[]{:S(2)}, u32[]{:S(2)}) collective-permute-start(bf16[288,128]{1,0:T(8,128)(2,1)S(1)} %get-tuple-element.48), channel_id=1, source_target_pairs={{0,1},{1,0},{2,3},{3,2},{4,5},{5,4},{6,7},{7,6},{8,9},{9,8},{10,11... | collective-permute-start | bytes 221192 | tf_op jit(solution)/shard_map/ppermute | solution.py:355
  11.3 0.5 %arrived.1 = (f32[48,576]{1,0:T(8,128)S(1)}, bf16[128,2048]{1,0:T(8,128)(2,1)S(1)}) custom-call(bf16[48,384]{1,0:T(8,128)(2,1)S(1)} %get-tuple-element.33.picked.refs_7_, bf16[576,128]{1,0:T(8,128)(2,1)S(1)} %get-tuple-element.34.own, bf16[16,512,128]{2,1,0:T(8,128)(2,1)S(1)} %get-tuple-element.30.value_expand.refs_4_, ...), custom_call_target="tpu_custom_call" | custom-call | flops 1048576 | bytes 1024 | tf_op jit(solution)/shard_map/arrived/pallas_call | solution.py:414
  11.9 0.2 %collective-permute-done.3.refs_12_ = bf16[288,128]{1,0:T(8,128)(2,1)S(1)} collective-permute-done((bf16[288,128]{1,0:T(8,128)(2,1)S(1)}, bf16[288,128]{1,0:T(8,128)(2,1)S(1)}, u32[]{:S(2)}, u32[]{:S(2)}) %collective-permute-start.3) | collective-permute-done | bytes 73760 | tf_op jit(solution)/shard_map/ppermute | solution.py:355
  12.1 0.2 %collective-permute-done.2.refs_11_ = bf16[288,128]{1,0:T(8,128)(2,1)S(1)} collective-permute-done((bf16[288,128]{1,0:T(8,128)(2,1)S(1)}, bf16[288,128]{1,0:T(8,128)(2,1)S(1)}, u32[]{:S(2)}, u32[]{:S(2)}) %collective-permute-start.2) | collective-permute-done | bytes 73760 | tf_op jit(solution)/shard_map/ppermute | solution.py:355
  12.2 0.5 %earlier.1 = (bf16[128,2048]{1,0:T(8,128)(2,1)S(1)}, bf16[48,576]{1,0:T(8,128)(2,1)S(1)}, bf16[4,48]{1,0:T(4,128)(2,1)S(1)}) custom-call(bf16[2048,576]{1,0:T(8,128)(2,1)S(1)} %get-tuple-element.26.refs_0_, f32[2048,128]{1,0:T(8,128)S(1)} %get-tuple-element.27.refs_1_, f32[2048,128]{1,0:T(8,128)S(1)} %get-tuple-element.28.refs_2_, ...), custom_call_target="tpu_custom_call" | custom-call | flops 1048576 | bytes 1024 | tf_op jit(solution)/shard_map/earlier/pallas_call | solution.py:429
  12.7 0.9 %collective-permute-done.sent_rows = bf16[64,640]{1,0:T(8,128)(2,1)S(1)} collective-permute-done((bf16[64,640]{1,0:T(8,128)(2,1)S(1)}, bf16[64,640]{1,0:T(8,128)(2,1)S(1)}, u32[]{:S(2)}, u32[]{:S(2)}) %collective-permute-start) | collective-permute-done | bytes 81952 | tf_op jit(solution)/shard_map/ppermute | solution.py:411
  13.6 0.8 %store.1 = (bf16[128,2048]{1,0:T(8,128)(2,1)}, bf16[3,16,576]{2,1,0:T(8,128)(2,1)}, bf16[3,4,16]{2,1,0:T(4,128)(2,1)}) custom-call(bf16[128,2048]{1,0:T(8,128)(2,1)S(1)} %get-tuple-element.40.result, bf16[48,576]{1,0:T(8,128)(2,1)S(1)} %get-tuple-element.41.encoded, bf16[4,48]{1,0:T(4,128)(2,1)S(1)} %get-tuple-element.42.scales, ...), custom_call_target="tpu_custom_call" | custom-call | flops 1048576 | bytes 1024 | tf_op jit(solution)/shard_map/store/pallas_call | solution.py:448
  (1 shorter events, 0.0 us)
Async XLA Ops:
  0.6 10.1 %collective-permute-start.1 = (bf16[576,128]{1,0:T(8,128)(2,1)}, bf16[576,128]{1,0:T(8,128)(2,1)S(1)}, u32[]{:S(2)}, u32[]{:S(2)}) collective-permute-start(bf16[576,128]{1,0:T(8,128)(2,1)} %bitcast.5), channel_id=1, source_target_pairs={{0,4},{1,9},{2,6},{3,11},{4,8},{5,13},{6,10},{7,15},{8,12},{9,1},{... | collective-permute-start | bytes 442376 | tf_op jit(solution)/shard_map/ppermute | solution.py:347
  8.6 5.0 %collective-permute-start = (bf16[64,640]{1,0:T(8,128)(2,1)S(1)}, bf16[64,640]{1,0:T(8,128)(2,1)S(1)}, u32[]{:S(2)}, u32[]{:S(2)}) collective-permute-start(bf16[64,640]{1,0:T(8,128)(2,1)S(1)} %get-tuple-element.25), channel_id=1, source_target_pairs={{0,12},{4,0},{8,4},{12,8},{1,13},{5,1},{9,5},{13,9},{2,14},{6,2},{... | collective-permute-start | bytes 245768 | tf_op jit(solution)/shard_map/ppermute | solution.py:411
  10.7 1.3 %collective-permute-start.3 = (bf16[288,128]{1,0:T(8,128)(2,1)S(1)}, bf16[288,128]{1,0:T(8,128)(2,1)S(1)}, u32[]{:S(2)}, u32[]{:S(2)}) collective-permute-start(bf16[288,128]{1,0:T(8,128)(2,1)S(1)} %get-tuple-element.47), channel_id=1, source_target_pairs={{0,1},{1,0},{2,3},{3,2},{4,5},{5,4},{6,7},{7,6},{8,9},{9,8},{10,11... | collective-permute-start | bytes 221192 | tf_op jit(solution)/shard_map/ppermute | solution.py:355
  10.8 1.4 %collective-permute-start.2 = (bf16[288,128]{1,0:T(8,128)(2,1)S(1)}, bf16[288,128]{1,0:T(8,128)(2,1)S(1)}, u32[]{:S(2)}, u32[]{:S(2)}) collective-permute-start(bf16[288,128]{1,0:T(8,128)(2,1)S(1)} %get-tuple-element.48), channel_id=1, source_target_pairs={{0,1},{1,0},{2,3},{3,2},{4,5},{5,4},{6,7},{7,6},{8,9},{9,8},{10,11... | collective-permute-start | bytes 221192 | tf_op jit(solution)/shard_map/ppermute | solution.py:355

commit v21 on v18

--- a/solution.py
+++ b/solution.py
@@ -152,7 +152,7 @@
         copy.wait()
     latents[...] = own[:LAT, :].T
     own_bias = visible_bias(prompt_pages, rows, 0)
-    index_work(n_cp, count, slot_count, prompt_pages, decode_owner, slot_offset, own[...], sent_rows, bias, picked, filled)
+    index_work(n_cp, count, slot_count, prompt_pages, decode_owner, slot_offset, own, latents, sent_rows, bias, picked, filled)
     scores, both = {}, {}
     for step in range(steps + 2):
         if step < steps:
@@ -164,8 +164,8 @@
             finish(step - 2, scores.pop(step - 2), both.pop(step - 2))
 
 
-def index_work(n_cp, count, slot_count, prompt_pages, decode_owner, slot_offset, block, sent_rows, bias, picked, filled):
-    rows = block.shape[1]
+def index_work(n_cp, count, slot_count, prompt_pages, decode_owner, slot_offset, own, latents, sent_rows, bias, picked, filled):
+    rows = own.shape[1]
     me = lax.axis_index("cp")
     behind = lax.rem(me + n_cp - 1, n_cp)
     targets, here = [], []
@@ -173,7 +173,10 @@
         here.append(valid & (page * PAGE // rows == me))
         targets.append(jnp.where(here[-1], lax.rem(page * PAGE, rows), -PAGE))
     choice = row_picker(targets, rows)
-    sent = lax.dot_general(choice, block, NT, preferred_element_type=jnp.float32)
+    sent = jnp.concatenate([
+        jnp.dot(choice, latents[...], preferred_element_type=jnp.float32),
+        lax.dot_general(choice, own[LAT:, :], NT, preferred_element_type=jnp.float32),
+    ], axis=1)
     encoded, scales = encode(sent, slot_lanes(here))
     kept = choice.shape[0]
     sent_rows[...] = jnp.zeros(sent_rows.shape, jnp.bfloat16)
@@ -373,7 +376,7 @@
     vmem = pl.BlockSpec(memory_space=pltpu.VMEM)
     hbm = pl.BlockSpec(memory_space=pltpu.HBM)
     params = pltpu.CompilerParams(vmem_limit_bytes=32 * 2**20)
-    group, chunks = 4, (heads // 4, heads // 4, heads // 2)
+    group, chunks = 4, (heads // 4,) * 4
     inputs = (prompt_pages, decode_owner, slot_offset, own, queries, key_absorb, value_expand)
     combined, result, peaks, totals, sent_rows, bias, picked, filled, own_copy, value_copy = pl.pallas_call(
         functools.partial(own_kernel, n_cp, count, chunks, group, slot_count),
@@ -457,7 +460,7 @@
         scratch_shapes=[
             pltpu.VMEM((slot_count, PAGE, ROW), jnp.bfloat16),
             pltpu.VMEM((slot_count, NBLK, PAGE), jnp.bfloat16),
-            pltpu.SemaphoreType.DMA((4 + 2,)),
+            pltpu.SemaphoreType.DMA((2 + 2,)),
         ],
         cost_estimate=pl.CostEstimate(flops=2**20, bytes_accessed=2**10, transcendentals=0),
         compiler_params=params,

time: 14.3 us -> 14.7 us (1.028)
  Pallas kernels: 6.46 us -> 6.93 us
    pallas_call x1, Pallas kernels: 4.57 us -> 5.06 us  [on_device(): pl.pallas_call(functools.partial(own_kernel, n_cp, count, chunks, group,...]
  transfers between devices with their start and end apart: 4 -> 4, of which waited for: 3 -> 3; matrix products, arithmetic and copies ran while one was open for 0% -> 0% of each run, Pallas kernels for 40% -> 42%
where the time goes in v21:
time: 14.7 us; the launch traced here: 14.6 us
  Pallas kernels  6.93 us (47%)
  starting transfers between devices  5.73 us (39%)
  waiting for transfers between devices  1.25 us (9%)
  between operations  0.67 us (5%)
    pallas_call x1, Pallas kernels, on_device(): pl.pallas_call(functools.partial(own_kernel, n_cp, count, chunks, group,...  5.06 us
    ppermute x1, starting transfers between devices, fetch(): blocks.append(lax.ppermute(own, ('cp', 'dec'), pairs))  3.08 us
    ppermute x1, starting transfers between devices, on_device(): lax.ppermute(sent_rows, 'cp', [(c, (c + n_cp - 1) % n_cp) for c in range(...  2.08 us
    ppermute x1, waiting for transfers between devices, on_device(): lax.ppermute(sent_rows, 'cp', [(c, (c + n_cp - 1) % n_cp) for c in range(...  0.88 us
    pallas_call x1, Pallas kernels, on_device(): pl.pallas_call(store_kernel, in_specs=[vmem] * len(operands), out_specs=[...  0.84 us
    ppermute x2, starting transfers between devices, swap(): lax.ppermute(part, 'dec', [(e, e ^ 1) for e in range(n_dec)])  0.57 us
    pallas_call x1, Pallas kernels, on_device(): pl.pallas_call(functools.partial(arrived_kernel, count // 2), in_specs=[v...  0.54 us
    pallas_call x1, Pallas kernels, on_device(): pl.pallas_call(functools.partial(earlier_kernel, count, group), in_specs=...  0.5 us
  transfers between devices with their start and end apart: 4, of which 3 were waited for; matrix products, arithmetic and copies ran while one was open for 0% of the time, Pallas kernels for 42%

profile of v21, /device:TPU:0, one launch (start us, length us, event | category | flops | bytes accessed | tf_op | source)
XLA Modules:
  0.0 14.6 jit_solution(7183515282721798794)
XLA Ops:
  0.6 3.1 %collective-permute-start.1 = (bf16[576,128]{1,0:T(8,128)(2,1)}, bf16[576,128]{1,0:T(8,128)(2,1)S(1)}, u32[]{:S(2)}, u32[]{:S(2)}) collective-permute-start(bf16[576,128]{1,0:T(8,128)(2,1)} %bitcast.5), channel_id=1, source_target_pairs={{0,4},{1,9},{2,6},{3,11},{4,8},{5,13},{6,10},{7,15},{8,12},{9,1},{... | collective-permute-start | bytes 442376 | tf_op jit(solution)/shard_map/ppermute | solution.py:350
  3.7 5.1 %own.1 = (bf16[2048,576]{1,0:T(8,128)(2,1)S(1)}, f32[2048,128]{1,0:T(8,128)S(1)}, f32[2048,128]{1,0:T(8,128)S(1)}, f32[2048,128]{1,0:T(8,128)S(1)}, bf16[64,640]...) custom-call(s32[2]{0:T(128)} %refs_0_.1, ...), custom_call_target="tpu_custom_call" | custom-call | flops 905969664 | bytes 5242880 | tf_op jit(solution)/shard_map/own/pallas_call | solution.py:381
  8.8 2.1 %collective-permute-start = (bf16[64,640]{1,0:T(8,128)(2,1)S(1)}, bf16[64,640]{1,0:T(8,128)(2,1)S(1)}, u32[]{:S(2)}, u32[]{:S(2)}) collective-permute-start(bf16[64,640]{1,0:T(8,128)(2,1)S(1)} %get-tuple-element.25), channel_id=1, source_target_pairs={{0,12},{4,0},{8,4},{12,8},{1,13},{5,1},{9,5},{13,9},{2,14},{6,2},{... | collective-permute-start | bytes 245768 | tf_op jit(solution)/shard_map/ppermute | solution.py:414
  10.9 0.0 collective-permute-done.1.refs_0_.refs_10_
  10.9 0.1 collective-permute-start.3
  11.0 0.5 %collective-permute-start.2 = (bf16[288,128]{1,0:T(8,128)(2,1)S(1)}, bf16[288,128]{1,0:T(8,128)(2,1)S(1)}, u32[]{:S(2)}, u32[]{:S(2)}) collective-permute-start(bf16[288,128]{1,0:T(8,128)(2,1)S(1)} %get-tuple-element.48), channel_id=1, source_target_pairs={{0,1},{1,0},{2,3},{3,2},{4,5},{5,4},{6,7},{7,6},{8,9},{9,8},{10,11... | collective-permute-start | bytes 221192 | tf_op jit(solution)/shard_map/ppermute | solution.py:358
  11.5 0.5 %arrived.1 = (f32[48,576]{1,0:T(8,128)S(1)}, bf16[128,2048]{1,0:T(8,128)(2,1)S(1)}) custom-call(bf16[48,384]{1,0:T(8,128)(2,1)S(1)} %get-tuple-element.33.picked.refs_7_, bf16[576,128]{1,0:T(8,128)(2,1)S(1)} %get-tuple-element.34.own, bf16[16,512,128]{2,1,0:T(8,128)(2,1)S(1)} %get-tuple-element.30.value_expand.refs_4_, ...), custom_call_target="tpu_custom_call" | custom-call | flops 1048576 | bytes 1024 | tf_op jit(solution)/shard_map/arrived/pallas_call | solution.py:417
  12.0 0.2 %collective-permute-done.3.refs_12_ = bf16[288,128]{1,0:T(8,128)(2,1)S(1)} collective-permute-done((bf16[288,128]{1,0:T(8,128)(2,1)S(1)}, bf16[288,128]{1,0:T(8,128)(2,1)S(1)}, u32[]{:S(2)}, u32[]{:S(2)}) %collective-permute-start.3) | collective-permute-done | bytes 73760 | tf_op jit(solution)/shard_map/ppermute | solution.py:358
  12.2 0.2 %collective-permute-done.2.refs_11_ = bf16[288,128]{1,0:T(8,128)(2,1)S(1)} collective-permute-done((bf16[288,128]{1,0:T(8,128)(2,1)S(1)}, bf16[288,128]{1,0:T(8,128)(2,1)S(1)}, u32[]{:S(2)}, u32[]{:S(2)}) %collective-permute-start.2) | collective-permute-done | bytes 73760 | tf_op jit(solution)/shard_map/ppermute | solution.py:358
  12.4 0.5 %earlier.1 = (bf16[128,2048]{1,0:T(8,128)(2,1)S(1)}, bf16[48,576]{1,0:T(8,128)(2,1)S(1)}, bf16[4,48]{1,0:T(4,128)(2,1)S(1)}) custom-call(bf16[2048,576]{1,0:T(8,128)(2,1)S(1)} %get-tuple-element.26.refs_0_, f32[2048,128]{1,0:T(8,128)S(1)} %get-tuple-element.27.refs_1_, f32[2048,128]{1,0:T(8,128)S(1)} %get-tuple-element.28.refs_2_, ...), custom_call_target="tpu_custom_call" | custom-call | flops 1048576 | bytes 1024 | tf_op jit(solution)/shard_map/earlier/pallas_call | solution.py:432
  12.9 0.9 %collective-permute-done.sent_rows = bf16[64,640]{1,0:T(8,128)(2,1)S(1)} collective-permute-done((bf16[64,640]{1,0:T(8,128)(2,1)S(1)}, bf16[64,640]{1,0:T(8,128)(2,1)S(1)}, u32[]{:S(2)}, u32[]{:S(2)}) %collective-permute-start) | collective-permute-done | bytes 81952 | tf_op jit(solution)/shard_map/ppermute | solution.py:414
  13.7 0.8 %store.1 = (bf16[128,2048]{1,0:T(8,128)(2,1)}, bf16[3,16,576]{2,1,0:T(8,128)(2,1)}, bf16[3,4,16]{2,1,0:T(4,128)(2,1)}) custom-call(bf16[128,2048]{1,0:T(8,128)(2,1)S(1)} %get-tuple-element.40.result, bf16[48,576]{1,0:T(8,128)(2,1)S(1)} %get-tuple-element.41.encoded, bf16[4,48]{1,0:T(4,128)(2,1)S(1)} %get-tuple-element.42.scales, ...), custom_call_target="tpu_custom_call" | custom-call | flops 1048576 | bytes 1024 | tf_op jit(solution)/shard_map/store/pallas_call | solution.py:451
  (1 shorter events, 0.0 us)
Async XLA Ops:
  0.6 10.2 %collective-permute-start.1 = (bf16[576,128]{1,0:T(8,128)(2,1)}, bf16[576,128]{1,0:T(8,128)(2,1)S(1)}, u32[]{:S(2)}, u32[]{:S(2)}) collective-permute-start(bf16[576,128]{1,0:T(8,128)(2,1)} %bitcast.5), channel_id=1, source_target_pairs={{0,4},{1,9},{2,6},{3,11},{4,8},{5,13},{6,10},{7,15},{8,12},{9,1},{... | collective-permute-start | bytes 442376 | tf_op jit(solution)/shard_map/ppermute | solution.py:350
  8.8 5.0 %collective-permute-start = (bf16[64,640]{1,0:T(8,128)(2,1)S(1)}, bf16[64,640]{1,0:T(8,128)(2,1)S(1)}, u32[]{:S(2)}, u32[]{:S(2)}) collective-permute-start(bf16[64,640]{1,0:T(8,128)(2,1)S(1)} %get-tuple-element.25), channel_id=1, source_target_pairs={{0,12},{4,0},{8,4},{12,8},{1,13},{5,1},{9,5},{13,9},{2,14},{6,2},{... | collective-permute-start | bytes 245768 | tf_op jit(solution)/shard_map/ppermute | solution.py:414
  10.9 1.3 %collective-permute-start.3 = (bf16[288,128]{1,0:T(8,128)(2,1)S(1)}, bf16[288,128]{1,0:T(8,128)(2,1)S(1)}, u32[]{:S(2)}, u32[]{:S(2)}) collective-permute-start(bf16[288,128]{1,0:T(8,128)(2,1)S(1)} %get-tuple-element.47), channel_id=1, source_target_pairs={{0,1},{1,0},{2,3},{3,2},{4,5},{5,4},{6,7},{7,6},{8,9},{9,8},{10,11... | collective-permute-start | bytes 221192 | tf_op jit(solution)/shard_map/ppermute | solution.py:358
  11.0 1.4 %collective-permute-start.2 = (bf16[288,128]{1,0:T(8,128)(2,1)S(1)}, bf16[288,128]{1,0:T(8,128)(2,1)S(1)}, u32[]{:S(2)}, u32[]{:S(2)}) collective-permute-start(bf16[288,128]{1,0:T(8,128)(2,1)S(1)} %get-tuple-element.48), channel_id=1, source_target_pairs={{0,1},{1,0},{2,3},{3,2},{4,5},{5,4},{6,7},{7,6},{8,9},{9,8},{10,11... | collective-permute-start | bytes 221192 | tf_op jit(solution)/shard_map/ppermute | solution.py:358

commit v22 on v18

--- a/solution.py
+++ b/solution.py
@@ -118,7 +118,7 @@
     steps = heads // group
 
     def absorb(g):
-        for copy in large.get(g * group, ())[:2]:
+        for copy in large.get(g * group, ())[:2 if g == 0 else 3]:
             copy.wait()
         for h in range(g * group, (g + 1) * group):
             at = h * HEAD
@@ -130,8 +130,6 @@
         return jnp.dot(combined[g * group * rows:(g + 1) * group * rows, :], own[...], preferred_element_type=jnp.float32)
 
     def value(g):
-        for copy in large.get(g * group, ())[2:]:
-            copy.wait()
         return [head_values(latents[...], value_expand, g * group + i) for i in range(0, group, 2)]
 
     def finish(g, scores, both):
@@ -155,6 +153,8 @@
     index_work(n_cp, count, slot_count, prompt_pages, decode_owner, slot_offset, own[...], sent_rows, bias, picked, filled)
     scores, both = {}, {}
     for step in range(steps + 2):
+        if step == 1:
+            large[0][2].wait()
         if step < steps:
             absorb(step)
         if 0 <= step - 1 < steps:
@@ -373,7 +373,7 @@
     vmem = pl.BlockSpec(memory_space=pltpu.VMEM)
     hbm = pl.BlockSpec(memory_space=pltpu.HBM)
     params = pltpu.CompilerParams(vmem_limit_bytes=32 * 2**20)
-    group, chunks = 4, (heads // 4, heads // 4, heads // 2)
+    group, chunks = 4, (heads // 2, heads // 2)
     inputs = (prompt_pages, decode_owner, slot_offset, own, queries, key_absorb, value_expand)
     combined, result, peaks, totals, sent_rows, bias, picked, filled, own_copy, value_copy = pl.pallas_call(
         functools.partial(own_kernel, n_cp, count, chunks, group, slot_count),

time: 14.3 us -> 14.2 us (level)
  the two profiles are of different devices: /device:TPU:0 before, /device:TPU:17 now
where the time goes in v22:
time: 14.2 us; the launch traced here: 14.1 us
  Pallas kernels  7.68 us (54%)
  starting transfers between devices  5.06 us (36%)
  between operations  0.68 us (5%)
  waiting for transfers between devices  0.64 us (5%)
    pallas_call x1, Pallas kernels, on_device(): pl.pallas_call(functools.partial(own_kernel, n_cp, count, chunks, group,...  4.07 us
    ppermute x1, starting transfers between devices, on_device(): lax.ppermute(sent_rows, 'cp', [(c, (c + n_cp - 1) % n_cp) for c in range(...  2.5 us
    ppermute x2, starting transfers between devices, swap(): lax.ppermute(part, 'dec', [(e, e ^ 1) for e in range(n_dec)])  2.5 us
    pallas_call x1, Pallas kernels, on_device(): pl.pallas_call(functools.partial(earlier_kernel, count, group), in_specs=...  2.22 us
    pallas_call x1, Pallas kernels, on_device(): pl.pallas_call(store_kernel, in_specs=[vmem] * len(operands), out_specs=[...  0.85 us
    ppermute x2, waiting for transfers between devices, swap(): lax.ppermute(part, 'dec', [(e, e ^ 1) for e in range(n_dec)])  0.64 us
    pallas_call x1, Pallas kernels, on_device(): pl.pallas_call(functools.partial(arrived_kernel, count // 2), in_specs=[v...  0.54 us
  transfers between devices with their start and end apart: 4, of which 2 were waited for; matrix products, arithmetic and copies ran while one was open for 0% of the time, Pallas kernels for 48%

profile of v22, /device:TPU:17, one launch (start us, length us, event | category | flops | bytes accessed | tf_op | source)
XLA Modules:
  0.0 14.1 jit_solution(222726156280086092)
XLA Ops:
  0.6 0.1 collective-permute-start.1
  0.7 4.1 %own.1 = (bf16[2048,576]{1,0:T(8,128)(2,1)S(1)}, f32[2048,128]{1,0:T(8,128)S(1)}, f32[2048,128]{1,0:T(8,128)S(1)}, f32[2048,128]{1,0:T(8,128)S(1)}, bf16[64,640]...) custom-call(s32[2]{0:T(128)} %refs_0_.1, ...), custom_call_target="tpu_custom_call" | custom-call | flops 905969664 | bytes 5242880 | tf_op jit(solution)/shard_map/own/pallas_call | solution.py:378
  4.8 2.5 %collective-permute-start = (bf16[64,640]{1,0:T(8,128)(2,1)S(1)}, bf16[64,640]{1,0:T(8,128)(2,1)S(1)}, u32[]{:S(2)}, u32[]{:S(2)}) collective-permute-start(bf16[64,640]{1,0:T(8,128)(2,1)S(1)} %get-tuple-element.25), channel_id=1, source_target_pairs={{0,12},{4,0},{8,4},{12,8},{1,13},{5,1},{9,5},{13,9},{2,14},{6,2},{... | collective-permute-start | bytes 245768 | tf_op jit(solution)/shard_map/ppermute | solution.py:411
  7.3 0.0 collective-permute-done.1.refs_0_.refs_10_
  7.3 2.4 %collective-permute-start.3 = (bf16[288,128]{1,0:T(8,128)(2,1)S(1)}, bf16[288,128]{1,0:T(8,128)(2,1)S(1)}, u32[]{:S(2)}, u32[]{:S(2)}) collective-permute-start(bf16[288,128]{1,0:T(8,128)(2,1)S(1)} %get-tuple-element.47), channel_id=1, source_target_pairs={{0,1},{1,0},{2,3},{3,2},{4,5},{5,4},{6,7},{7,6},{8,9},{9,8},{10,11... | collective-permute-start | bytes 221192 | tf_op jit(solution)/shard_map/ppermute | solution.py:355
  9.7 0.1 collective-permute-start.2
  9.8 0.5 %arrived.1 = (f32[48,576]{1,0:T(8,128)S(1)}, bf16[128,2048]{1,0:T(8,128)(2,1)S(1)}) custom-call(bf16[48,384]{1,0:T(8,128)(2,1)S(1)} %get-tuple-element.33.picked.refs_7_, bf16[576,128]{1,0:T(8,128)(2,1)S(1)} %get-tuple-element.34.own, bf16[16,512,128]{2,1,0:T(8,128)(2,1)S(1)} %get-tuple-element.30.value_expand.refs_4_, ...), custom_call_target="tpu_custom_call" | custom-call | flops 1048576 | bytes 1024 | tf_op jit(solution)/shard_map/arrived/pallas_call | solution.py:414
  10.3 0.3 %collective-permute-done.3.refs_12_ = bf16[288,128]{1,0:T(8,128)(2,1)S(1)} collective-permute-done((bf16[288,128]{1,0:T(8,128)(2,1)S(1)}, bf16[288,128]{1,0:T(8,128)(2,1)S(1)}, u32[]{:S(2)}, u32[]{:S(2)}) %collective-permute-start.3) | collective-permute-done | bytes 73760 | tf_op jit(solution)/shard_map/ppermute | solution.py:355
  10.6 0.4 %collective-permute-done.2.refs_11_ = bf16[288,128]{1,0:T(8,128)(2,1)S(1)} collective-permute-done((bf16[288,128]{1,0:T(8,128)(2,1)S(1)}, bf16[288,128]{1,0:T(8,128)(2,1)S(1)}, u32[]{:S(2)}, u32[]{:S(2)}) %collective-permute-start.2) | collective-permute-done | bytes 73760 | tf_op jit(solution)/shard_map/ppermute | solution.py:355
  11.0 2.2 %earlier.1 = (bf16[128,2048]{1,0:T(8,128)(2,1)S(1)}, bf16[48,576]{1,0:T(8,128)(2,1)S(1)}, bf16[4,48]{1,0:T(4,128)(2,1)S(1)}) custom-call(bf16[2048,576]{1,0:T(8,128)(2,1)S(1)} %get-tuple-element.26.refs_0_, f32[2048,128]{1,0:T(8,128)S(1)} %get-tuple-element.27.refs_1_, f32[2048,128]{1,0:T(8,128)S(1)} %get-tuple-element.28.refs_2_, ...), custom_call_target="tpu_custom_call" | custom-call | flops 1048576 | bytes 1024 | tf_op jit(solution)/shard_map/earlier/pallas_call | solution.py:429
  13.2 0.0 collective-permute-done.sent_rows
  13.2 0.9 %store.1 = (bf16[128,2048]{1,0:T(8,128)(2,1)}, bf16[3,16,576]{2,1,0:T(8,128)(2,1)}, bf16[3,4,16]{2,1,0:T(4,128)(2,1)}) custom-call(bf16[128,2048]{1,0:T(8,128)(2,1)S(1)} %get-tuple-element.40.result, bf16[48,576]{1,0:T(8,128)(2,1)S(1)} %get-tuple-element.41.encoded, bf16[4,48]{1,0:T(4,128)(2,1)S(1)} %get-tuple-element.42.scales, ...), custom_call_target="tpu_custom_call" | custom-call | flops 1048576 | bytes 1024 | tf_op jit(solution)/shard_map/store/pallas_call | solution.py:448
  (1 shorter events, 0.0 us)
Async XLA Ops:
  0.6 6.6 %collective-permute-start.1 = (bf16[576,128]{1,0:T(8,128)(2,1)}, bf16[576,128]{1,0:T(8,128)(2,1)S(1)}, u32[]{:S(2)}, u32[]{:S(2)}) collective-permute-start(bf16[576,128]{1,0:T(8,128)(2,1)} %bitcast.5), channel_id=1, source_target_pairs={{0,4},{1,9},{2,6},{3,11},{4,8},{5,13},{6,10},{7,15},{8,12},{9,1},{... | collective-permute-start | bytes 442376 | tf_op jit(solution)/shard_map/ppermute | solution.py:347
  4.8 8.4 %collective-permute-start = (bf16[64,640]{1,0:T(8,128)(2,1)S(1)}, bf16[64,640]{1,0:T(8,128)(2,1)S(1)}, u32[]{:S(2)}, u32[]{:S(2)}) collective-permute-start(bf16[64,640]{1,0:T(8,128)(2,1)S(1)} %get-tuple-element.25), channel_id=1, source_target_pairs={{0,12},{4,0},{8,4},{12,8},{1,13},{5,1},{9,5},{13,9},{2,14},{6,2},{... | collective-permute-start | bytes 245768 | tf_op jit(solution)/shard_map/ppermute | solution.py:411
  7.3 3.3 %collective-permute-start.3 = (bf16[288,128]{1,0:T(8,128)(2,1)S(1)}, bf16[288,128]{1,0:T(8,128)(2,1)S(1)}, u32[]{:S(2)}, u32[]{:S(2)}) collective-permute-start(bf16[288,128]{1,0:T(8,128)(2,1)S(1)} %get-tuple-element.47), channel_id=1, source_target_pairs={{0,1},{1,0},{2,3},{3,2},{4,5},{5,4},{6,7},{7,6},{8,9},{9,8},{10,11... | collective-permute-start | bytes 221192 | tf_op jit(solution)/shard_map/ppermute | solution.py:355
  9.7 1.3 %collective-permute-start.2 = (bf16[288,128]{1,0:T(8,128)(2,1)S(1)}, bf16[288,128]{1,0:T(8,128)(2,1)S(1)}, u32[]{:S(2)}, u32[]{:S(2)}) collective-permute-start(bf16[288,128]{1,0:T(8,128)(2,1)S(1)} %get-tuple-element.48), channel_id=1, source_target_pairs={{0,1},{1,0},{2,3},{3,2},{4,5},{5,4},{6,7},{7,6},{8,9},{9,8},{10,11... | collective-permute-start | bytes 221192 | tf_op jit(solution)/shard_map/ppermute | solution.py:355

commit v23 on v22

--- a/solution.py
+++ b/solution.py
@@ -234,8 +234,9 @@
 
 
 def earlier_kernel(count, group, *refs):
-    combined, own_result, peaks, totals, value_expand, bias, fetched_values, picked, found, filled = refs[:10]
-    arrived, (result, encoded, scales, keys, latents) = refs[10:-5], refs[-5:]
+    combined, own_result, peaks, totals, value_expand, bias, fetched_values, picked, found, filled, sent_rows = refs[:11]
+    arrived = refs[11:-9]
+    attended, page_cache, page_scales, keys, latents, result, cache_buf, scale_buf, sems = refs[-9:]
     rows, width = bias.shape
     heads = value_expand.shape[0]
     steps = heads // group
@@ -289,7 +290,26 @@
             rotary = swapped_block(i)[LAT:]
             rotary_rows = rotary_rows + lax.dot_general(choice, rotary, NT, preferred_element_type=jnp.float32)
         every = jnp.concatenate([latent_rows, rotary_rows], axis=1)
-        encoded[...], scales[...] = encode(every, filled[:1, :every.shape[0]])
+        kept = every.shape[0]
+        encoded, scales = encode(every, filled[:1, :kept])
+        scales = scales + sent_rows[kept:kept + NBLK, :kept]
+        for c in range(page_cache.shape[0]):
+            part = slice(c * PAGE, (c + 1) * PAGE)
+            cache_buf[c] = encoded[part, :] + sent_rows[part, :ROW]
+            scale_buf[c] = scales[:, part]
+
+    def send(g):
+        at = pl.ds(g * group * VDIM, group * VDIM)
+        return pltpu.make_async_copy(result.at[:, at], attended.at[:, at], sems.at[g])
+
+    cache_copies = [
+        pltpu.make_async_copy(cache_buf, page_cache, sems.at[steps]),
+        pltpu.make_async_copy(scale_buf, page_scales, sems.at[steps + 1]),
+    ]
+
+    def send_most():
+        for copy in cache_copies + [send(g) for g in range(steps - 1)]:
+            copy.start()
 
     for i in range(len(arrived) // (1 + SWAP)):
         latents[i * rows:(i + 1) * rows, :] = swapped_block(i)[:LAT].T
@@ -300,6 +320,7 @@
             part = slice(h * rows, (h + 1) * rows)
             result[:, h * VDIM:(h + 1) * VDIM] = (own_result[part, :] / totals[part, :]).astype(jnp.bfloat16)
         encode_found()
+        send_most()
 
     @pl.when(lax.axis_index("cp") > 0)
     def _():
@@ -313,30 +334,16 @@
                 scores[step] = score(step)
             if step == 2:
                 encode_found()
+            if step == steps + 1:
+                send_most()
             if 0 <= step - 2:
                 finish(step - 2, *weights.pop(step - 2), values.pop(step - 2))
             if 0 <= step - 1 < steps:
                 values[step - 1] = value(step - 1)
                 weights[step - 1] = weigh(step - 1, scores.pop(step - 1))
 
-
-def store_kernel(result, encoded, scales, sent_rows, attended, page_cache, page_scales, cache_buf, scale_buf, sems):
-    count = sems.shape[0] - 2
-    wide = result.shape[1] // count
-    copies = []
-    for i in range(count):
-        some = pl.ds(i * wide, wide)
-        copies.append(pltpu.make_async_copy(result.at[:, some], attended.at[:, some], sems.at[i]))
-        copies[-1].start()
-    kept = encoded.shape[0]
-    for c in range(page_cache.shape[0]):
-        part = slice(c * PAGE, (c + 1) * PAGE)
-        cache_buf[c] = encoded[part, :] + sent_rows[part, :ROW]
-        scale_buf[c] = (scales[...] + sent_rows[kept:kept + NBLK, :kept])[:, part]
-    for i, (source, target) in enumerate(((cache_buf, page_cache), (scale_buf, page_scales))):
-        copies.append(pltpu.make_async_copy(source, target, sems.at[count + i]))
-        copies[-1].start()
-    for copy in copies:
+    send(steps - 1).start()
+    for copy in cache_copies + [send(g) for g in range(steps)]:
         copy.wait()
 
 
@@ -425,28 +432,9 @@
     )(picked, own_copy, value_copy, *blocks)
 
     group = 4 if count <= 4 else 2
-    operands = (combined, result, peaks, totals, value_copy, bias, fetched_values, picked, found, filled, *pieces)
-    attended, encoded, scales = pl.pallas_call(
+    operands = (combined, result, peaks, totals, value_copy, bias, fetched_values, picked, found, filled, sent_rows, *pieces)
+    attended, page_cache, page_scales = pl.pallas_call(
         functools.partial(earlier_kernel, count, group),
-        in_specs=[vmem] * len(operands),
-        out_specs=[vmem] * 3,
-        out_shape=[
-            jax.ShapeDtypeStruct((rows, heads * VDIM), jnp.bfloat16),
-            jax.ShapeDtypeStruct((kept, ROW), jnp.bfloat16),
-            jax.ShapeDtypeStruct((NBLK, kept), jnp.bfloat16),
-        ],
-        scratch_shapes=[
-            pltpu.VMEM((ROW, count * rows), jnp.bfloat16),
-            pltpu.VMEM((len(blocks) * rows, LAT), jnp.bfloat16),
-        ],
-        cost_estimate=pl.CostEstimate(flops=2**20, bytes_accessed=2**10, transcendentals=0),
-        compiler_params=params,
-        name="earlier",
-    )(*operands)
-    sent_rows, attended = lax.optimization_barrier((sent_rows, attended))
-    operands = (attended, encoded, scales, sent_rows)
-    attended, page_cache, page_scales = pl.pallas_call(
-        store_kernel,
         in_specs=[vmem] * len(operands),
         out_specs=[hbm] * 3,
         out_shape=[
@@ -455,13 +443,16 @@
             jax.ShapeDtypeStruct((slot_count, NBLK, PAGE), jnp.bfloat16),
         ],
         scratch_shapes=[
+            pltpu.VMEM((ROW, count * rows), jnp.bfloat16),
+            pltpu.VMEM((len(blocks) * rows, LAT), jnp.bfloat16),
+            pltpu.VMEM((rows, heads * VDIM), jnp.bfloat16),
             pltpu.VMEM((slot_count, PAGE, ROW), jnp.bfloat16),
             pltpu.VMEM((slot_count, NBLK, PAGE), jnp.bfloat16),
-            pltpu.SemaphoreType.DMA((4 + 2,)),
+            pltpu.SemaphoreType.DMA((heads // group + 2,)),
         ],
         cost_estimate=pl.CostEstimate(flops=2**20, bytes_accessed=2**10, transcendentals=0),
         compiler_params=params,
-        name="store",
+        name="earlier",
     )(*operands)
     page_cache = page_cache.reshape(1, 1, slot_count, PAGE, ROW)
     page_scales = page_scales.transpose(0, 2, 1).reshape(1, 1, slot_count, PAGE, NBLK)

time: 14.2 us -> 14.5 us (1.021)
  the two profiles are of different devices: /device:TPU:17 before, /device:TPU:0 now
where the time goes in v23:
time: 14.5 us; the launch traced here: 14.2 us
  Pallas kernels  6.04 us (42%)
  starting transfers between devices  5.76 us (40%)
  waiting for transfers between devices  1.73 us (12%)
  between operations  0.66 us (5%)
    pallas_call x1, Pallas kernels, on_device(): pl.pallas_call(functools.partial(own_kernel, n_cp, count, chunks, group,...  4.05 us
    ppermute x1, starting transfers between devices, fetch(): blocks.append(lax.ppermute(own, ('cp', 'dec'), pairs))  3.08 us
    ppermute x1, starting transfers between devices, on_device(): lax.ppermute(sent_rows, 'cp', [(c, (c + n_cp - 1) % n_cp) for c in range(...  2.11 us
    ppermute x1, waiting for transfers between devices, on_device(): lax.ppermute(sent_rows, 'cp', [(c, (c + n_cp - 1) % n_cp) for c in range(...  1.66 us
    pallas_call x1, Pallas kernels, on_device(): pl.pallas_call(functools.partial(earlier_kernel, count, group), in_specs=...  1.45 us
    ppermute x2, starting transfers between devices, swap(): lax.ppermute(part, 'dec', [(e, e ^ 1) for e in range(n_dec)])  0.58 us
    pallas_call x1, Pallas kernels, on_device(): pl.pallas_call(functools.partial(arrived_kernel, count // 2), in_specs=[v...  0.54 us
  transfers between devices with their start and end apart: 4, of which 2 were waited for; matrix products, arithmetic and copies ran while one was open for 0% of the time, Pallas kernels for 32%

profile of v23, /device:TPU:0, one launch (start us, length us, event | category | flops | bytes accessed | tf_op | source)
XLA Modules:
  0.0 14.2 jit_solution(13325166452594278731)
XLA Ops:
  0.6 3.1 %collective-permute-start = (bf16[576,128]{1,0:T(8,128)(2,1)}, bf16[576,128]{1,0:T(8,128)(2,1)S(1)}, u32[]{:S(2)}, u32[]{:S(2)}) collective-permute-start(bf16[576,128]{1,0:T(8,128)(2,1)} %bitcast.5), channel_id=1, source_target_pairs={{0,4},{1,9},{2,6},{3,11},{4,8},{5,13},{6,10},{7,15},{8,12},{9,1},{... | collective-permute-start | bytes 442376 | tf_op jit(solution)/shard_map/ppermute | solution.py:354
  3.7 4.1 %own.1 = (bf16[2048,576]{1,0:T(8,128)(2,1)S(1)}, f32[2048,128]{1,0:T(8,128)S(1)}, f32[2048,128]{1,0:T(8,128)S(1)}, f32[2048,128]{1,0:T(8,128)S(1)}, bf16[64,640]...) custom-call(s32[2]{0:T(128)} %refs_0_.1, ...), custom_call_target="tpu_custom_call" | custom-call | flops 905969664 | bytes 5242880 | tf_op jit(solution)/shard_map/own/pallas_call | solution.py:385
  7.8 2.1 %collective-permute-start.1 = (bf16[64,640]{1,0:T(8,128)(2,1)S(1)}, bf16[64,640]{1,0:T(8,128)(2,1)S(1)}, u32[]{:S(2)}, u32[]{:S(2)}) collective-permute-start(bf16[64,640]{1,0:T(8,128)(2,1)S(1)} %get-tuple-element.33), channel_id=1, source_target_pairs={{0,12},{4,0},{8,4},{12,8},{1,13},{5,1},{9,5},{13,9},{2,14},{6,2},{... | collective-permute-start | bytes 245768 | tf_op jit(solution)/shard_map/ppermute | solution.py:418
  9.9 0.1 collective-permute-done.refs_0_.refs_11_
  10.0 0.3 %collective-permute-start.3 = (bf16[288,128]{1,0:T(8,128)(2,1)S(1)}, bf16[288,128]{1,0:T(8,128)(2,1)S(1)}, u32[]{:S(2)}, u32[]{:S(2)}) collective-permute-start(bf16[288,128]{1,0:T(8,128)(2,1)S(1)} %get-tuple-element.37), channel_id=1, source_target_pairs={{0,1},{1,0},{2,3},{3,2},{4,5},{5,4},{6,7},{7,6},{8,9},{9,8},{10,11... | collective-permute-start | bytes 221192 | tf_op jit(solution)/shard_map/ppermute | solution.py:362
  10.3 0.3 %collective-permute-start.2 = (bf16[288,128]{1,0:T(8,128)(2,1)S(1)}, bf16[288,128]{1,0:T(8,128)(2,1)S(1)}, u32[]{:S(2)}, u32[]{:S(2)}) collective-permute-start(bf16[288,128]{1,0:T(8,128)(2,1)S(1)} %get-tuple-element.38), channel_id=1, source_target_pairs={{0,1},{1,0},{2,3},{3,2},{4,5},{5,4},{6,7},{7,6},{8,9},{9,8},{10,11... | collective-permute-start | bytes 221192 | tf_op jit(solution)/shard_map/ppermute | solution.py:362
  10.5 0.5 %arrived.1 = (f32[48,576]{1,0:T(8,128)S(1)}, bf16[128,2048]{1,0:T(8,128)(2,1)S(1)}) custom-call(bf16[48,384]{1,0:T(8,128)(2,1)S(1)} %get-tuple-element.27.picked.refs_7_, bf16[576,128]{1,0:T(8,128)(2,1)S(1)} %get-tuple-element.28.own, bf16[16,512,128]{2,1,0:T(8,128)(2,1)S(1)} %get-tuple-element.24.value_expand.refs_4_, ...), custom_call_target="tpu_custom_call" | custom-call | flops 1048576 | bytes 1024 | tf_op jit(solution)/shard_map/arrived/pallas_call | solution.py:421
  11.1 1.7 %collective-permute-done.1.refs_10_ = bf16[64,640]{1,0:T(8,128)(2,1)S(1)} collective-permute-done((bf16[64,640]{1,0:T(8,128)(2,1)S(1)}, bf16[64,640]{1,0:T(8,128)(2,1)S(1)}, u32[]{:S(2)}, u32[]{:S(2)}) %collective-permute-start.1) | collective-permute-done | bytes 81952 | tf_op jit(solution)/shard_map/ppermute | solution.py:418
  12.7 0.0 collective-permute-done.3.refs_13_
  12.7 0.0 collective-permute-done.2.refs_12_
  12.7 1.4 %earlier.1 = (bf16[128,2048]{1,0:T(8,128)(2,1)}, bf16[3,16,576]{2,1,0:T(8,128)(2,1)}, bf16[3,4,16]{2,1,0:T(4,128)(2,1)}) custom-call(bf16[2048,576]{1,0:T(8,128)(2,1)S(1)} %get-tuple-element.20.refs_0_, f32[2048,128]{1,0:T(8,128)S(1)} %get-tuple-element.21.refs_1_, f32[2048,128]{1,0:T(8,128)S(1)} %get-tuple-element.22.refs_2_, ...), custom_call_target="tpu_custom_call" | custom-call | flops 1048576 | bytes 1024 | tf_op jit(solution)/shard_map/earlier/pallas_call | solution.py:436
  (1 shorter events, 0.0 us)
Async XLA Ops:
  0.6 9.3 %collective-permute-start = (bf16[576,128]{1,0:T(8,128)(2,1)}, bf16[576,128]{1,0:T(8,128)(2,1)S(1)}, u32[]{:S(2)}, u32[]{:S(2)}) collective-permute-start(bf16[576,128]{1,0:T(8,128)(2,1)} %bitcast.5), channel_id=1, source_target_pairs={{0,4},{1,9},{2,6},{3,11},{4,8},{5,13},{6,10},{7,15},{8,12},{9,1},{... | collective-permute-start | bytes 442376 | tf_op jit(solution)/shard_map/ppermute | solution.py:354
  7.8 5.0 %collective-permute-start.1 = (bf16[64,640]{1,0:T(8,128)(2,1)S(1)}, bf16[64,640]{1,0:T(8,128)(2,1)S(1)}, u32[]{:S(2)}, u32[]{:S(2)}) collective-permute-start(bf16[64,640]{1,0:T(8,128)(2,1)S(1)} %get-tuple-element.33), channel_id=1, source_target_pairs={{0,12},{4,0},{8,4},{12,8},{1,13},{5,1},{9,5},{13,9},{2,14},{6,2},{... | collective-permute-start | bytes 245768 | tf_op jit(solution)/shard_map/ppermute | solution.py:418
  10.0 2.8 %collective-permute-start.3 = (bf16[288,128]{1,0:T(8,128)(2,1)S(1)}, bf16[288,128]{1,0:T(8,128)(2,1)S(1)}, u32[]{:S(2)}, u32[]{:S(2)}) collective-permute-start(bf16[288,128]{1,0:T(8,128)(2,1)S(1)} %get-tuple-element.37), channel_id=1, source_target_pairs={{0,1},{1,0},{2,3},{3,2},{4,5},{5,4},{6,7},{7,6},{8,9},{9,8},{10,11... | collective-permute-start | bytes 221192 | tf_op jit(solution)/shard_map/ppermute | solution.py:362
  10.3 2.5 %collective-permute-start.2 = (bf16[288,128]{1,0:T(8,128)(2,1)S(1)}, bf16[288,128]{1,0:T(8,128)(2,1)S(1)}, u32[]{:S(2)}, u32[]{:S(2)}) collective-permute-start(bf16[288,128]{1,0:T(8,128)(2,1)S(1)} %get-tuple-element.38), channel_id=1, source_target_pairs={{0,1},{1,0},{2,3},{3,2},{4,5},{5,4},{6,7},{7,6},{8,9},{9,8},{10,11... | collective-permute-start | bytes 221192 | tf_op jit(solution)/shard_map/ppermute | solution.py:362

commit v24 on v22

--- a/solution.py
+++ b/solution.py
@@ -235,7 +235,7 @@
 
 def earlier_kernel(count, group, *refs):
     combined, own_result, peaks, totals, value_expand, bias, fetched_values, picked, found, filled = refs[:10]
-    arrived, (result, encoded, scales, keys, latents) = refs[10:-5], refs[-5:]
+    arrived, (result, encoded, scales, latents) = refs[10:-4], refs[-4:]
     rows, width = bias.shape
     heads = value_expand.shape[0]
     steps = heads // group
@@ -245,7 +245,10 @@
         return slice(at, at + group * rows)
 
     def score(g):
-        scores = jnp.dot(combined[span(g), :], keys[...], preferred_element_type=jnp.float32)
+        blocks = []
+        for i in range(count // 2):
+            blocks += [arrived[i * (1 + SWAP)][...], swapped_block(i)]
+        scores = jnp.dot(combined[span(g), :], jnp.concatenate(blocks, axis=1), preferred_element_type=jnp.float32)
         return (scores.reshape(group, rows, width) + bias[...][None]).reshape(group * rows, width)
 
     def weigh(g, scores):
@@ -303,10 +306,6 @@
 
     @pl.when(lax.axis_index("cp") > 0)
     def _():
-        for i in range(count // 2):
-            at = 2 * i * rows
-            keys[:, at:at + rows] = arrived[i * (1 + SWAP)][...]
-            keys[:, at + rows:at + 2 * rows] = swapped_block(i)
         scores, values, weights = {}, {}, {}
         for step in range(steps + 2):
             if step < steps:
@@ -436,7 +435,6 @@
             jax.ShapeDtypeStruct((NBLK, kept), jnp.bfloat16),
         ],
         scratch_shapes=[
-            pltpu.VMEM((ROW, count * rows), jnp.bfloat16),
             pltpu.VMEM((len(blocks) * rows, LAT), jnp.bfloat16),
         ],
         cost_estimate=pl.CostEstimate(flops=2**20, bytes_accessed=2**10, transcendentals=0),
@@ -457,7 +455,7 @@
         scratch_shapes=[
             pltpu.VMEM((slot_count, PAGE, ROW), jnp.bfloat16),
             pltpu.VMEM((slot_count, NBLK, PAGE), jnp.bfloat16),
-            pltpu.SemaphoreType.DMA((4 + 2,)),
+            pltpu.SemaphoreType.DMA((2 + 2,)),
         ],
         cost_estimate=pl.CostEstimate(flops=2**20, bytes_accessed=2**10, transcendentals=0),
         compiler_params=params,

time: 14.2 us -> 14.2 us (level)
  no operation moved by 1% of the time
where the time goes in v24:
time: 14.2 us; the launch traced here: 14.1 us
  Pallas kernels  7.66 us (54%)
  starting transfers between devices  5.06 us (36%)
  between operations  0.68 us (5%)
  waiting for transfers between devices  0.64 us (5%)
    pallas_call x1, Pallas kernels, on_device(): pl.pallas_call(functools.partial(own_kernel, n_cp, count, chunks, group,...  4.07 us
    ppermute x1, starting transfers between devices, on_device(): lax.ppermute(sent_rows, 'cp', [(c, (c + n_cp - 1) % n_cp) for c in range(...  2.5 us
    ppermute x2, starting transfers between devices, swap(): lax.ppermute(part, 'dec', [(e, e ^ 1) for e in range(n_dec)])  2.5 us
    pallas_call x1, Pallas kernels, on_device(): pl.pallas_call(functools.partial(earlier_kernel, count, group), in_specs=...  2.22 us
    pallas_call x1, Pallas kernels, on_device(): pl.pallas_call(store_kernel, in_specs=[vmem] * len(operands), out_specs=[...  0.84 us
    ppermute x2, waiting for transfers between devices, swap(): lax.ppermute(part, 'dec', [(e, e ^ 1) for e in range(n_dec)])  0.64 us
    pallas_call x1, Pallas kernels, on_device(): pl.pallas_call(functools.partial(arrived_kernel, count // 2), in_specs=[v...  0.54 us
  transfers between devices with their start and end apart: 4, of which 2 were waited for; matrix products, arithmetic and copies ran while one was open for 0% of the time, Pallas kernels for 48%

profile of v24, /device:TPU:17, one launch (start us, length us, event | category | flops | bytes accessed | tf_op | source)
XLA Modules:
  0.0 14.1 jit_solution(12587161245428190684)
XLA Ops:
  0.6 0.1 collective-permute-start.1
  0.7 4.1 %own.1 = (bf16[2048,576]{1,0:T(8,128)(2,1)S(1)}, f32[2048,128]{1,0:T(8,128)S(1)}, f32[2048,128]{1,0:T(8,128)S(1)}, f32[2048,128]{1,0:T(8,128)S(1)}, bf16[64,640]...) custom-call(s32[2]{0:T(128)} %refs_0_.1, ...), custom_call_target="tpu_custom_call" | custom-call | flops 905969664 | bytes 5242880 | tf_op jit(solution)/shard_map/own/pallas_call | solution.py:377
  4.8 2.5 %collective-permute-start = (bf16[64,640]{1,0:T(8,128)(2,1)S(1)}, bf16[64,640]{1,0:T(8,128)(2,1)S(1)}, u32[]{:S(2)}, u32[]{:S(2)}) collective-permute-start(bf16[64,640]{1,0:T(8,128)(2,1)S(1)} %get-tuple-element.25), channel_id=1, source_target_pairs={{0,12},{4,0},{8,4},{12,8},{1,13},{5,1},{9,5},{13,9},{2,14},{6,2},{... | collective-permute-start | bytes 245768 | tf_op jit(solution)/shard_map/ppermute | solution.py:410
  7.3 0.0 collective-permute-done.1.refs_0_.refs_10_
  7.3 2.4 %collective-permute-start.3 = (bf16[288,128]{1,0:T(8,128)(2,1)S(1)}, bf16[288,128]{1,0:T(8,128)(2,1)S(1)}, u32[]{:S(2)}, u32[]{:S(2)}) collective-permute-start(bf16[288,128]{1,0:T(8,128)(2,1)S(1)} %get-tuple-element.47), channel_id=1, source_target_pairs={{0,1},{1,0},{2,3},{3,2},{4,5},{5,4},{6,7},{7,6},{8,9},{9,8},{10,11... | collective-permute-start | bytes 221192 | tf_op jit(solution)/shard_map/ppermute | solution.py:354
  9.7 0.1 collective-permute-start.2
  9.8 0.5 %arrived.1 = (f32[48,576]{1,0:T(8,128)S(1)}, bf16[128,2048]{1,0:T(8,128)(2,1)S(1)}) custom-call(bf16[48,384]{1,0:T(8,128)(2,1)S(1)} %get-tuple-element.33.picked.refs_7_, bf16[576,128]{1,0:T(8,128)(2,1)S(1)} %get-tuple-element.34.own, bf16[16,512,128]{2,1,0:T(8,128)(2,1)S(1)} %get-tuple-element.30.value_expand.refs_4_, ...), custom_call_target="tpu_custom_call" | custom-call | flops 1048576 | bytes 1024 | tf_op jit(solution)/shard_map/arrived/pallas_call | solution.py:413
  10.3 0.3 %collective-permute-done.3.refs_12_ = bf16[288,128]{1,0:T(8,128)(2,1)S(1)} collective-permute-done((bf16[288,128]{1,0:T(8,128)(2,1)S(1)}, bf16[288,128]{1,0:T(8,128)(2,1)S(1)}, u32[]{:S(2)}, u32[]{:S(2)}) %collective-permute-start.3) | collective-permute-done | bytes 73760 | tf_op jit(solution)/shard_map/ppermute | solution.py:354
  10.6 0.4 %collective-permute-done.2.refs_11_ = bf16[288,128]{1,0:T(8,128)(2,1)S(1)} collective-permute-done((bf16[288,128]{1,0:T(8,128)(2,1)S(1)}, bf16[288,128]{1,0:T(8,128)(2,1)S(1)}, u32[]{:S(2)}, u32[]{:S(2)}) %collective-permute-start.2) | collective-permute-done | bytes 73760 | tf_op jit(solution)/shard_map/ppermute | solution.py:354
  11.0 2.2 %earlier.1 = (bf16[128,2048]{1,0:T(8,128)(2,1)S(1)}, bf16[48,576]{1,0:T(8,128)(2,1)S(1)}, bf16[4,48]{1,0:T(4,128)(2,1)S(1)}) custom-call(bf16[2048,576]{1,0:T(8,128)(2,1)S(1)} %get-tuple-element.26.refs_0_, f32[2048,128]{1,0:T(8,128)S(1)} %get-tuple-element.27.refs_1_, f32[2048,128]{1,0:T(8,128)S(1)} %get-tuple-element.28.refs_2_, ...), custom_call_target="tpu_custom_call" | custom-call | flops 1048576 | bytes 1024 | tf_op jit(solution)/shard_map/earlier/pallas_call | solution.py:428
  13.2 0.0 collective-permute-done.sent_rows
  13.2 0.8 %store.1 = (bf16[128,2048]{1,0:T(8,128)(2,1)}, bf16[3,16,576]{2,1,0:T(8,128)(2,1)}, bf16[3,4,16]{2,1,0:T(4,128)(2,1)}) custom-call(bf16[128,2048]{1,0:T(8,128)(2,1)S(1)} %get-tuple-element.40.result, bf16[48,576]{1,0:T(8,128)(2,1)S(1)} %get-tuple-element.41.encoded, bf16[4,48]{1,0:T(4,128)(2,1)S(1)} %get-tuple-element.42.scales, ...), custom_call_target="tpu_custom_call" | custom-call | flops 1048576 | bytes 1024 | tf_op jit(solution)/shard_map/store/pallas_call | solution.py:446
  (1 shorter events, 0.0 us)
Async XLA Ops:
  0.6 6.6 %collective-permute-start.1 = (bf16[576,128]{1,0:T(8,128)(2,1)}, bf16[576,128]{1,0:T(8,128)(2,1)S(1)}, u32[]{:S(2)}, u32[]{:S(2)}) collective-permute-start(bf16[576,128]{1,0:T(8,128)(2,1)} %bitcast.5), channel_id=1, source_target_pairs={{0,4},{1,9},{2,6},{3,11},{4,8},{5,13},{6,10},{7,15},{8,12},{9,1},{... | collective-permute-start | bytes 442376 | tf_op jit(solution)/shard_map/ppermute | solution.py:346
  4.8 8.4 %collective-permute-start = (bf16[64,640]{1,0:T(8,128)(2,1)S(1)}, bf16[64,640]{1,0:T(8,128)(2,1)S(1)}, u32[]{:S(2)}, u32[]{:S(2)}) collective-permute-start(bf16[64,640]{1,0:T(8,128)(2,1)S(1)} %get-tuple-element.25), channel_id=1, source_target_pairs={{0,12},{4,0},{8,4},{12,8},{1,13},{5,1},{9,5},{13,9},{2,14},{6,2},{... | collective-permute-start | bytes 245768 | tf_op jit(solution)/shard_map/ppermute | solution.py:410
  7.3 3.3 %collective-permute-start.3 = (bf16[288,128]{1,0:T(8,128)(2,1)S(1)}, bf16[288,128]{1,0:T(8,128)(2,1)S(1)}, u32[]{:S(2)}, u32[]{:S(2)}) collective-permute-start(bf16[288,128]{1,0:T(8,128)(2,1)S(1)} %get-tuple-element.47), channel_id=1, source_target_pairs={{0,1},{1,0},{2,3},{3,2},{4,5},{5,4},{6,7},{7,6},{8,9},{9,8},{10,11... | collective-permute-start | bytes 221192 | tf_op jit(solution)/shard_map/ppermute | solution.py:354
  9.7 1.3 %collective-permute-start.2 = (bf16[288,128]{1,0:T(8,128)(2,1)S(1)}, bf16[288,128]{1,0:T(8,128)(2,1)S(1)}, u32[]{:S(2)}, u32[]{:S(2)}) collective-permute-start(bf16[288,128]{1,0:T(8,128)(2,1)S(1)} %get-tuple-element.48), channel_id=1, source_target_pairs={{0,1},{1,0},{2,3},{3,2},{4,5},{5,4},{6,7},{7,6},{8,9},{9,8},{10,11... | collective-permute-start | bytes 221192 | tf_op jit(solution)/shard_map/ppermute | solution.py:354
